TPU v7x, 32 devices: a whole 2x2x4 slice. The times are simulated.
32 devices in a mesh: dp: 4 (over x, core), ctx: 8 (over z, y).
Axes of the slice: x: 2, y: 2, z: 4, core: 2. Of those that a mesh axis runs over, the one named last changes fastest.
Arguments:
- tokens: bfloat16 [4, 1024, 512], P('dp', 'ctx'), may hold values from -6 to 6
- mixer_gain: float32 [512], P(('dp', 'ctx')), may hold values from 0.1 to 1.9
- in_proj: float32 [512, 2048], P(('dp', 'ctx')), may hold values from -0.25 to 0.25
- conv_weight: float32 [1024, 4], P(('dp', 'ctx')), may hold values from -3 to 3
- conv_bias: float32 [1024], P(('dp', 'ctx')), may hold values from -3 to 3
- x_proj: float32 [1024, 64], P(('dp', 'ctx')), may hold values from -0.1875 to 0.1875
- dt_proj: float32 [32, 1024], P(None, ('dp', 'ctx')), may hold values from -1 to 1
- dt_bias: float32 [1024], P(('dp', 'ctx')), may hold values from -6 to 0
- a_log: float32 [1024, 16], P(('dp', 'ctx')), may hold values from -4 to 1
- d_skip: float32 [1024], P(('dp', 'ctx')), may hold values from 0.5 to 1.5
- out_proj: float32 [1024, 512], P(('dp', 'ctx')), may hold values from -0.75 to 0.75
- attn_gain: float32 [512], P(('dp', 'ctx')), may hold values from 0.1 to 1.9
- w_query: float32 [512, 512], P(('dp', 'ctx')), may hold values from -0.375 to 0.375
- w_key: float32 [512, 512], P(('dp', 'ctx')), may hold values from -0.375 to 0.375
- w_value: float32 [512, 512], P(('dp', 'ctx')), may hold values from -0.25 to 0.25
- w_output: float32 [512, 512], P(('dp', 'ctx')), may hold values from -2 to 2
- cotangent: bfloat16 [4, 1024, 512], P('dp', 'ctx'), may hold values from -6 to 6
Outputs:
- result: bfloat16 [4, 1024, 512], P('dp', 'ctx')
- grad_tokens: bfloat16 [4, 1024, 512], P('dp', 'ctx')
- grad_mixer_gain: float32 [512], P(('dp', 'ctx'))
- grad_in_proj: float32 [512, 2048], P(('dp', 'ctx'))
- grad_conv_weight: float32 [1024, 4], P(('dp', 'ctx'))
- grad_conv_bias: float32 [1024], P(('dp', 'ctx'))
- grad_x_proj: float32 [1024, 64], P(('dp', 'ctx'))
- grad_dt_proj: float32 [32, 1024], P(None, ('dp', 'ctx'))
- grad_dt_bias: float32 [1024], P(('dp', 'ctx'))
- grad_a_log: float32 [1024, 16], P(('dp', 'ctx'))
- grad_d_skip: float32 [1024], P(('dp', 'ctx'))
- grad_out_proj: float32 [1024, 512], P(('dp', 'ctx'))
- grad_attn_gain: float32 [512], P(('dp', 'ctx'))
- grad_w_query: float32 [512, 512], P(('dp', 'ctx'))
- grad_w_key: float32 [512, 512], P(('dp', 'ctx'))
- grad_w_value: float32 [512, 512], P(('dp', 'ctx'))
- grad_w_output: float32 [512, 512], P(('dp', 'ctx'))
All inputs are finite; a program needn't handle non-finite values.
Results may differ from a plain program's by a relative error of at most 0.04.
The roundings to bfloat16 on the way count: a program that leaves them out, or rounds other values in their place, can miss the bound.
Values may be sent and summed in bfloat16 or wider, within the bound.
No kernel may reach another device: no remote copies, remote signals or barrier semaphores. Data moves between devices by JAX's collectives and lax.ppermute only.
A program may use at most 192 MiB of HBM per device.

v0:
```python
import functools

import jax
import jax.numpy as jnp
from jax import lax
from jax.experimental import pallas as pl
from jax.experimental.pallas import tpu as pltpu
from jax.sharding import PartitionSpec as P

D = 512
E = 1024
NS = 16
RANK = 32
KW = 4
HEADS = 8
HDIM = 64
LG = 8
HALO = 16
BLOCKS = 32
ALL = ("dp", "ctx")
EPS = 1e-05
LOG2E = 1.4426950408889634
LN2 = 0.6931471805599453
F32 = jnp.float32
BF16 = jnp.bfloat16
VM = pl.BlockSpec(memory_space=pltpu.VMEM)

Z_MASKS = (0, 4, 2, 6)
XY_MASKS = (0, 1, 16, 17)
CORE = 8
HALF_MASKS = tuple(xy | zz for xy in XY_MASKS for zz in Z_MASKS)
FULL_MASKS = HALF_MASKS + tuple(mask | CORE for mask in HALF_MASKS)
CHUNK_MASKS = tuple((16 if c & 1 else 0) | (1 if c & 2 else 0) | (8 if c & 4 else 0) for c in range(8))

ROW_X = 0
ROW_DT = 64
ROW_A = 96
ROW_CW = 112
ROW_CB = 116
ROW_DB = 117
ROW_SK = 118
ROW_G1 = 119
ROW_G2 = 120
SMALL_ROWS = 128


ANY = pl.BlockSpec(memory_space=pl.ANY)
FAR = pl.BlockSpec(memory_space=pltpu.HBM)
WHOLE = pl.BlockSpec()


def run(kernel, ins, outs, scratch=(), limit=12, raw=(), far=(), after=(), final=False, us=2):
    first, count = len(ins) + len(raw) + len(far), len(after)

    def inner(*refs):
        kernel(*refs[:first], *refs[first + count :])

    return pl.pallas_call(
        inner,
        out_shape=[jax.ShapeDtypeStruct(shape, dtype) for shape, dtype in outs],
        in_specs=[VM] * len(ins) + [ANY] * len(raw) + [FAR] * len(far) + [ANY] * count,
        out_specs=[WHOLE if final else VM] * len(outs),
        scratch_shapes=list(scratch),
        compiler_params=pltpu.CompilerParams(vmem_limit_bytes=limit * 2**20),
        cost_estimate=pl.CostEstimate(flops=int(us * 1e3), bytes_accessed=int(us * 3e3), transcendentals=0),
    )(*ins, *raw, *far, *after)


def nn(left, right):
    return lax.dot_general(left, right, (((1,), (0,)), ((), ())), preferred_element_type=F32)


def nt(left, right):
    return lax.dot_general(left, right, (((1,), (1,)), ((), ())), preferred_element_type=F32)


def tn(left, right):
    return lax.dot_general(left, right, (((0,), (0,)), ((), ())), preferred_element_type=F32)


def sigmoid(value):
    return 1.0 / (1.0 + jnp.exp(-value))


class Plan:
    def __init__(self, mesh):
        self.dp, self.ctx = mesh.shape["dp"], mesh.shape["ctx"]
        self.fast = (self.dp, self.ctx) == (4, 8)
        self.chunks = self.ctx
        if self.fast:
            self.grad_masks = (FULL_MASKS[:16], FULL_MASKS[16:])
        else:
            self.grad_masks = (tuple(range(BLOCKS)),)

    def place(self, seq, chunk):
        return CHUNK_MASKS[chunk] | ((0, 2, 1, 3)[seq] << 1)

    def me(self):
        if self.fast:
            return lax.axis_index("dp") * 8 + lax.axis_index("ctx")
        return 0

    def chunk(self):
        if self.fast:
            lin = lax.axis_index("dp") * 8 + lax.axis_index("ctx")
            return ((lin >> 4) & 1) + (lin & 1) * 2 + ((lin >> 3) & 1) * 4
        return lax.axis_index("ctx")

    def swap(self, value):
        if self.fast:
            groups = [[self.place(s, c) for c in range(8)] for s in range(4)]
            return lax.all_to_all(value, ALL, 0, 0, tiled=True, axis_index_groups=groups)
        return lax.all_to_all(value, "ctx", 0, 0, tiled=True)


def send(value, mask):
    return lax.ppermute(value, ALL, [(i, i ^ mask) for i in range(32)])


def start_blocks(target, pieces, masks, me, sem, row_in, rows, first, cols):
    per_piece = len(masks) // len(pieces)
    height = pieces[0].shape[0] // per_piece
    for i, piece in enumerate(pieces):
        for k in range(per_piece):
            block = me ^ masks[i * per_piece + k]
            pltpu.make_async_copy(
                piece.at[pl.ds(k * height + row_in, rows), pl.ds(first, cols)],
                target.at[pl.ds(pl.multiple_of(block * rows, 16), rows), :],
                sem,
            ).start()


def wait_whole(target, sem):
    pltpu.make_async_copy(target, target, sem).wait()


def swap_blocks(value, me):
    rows, lanes = value.shape
    for bit in (16, 8, 4):
        half = bit * 32
        parts = [value[:, i : i + half] for i in range(0, lanes, half)]
        other = jnp.concatenate([parts[i ^ 1] for i in range(len(parts))], axis=1)
        value = jnp.where((me & bit) != 0, other, value)
    groups = []
    odd = (lax.broadcasted_iota(jnp.int32, (rows, 128), 1) & 32) != 0
    for i in range(0, lanes, 128):
        part = value[:, i : i + 128]
        part = jnp.where((me & 2) != 0, pltpu.roll(part, 64, 1), part)
        other = jnp.where(odd, pltpu.roll(part, 32, 1), pltpu.roll(part, 96, 1))
        groups.append(jnp.where((me & 1) != 0, other, part))
    return jnp.concatenate(groups, axis=1)


def pack_kernel(in_proj, x_proj, dt_proj, a_log, conv_w, conv_b, dt_bias, d_skip, gain_one, gain_two,
                out_proj, w_q, w_k, w_v, w_o, one, two, rows, *rest):
    (b_in, b_x, b_dt, b_a, b_cw, b_cb, b_db, b_sk, b_g1, b_g2, b_out, b_q, b_k, b_v, b_o, sems) = rest
    copies = [
        pltpu.make_async_copy(src, dst, sems.at[i])
        for i, (src, dst) in enumerate(
            zip((in_proj, x_proj, dt_proj, a_log, conv_w, conv_b, dt_bias, d_skip, gain_one, gain_two, out_proj, w_q,
                 w_k, w_v, w_o),
                (b_in, b_x, b_dt, b_a, b_cw, b_cb, b_db, b_sk, b_g1, b_g2, b_out, b_q, b_k, b_v, b_o))
        )
    ]
    for copy in copies:
        copy.start()
    for copy in copies:
        copy.wait()
    one[:, : 2 * E] = b_in[...].astype(BF16)
    two[:, :D] = b_out[...].astype(BF16)
    two[:16, D : 2 * D] = b_q[...].astype(BF16)
    two[:16, 2 * D :] = b_k[...].astype(BF16)
    two[16:, D : 2 * D] = b_v[...].astype(BF16)
    two[16:, 2 * D :] = b_o[...].astype(BF16)
    rows[...] = jnp.zeros_like(rows)
    rows[ROW_X : ROW_X + 64, :] = b_x[...].T
    rows[ROW_DT : ROW_DT + RANK, :] = b_dt[...]
    rows[ROW_A : ROW_A + NS, :] = b_a[...]
    rows[ROW_CW : ROW_CW + KW, :] = b_cw[...]
    rows[ROW_CB : ROW_CB + 1, :] = b_cb[...]
    rows[ROW_DB : ROW_DB + 1, :] = b_db[...]
    rows[ROW_SK : ROW_SK + 1, :] = b_sk[...]
    rows[ROW_G1 : ROW_G1 + 1, :16] = b_g1[...]
    rows[ROW_G2 : ROW_G2 + 1, :16] = b_g2[...]
    one[:, 2 * E :] = jnp.concatenate([rows[16 * q : 16 * q + 16, :] for q in range(8)], axis=1).astype(BF16)


def join_smalls(target, smalls, masks, me):
    place = {mask: p for p, mask in enumerate(masks)}
    for q in range(8):
        for g in range(LG):
            target[16 * q : 16 * q + 16, 128 * g : 128 * g + 128] = jnp.concatenate(
                [smalls[16 * place[m] : 16 * place[m] + 16, 32 * q : 32 * q + 32].astype(F32) for m in range(4 * g, 4 * g + 4)],
                axis=1,
            )
    target[...] = swap_blocks(target[...], me)


def gain_row(pm, row):
    return jnp.concatenate([pm[row : row + 1, 32 * s : 32 * s + 16] for s in range(BLOCKS)], axis=1)


def spread(target, source):
    count = source.shape[0]
    for s in range(LG):
        target[pl.ds(s, count, stride=LG), :] = source[:, s * 128 : (s + 1) * 128]


def gathered(source, count):
    return jnp.concatenate([source[pl.ds(s, count, stride=LG), :] for s in range(LG)], axis=1)


def broadcast_rows(target, proj, first):
    for n in range(NS):
        target[n] = jnp.broadcast_to(proj[:, first + n : first + n + 1], target.shape[1:])


def at8(ref, index):
    return ref[pl.ds(pl.multiple_of(index * 8, 8), 8), :]


def front_kernel(plan, np_, masks, tok, halo, *refs):
    pieces = refs[:np_]
    (normed, u_out, z_out, conv_out, act_out, proj_out, sig_out, dt3, au3, a3, state, weight, pm, gains, bx, smalls, sems) = refs[np_:]
    me = plan.me()
    start_blocks(weight, pieces, masks, me, sems.at[0], 0, 16, 0, 2 * E)
    height = smalls.shape[0] // np_
    for i, piece in enumerate(pieces):
        pltpu.make_async_copy(
            piece.at[:, pl.ds(2 * E, 256)], smalls.at[pl.ds(i * height, height), :], sems.at[1]).start()
    wait_whole(smalls, sems.at[1])
    join_smalls(pm, smalls, masks, me)
    gain = gain_row(pm, ROW_G1)
    gains[0:1, :] = gain
    gains[1:2, :] = gain_row(pm, ROW_G2)
    tokens = tok.shape[0]
    x = jnp.concatenate([halo[...].astype(F32), tok[...].astype(F32)], axis=0)
    r = lax.rsqrt(jnp.mean(x * x, axis=-1, keepdims=True) + EPS)
    low = (x * r * gain).astype(BF16)
    normed[...] = low
    wait_whole(weight, sems.at[0])
    u_out[...] = nn(low, weight[:, :E])
    z_out[...] = nn(low[HALO:], weight[:, E:])
    conv = pm[ROW_CB : ROW_CB + 1, :]
    for k in range(KW):
        conv = conv + pm[ROW_CW + k : ROW_CW + k + 1, :] * u_out[HALO - 3 + k : HALO - 3 + k + tokens, :]
    conv_out[...] = conv
    act = (conv * sigmoid(conv)).astype(BF16)
    act_out[...] = act
    proj = nt(act, pm[ROW_X : ROW_X + 64, :].astype(BF16))
    proj_out[:, :64] = proj
    proj_out[:, 64:] = jnp.zeros((tokens, 64), F32)
    pre = nn(proj[:, :RANK].astype(BF16), pm[ROW_DT : ROW_DT + RANK, :].astype(BF16)) + pm[ROW_DB : ROW_DB + 1, :]
    sig_out[...] = sigmoid(pre)
    step = jnp.maximum(pre, 0.0) + jnp.log1p(jnp.exp(-jnp.abs(pre)))
    spread(dt3, step)
    spread(au3, act.astype(F32))
    spread(a3, -LOG2E * jnp.exp(pm[ROW_A : ROW_A + NS, :]))
    broadcast_rows(bx, proj, RANK)
    decay = [a3[8 * n : 8 * n + 8, :] for n in range(NS)]

    def advance(t, carried):
        held, total = carried
        size = at8(dt3, t)
        drive = size * at8(au3, t)
        held = tuple(
            jnp.exp2(size * decay[n]) * held[n] + drive * bx[n, pl.ds(t, 1), :] for n in range(NS)
        )
        return held, total + size

    zero = jnp.zeros((8, 128), F32)
    held, total = lax.fori_loop(0, tokens, advance, ((zero,) * NS, zero), unroll=4)
    state[...] = jnp.concatenate([*held, total, zero], axis=0).astype(BF16)


def combine_kernel(plan, forward, states, a3, entry, states_f):
    states_f[...] = states[...].astype(F32)
    decay = [a3[8 * n : 8 * n + 8, :] for n in range(NS)]
    zero = jnp.zeros((8, 128), F32)

    def combine(i, held):
        base = (i if forward else plan.chunks - 1 - i) * 144
        total = states_f[pl.ds(pl.multiple_of(base + 128, 8), 8), :]
        return tuple(
            jnp.exp2(total * decay[n]) * held[n] + states_f[pl.ds(pl.multiple_of(base + 8 * n, 8), 8), :]
            for n in range(NS)
        )

    count = plan.chunk() if forward else plan.chunks - 1 - plan.chunk()
    held = lax.fori_loop(0, count, combine, (zero,) * NS)
    entry[...] = jnp.concatenate([*held, zero, zero], axis=0)


def merge_kernel(plan, step, forward, own, other, before, a3, group, entry):
    later = ((plan.chunk() >> step) & 1) == (1 if forward else 0)
    mine, theirs = own[...].astype(F32), other[...].astype(F32)
    first, second = jnp.where(later, theirs, mine), jnp.where(later, mine, theirs)
    decay = a3[...]
    spread_total = lambda value: jnp.concatenate([value[128:136, :]] * NS, axis=0)
    joint = jnp.exp2(spread_total(second) * decay) * first[:128, :] + second[:128, :]
    group[:128, :] = joint.astype(BF16)
    group[128:, :] = (first[128:, :] + second[128:, :]).astype(BF16)
    held = before[...]
    inner = held[:128, :] + jnp.exp2(spread_total(held) * decay) * theirs[:128, :]
    entry[:128, :] = jnp.where(later, inner, held[:128, :])
    entry[128:, :] = jnp.where(later, held[128:, :] + theirs[128:, :], held[128:, :])


def exchange(plan, state, a3, forward):
    if plan.fast:
        group, entry = state, jnp.zeros((144, 128), F32)
        for step in range(3):
            group, entry = run(
                functools.partial(merge_kernel, plan, step, forward),
                [group, send(group, CHUNK_MASKS[1 << step]), entry, a3], [((144, 128), BF16), ((144, 128), F32)])
        return entry
    states = lax.all_gather(state, "ctx", axis=0, tiled=True)
    return run(
        functools.partial(combine_kernel, plan, forward), [states, a3], [((144, 128), F32)],
        [pltpu.VMEM((144 * plan.chunks, 128), F32)])[0]


def mid_kernel(plan, nb, masks, *refs):
    tok, dt3, au3, proj, a3, z_in, pm, gains, cot, entry = refs[:10]
    pieces = refs[10 : 10 + nb]
    pay, mamba, gated_out, middle_out, all_states, w_out, w_qk, w_vo, y3, bx, cx, sems = refs[10 + nb :]
    tokens = tok.shape[0]
    me = plan.me()
    start_blocks(w_out, pieces, masks, me, sems.at[0], 0, 32, 0, D)
    start_blocks(w_qk, pieces, masks, me, sems.at[1], 0, 16, D, 2 * D)
    start_blocks(w_vo, pieces, masks, me, sems.at[2], 16, 16, D, 2 * D)
    broadcast_rows(bx, proj, RANK)
    broadcast_rows(cx, proj, RANK + NS)
    decay = [a3[8 * n : 8 * n + 8, :] for n in range(NS)]
    held = tuple(entry[8 * n : 8 * n + 8, :] for n in range(NS))
    all_states[:128, :] = entry[:128, :]

    def advance(t, held):
        size = at8(dt3, t)
        drive = size * at8(au3, t)
        base = pl.multiple_of(t * 128 + 128, 128)
        held = tuple(
            jnp.exp2(size * decay[n]) * held[n] + drive * bx[n, pl.ds(t, 1), :] for n in range(NS)
        )
        for n in range(NS):
            all_states[pl.ds(base + 8 * n, 8), :] = held[n]
        y = held[0] * cx[0, pl.ds(t, 1), :]
        for n in range(1, NS):
            y = y + held[n] * cx[n, pl.ds(t, 1), :]
        y3[pl.ds(pl.multiple_of(t * 8, 8), 8), :] = y
        return held

    lax.fori_loop(0, tokens, advance, held, unroll=4)
    act = gathered(au3, tokens)
    y = gathered(y3, tokens) + pm[ROW_SK : ROW_SK + 1, :] * act
    mamba[...] = y
    z = z_in[...]
    gated = (y * (z * sigmoid(z))).astype(BF16)
    gated_out[...] = gated
    wait_whole(w_out, sems.at[0])
    wait_whole(w_qk, sems.at[1])
    wait_whole(w_vo, sems.at[2])
    middle = tok[...].astype(F32) + nn(gated, w_out[...])
    middle_out[...] = middle
    r = lax.rsqrt(jnp.mean(middle * middle, axis=-1, keepdims=True) + EPS)
    low = (middle * r * gains[1:2, :]).astype(BF16)
    quads = (
        nn(low, w_qk[:, :D]).astype(BF16),
        nn(low, w_qk[:, D:]).astype(BF16),
        nn(low, w_vo[:, :D]).astype(BF16),
        nt(cot[...], w_vo[:, D:]).astype(BF16),
    )
    for h in range(HEADS):
        for i, part in enumerate(quads):
            pay[h * tokens : (h + 1) * tokens, i * HDIM : (i + 1) * HDIM] = part[:, h * HDIM : (h + 1) * HDIM]


def attention_kernel(pay, back, q_s, k_s, v_s, g_s, kt, vt, dk, dv):
    length = pay.shape[0]
    rows = 256
    q_s[...] = pay[:, :HDIM]
    k_s[...] = pay[:, HDIM : 2 * HDIM]
    v_s[...] = pay[:, 2 * HDIM : 3 * HDIM]
    g_s[...] = pay[:, 3 * HDIM :]
    kt[...] = k_s[...].T
    vt[...] = v_s[...].T
    dk[...] = jnp.zeros_like(dk)
    dv[...] = jnp.zeros_like(dv)
    scale = HDIM**-0.5
    key_at = lax.broadcasted_iota(jnp.int32, (rows, rows), 0)
    query_at = lax.broadcasted_iota(jnp.int32, (rows, rows), 1)
    for i in range(length // rows):
        first, last = i * rows, (i + 1) * rows
        query = q_s[first:last, :]
        grad = g_s[first:last, :]
        scores = nt(k_s[:last, :], query) * scale
        diagonal = jnp.where(key_at <= query_at, scores[first:, :], -1e30)
        scores = diagonal if i == 0 else jnp.concatenate([scores[:first, :], diagonal], axis=0)
        expo = jnp.exp(scores - jnp.max(scores, axis=0, keepdims=True))
        soft = expo * (1.0 / jnp.sum(expo, axis=0, keepdims=True))
        soft_low = soft.astype(BF16)
        grad_p = nt(v_s[:last, :], grad)
        dot = jnp.sum(soft * grad_p, axis=0, keepdims=True)
        grad_s = (soft * (grad_p - dot)).astype(BF16)
        raw = nn(vt[:, :last], soft_low)
        grad_q = nn(kt[:, :last], grad_s) * scale
        back[first:last, :HDIM] = raw.T.astype(BF16)
        back[first:last, HDIM : 2 * HDIM] = grad_q.T.astype(BF16)
        dk[:last, :] += nn(grad_s, query)
        dv[:last, :] += nn(soft_low, grad)
    back[:, 2 * HDIM : 3 * HDIM] = (dk[...] * scale).astype(BF16)
    back[:, 3 * HDIM :] = dv[...].astype(BF16)


def turn_kernel(plan, got, middle, cot, gains, z_in, mamba, dt3, proj, a3, w_out, w_qk, w_vo, first,
                att, gq, gk, gv, grad_middle, mix, gz, gy3, state, gain_grad, cx):
    tokens = middle.shape[0]
    broadcast_rows(cx, proj, RANK + NS)
    for h in range(HEADS):
        for i, part in enumerate((att, gq, gk, gv)):
            part[:, h * HDIM : (h + 1) * HDIM] = got[h * tokens : (h + 1) * tokens, i * HDIM : (i + 1) * HDIM]
    grad_n = nt(gq[...], w_qk[:, :D]) + nt(gk[...], w_qk[:, D:]) + nt(gv[...], w_vo[:, :D])
    mid = middle[...]
    r = lax.rsqrt(jnp.mean(mid * mid, axis=-1, keepdims=True) + EPS)
    gain_grad[...] = jnp.sum(grad_n * mid * r, axis=0, keepdims=True)
    q = grad_n * gains[1:2, :]
    gm = cot[...].astype(F32) + r * q - mid * (r * r * r) * jnp.mean(q * mid, axis=-1, keepdims=True)
    grad_middle[...] = gm
    low = gm.astype(BF16)
    mix[...] = low
    grad_gated = nt(low, w_out[...])
    z = z_in[...]
    s = sigmoid(z)
    spread(gy3, grad_gated * (z * s))
    gz[...] = (grad_gated * mamba[...] * (s * (1.0 + z * (1.0 - s)))).astype(BF16)
    decay = [a3[8 * n : 8 * n + 8, :] for n in range(NS)]

    def retreat(i, carried):
        t = tokens - 1 - i
        size = at8(dt3, t)
        grad = at8(gy3, t)
        return tuple(
            jnp.exp2(size * decay[n]) * (carried[n] + grad * cx[n, pl.ds(t, 1), :]) for n in range(NS)
        )

    zero = jnp.zeros((8, 128), F32)
    carried = lax.fori_loop(0, tokens, retreat, (zero,) * NS, unroll=4)
    state[:128, :] = jnp.concatenate(carried, axis=0).astype(BF16)
    state[128:, :] = first[128:, :]


def pack_blocks(plan, outs, source, rows, height, row, first, col=0, cols=None):
    me = plan.me()
    cols = source.shape[1] if cols is None else cols
    for out, masks in zip(outs, plan.grad_masks):
        for k, mask in enumerate(masks):
            block = me ^ mask
            out[k * height + row : k * height + row + rows, first : first + cols] = source[
                pl.ds(pl.multiple_of(block * rows, 16), rows), col : col + cols
            ].astype(BF16)


def weights_kernel(plan, no, att, gq, gk, gv, mix, gated, middle, gains, cot, w_vo, normed, gz, *refs):
    result, outs = refs[0], refs[1 : 1 + no]
    small, large, wide = refs[1 + no :]
    mid = middle[...]
    result[...] = (mid + nn(att[...], w_vo[:, D:])).astype(BF16)
    r = lax.rsqrt(jnp.mean(mid * mid, axis=-1, keepdims=True) + EPS)
    low = (mid * r * gains[1:2, :]).astype(BF16)
    large[...] = tn(gated[...], mix[...])
    pack_blocks(plan, outs, large, 32, 32, 0, 0)
    small[...] = tn(low, gq[...])
    pack_blocks(plan, outs, small, 16, 32, 0, D)
    small[...] = tn(low, gk[...])
    pack_blocks(plan, outs, small, 16, 32, 0, 2 * D)
    small[...] = tn(low, gv[...])
    pack_blocks(plan, outs, small, 16, 32, 16, D)
    small[...] = tn(att[...], cot[...])
    pack_blocks(plan, outs, small, 16, 32, 16, 2 * D)
    wide[...] = tn(normed[HALO:, :], gz[...])
    pack_blocks(plan, outs, wide, 16, 32, 0, 3 * D, 0, D)
    pack_blocks(plan, outs, wide, 16, 32, 16, 3 * D, D, D)


def back_kernel(plan, dt3, au3, gy3, a3, proj, pm, all_states, sig, act, conv_in, u_in, leaving,
                small_grads, gu_out, bx, cx, grads, gs3, ga3, gal, skip3, low_rank, padded):
    tokens = dt3.shape[0] // LG
    broadcast_rows(bx, proj, RANK)
    broadcast_rows(cx, proj, RANK + NS)
    decay = [a3[8 * n : 8 * n + 8, :] for n in range(NS)]
    zero = jnp.zeros((8, 128), F32)
    spread(skip3, pm[ROW_SK : ROW_SK + 1, :])
    skip = skip3[...]

    carried = tuple(leaving[8 * n : 8 * n + 8, :] for n in range(NS))
    gal[...] = jnp.zeros_like(gal)

    def retreat(i, state):
        carried, skipped = state
        t = tokens - 1 - i
        size, value, grad = at8(dt3, t), at8(au3, t), at8(gy3, t)
        base = pl.multiple_of(t * 128, 128)
        from_b = zero
        from_a = zero
        fresh = []
        for n in range(NS):
            g = carried[n] + grad * cx[n, pl.ds(t, 1), :]
            grads[pl.ds(base + 8 * n, 8), :] = g
            w = jnp.exp2(size * decay[n]) * g
            q = w * all_states[pl.ds(base + 8 * n, 8), :]
            from_a = from_a + decay[n] * q
            from_b = from_b + g * bx[n, pl.ds(t, 1), :]
            gal[8 * n : 8 * n + 8, :] += size * q
            fresh.append(w)
        at = pl.ds(pl.multiple_of(t * 8, 8), 8)
        gs3[at, :] = from_a * LN2 + from_b * value
        ga3[at, :] = from_b * size + skip * grad
        return tuple(fresh), skipped + grad * value

    _, skipped = lax.fori_loop(0, tokens, retreat, (carried, zero), unroll=2)

    span = 16
    row_t = lax.broadcasted_iota(jnp.int32, (span, span * NS), 0)
    col_t = lax.broadcasted_iota(jnp.int32, (span, span * NS), 1) // NS
    pick = (
        lax.broadcasted_iota(jnp.int32, (span * NS, NS), 0) % NS
        == lax.broadcasted_iota(jnp.int32, (span * NS, NS), 1)
    ).astype(BF16)
    for block in range(tokens // span):
        total_b = jnp.zeros((span, span * NS), F32)
        total_c = jnp.zeros((span, span * NS), F32)
        for s in range(LG):
            rows = pl.ds(block * span * 8 + s, span, stride=LG)
            grad_rows = grads[pl.ds(block * span * 128 + s, span * NS, stride=LG), :].astype(BF16)
            held_rows = all_states[pl.ds((block * span + 1) * 128 + s, span * NS, stride=LG), :].astype(BF16)
            total_b = total_b + nt((dt3[rows, :] * au3[rows, :]).astype(BF16), grad_rows)
            total_c = total_c + nt(gy3[rows, :].astype(BF16), held_rows)
        own_b = jnp.where(row_t == col_t, total_b, 0.0).astype(BF16)
        own_c = jnp.where(row_t == col_t, total_c, 0.0).astype(BF16)
        low_rank[block * span : (block + 1) * span, RANK : RANK + NS] = nn(own_b, pick)
        low_rank[block * span : (block + 1) * span, RANK + NS : RANK + 2 * NS] = nn(own_c, pick)

    grad_pre = gathered(gs3, tokens) * sig[...]
    grad_pre_low = grad_pre.astype(BF16)
    low_rank[:, :RANK] = nt(grad_pre_low, pm[ROW_DT : ROW_DT + RANK, :].astype(BF16))
    projected = low_rank[:, :64].astype(BF16)
    small_grads[ROW_X : ROW_X + 64, :] = tn(projected, act[...])
    small_grads[ROW_DT : ROW_DT + RANK, :] = tn(proj[:, :RANK].astype(BF16), grad_pre_low)
    true_a = -jnp.exp(pm[ROW_A : ROW_A + NS, :])
    small_grads[ROW_A : ROW_A + NS, :] = gathered(gal, NS) * true_a
    small_grads[ROW_DB : ROW_DB + 1, :] = jnp.sum(grad_pre, axis=0, keepdims=True)
    skip3[...] = skipped
    small_grads[ROW_SK : ROW_SK + 1, :] = gathered(skip3, 1)
    small_grads[ROW_G1:, :] = jnp.zeros((SMALL_ROWS - ROW_G1, E), F32)
    conv = conv_in[...]
    s = sigmoid(conv)
    grad_act = gathered(ga3, tokens) + nn(projected, pm[ROW_X : ROW_X + 64, :].astype(BF16))
    grad_conv = grad_act * (s * (1.0 + conv * (1.0 - s)))
    small_grads[ROW_CB : ROW_CB + 1, :] = jnp.sum(grad_conv, axis=0, keepdims=True)
    for k in range(KW):
        small_grads[ROW_CW + k : ROW_CW + k + 1, :] = jnp.sum(
            grad_conv * u_in[HALO - 3 + k : HALO - 3 + k + tokens, :], axis=0, keepdims=True
        )
    padded[:HALO, :] = jnp.zeros((HALO, E), F32)
    padded[HALO : HALO + tokens, :] = grad_conv
    padded[HALO + tokens :, :] = jnp.zeros((HALO, E), F32)
    gu = jnp.zeros((HALO + tokens, E), F32)
    for k in range(KW):
        gu = gu + pm[ROW_CW + k : ROW_CW + k + 1, :] * padded[3 - k : 3 - k + HALO + tokens, :]
    gu_out[...] = gu.astype(BF16)


def last_kernel(plan, no, tok, halo, gains, gu, gz, grad_middle, weight, normed, small_grads, gain_two, *refs):
    outs = refs[:no]
    own, before, large, spaced = refs[no:]
    me = plan.me()
    large[...] = tn(normed[...], gu[...])
    pack_blocks(plan, outs, large, 16, 16, 0, 0)
    x = jnp.concatenate([halo[...].astype(F32), tok[...].astype(F32)], axis=0)
    r = lax.rsqrt(jnp.mean(x * x, axis=-1, keepdims=True) + EPS)
    from_z = nt(gz[...], weight[:, E:])
    grad_n = nt(gu[...], weight[:, :E]) + jnp.concatenate([jnp.zeros((HALO, D), F32), from_z], axis=0)
    gain_one = jnp.sum(grad_n * x * r, axis=0, keepdims=True)
    q = grad_n * gains[0:1, :]
    base = r * q - x * (r * r * r) * jnp.mean(q * x, axis=-1, keepdims=True)
    own[...] = (grad_middle[...] + base[HALO:, :]).astype(BF16)
    before[...] = base[:HALO, :].astype(BF16)
    spaced[...] = small_grads[...]
    blank = jnp.zeros((1, 16), F32)
    for row, grad in ((ROW_G1, gain_one), (ROW_G2, gain_two[...])):
        spaced[row : row + 1, :] = jnp.concatenate(
            [part for s in range(BLOCKS) for part in (grad[:, 16 * s : 16 * s + 16], blank)], axis=1)
    spaced[...] = swap_blocks(spaced[...], me)
    for out, masks in zip(outs, plan.grad_masks):
        for k, m in enumerate(masks):
            out[16 * k : 16 * k + 16, E:] = jnp.concatenate(
                [spaced[16 * q : 16 * q + 16, 32 * m : 32 * m + 32] for q in range(8)], axis=1).astype(BF16)


def total_of(ins):
    total = ins[0][...].astype(F32)
    for other in ins[1:]:
        total = total + other[...].astype(F32)
    return total


def finish_kernel(*refs):
    u_ins, ins = refs[:4], refs[4:6]
    out_g, q_g, k_g, v_g, o_g, in_g, x_g, dt_g, a_g, cw_g, cb_g, db_g, sk_g, g1_g, g2_g, rows = refs[6:]
    total = total_of(ins)
    out_g[...] = total[:, :D]
    q_g[...] = total[:16, D : 2 * D]
    k_g[...] = total[:16, 2 * D : 3 * D]
    v_g[...] = total[16:, D : 2 * D]
    o_g[...] = total[16:, 2 * D : 3 * D]
    in_g[:, E : E + D] = total[:16, 3 * D :]
    in_g[:, E + D :] = total[16:, 3 * D :]
    total = total_of(u_ins)
    in_g[:, :E] = total[:, :E]
    for q in range(8):
        rows[16 * q : 16 * q + 16, :] = total[:, E + 32 * q : E + 32 * q + 32]
    x_g[...] = rows[ROW_X : ROW_X + 64, :].T
    dt_g[...] = rows[ROW_DT : ROW_DT + RANK, :]
    a_g[...] = rows[ROW_A : ROW_A + NS, :]
    cw_g[...] = rows[ROW_CW : ROW_CW + KW, :]
    cb_g[...] = rows[ROW_CB : ROW_CB + 1, :]
    db_g[...] = rows[ROW_DB : ROW_DB + 1, :]
    sk_g[...] = rows[ROW_SK : ROW_SK + 1, :]
    g1_g[...] = rows[ROW_G1 : ROW_G1 + 1, :16]
    g2_g[...] = rows[ROW_G2 : ROW_G2 + 1, :16]


def join_kernel(counts, *refs):
    ins, outs, sems = refs[: sum(counts)], refs[sum(counts) : -1], refs[-1]
    at = 0
    for i, count in enumerate(counts):
        rows = outs[i].shape[0] // count
        for k in range(count):
            pltpu.make_async_copy(ins[at + k], outs[i].at[pl.ds(k * rows, rows), :], sems.at[i]).start()
        at += count
    for i, out in enumerate(outs):
        wait_whole(out, sems.at[i])


def join(groups, after=()):
    counts = [len(group) for group in groups]
    outs = [((group[0].shape[0] * len(group), group[0].shape[1]), group[0].dtype) for group in groups]
    return run(
        functools.partial(join_kernel, counts), [], outs, [pltpu.SemaphoreType.DMA((len(groups),))],
        raw=[part for group in groups for part in group], after=after)


def spread_out(value, stage):
    return [value] + [send(value, mask) for mask in stage[1:]]


def cut_one_kernel(keep, got, a_keep, a_give, b_keep, b_give):
    half, quarter, cols = keep.shape[0] // 2, keep.shape[0] // 4, keep.shape[1] // 2
    add = lambda rows, lanes: (keep[rows, lanes].astype(F32) + got[rows, lanes].astype(F32)).astype(BF16)
    left, right = slice(0, cols), slice(cols, 2 * cols)
    a_keep[...] = add(slice(0, half), left)
    a_give[...] = add(slice(half, 2 * half), left)
    for i in range(2):
        b_keep[i * quarter : (i + 1) * quarter, :] = add(slice(2 * i * quarter, (2 * i + 1) * quarter), right)
        b_give[i * quarter : (i + 1) * quarter, :] = add(slice((2 * i + 1) * quarter, (2 * i + 2) * quarter), right)


def cut_two_kernel(a_own, a_got, b_own, b_got, a_keep, a_give, b_keep, b_give):
    rows = a_own.shape[0] // 2
    for own, got, keep, give in ((a_own, a_got, a_keep, a_give), (b_own, b_got, b_keep, b_give)):
        for out, part in ((keep, slice(0, rows)), (give, slice(rows, 2 * rows))):
            out[...] = (own[part, :].astype(F32) + got[part, :].astype(F32)).astype(BF16)


def add_rows(out, rows, ins, cols=slice(None), to=slice(None)):
    total = ins[0][rows, cols].astype(F32)
    for other in ins[1:]:
        total = total + other[rows, cols].astype(F32)
    out[:, to] = total.astype(out.dtype)


def cut_three_kernel(u_own, u_got, a_own, a_got, b_own, b_got, u_0, u_1, u_2, u_3, keep, give):
    rows = u_0.shape[0]
    for i, out in enumerate((u_0, u_1, u_2, u_3)):
        add_rows(out, slice(i * rows, (i + 1) * rows), (u_own, u_got))
    rows, cols = keep.shape[0], a_own.shape[1]
    for i, out in enumerate((keep, give)):
        part = slice(i * rows, (i + 1) * rows)
        add_rows(out, part, (a_own, a_got), to=slice(0, cols))
        add_rows(out, part, (b_own, b_got), to=slice(cols, 2 * cols))


def cut_four_kernel(u_own, u_a, u_b, u_c, own, got, u_0, u_1, u_2, u_3, keep, give):
    rows = u_0.shape[0]
    for i, out in enumerate((u_0, u_1, u_2, u_3)):
        add_rows(out, slice(i * rows, (i + 1) * rows), (u_own, u_a, u_b, u_c))
    rows = keep.shape[0]
    for i, out in enumerate((keep, give)):
        add_rows(out, slice(i * rows, (i + 1) * rows), (own, got))


def body(plan, *args):
    (tokens, mixer_gain, in_proj, conv_weight, conv_bias, x_proj, dt_proj, dt_bias, a_log, d_skip, out_proj,
     attn_gain, w_query, w_key, w_value, w_output, cotangent) = args
    count = tokens.shape[1]
    tok0, cot0 = tokens.reshape(count, D), cotangent.reshape(count, D)
    chunks = plan.chunks
    devices = plan.dp * plan.ctx
    share, width = E // devices, D // devices
    if plan.fast:
        masks = FULL_MASKS
        home = [(s * 8 + c, plan.place(s, c)) for s in range(4) for c in range(8)]
        tok = lax.ppermute(tok0, ALL, home)
        halo = lax.ppermute(
            tok0[count - HALO :], ALL, [(s * 8 + c, plan.place(s, c + 1)) for s in range(4) for c in range(7)]
        )
        raw = [in_proj, x_proj, dt_proj, a_log.T, conv_weight.T, conv_bias[None], dt_bias[None], d_skip[None],
               mixer_gain[None], attn_gain[None], out_proj, w_query, w_key, w_value, w_output]
        pack_one, pack_two = run(
            pack_kernel, [], [((16, 2 * E + 256), BF16), ((32, 3 * D), BF16)],
            [pltpu.VMEM((SMALL_ROWS, 32), F32)] + [pltpu.VMEM(value.shape, F32) for value in raw]
            + [pltpu.SemaphoreType.DMA((len(raw),))], far=raw, limit=60)
        one, two, cot = join([[pack_one, send(pack_one, 4)], [pack_two], [cot0]], [tok, halo])
        two_far = send(two, 4)
        cot = lax.ppermute(cot, ALL, home)
        one, two = join([[one, send(one, 2)], [two, two_far]], [cot])
        two_far = send(two, 2)
        one, two = join([spread_out(one, XY_MASKS), [two, two_far]])
        one = [one, send(one, CORE)]
        near_two = spread_out(two, XY_MASKS)
    else:
        masks = tuple(range(BLOCKS))
        tok, cot = tok0, cot0
        halo = lax.ppermute(tok0[count - HALO :], "ctx", [(c, c + 1) for c in range(chunks - 1)])
        smalls = jnp.concatenate(
            [x_proj.T, dt_proj, a_log.T, conv_weight.T, conv_bias[None], dt_bias[None], d_skip[None],
             jnp.pad(mixer_gain, (0, share - width))[None], jnp.pad(attn_gain, (0, share - width))[None],
             jnp.zeros((SMALL_ROWS - ROW_G2 - 1, share), F32)], axis=0).astype(BF16)
        small_all = lax.all_gather(smalls, ALL, axis=1, tiled=True)
        apart = lambda row: jnp.pad(
            small_all[row].reshape(devices, share)[:, :width].reshape(BLOCKS, 16), ((0, 0), (0, 16))).reshape(1, E)
        small_all = jnp.concatenate(
            [small_all[:ROW_G1], apart(ROW_G1), apart(ROW_G2), small_all[ROW_G2 + 1 :]], axis=0)
        small_all = small_all.reshape(8, 16, BLOCKS, 32).transpose(2, 1, 0, 3).reshape(BLOCKS * 16, 256)
        whole = lambda value: lax.all_gather(value.astype(BF16), ALL, axis=0, tiled=True)
        one = [jnp.concatenate([whole(in_proj), small_all], axis=1)]
        out_all, q_all, k_all, v_all, o_all = (whole(w) for w in (out_proj, w_query, w_key, w_value, w_output))
        cut = lambda value: value.reshape(BLOCKS, 16, D)
        side = jnp.concatenate(
            [jnp.concatenate([cut(q_all), cut(k_all)], axis=2), jnp.concatenate([cut(v_all), cut(o_all)], axis=2)], axis=1)
        two = [jnp.concatenate([out_all.reshape(BLOCKS, 32, D), side], axis=2).reshape(BLOCKS * 32, 3 * D)]

    no = len(plan.grad_masks)
    rows3 = count * LG
    (normed, u_pre, z, conv, act, proj, sig, dt3, au3, a3, state, w_in, pm, gains) = run(
        functools.partial(front_kernel, plan, len(one), masks),
        [tok, halo],
        [((HALO + count, D), BF16), ((HALO + count, E), F32), ((count, E), F32), ((count, E), F32),
         ((count, E), BF16), ((count, 128), F32), ((count, E), F32), ((rows3, 128), F32), ((rows3, 128), F32),
         ((128, 128), F32), ((144, 128), BF16), ((D, 2 * E), BF16), ((SMALL_ROWS, E), F32), ((8, D), F32)],
        [pltpu.VMEM((NS, count, 128), F32), pltpu.VMEM((BLOCKS * 16, 256), BF16), pltpu.SemaphoreType.DMA((2,))],
        raw=one, us=6,
    )
    entry = exchange(plan, state, a3, True)
    if plan.fast:
        (held,) = join([near_two], [entry])
        two = [held, send(held, CORE)]
    rows_scratch = pltpu.VMEM((NS, count, 128), F32)
    pay, mamba, gated, middle, all_states, w_out, w_qk, w_vo = run(
        functools.partial(mid_kernel, plan, len(two), masks),
        [tok, dt3, au3, proj, a3, z, pm, gains, cot, entry],
        [((HEADS * count, 4 * HDIM), BF16), ((count, E), F32), ((count, E), BF16), ((count, D), F32),
         (((count + 1) * 128, 128), F32), ((E, D), BF16), ((D, 2 * D), BF16), ((D, 2 * D), BF16)],
        [pltpu.VMEM((rows3, 128), F32), rows_scratch, rows_scratch, pltpu.SemaphoreType.DMA((3,))],
        raw=two, us=6,
    )
    got = attend(plan, pay, count)
    (att, gq, gk, gv, grad_middle, mix, gz, gy3, later, gain_grad_two) = run(
        functools.partial(turn_kernel, plan),
        [got, middle, cot, gains, z, mamba, dt3, proj, a3, w_out, w_qk, w_vo, state],
        [((count, D), BF16)] * 4 + [((count, D), F32), ((count, D), BF16), ((count, E), BF16), ((rows3, 128), F32),
                                    ((144, 128), BF16), ((1, D), F32)],
        [rows_scratch],
    )
    blocks = [len(masks_of) for masks_of in plan.grad_masks]
    result, *one_grads = run(
        functools.partial(weights_kernel, plan, no),
        [att, gq, gk, gv, mix, gated, middle, gains, cot, w_vo, normed, gz],
        [((count, D), BF16)] + [((n * 32, 4 * D), BF16) for n in blocks],
        [pltpu.VMEM((D, D), F32), pltpu.VMEM((E, D), F32), pltpu.VMEM((D, E), F32)],
    )
    leaving = exchange(plan, later, a3, False)
    one_parts = []
    if plan.fast:
        result = lax.ppermute(result, ALL, [(b, a) for a, b in home])
        rows = blocks[0] * 32
        one_parts = run(
            cut_one_kernel, [one_grads[0], send(one_grads[1], CORE)], [((rows // 2, 2 * D), BF16)] * 4, after=[leaving, result])
    small_grads, gu = run(
        functools.partial(back_kernel, plan),
        [dt3, au3, gy3, a3, proj, pm, all_states, sig, act, conv, u_pre, leaving],
        [((SMALL_ROWS, E), F32), ((HALO + count, E), BF16)],
        [rows_scratch, rows_scratch,
         pltpu.VMEM((count * 128, 128), F32), pltpu.VMEM((rows3, 128), F32), pltpu.VMEM((rows3, 128), F32),
         pltpu.VMEM((128, 128), F32), pltpu.VMEM((8, 128), F32), pltpu.VMEM((count, 128), F32),
         pltpu.VMEM((count + 2 * HALO, E), F32)],
        limit=32, after=one_parts[:1], us=11,
    )
    if plan.fast:
        a_keep, a_give, b_keep, b_give = one_parts
        one_parts = run(
            cut_two_kernel, [a_keep, send(a_give, 16), b_keep, send(b_give, 1)], [((rows // 4, 2 * D), BF16)] * 4,
            after=[gu])
    *two_grads, own, before = run(
        functools.partial(last_kernel, plan, no),
        [tok, halo, gains, gu, gz, grad_middle, w_in, normed, small_grads, gain_grad_two],
        [((n * 16, E + 256), BF16) for n in blocks] + [((count, D), BF16), ((HALO, D), BF16)],
        [pltpu.VMEM((D, E), F32), pltpu.VMEM((SMALL_ROWS, E), F32)], after=one_parts[:1],
    )
    if plan.fast:
        away = [(b, a) for a, b in home]
        grad_tok = lax.ppermute(own, ALL, away)
        tail = lax.ppermute(
            before, ALL, [(plan.place(s, c + 1), s * 8 + c) for s in range(4) for c in range(7)])
        a_keep, a_give, b_keep, b_give = one_parts
        sends = lambda parts, stage: [parts[0]] + [send(part, mask) for part, mask in zip(parts[1:], stage[1:])]
        n = blocks[0]
        *u_parts, keep, give = run(
            cut_three_kernel, [two_grads[0], send(two_grads[1], CORE), a_keep, send(a_give, 1), b_keep, send(b_give, 16)],
            [((n * 4, E + 256), BF16)] * 4 + [((n * 4, 4 * D), BF16)] * 2, after=[grad_tok])
        *u_parts, keep, give = run(
            cut_four_kernel, [*sends(u_parts, XY_MASKS), keep, send(give, 2)],
            [((n, E + 256), BF16)] * 4 + [((n * 2, 4 * D), BF16)] * 2, after=[tail])
        out_g, q_g, k_g, v_g, o_g, in_g, x_g, dt_g, a_g, cw_g, cb_g, db_g, sk_g, g1_g, g2_g = run(
            finish_kernel, [*sends(u_parts, Z_MASKS), keep, send(give, 4)],
            [((32, D), F32)] + [((16, D), F32)] * 4
            + [((16, 2 * E), F32), ((32, 64), F32), ((32, 32), F32), ((NS, 32), F32), ((KW, 32), F32)]
            + [((1, 32), F32)] * 3 + [((1, 16), F32)] * 2,
            [pltpu.VMEM((SMALL_ROWS, 32), F32)], final=True)
        a_g, cw_g = a_g.T, cw_g.T
        vectors = [value[0] for value in (cb_g, db_g, sk_g, g1_g, g2_g)]
    else:
        grad_tok = own
        tail = lax.ppermute(before, "ctx", [(c + 1, c) for c in range(chunks - 1)])
        scatter = lambda value, dim=0: lax.psum_scatter(value.astype(F32), ALL, scatter_dimension=dim, tiled=True)
        blocks_one = one_grads[0].reshape(BLOCKS, 32, 4 * D)
        part = lambda row, rows, col: scatter(blocks_one[:, row : row + rows, col * D : (col + 1) * D].reshape(-1, D))
        out_g, q_g, k_g, v_g, o_g = part(0, 32, 0), part(0, 16, 1), part(0, 16, 2), part(16, 16, 1), part(16, 16, 2)
        in_g = jnp.concatenate([scatter(two_grads[0][:, :E]), part(0, 16, 3), part(16, 16, 3)], axis=1)
        small = two_grads[0][:, E:].reshape(BLOCKS, 16, 8, 32).transpose(2, 1, 0, 3).reshape(SMALL_ROWS, E)
        close = lambda row: scatter(small[row].reshape(BLOCKS, 32)[:, :16].reshape(D))
        g1, g2 = close(ROW_G1), close(ROW_G2)
        mine = scatter(small, 1)
        x_g, dt_g, a_g, cw_g = (
            mine[ROW_X : ROW_X + 64].T, mine[ROW_DT : ROW_DT + RANK], mine[ROW_A : ROW_A + NS].T, mine[ROW_CW : ROW_CW + KW].T)
        vectors = [mine[ROW_CB], mine[ROW_DB], mine[ROW_SK], g1, g2]
    last = (grad_tok[count - HALO :].astype(F32) + tail.astype(F32)).astype(BF16)
    grad_tok = jnp.concatenate([grad_tok[: count - HALO], last], axis=0)
    cb_v, db_v, sk_v, g1_v, g2_v = vectors
    return (
        result[None], grad_tok[None], g1_v, in_g, cw_g, cb_v, x_g, dt_g, db_v, a_g, sk_v, out_g, g2_v, q_g, k_g, v_g, o_g,
    )


def attend(plan, pay, count):
    if plan.chunks == HEADS:
        held = plan.swap(pay)
        length = held.shape[0]
        half = pltpu.VMEM((length, HDIM), BF16)
        flat = pltpu.VMEM((HDIM, length), BF16)
        wide = pltpu.VMEM((length, HDIM), F32)
        (back,) = run(
            attention_kernel, [held], [((length, 4 * HDIM), BF16)], [half] * 4 + [flat] * 2 + [wide] * 2, us=4
        )
        return plan.swap(back)
    parts = pay.reshape(HEADS, count, 4, HDIM)
    query, key, value, grad = (parts[:, :, i] for i in range(4))
    key, value = (lax.all_gather(part, "ctx", axis=1, tiled=True) for part in (key, value))
    query_at = lax.axis_index("ctx") * count + jnp.arange(count)
    allowed = jnp.arange(key.shape[1])[None, :] <= query_at[:, None]
    scale = HDIM**-0.5
    dots = functools.partial(jnp.einsum, preferred_element_type=F32)
    scores = jnp.where(allowed, dots("hqd,hkd->hqk", query, key) * scale, -1e30)
    soft = jax.nn.softmax(scores, axis=-1)
    soft_low = soft.astype(BF16)
    grad_p = dots("hqd,hkd->hqk", grad, value)
    grad_s = (soft * (grad_p - jnp.sum(soft * grad_p, axis=-1, keepdims=True))).astype(BF16)
    raw = dots("hqk,hkd->hqd", soft_low, value).astype(BF16)
    grad_q = (dots("hqk,hkd->hqd", grad_s, key) * scale).astype(BF16)
    grads = (dots("hqk,hqd->hkd", grad_s, query) * scale, dots("hqk,hqd->hkd", soft_low, grad))
    grad_k, grad_v = (
        lax.psum_scatter(part.astype(BF16), "ctx", scatter_dimension=1, tiled=True) for part in grads
    )
    return jnp.concatenate([raw, grad_q, grad_k, grad_v], axis=-1).reshape(HEADS * count, 4 * HDIM)


def solution(mesh):
    plan = Plan(mesh)
    split, rows, cols = P(ALL), P(ALL, None), P(None, ALL)
    acts = P("dp", "ctx", None)
    return jax.shard_map(
        functools.partial(body, plan),
        mesh=mesh,
        in_specs=(acts, split, rows, rows, split, rows, cols, split, rows, split, rows, split, rows, rows, rows, rows, acts),
        out_specs=(acts, acts, split, rows, rows, split, rows, cols, split, rows, split, rows, split, rows, rows, rows, rows),
        check_vma=False,
    )
```

profile of v0, /device:TPU:6, one launch (start us, length us, event | category | flops | bytes accessed | tf_op | source)
XLA Modules:
  0.0 188.3 jit_solution(6269080031446453954)
XLA Ops:
  0.7 3.4 %collective-permute-start = (bf16[128,512]{1,0:T(8,128)(2,1)}, bf16[128,512]{1,0:T(8,128)(2,1)S(1)}, u32[]{:S(2)}, u32[]{:S(2)}) collective-permute-start(bf16[128,512]{1,0:T(8,128)(2,1)} %bitcast.33), channel_id=1, source_target_pairs={{0,0},{1,16},{2,1},{3,17},{4,8},{5,24},{6,9},{7,25},{8,4},{9,20},{... | collective-permute-start | bytes 393224 | tf_op jit(solution)/shard_map/ppermute | solution.py:713
  4.1 2.0 %shard_map.296 = (bf16[16,2304]{1,0:T(8,128)(2,1)}, bf16[32,1536]{1,0:T(8,128)(2,1)}) custom-call(f32[16,2048]{1,0:T(8,128)} %refs_0_.1, f32[32,64]{1,0:T(8,128)} %refs_1_.1, f32[32,32]{1,0:T(8,128)} %refs_2_.1, f32[16,32]{1,0:T(8,128)} %bitcast.31, f32[4,32]{1,0:T(4,128)} %bitcast.32, f32[1,32]{1,0:T(1,128)} %bitcast.34, f32[1,32]{1,0:T(1,128)} %bitcast.35, ...), custom_call_target="tpu_custom_call" | custom-call | flops 2000 | bytes 6000 | tf_op jit(solution)/shard_map/pallas_call | solution.py:58
  6.1 1.1 collective-permute-start.2
  7.9 4.0 %collective-permute-start.1 = (bf16[16,512]{1,0:T(8,128)(2,1)S(1)}, bf16[16,512]{1,0:T(8,128)(2,1)S(1)}, u32[]{:S(2)}, u32[]{:S(2)}) collective-permute-start(bf16[16,512]{1,0:T(8,128)(2,1)S(1)} %slice_bitcast_fusion), channel_id=1, source_target_pairs={{0,16},{1,1},{2,17},{3,8},{4,24},{5,9},{6,25},{8,20},{9,5},{10,21}... | collective-permute-start | bytes 49160 | tf_op jit(solution)/shard_map/ppermute | solution.py:714
  12.0 3.4 %collective-permute-done.1.refs_5_.refs_1_ = bf16[16,512]{1,0:T(8,128)(2,1)S(1)} collective-permute-done((bf16[16,512]{1,0:T(8,128)(2,1)S(1)}, bf16[16,512]{1,0:T(8,128)(2,1)S(1)}, u32[]{:S(2)}, u32[]{:S(2)}) %collective-permute-start.1) | collective-permute-done | bytes 16416 | tf_op jit(solution)/shard_map/ppermute | solution.py:714
  18.6 2.5 %collective-permute-start.5 = (bf16[128,512]{1,0:T(8,128)(2,1)S(1)}, bf16[128,512]{1,0:T(8,128)(2,1)S(1)}, u32[]{:S(2)}, u32[]{:S(2)}) collective-permute-start(bf16[128,512]{1,0:T(8,128)(2,1)S(1)} %get-tuple-element.116), channel_id=1, source_target_pairs={{0,0},{1,16},{2,1},{3,17},{4,8},{5,24},{6,9},{7,25},{8,4},{9,20},{... | collective-permute-start | bytes 393224 | tf_op jit(solution)/shard_map/ppermute | solution.py:725
  21.1 2.8 %collective-permute-start.4 = (bf16[32,1536]{1,0:T(8,128)(2,1)S(1)}, bf16[32,1536]{1,0:T(8,128)(2,1)S(1)}, u32[]{:S(2)}, u32[]{:S(2)}) collective-permute-start(bf16[32,1536]{1,0:T(8,128)(2,1)S(1)} %get-tuple-element.115.refs_2_), channel_id=1, source_target_pairs={{0,4},{1,5},{2,6},{3,7},{4,0},{5,1},{6,2},{7,3},{8,12},{9,13},{10,... | collective-permute-start | bytes 294920 | tf_op jit(solution)/shard_map/ppermute | solution.py:117
  23.9 8.7 %collective-permute-done.4.refs_3_ = bf16[32,1536]{1,0:T(8,128)(2,1)S(1)} collective-permute-done((bf16[32,1536]{1,0:T(8,128)(2,1)S(1)}, bf16[32,1536]{1,0:T(8,128)(2,1)S(1)}, u32[]{:S(2)}, u32[]{:S(2)}) %collective-permute-start.4) | collective-permute-done | bytes 98336 | tf_op jit(solution)/shard_map/ppermute | solution.py:117
  33.3 2.5 %collective-permute-start.7 = (bf16[64,2304]{1,0:T(8,128)(2,1)S(1)}, bf16[64,2304]{1,0:T(8,128)(2,1)S(1)}, u32[]{:S(2)}, u32[]{:S(2)}) collective-permute-start(bf16[64,2304]{1,0:T(8,128)(2,1)S(1)} %get-tuple-element.117.refs_0_), channel_id=1, source_target_pairs={{0,16},{1,17},{2,18},{3,19},{4,20},{5,21},{6,22},{7,23},{8,24},{9,... | collective-permute-start | bytes 884744 | tf_op jit(solution)/shard_map/ppermute | solution.py:117
  35.8 1.0 collective-permute-start.6
  36.8 6.1 %collective-permute-done.9.refs_5_ = bf16[64,1536]{1,0:T(8,128)(2,1)S(1)} collective-permute-done((bf16[64,1536]{1,0:T(8,128)(2,1)S(1)}, bf16[64,1536]{1,0:T(8,128)(2,1)S(1)}, u32[]{:S(2)}, u32[]{:S(2)}) %collective-permute-start.9) | collective-permute-done | bytes 196640 | tf_op jit(solution)/shard_map/ppermute | solution.py:117
  42.8 1.2 collective-permute-done.8.refs_3_
  44.1 4.9 %collective-permute-done.7.refs_2_ = bf16[64,2304]{1,0:T(8,128)(2,1)S(1)} collective-permute-done((bf16[64,2304]{1,0:T(8,128)(2,1)S(1)}, bf16[64,2304]{1,0:T(8,128)(2,1)S(1)}, u32[]{:S(2)}, u32[]{:S(2)}) %collective-permute-start.7) | collective-permute-done | bytes 294944 | tf_op jit(solution)/shard_map/ppermute | solution.py:117
  51.3 1.5 collective-permute-start.15
  52.8 1.2 collective-permute-start.14
  53.9 6.1 %shard_map.300 = (bf16[144,512]{1,0:T(8,128)(2,1)S(1)}, f32[144,1024]{1,0:T(8,128)S(1)}, f32[128,1024]{1,0:T(8,128)S(1)}, f32[128,1024]{1,0:T(8,128)S(1)}, bf16[...) custom-call(bf16[128,512]{1,0:T(8,128)(2,1)S(1)} %collective-permute, ...), custom_call_target="tpu_custom_call" | custom-call | flops 6000 | bytes 18000 | tf_op jit(solution)/shard_map/pallas_call | solution.py:58
  60.9 10.6 %collective-permute-done.11.refs_1_ = bf16[144,128]{1,0:T(8,128)(2,1)S(1)} collective-permute-done((bf16[144,128]{1,0:T(8,128)(2,1)S(1)}, bf16[144,128]{1,0:T(8,128)(2,1)S(1)}, u32[]{:S(2)}, u32[]{:S(2)}) %collective-permute-start.11) | collective-permute-done | bytes 36896 | tf_op jit(solution)/shard_map/ppermute | solution.py:117
  71.5 1.2 collective-permute-start.12
  72.7 2.8 %collective-permute-done.12.refs_1_ = bf16[144,128]{1,0:T(8,128)(2,1)S(1)} collective-permute-done((bf16[144,128]{1,0:T(8,128)(2,1)S(1)}, bf16[144,128]{1,0:T(8,128)(2,1)S(1)}, u32[]{:S(2)}, u32[]{:S(2)}) %collective-permute-start.12) | collective-permute-done | bytes 36896 | tf_op jit(solution)/shard_map/ppermute | solution.py:117
  75.7 1.2 collective-permute-done.13.refs_1_
  78.5 3.2 %collective-permute-done.17.refs_11_ = bf16[512,1536]{1,0:T(8,128)(2,1)S(1)} collective-permute-done((bf16[512,1536]{1,0:T(8,128)(2,1)S(1)}, bf16[512,1536]{1,0:T(8,128)(2,1)S(1)}, u32[]{:S(2)}, u32[]{:S(2)}) %collective-permute-start.17) | collective-permute-done | bytes 1572896 | tf_op jit(solution)/shard_map/ppermute | solution.py:117
  81.8 6.3 %shard_map.305 = (bf16[1024,256]{1,0:T(8,128)(2,1)S(1)}, f32[128,1024]{1,0:T(8,128)S(1)}, bf16[128,1024]{1,0:T(8,128)(2,1)S(1)}, f32[128,512]{1,0:T(8,128)S(1)},...) custom-call(bf16[128,512]{1,0:T(8,128)(2,1)S(1)} %collective-permute, ...), custom_call_target="tpu_custom_call" | custom-call | flops 6000 | bytes 18000 | tf_op jit(solution)/shard_map/pallas_call | solution.py:58
  88.1 11.4 %all_to_all.22 = bf16[8,128,256]{2,1,0:T(8,128)(2,1)S(1)} all-to-all(bf16[8,128,256]{2,1,0:T(8,128)(2,1)S(1)} %bitcast.29), channel_id=1, replica_groups={{0,16,1,17,8,24,9,25},{4,20,5,21,12,28,13,29},{2,18,3,19,10,26,11,27},{..., dimensions={0} | all-to-all | bytes 1048576 | tf_op jit(solution)/shard_map/all_to_all | solution.py:112
  99.4 3.9 %shard_map.306 = bf16[1024,256]{1,0:T(8,128)(2,1)S(1)} custom-call(bf16[1024,256]{1,0:T(8,128)(2,1)S(1)} %bitcast.26), custom_call_target="tpu_custom_call" | custom-call | flops 4000 | bytes 12000 | tf_op jit(solution)/shard_map/pallas_call | solution.py:58
  103.4 11.8 %all_to_all.23 = bf16[8,128,256]{2,1,0:T(8,128)(2,1)S(1)} all-to-all(bf16[8,128,256]{2,1,0:T(8,128)(2,1)S(1)} %bitcast.27), channel_id=1, replica_groups={{0,16,1,17,8,24,9,25},{4,20,5,21,12,28,13,29},{2,18,3,19,10,26,11,27},{..., dimensions={0} | all-to-all | bytes 1048576 | tf_op jit(solution)/shard_map/all_to_all | solution.py:112
  115.2 3.0 %shard_map.307 = (bf16[128,512]{1,0:T(8,128)(2,1)S(1)}, bf16[128,512]{1,0:T(8,128)(2,1)S(1)}, bf16[128,512]{1,0:T(8,128)(2,1)S(1)}, bf16[128,512]{1,0:T(8,128)(2...) custom-call(bf16[1024,256]{1,0:T(8,128)(2,1)S(1)} %bitcast.25, ...), custom_call_target="tpu_custom_call" | custom-call | flops 2000 | bytes 6000 | tf_op jit(solution)/shard_map/pallas_call | solution.py:58
  118.2 1.7 shard_map.308
  120.0 2.9 %collective-permute-start.18 = (bf16[128,512]{1,0:T(8,128)(2,1)S(1)}, bf16[128,512]{1,0:T(8,128)(2,1)S(1)}, u32[]{:S(2)}, u32[]{:S(2)}) collective-permute-start(bf16[128,512]{1,0:T(8,128)(2,1)S(1)} %get-tuple-element.148), channel_id=1, source_target_pairs={{0,0},{16,1},{1,2},{17,3},{8,4},{24,5},{9,6},{25,7},{4,8},{20,9},{... | collective-permute-start | bytes 393224 | tf_op jit(solution)/shard_map/ppermute | solution.py:795
  122.9 1.3 collective-permute-start.19
  124.2 2.7 %collective-permute-done.19.refs_1_ = bf16[144,128]{1,0:T(8,128)(2,1)S(1)} collective-permute-done((bf16[144,128]{1,0:T(8,128)(2,1)S(1)}, bf16[144,128]{1,0:T(8,128)(2,1)S(1)}, u32[]{:S(2)}, u32[]{:S(2)}) %collective-permute-start.19) | collective-permute-done | bytes 36896 | tf_op jit(solution)/shard_map/ppermute | solution.py:117
  127.0 2.1 %collective-permute-start.20 = (bf16[144,128]{1,0:T(8,128)(2,1)S(1)}, bf16[144,128]{1,0:T(8,128)(2,1)S(1)}, u32[]{:S(2)}, u32[]{:S(2)}) collective-permute-start(bf16[144,128]{1,0:T(8,128)(2,1)S(1)} %get-tuple-element.156.refs_0_), channel_id=1, source_target_pairs={{0,1},{1,0},{2,3},{3,2},{4,5},{5,4},{6,7},{7,6},{8,9},{9,8},{10,11... | collective-permute-start | bytes 110600 | tf_op jit(solution)/shard_map/ppermute | solution.py:117
  129.0 2.0 %collective-permute-done.20.refs_1_ = bf16[144,128]{1,0:T(8,128)(2,1)S(1)} collective-permute-done((bf16[144,128]{1,0:T(8,128)(2,1)S(1)}, bf16[144,128]{1,0:T(8,128)(2,1)S(1)}, u32[]{:S(2)}, u32[]{:S(2)}) %collective-permute-start.20) | collective-permute-done | bytes 36896 | tf_op jit(solution)/shard_map/ppermute | solution.py:117
  133.6 2.2 %collective-permute-start.23 = (bf16[256,1024]{1,0:T(8,128)(2,1)S(1)}, bf16[256,1024]{1,0:T(8,128)(2,1)S(1)}, u32[]{:S(2)}, u32[]{:S(2)}) collective-permute-start(bf16[256,1024]{1,0:T(8,128)(2,1)S(1)} %get-tuple-element.169), channel_id=1, source_target_pairs={{0,16},{1,17},{2,18},{3,19},{4,20},{5,21},{6,22},{7,23},{8,24},{9,... | collective-permute-start | bytes 1572872 | tf_op jit(solution)/shard_map/ppermute | solution.py:117
  135.7 1.0 collective-permute-start.24
  136.8 10.8 %shard_map.313 = (f32[128,1024]{1,0:T(8,128)S(1)}, bf16[144,1024]{1,0:T(8,128)(2,1)S(1)}) custom-call(f32[1024,128]{1,0:T(8,128)S(1)} %get-tuple-element.120.refs_1_.refs_6_.refs_0_, f32[1024,128]{1,0:T(8,128)S(1)} %get-tuple-element.121.refs_2_.refs_1_, f32[1024,128]{1,0:T(8,128)S(1)} %get-tuple-element.149.refs_2_, ...), custom_call_target="tpu_custom_call" | custom-call | flops 11000 | bytes 33000 | tf_op jit(solution)/shard_map/pallas_call | solution.py:58
  148.0 1.5 collective-permute-done.24.refs_3_
  149.7 1.8 shard_map.315
  151.6 1.1 collective-permute-start.28
  153.5 4.0 %collective-permute-start.25 = (bf16[128,512]{1,0:T(8,128)(2,1)S(1)}, bf16[128,512]{1,0:T(8,128)(2,1)S(1)}, u32[]{:S(2)}, u32[]{:S(2)}) collective-permute-start(bf16[128,512]{1,0:T(8,128)(2,1)S(1)} %get-tuple-element.173), channel_id=1, source_target_pairs={{0,0},{16,1},{1,2},{17,3},{8,4},{24,5},{9,6},{25,7},{4,8},{20,9},{... | collective-permute-start | bytes 393224 | tf_op jit(solution)/shard_map/ppermute | solution.py:822
  157.5 6.5 %collective-permute-done.25.refs_6_ = bf16[128,512]{1,0:T(8,128)(2,1)S(1)} collective-permute-done((bf16[128,512]{1,0:T(8,128)(2,1)S(1)}, bf16[128,512]{1,0:T(8,128)(2,1)S(1)}, u32[]{:S(2)}, u32[]{:S(2)}) %collective-permute-start.25) | collective-permute-done | bytes 131104 | tf_op jit(solution)/shard_map/ppermute | solution.py:822
  164.5 2.7 %collective-permute-start.30 = (bf16[64,1280]{1,0:T(8,128)(2,1)S(1)}, bf16[64,1280]{1,0:T(8,128)(2,1)S(1)}, u32[]{:S(2)}, u32[]{:S(2)}) collective-permute-start(bf16[64,1280]{1,0:T(8,128)(2,1)S(1)} %get-tuple-element.181), channel_id=1, source_target_pairs={{0,1},{1,0},{2,3},{3,2},{4,5},{5,4},{6,7},{7,6},{8,9},{9,8},{10,11... | collective-permute-start | bytes 491528 | tf_op jit(solution)/shard_map/ppermute | solution.py:117
  167.2 1.4 collective-permute-start.32
  168.6 3.0 %collective-permute-start.26 = (bf16[16,512]{1,0:T(8,128)(2,1)S(1)}, bf16[16,512]{1,0:T(8,128)(2,1)S(1)}, u32[]{:S(2)}, u32[]{:S(2)}) collective-permute-start(bf16[16,512]{1,0:T(8,128)(2,1)S(1)} %get-tuple-element.174), channel_id=1, source_target_pairs={{16,0},{1,1},{17,2},{8,3},{24,4},{9,5},{25,6},{20,8},{5,9},{21,10}... | collective-permute-start | bytes 49160 | tf_op jit(solution)/shard_map/ppermute | solution.py:823
  171.7 3.5 %collective-permute-done.26.refs_6_ = bf16[16,512]{1,0:T(8,128)(2,1)S(1)} collective-permute-done((bf16[16,512]{1,0:T(8,128)(2,1)S(1)}, bf16[16,512]{1,0:T(8,128)(2,1)S(1)}, u32[]{:S(2)}, u32[]{:S(2)}) %collective-permute-start.26) | collective-permute-done | bytes 16416 | tf_op jit(solution)/shard_map/ppermute | solution.py:823
  175.3 2.3 %collective-permute-start.37 = (bf16[32,2048]{1,0:T(8,128)(2,1)S(1)}, bf16[32,2048]{1,0:T(8,128)(2,1)S(1)}, u32[]{:S(2)}, u32[]{:S(2)}) collective-permute-start(bf16[32,2048]{1,0:T(8,128)(2,1)S(1)} %get-tuple-element.191), channel_id=1, source_target_pairs={{0,4},{1,5},{2,6},{3,7},{4,0},{5,1},{6,2},{7,3},{8,12},{9,13},{10,... | collective-permute-start | bytes 393224 | tf_op jit(solution)/shard_map/ppermute | solution.py:117
  178.4 1.4 collective-permute-start.35
  179.8 2.3 %collective-permute-start.36 = (bf16[16,1280]{1,0:T(8,128)(2,1)S(1)}, bf16[16,1280]{1,0:T(8,128)(2,1)S(1)}, u32[]{:S(2)}, u32[]{:S(2)}) collective-permute-start(bf16[16,1280]{1,0:T(8,128)(2,1)S(1)} %get-tuple-element.189), channel_id=1, source_target_pairs={{0,6},{1,7},{2,4},{3,5},{4,2},{5,3},{6,0},{7,1},{8,14},{9,15},{10,... | collective-permute-start | bytes 122888 | tf_op jit(solution)/shard_map/ppermute | solution.py:117
  182.7 4.0 %collective-permute-done.34.refs_1_ = bf16[16,1280]{1,0:T(8,128)(2,1)S(1)} collective-permute-done((bf16[16,1280]{1,0:T(8,128)(2,1)S(1)}, bf16[16,1280]{1,0:T(8,128)(2,1)S(1)}, u32[]{:S(2)}, u32[]{:S(2)}) %collective-permute-start.34) | collective-permute-done | bytes 40992 | tf_op jit(solution)/shard_map/ppermute | solution.py:117
  (65 shorter events, 17.4 us)
Async XLA Ops:
  0.7 14.7 %collective-permute-start = (bf16[128,512]{1,0:T(8,128)(2,1)}, bf16[128,512]{1,0:T(8,128)(2,1)S(1)}, u32[]{:S(2)}, u32[]{:S(2)}) collective-permute-start(bf16[128,512]{1,0:T(8,128)(2,1)} %bitcast.33), channel_id=1, source_target_pairs={{0,0},{1,16},{2,1},{3,17},{4,8},{5,24},{6,9},{7,25},{8,4},{9,20},{... | collective-permute-start | bytes 393224 | tf_op jit(solution)/shard_map/ppermute | solution.py:713
  6.1 9.3 %collective-permute-start.2 = (bf16[16,2304]{1,0:T(8,128)(2,1)}, bf16[16,2304]{1,0:T(8,128)(2,1)S(1)}, u32[]{:S(2)}, u32[]{:S(2)}) collective-permute-start(bf16[16,2304]{1,0:T(8,128)(2,1)} %get-tuple-element.112.refs_0_), channel_id=1, source_target_pairs={{0,4},{1,5},{2,6},{3,7},{4,0},{5,1},{6,2},{7,3},{8,12},{9,13},{10,... | collective-permute-start | bytes 221192 | tf_op jit(solution)/shard_map/ppermute | solution.py:117
  7.9 7.4 %collective-permute-start.1 = (bf16[16,512]{1,0:T(8,128)(2,1)S(1)}, bf16[16,512]{1,0:T(8,128)(2,1)S(1)}, u32[]{:S(2)}, u32[]{:S(2)}) collective-permute-start(bf16[16,512]{1,0:T(8,128)(2,1)S(1)} %slice_bitcast_fusion), channel_id=1, source_target_pairs={{0,16},{1,1},{2,17},{3,8},{4,24},{5,9},{6,25},{8,20},{9,5},{10,21}... | collective-permute-start | bytes 49160 | tf_op jit(solution)/shard_map/ppermute | solution.py:714
  15.4 0.9 copy-start
  16.3 0.9 copy-start.1
  17.2 0.9 copy-start.2
  18.5 14.0 %collective-permute-start.3 = (bf16[32,2304]{1,0:T(8,128)(2,1)S(1)}, bf16[32,2304]{1,0:T(8,128)(2,1)S(1)}, u32[]{:S(2)}, u32[]{:S(2)}) collective-permute-start(bf16[32,2304]{1,0:T(8,128)(2,1)S(1)} %get-tuple-element.114.refs_0_), channel_id=1, source_target_pairs={{0,2},{1,3},{2,0},{3,1},{4,6},{5,7},{6,4},{7,5},{8,10},{9,11},{10,... | collective-permute-start | bytes 442376 | tf_op jit(solution)/shard_map/ppermute | solution.py:117
  18.6 13.9 %collective-permute-start.5 = (bf16[128,512]{1,0:T(8,128)(2,1)S(1)}, bf16[128,512]{1,0:T(8,128)(2,1)S(1)}, u32[]{:S(2)}, u32[]{:S(2)}) collective-permute-start(bf16[128,512]{1,0:T(8,128)(2,1)S(1)} %get-tuple-element.116), channel_id=1, source_target_pairs={{0,0},{1,16},{2,1},{3,17},{4,8},{5,24},{6,9},{7,25},{8,4},{9,20},{... | collective-permute-start | bytes 393224 | tf_op jit(solution)/shard_map/ppermute | solution.py:725
  21.1 11.4 %collective-permute-start.4 = (bf16[32,1536]{1,0:T(8,128)(2,1)S(1)}, bf16[32,1536]{1,0:T(8,128)(2,1)S(1)}, u32[]{:S(2)}, u32[]{:S(2)}) collective-permute-start(bf16[32,1536]{1,0:T(8,128)(2,1)S(1)} %get-tuple-element.115.refs_2_), channel_id=1, source_target_pairs={{0,4},{1,5},{2,6},{3,7},{4,0},{5,1},{6,2},{7,3},{8,12},{9,13},{10,... | collective-permute-start | bytes 294920 | tf_op jit(solution)/shard_map/ppermute | solution.py:117
  33.2 10.9 %collective-permute-start.8 = (bf16[64,2304]{1,0:T(8,128)(2,1)S(1)}, bf16[64,2304]{1,0:T(8,128)(2,1)S(1)}, u32[]{:S(2)}, u32[]{:S(2)}) collective-permute-start(bf16[64,2304]{1,0:T(8,128)(2,1)S(1)} %get-tuple-element.117.refs_0_), channel_id=1, source_target_pairs={{0,17},{1,16},{2,19},{3,18},{4,21},{5,20},{6,23},{7,22},{8,25},{9,... | collective-permute-start | bytes 884744 | tf_op jit(solution)/shard_map/ppermute | solution.py:117
  33.3 15.7 %collective-permute-start.7 = (bf16[64,2304]{1,0:T(8,128)(2,1)S(1)}, bf16[64,2304]{1,0:T(8,128)(2,1)S(1)}, u32[]{:S(2)}, u32[]{:S(2)}) collective-permute-start(bf16[64,2304]{1,0:T(8,128)(2,1)S(1)} %get-tuple-element.117.refs_0_), channel_id=1, source_target_pairs={{0,16},{1,17},{2,18},{3,19},{4,20},{5,21},{6,22},{7,23},{8,24},{9,... | collective-permute-start | bytes 884744 | tf_op jit(solution)/shard_map/ppermute | solution.py:117
  35.8 13.7 %collective-permute-start.6 = (bf16[64,2304]{1,0:T(8,128)(2,1)S(1)}, bf16[64,2304]{1,0:T(8,128)(2,1)S(1)}, u32[]{:S(2)}, u32[]{:S(2)}) collective-permute-start(bf16[64,2304]{1,0:T(8,128)(2,1)S(1)} %get-tuple-element.117.refs_0_), channel_id=1, source_target_pairs={{0,1},{1,0},{2,3},{3,2},{4,5},{5,4},{6,7},{7,6},{8,9},{9,8},{10,11... | collective-permute-start | bytes 884744 | tf_op jit(solution)/shard_map/ppermute | solution.py:117
  36.8 6.1 %collective-permute-start.9 = (bf16[64,1536]{1,0:T(8,128)(2,1)S(1)}, bf16[64,1536]{1,0:T(8,128)(2,1)S(1)}, u32[]{:S(2)}, u32[]{:S(2)}) collective-permute-start(bf16[64,1536]{1,0:T(8,128)(2,1)S(1)} %get-tuple-element.118.refs_4_), channel_id=1, source_target_pairs={{0,2},{1,3},{2,0},{3,1},{4,6},{5,7},{6,4},{7,5},{8,10},{9,11},{10,... | collective-permute-start | bytes 589832 | tf_op jit(solution)/shard_map/ppermute | solution.py:117
  50.3 3.6 %collective-permute-start.10 = (bf16[256,2304]{1,0:T(8,128)(2,1)S(1)}, bf16[256,2304]{1,0:T(8,128)(2,1)S(1)}, u32[]{:S(2)}, u32[]{:S(2)}) collective-permute-start(bf16[256,2304]{1,0:T(8,128)(2,1)S(1)} %get-tuple-element.119.refs_2_), channel_id=1, source_target_pairs={{0,8},{1,9},{2,10},{3,11},{4,12},{5,13},{6,14},{7,15},{8,0},{9,1},... | collective-permute-start | bytes 3538952 | tf_op jit(solution)/shard_map/ppermute | solution.py:117
  50.4 27.2 %collective-permute-start.16 = (bf16[128,1536]{1,0:T(8,128)(2,1)S(1)}, bf16[128,1536]{1,0:T(8,128)(2,1)S(1)}, u32[]{:S(2)}, u32[]{:S(2)}) collective-permute-start(bf16[128,1536]{1,0:T(8,128)(2,1)S(1)} %get-tuple-element.133.refs_0_), channel_id=1, source_target_pairs={{0,17},{1,16},{2,19},{3,18},{4,21},{5,20},{6,23},{7,22},{8,25},{9,... | collective-permute-start | bytes 1179656 | tf_op jit(solution)/shard_map/ppermute | solution.py:117
  51.3 26.3 %collective-permute-start.15 = (bf16[128,1536]{1,0:T(8,128)(2,1)S(1)}, bf16[128,1536]{1,0:T(8,128)(2,1)S(1)}, u32[]{:S(2)}, u32[]{:S(2)}) collective-permute-start(bf16[128,1536]{1,0:T(8,128)(2,1)S(1)} %get-tuple-element.133.refs_0_), channel_id=1, source_target_pairs={{0,16},{1,17},{2,18},{3,19},{4,20},{5,21},{6,22},{7,23},{8,24},{9,... | collective-permute-start | bytes 1179656 | tf_op jit(solution)/shard_map/ppermute | solution.py:117
  52.8 24.8 %collective-permute-start.14 = (bf16[128,1536]{1,0:T(8,128)(2,1)S(1)}, bf16[128,1536]{1,0:T(8,128)(2,1)S(1)}, u32[]{:S(2)}, u32[]{:S(2)}) collective-permute-start(bf16[128,1536]{1,0:T(8,128)(2,1)S(1)} %get-tuple-element.133.refs_0_), channel_id=1, source_target_pairs={{0,1},{1,0},{2,3},{3,2},{4,5},{5,4},{6,7},{7,6},{8,9},{9,8},{10,11... | collective-permute-start | bytes 1179656 | tf_op jit(solution)/shard_map/ppermute | solution.py:117
  60.1 11.4 %collective-permute-start.11 = (bf16[144,128]{1,0:T(8,128)(2,1)S(1)}, bf16[144,128]{1,0:T(8,128)(2,1)S(1)}, u32[]{:S(2)}, u32[]{:S(2)}) collective-permute-start(bf16[144,128]{1,0:T(8,128)(2,1)S(1)} %get-tuple-element.127.refs_0_.refs_12_), channel_id=1, source_target_pairs={{0,16},{1,17},{2,18},{3,19},{4,20},{5,21},{6,22},{7,23},{8,24},{9,... | collective-permute-start | bytes 110600 | tf_op jit(solution)/shard_map/ppermute | solution.py:117
  71.5 4.0 %collective-permute-start.12 = (bf16[144,128]{1,0:T(8,128)(2,1)S(1)}, bf16[144,128]{1,0:T(8,128)(2,1)S(1)}, u32[]{:S(2)}, u32[]{:S(2)}) collective-permute-start(bf16[144,128]{1,0:T(8,128)(2,1)S(1)} %get-tuple-element.128.refs_0_), channel_id=1, source_target_pairs={{0,1},{1,0},{2,3},{3,2},{4,5},{5,4},{6,7},{7,6},{8,9},{9,8},{10,11... | collective-permute-start | bytes 110600 | tf_op jit(solution)/shard_map/ppermute | solution.py:117
  75.6 1.3 collective-permute-start.13
  78.3 3.5 %collective-permute-start.17 = (bf16[512,1536]{1,0:T(8,128)(2,1)S(1)}, bf16[512,1536]{1,0:T(8,128)(2,1)S(1)}, u32[]{:S(2)}, u32[]{:S(2)}) collective-permute-start(bf16[512,1536]{1,0:T(8,128)(2,1)S(1)} %shard_map.304.refs_10_), channel_id=1, source_target_pairs={{0,8},{1,9},{2,10},{3,11},{4,12},{5,13},{6,14},{7,15},{8,0},{9,1},... | collective-permute-start | bytes 4718600 | tf_op jit(solution)/shard_map/ppermute | solution.py:117
  119.9 13.2 %collective-permute-start.22 = (bf16[512,2048]{1,0:T(8,128)(2,1)S(1)}, bf16[512,2048]{1,0:T(8,128)(2,1)S(1)}, u32[]{:S(2)}, u32[]{:S(2)}) collective-permute-start(bf16[512,2048]{1,0:T(8,128)(2,1)S(1)} %get-tuple-element.162), channel_id=1, source_target_pairs={{0,8},{1,9},{2,10},{3,11},{4,12},{5,13},{6,14},{7,15},{8,0},{9,1},... | collective-permute-start | bytes 6291464 | tf_op jit(solution)/shard_map/ppermute | solution.py:117
  120.0 13.1 %collective-permute-start.18 = (bf16[128,512]{1,0:T(8,128)(2,1)S(1)}, bf16[128,512]{1,0:T(8,128)(2,1)S(1)}, u32[]{:S(2)}, u32[]{:S(2)}) collective-permute-start(bf16[128,512]{1,0:T(8,128)(2,1)S(1)} %get-tuple-element.148), channel_id=1, source_target_pairs={{0,0},{16,1},{1,2},{17,3},{8,4},{24,5},{9,6},{25,7},{4,8},{20,9},{... | collective-permute-start | bytes 393224 | tf_op jit(solution)/shard_map/ppermute | solution.py:795
  122.9 4.0 %collective-permute-start.19 = (bf16[144,128]{1,0:T(8,128)(2,1)S(1)}, bf16[144,128]{1,0:T(8,128)(2,1)S(1)}, u32[]{:S(2)}, u32[]{:S(2)}) collective-permute-start(bf16[144,128]{1,0:T(8,128)(2,1)S(1)} %get-tuple-element.155.refs_0_), channel_id=1, source_target_pairs={{0,16},{1,17},{2,18},{3,19},{4,20},{5,21},{6,22},{7,23},{8,24},{9,... | collective-permute-start | bytes 110600 | tf_op jit(solution)/shard_map/ppermute | solution.py:117
  127.0 4.0 %collective-permute-start.20 = (bf16[144,128]{1,0:T(8,128)(2,1)S(1)}, bf16[144,128]{1,0:T(8,128)(2,1)S(1)}, u32[]{:S(2)}, u32[]{:S(2)}) collective-permute-start(bf16[144,128]{1,0:T(8,128)(2,1)S(1)} %get-tuple-element.156.refs_0_), channel_id=1, source_target_pairs={{0,1},{1,0},{2,3},{3,2},{4,5},{5,4},{6,7},{7,6},{8,9},{9,8},{10,11... | collective-permute-start | bytes 110600 | tf_op jit(solution)/shard_map/ppermute | solution.py:117
  131.0 1.4 collective-permute-start.21
  133.6 14.4 %collective-permute-start.23 = (bf16[256,1024]{1,0:T(8,128)(2,1)S(1)}, bf16[256,1024]{1,0:T(8,128)(2,1)S(1)}, u32[]{:S(2)}, u32[]{:S(2)}) collective-permute-start(bf16[256,1024]{1,0:T(8,128)(2,1)S(1)} %get-tuple-element.169), channel_id=1, source_target_pairs={{0,16},{1,17},{2,18},{3,19},{4,20},{5,21},{6,22},{7,23},{8,24},{9,... | collective-permute-start | bytes 1572872 | tf_op jit(solution)/shard_map/ppermute | solution.py:117
  135.7 13.7 %collective-permute-start.24 = (bf16[256,1024]{1,0:T(8,128)(2,1)S(1)}, bf16[256,1024]{1,0:T(8,128)(2,1)S(1)}, u32[]{:S(2)}, u32[]{:S(2)}) collective-permute-start(bf16[256,1024]{1,0:T(8,128)(2,1)S(1)} %get-tuple-element.171), channel_id=1, source_target_pairs={{0,1},{1,0},{2,3},{3,2},{4,5},{5,4},{6,7},{7,6},{8,9},{9,8},{10,11... | collective-permute-start | bytes 1572872 | tf_op jit(solution)/shard_map/ppermute | solution.py:117
  151.5 12.6 %collective-permute-start.27 = (bf16[256,1280]{1,0:T(8,128)(2,1)S(1)}, bf16[256,1280]{1,0:T(8,128)(2,1)S(1)}, u32[]{:S(2)}, u32[]{:S(2)}) collective-permute-start(bf16[256,1280]{1,0:T(8,128)(2,1)S(1)} %get-tuple-element.176), channel_id=1, source_target_pairs={{0,8},{1,9},{2,10},{3,11},{4,12},{5,13},{6,14},{7,15},{8,0},{9,1},... | collective-permute-start | bytes 1966088 | tf_op jit(solution)/shard_map/ppermute | solution.py:117
  151.6 12.5 %collective-permute-start.28 = (bf16[128,1024]{1,0:T(8,128)(2,1)S(1)}, bf16[128,1024]{1,0:T(8,128)(2,1)S(1)}, u32[]{:S(2)}, u32[]{:S(2)}) collective-permute-start(bf16[128,1024]{1,0:T(8,128)(2,1)S(1)} %get-tuple-element.177), channel_id=1, source_target_pairs={{0,1},{1,0},{2,3},{3,2},{4,5},{5,4},{6,7},{7,6},{8,9},{9,8},{10,11... | collective-permute-start | bytes 786440 | tf_op jit(solution)/shard_map/ppermute | solution.py:117
  152.7 11.4 %collective-permute-start.29 = (bf16[128,1024]{1,0:T(8,128)(2,1)S(1)}, bf16[128,1024]{1,0:T(8,128)(2,1)S(1)}, u32[]{:S(2)}, u32[]{:S(2)}) collective-permute-start(bf16[128,1024]{1,0:T(8,128)(2,1)S(1)} %get-tuple-element.179), channel_id=1, source_target_pairs={{0,16},{1,17},{2,18},{3,19},{4,20},{5,21},{6,22},{7,23},{8,24},{9,... | collective-permute-start | bytes 786440 | tf_op jit(solution)/shard_map/ppermute | solution.py:117
  153.5 10.6 %collective-permute-start.25 = (bf16[128,512]{1,0:T(8,128)(2,1)S(1)}, bf16[128,512]{1,0:T(8,128)(2,1)S(1)}, u32[]{:S(2)}, u32[]{:S(2)}) collective-permute-start(bf16[128,512]{1,0:T(8,128)(2,1)S(1)} %get-tuple-element.173), channel_id=1, source_target_pairs={{0,0},{16,1},{1,2},{17,3},{8,4},{24,5},{9,6},{25,7},{4,8},{20,9},{... | collective-permute-start | bytes 393224 | tf_op jit(solution)/shard_map/ppermute | solution.py:822
  164.4 10.8 %collective-permute-start.33 = (bf16[64,2048]{1,0:T(8,128)(2,1)S(1)}, bf16[64,2048]{1,0:T(8,128)(2,1)S(1)}, u32[]{:S(2)}, u32[]{:S(2)}) collective-permute-start(bf16[64,2048]{1,0:T(8,128)(2,1)S(1)} %get-tuple-element.185), channel_id=1, source_target_pairs={{0,2},{1,3},{2,0},{3,1},{4,6},{5,7},{6,4},{7,5},{8,10},{9,11},{10,... | collective-permute-start | bytes 786440 | tf_op jit(solution)/shard_map/ppermute | solution.py:117
  164.5 10.7 %collective-permute-start.30 = (bf16[64,1280]{1,0:T(8,128)(2,1)S(1)}, bf16[64,1280]{1,0:T(8,128)(2,1)S(1)}, u32[]{:S(2)}, u32[]{:S(2)}) collective-permute-start(bf16[64,1280]{1,0:T(8,128)(2,1)S(1)} %get-tuple-element.181), channel_id=1, source_target_pairs={{0,1},{1,0},{2,3},{3,2},{4,5},{5,4},{6,7},{7,6},{8,9},{9,8},{10,11... | collective-permute-start | bytes 491528 | tf_op jit(solution)/shard_map/ppermute | solution.py:117
  167.2 8.0 %collective-permute-start.31 = (bf16[64,1280]{1,0:T(8,128)(2,1)S(1)}, bf16[64,1280]{1,0:T(8,128)(2,1)S(1)}, u32[]{:S(2)}, u32[]{:S(2)}) collective-permute-start(bf16[64,1280]{1,0:T(8,128)(2,1)S(1)} %get-tuple-element.182), channel_id=1, source_target_pairs={{0,16},{1,17},{2,18},{3,19},{4,20},{5,21},{6,22},{7,23},{8,24},{9,... | collective-permute-start | bytes 491528 | tf_op jit(solution)/shard_map/ppermute | solution.py:117
  167.2 8.0 %collective-permute-start.32 = (bf16[64,1280]{1,0:T(8,128)(2,1)S(1)}, bf16[64,1280]{1,0:T(8,128)(2,1)S(1)}, u32[]{:S(2)}, u32[]{:S(2)}) collective-permute-start(bf16[64,1280]{1,0:T(8,128)(2,1)S(1)} %get-tuple-element.183), channel_id=1, source_target_pairs={{0,17},{1,16},{2,19},{3,18},{4,21},{5,20},{6,23},{7,22},{8,25},{9,... | collective-permute-start | bytes 491528 | tf_op jit(solution)/shard_map/ppermute | solution.py:117
  168.6 6.5 %collective-permute-start.26 = (bf16[16,512]{1,0:T(8,128)(2,1)S(1)}, bf16[16,512]{1,0:T(8,128)(2,1)S(1)}, u32[]{:S(2)}, u32[]{:S(2)}) collective-permute-start(bf16[16,512]{1,0:T(8,128)(2,1)S(1)} %get-tuple-element.174), channel_id=1, source_target_pairs={{16,0},{1,1},{17,2},{8,3},{24,4},{9,5},{25,6},{20,8},{5,9},{21,10}... | collective-permute-start | bytes 49160 | tf_op jit(solution)/shard_map/ppermute | solution.py:823
  175.3 11.4 %collective-permute-start.37 = (bf16[32,2048]{1,0:T(8,128)(2,1)S(1)}, bf16[32,2048]{1,0:T(8,128)(2,1)S(1)}, u32[]{:S(2)}, u32[]{:S(2)}) collective-permute-start(bf16[32,2048]{1,0:T(8,128)(2,1)S(1)} %get-tuple-element.191), channel_id=1, source_target_pairs={{0,4},{1,5},{2,6},{3,7},{4,0},{5,1},{6,2},{7,3},{8,12},{9,13},{10,... | collective-permute-start | bytes 393224 | tf_op jit(solution)/shard_map/ppermute | solution.py:117
  177.6 9.1 %collective-permute-start.34 = (bf16[16,1280]{1,0:T(8,128)(2,1)S(1)}, bf16[16,1280]{1,0:T(8,128)(2,1)S(1)}, u32[]{:S(2)}, u32[]{:S(2)}) collective-permute-start(bf16[16,1280]{1,0:T(8,128)(2,1)S(1)} %get-tuple-element.187), channel_id=1, source_target_pairs={{0,4},{1,5},{2,6},{3,7},{4,0},{5,1},{6,2},{7,3},{8,12},{9,13},{10,... | collective-permute-start | bytes 122888 | tf_op jit(solution)/shard_map/ppermute | solution.py:117
  178.4 8.3 %collective-permute-start.35 = (bf16[16,1280]{1,0:T(8,128)(2,1)S(1)}, bf16[16,1280]{1,0:T(8,128)(2,1)S(1)}, u32[]{:S(2)}, u32[]{:S(2)}) collective-permute-start(bf16[16,1280]{1,0:T(8,128)(2,1)S(1)} %get-tuple-element.188), channel_id=1, source_target_pairs={{0,2},{1,3},{2,0},{3,1},{4,6},{5,7},{6,4},{7,5},{8,10},{9,11},{10,... | collective-permute-start | bytes 122888 | tf_op jit(solution)/shard_map/ppermute | solution.py:117
  179.8 7.0 %collective-permute-start.36 = (bf16[16,1280]{1,0:T(8,128)(2,1)S(1)}, bf16[16,1280]{1,0:T(8,128)(2,1)S(1)}, u32[]{:S(2)}, u32[]{:S(2)}) collective-permute-start(bf16[16,1280]{1,0:T(8,128)(2,1)S(1)} %get-tuple-element.189), channel_id=1, source_target_pairs={{0,6},{1,7},{2,4},{3,5},{4,2},{5,3},{6,0},{7,1},{8,14},{9,15},{10,... | collective-permute-start | bytes 122888 | tf_op jit(solution)/shard_map/ppermute | solution.py:117
where the time goes:
time: 191 us; the launch traced here: 188 us
  waiting for transfers between devices  64.1 us (34%)
  starting transfers between devices  53.6 us (28%)
  Pallas kernels  41.7 us (22%)
  blocking collectives  23.2 us (12%)
  local copies, waits for them, and re-layouts  4.07 us (2%)
    ppermute x32, waiting for transfers between devices, send(): return lax.ppermute(value, ALL, [(i, i ^ mask) for i in range(32)])  50.7 us
    pallas_call x23, Pallas kernels, run(): pl.pallas_call(inner, out_shape=[jax.ShapeDtypeStruct(shape, dtype) for s...  41.7 us
    ppermute x32, starting transfers between devices, send(): return lax.ppermute(value, ALL, [(i, i ^ mask) for i in range(32)])  33.6 us
    all_to_all x2, blocking collectives, swap(): lax.all_to_all(value, ALL, 0, 0, tiled=True, axis_index_groups=groups)  23.2 us
    ppermute x1, waiting for transfers between devices, body(): grad_tok = lax.ppermute(own, ALL, away)  6.55 us
    ppermute x1, starting transfers between devices, body(): grad_tok = lax.ppermute(own, ALL, away)  4.05 us
    ppermute x1, starting transfers between devices, body(): lax.ppermute(tok0[count - HALO:], ALL, [(s * 8 + c, plan.place(s, c + 1))...  4.02 us
  transfers between devices with their start and end apart: 38, of which 18 were waited for; matrix products, arithmetic and copies ran while one was open for 1% of the time, Pallas kernels for 11%

commit v1 on v0

--- a/solution.py
+++ b/solution.py
@@ -117,7 +117,7 @@
     return lax.ppermute(value, ALL, [(i, i ^ mask) for i in range(32)])
 
 
-def start_blocks(target, pieces, masks, me, sem, row_in, rows, first, cols):
+def start_blocks(target, pieces, masks, me, sem, row_in, rows, first, cols, to=0):
     per_piece = len(masks) // len(pieces)
     height = pieces[0].shape[0] // per_piece
     for i, piece in enumerate(pieces):
@@ -125,7 +125,7 @@
             block = me ^ masks[i * per_piece + k]
             pltpu.make_async_copy(
                 piece.at[pl.ds(k * height + row_in, rows), pl.ds(first, cols)],
-                target.at[pl.ds(pl.multiple_of(block * rows, 16), rows), :],
+                target.at[pl.ds(pl.multiple_of(block * rows, 16), rows), pl.ds(to, cols)],
                 sem,
             ).start()
 
@@ -166,12 +166,14 @@
         copy.start()
     for copy in copies:
         copy.wait()
-    one[:, : 2 * E] = b_in[...].astype(BF16)
+    one[:, :E] = b_in[:, :E].astype(BF16)
+    two[:16, 3 * D :] = b_in[:, E : E + D].astype(BF16)
+    two[16:, 3 * D :] = b_in[:, E + D :].astype(BF16)
     two[:, :D] = b_out[...].astype(BF16)
     two[:16, D : 2 * D] = b_q[...].astype(BF16)
-    two[:16, 2 * D :] = b_k[...].astype(BF16)
+    two[:16, 2 * D : 3 * D] = b_k[...].astype(BF16)
     two[16:, D : 2 * D] = b_v[...].astype(BF16)
-    two[16:, 2 * D :] = b_o[...].astype(BF16)
+    two[16:, 2 * D : 3 * D] = b_o[...].astype(BF16)
     rows[...] = jnp.zeros_like(rows)
     rows[ROW_X : ROW_X + 64, :] = b_x[...].T
     rows[ROW_DT : ROW_DT + RANK, :] = b_dt[...]
@@ -182,7 +184,7 @@
     rows[ROW_SK : ROW_SK + 1, :] = b_sk[...]
     rows[ROW_G1 : ROW_G1 + 1, :16] = b_g1[...]
     rows[ROW_G2 : ROW_G2 + 1, :16] = b_g2[...]
-    one[:, 2 * E :] = jnp.concatenate([rows[16 * q : 16 * q + 16, :] for q in range(8)], axis=1).astype(BF16)
+    one[:, E:] = jnp.concatenate([rows[16 * q : 16 * q + 16, :] for q in range(8)], axis=1).astype(BF16)
 
 
 def join_smalls(target, smalls, masks, me):
@@ -221,13 +223,13 @@
 
 def front_kernel(plan, np_, masks, tok, halo, *refs):
     pieces = refs[:np_]
-    (normed, u_out, z_out, conv_out, act_out, proj_out, sig_out, dt3, au3, a3, state, weight, pm, gains, bx, smalls, sems) = refs[np_:]
+    (normed, u_out, conv_out, act_out, proj_out, sig_out, dt3, au3, a3, state, weight, pm, gains, bx, cx, smalls, sems) = refs[np_:]
     me = plan.me()
-    start_blocks(weight, pieces, masks, me, sems.at[0], 0, 16, 0, 2 * E)
+    start_blocks(weight, pieces, masks, me, sems.at[0], 0, 16, 0, E)
     height = smalls.shape[0] // np_
     for i, piece in enumerate(pieces):
         pltpu.make_async_copy(
-            piece.at[:, pl.ds(2 * E, 256)], smalls.at[pl.ds(i * height, height), :], sems.at[1]).start()
+            piece.at[:, pl.ds(E, 256)], smalls.at[pl.ds(i * height, height), :], sems.at[1]).start()
     wait_whole(smalls, sems.at[1])
     join_smalls(pm, smalls, masks, me)
     gain = gain_row(pm, ROW_G1)
@@ -239,8 +241,7 @@
     low = (x * r * gain).astype(BF16)
     normed[...] = low
     wait_whole(weight, sems.at[0])
-    u_out[...] = nn(low, weight[:, :E])
-    z_out[...] = nn(low[HALO:], weight[:, E:])
+    u_out[...] = nn(low, weight[...])
     conv = pm[ROW_CB : ROW_CB + 1, :]
     for k in range(KW):
         conv = conv + pm[ROW_CW + k : ROW_CW + k + 1, :] * u_out[HALO - 3 + k : HALO - 3 + k + tokens, :]
@@ -257,6 +258,7 @@
     spread(au3, act.astype(F32))
     spread(a3, -LOG2E * jnp.exp(pm[ROW_A : ROW_A + NS, :]))
     broadcast_rows(bx, proj, RANK)
+    broadcast_rows(cx, proj, RANK + NS)
     decay = [a3[8 * n : 8 * n + 8, :] for n in range(NS)]
 
     def advance(t, carried):
@@ -306,31 +308,33 @@
     entry[128:, :] = jnp.where(later, held[128:, :] + theirs[128:, :], held[128:, :])
 
 
-def exchange(plan, state, a3, forward):
+def exchange(plan, state, a3, forward, beside=lambda step, entry: []):
     if plan.fast:
-        group, entry = state, jnp.zeros((144, 128), F32)
+        group, entry, firsts = state, jnp.zeros((144, 128), F32), []
         for step in range(3):
+            other = send(group, CHUNK_MASKS[1 << step])
             group, entry = run(
-                functools.partial(merge_kernel, plan, step, forward),
-                [group, send(group, CHUNK_MASKS[1 << step]), entry, a3], [((144, 128), BF16), ((144, 128), F32)])
-        return entry
+                functools.partial(merge_kernel, plan, step, forward), [group, other, entry, a3],
+                [((144, 128), BF16), ((144, 128), F32)], after=beside(step, entry if step else group))
+            firsts.append(entry)
+        return entry, firsts
     states = lax.all_gather(state, "ctx", axis=0, tiled=True)
     return run(
         functools.partial(combine_kernel, plan, forward), [states, a3], [((144, 128), F32)],
-        [pltpu.VMEM((144 * plan.chunks, 128), F32)])[0]
+        [pltpu.VMEM((144 * plan.chunks, 128), F32)])[0], []
 
 
 def mid_kernel(plan, nb, masks, *refs):
-    tok, dt3, au3, proj, a3, z_in, pm, gains, cot, entry = refs[:10]
-    pieces = refs[10 : 10 + nb]
-    pay, mamba, gated_out, middle_out, all_states, w_out, w_qk, w_vo, y3, bx, cx, sems = refs[10 + nb :]
+    tok, dt3, au3, a3, normed, pm, gains, cot, entry, bx, cx = refs[:11]
+    pieces = refs[11 : 11 + nb]
+    pay, mamba, gated_out, middle_out, all_states, w_out, w_qk, w_vo, w_z, z_out, y3, sems = refs[11 + nb :]
     tokens = tok.shape[0]
     me = plan.me()
+    start_blocks(w_z, pieces, masks, me, sems.at[3], 0, 16, 3 * D, D)
+    start_blocks(w_z, pieces, masks, me, sems.at[3], 16, 16, 3 * D, D, D)
     start_blocks(w_out, pieces, masks, me, sems.at[0], 0, 32, 0, D)
     start_blocks(w_qk, pieces, masks, me, sems.at[1], 0, 16, D, 2 * D)
     start_blocks(w_vo, pieces, masks, me, sems.at[2], 16, 16, D, 2 * D)
-    broadcast_rows(bx, proj, RANK)
-    broadcast_rows(cx, proj, RANK + NS)
     decay = [a3[8 * n : 8 * n + 8, :] for n in range(NS)]
     held = tuple(entry[8 * n : 8 * n + 8, :] for n in range(NS))
     all_states[:128, :] = entry[:128, :]
@@ -354,7 +358,9 @@
     act = gathered(au3, tokens)
     y = gathered(y3, tokens) + pm[ROW_SK : ROW_SK + 1, :] * act
     mamba[...] = y
-    z = z_in[...]
+    wait_whole(w_z, sems.at[3])
+    z = nn(normed[HALO:, :], w_z[...])
+    z_out[...] = z
     gated = (y * (z * sigmoid(z))).astype(BF16)
     gated_out[...] = gated
     wait_whole(w_out, sems.at[0])
@@ -412,10 +418,9 @@
     back[:, 3 * HDIM :] = dv[...].astype(BF16)
 
 
-def turn_kernel(plan, got, middle, cot, gains, z_in, mamba, dt3, proj, a3, w_out, w_qk, w_vo, first,
-                att, gq, gk, gv, grad_middle, mix, gz, gy3, state, gain_grad, cx):
+def turn_kernel(plan, got, middle, cot, gains, z_in, mamba, dt3, cx, a3, w_out, w_qk, w_vo, first,
+                att, gq, gk, gv, grad_middle, mix, gz, gy3, state, gain_grad):
     tokens = middle.shape[0]
-    broadcast_rows(cx, proj, RANK + NS)
     for h in range(HEADS):
         for i, part in enumerate((att, gq, gk, gv)):
             part[:, h * HDIM : (h + 1) * HDIM] = got[h * tokens : (h + 1) * tokens, i * HDIM : (i + 1) * HDIM]
@@ -458,6 +463,10 @@
             out[k * height + row : k * height + row + rows, first : first + cols] = source[
                 pl.ds(pl.multiple_of(block * rows, 16), rows), col : col + cols
             ].astype(BF16)
+
+
+def grad_c_kernel(gy3, all_states, grad_c):
+    diagonal_sums(grad_c, 0, lambda rows: gy3[rows, :], all_states, 1)
 
 
 def weights_kernel(plan, no, att, gq, gk, gv, mix, gated, middle, gains, cot, w_vo, normed, gz, *refs):
@@ -482,11 +491,25 @@
     pack_blocks(plan, outs, wide, 16, 32, 16, 3 * D, D, D)
 
 
-def back_kernel(plan, dt3, au3, gy3, a3, proj, pm, all_states, sig, act, conv_in, u_in, leaving,
-                small_grads, gu_out, bx, cx, grads, gs3, ga3, gal, skip3, low_rank, padded):
+def diagonal_sums(out, col, channels, held, offset, span=16):
+    row_t = lax.broadcasted_iota(jnp.int32, (span, span * NS), 0)
+    col_t = lax.broadcasted_iota(jnp.int32, (span, span * NS), 1) // NS
+    pick = (
+        lax.broadcasted_iota(jnp.int32, (span * NS, NS), 0) % NS
+        == lax.broadcasted_iota(jnp.int32, (span * NS, NS), 1)
+    ).astype(BF16)
+    for block in range(out.shape[0] // span):
+        total = jnp.zeros((span, span * NS), F32)
+        for s in range(LG):
+            held_rows = held[pl.ds((block * span + offset) * 128 + s, span * NS, stride=LG), :].astype(BF16)
+            total = total + nt(channels(pl.ds(block * span * 8 + s, span, stride=LG)).astype(BF16), held_rows)
+        own = jnp.where(row_t == col_t, total, 0.0).astype(BF16)
+        out[block * span : (block + 1) * span, col : col + NS] = nn(own, pick)
+
+
+def back_kernel(plan, dt3, au3, gy3, a3, proj, pm, all_states, sig, act, conv_in, u_in, leaving, bx, cx, grad_c,
+                small_grads, gu_out, grads, gs3, ga3, gal, skip3, low_rank, padded):
     tokens = dt3.shape[0] // LG
-    broadcast_rows(bx, proj, RANK)
-    broadcast_rows(cx, proj, RANK + NS)
     decay = [a3[8 * n : 8 * n + 8, :] for n in range(NS)]
     zero = jnp.zeros((8, 128), F32)
     spread(skip3, pm[ROW_SK : ROW_SK + 1, :])
@@ -517,28 +540,10 @@
         ga3[at, :] = from_b * size + skip * grad
         return tuple(fresh), skipped + grad * value
 
-    _, skipped = lax.fori_loop(0, tokens, retreat, (carried, zero), unroll=2)
-
-    span = 16
-    row_t = lax.broadcasted_iota(jnp.int32, (span, span * NS), 0)
-    col_t = lax.broadcasted_iota(jnp.int32, (span, span * NS), 1) // NS
-    pick = (
-        lax.broadcasted_iota(jnp.int32, (span * NS, NS), 0) % NS
-        == lax.broadcasted_iota(jnp.int32, (span * NS, NS), 1)
-    ).astype(BF16)
-    for block in range(tokens // span):
-        total_b = jnp.zeros((span, span * NS), F32)
-        total_c = jnp.zeros((span, span * NS), F32)
-        for s in range(LG):
-            rows = pl.ds(block * span * 8 + s, span, stride=LG)
-            grad_rows = grads[pl.ds(block * span * 128 + s, span * NS, stride=LG), :].astype(BF16)
-            held_rows = all_states[pl.ds((block * span + 1) * 128 + s, span * NS, stride=LG), :].astype(BF16)
-            total_b = total_b + nt((dt3[rows, :] * au3[rows, :]).astype(BF16), grad_rows)
-            total_c = total_c + nt(gy3[rows, :].astype(BF16), held_rows)
-        own_b = jnp.where(row_t == col_t, total_b, 0.0).astype(BF16)
-        own_c = jnp.where(row_t == col_t, total_c, 0.0).astype(BF16)
-        low_rank[block * span : (block + 1) * span, RANK : RANK + NS] = nn(own_b, pick)
-        low_rank[block * span : (block + 1) * span, RANK + NS : RANK + 2 * NS] = nn(own_c, pick)
+    _, skipped = lax.fori_loop(0, tokens, retreat, (carried, zero), unroll=4)
+
+    diagonal_sums(low_rank, RANK, lambda rows: dt3[rows, :] * au3[rows, :], grads, 0)
+    low_rank[:, RANK + NS : RANK + 2 * NS] = grad_c[:, :NS]
 
     grad_pre = gathered(gs3, tokens) * sig[...]
     grad_pre_low = grad_pre.astype(BF16)
@@ -570,7 +575,7 @@
     gu_out[...] = gu.astype(BF16)
 
 
-def last_kernel(plan, no, tok, halo, gains, gu, gz, grad_middle, weight, normed, small_grads, gain_two, *refs):
+def last_kernel(plan, no, tok, halo, gains, gu, gz, grad_middle, w_u, w_z, normed, small_grads, gain_two, *refs):
     outs = refs[:no]
     own, before, large, spaced = refs[no:]
     me = plan.me()
@@ -578,13 +583,13 @@
     pack_blocks(plan, outs, large, 16, 16, 0, 0)
     x = jnp.concatenate([halo[...].astype(F32), tok[...].astype(F32)], axis=0)
     r = lax.rsqrt(jnp.mean(x * x, axis=-1, keepdims=True) + EPS)
-    from_z = nt(gz[...], weight[:, E:])
-    grad_n = nt(gu[...], weight[:, :E]) + jnp.concatenate([jnp.zeros((HALO, D), F32), from_z], axis=0)
+    from_z = nt(gz[...], w_z[...])
+    grad_n = nt(gu[...], w_u[...]) + jnp.concatenate([jnp.zeros((HALO, D), F32), from_z], axis=0)
     gain_one = jnp.sum(grad_n * x * r, axis=0, keepdims=True)
     q = grad_n * gains[0:1, :]
     base = r * q - x * (r * r * r) * jnp.mean(q * x, axis=-1, keepdims=True)
-    own[...] = (grad_middle[...] + base[HALO:, :]).astype(BF16)
-    before[...] = base[:HALO, :].astype(BF16)
+    own[...] = grad_middle[...] + base[HALO:, :]
+    before[...] = base[:HALO, :]
     spaced[...] = small_grads[...]
     blank = jnp.zeros((1, 16), F32)
     for row, grad in ((ROW_G1, gain_one), (ROW_G2, gain_two[...])):
@@ -605,7 +610,10 @@
 
 
 def finish_kernel(*refs):
-    u_ins, ins = refs[:4], refs[4:6]
+    (own, result), refs = refs[:2], refs[2:]
+    u_ins, ins, (own_out, result_out), refs = refs[:4], refs[4:6], refs[6:8], refs[2:]
+    own_out[...] = own[...]
+    result_out[...] = result[...]
     out_g, q_g, k_g, v_g, o_g, in_g, x_g, dt_g, a_g, cw_g, cb_g, db_g, sk_g, g1_g, g2_g, rows = refs[6:]
     total = total_of(ins)
     out_g[...] = total[:, :D]
@@ -642,12 +650,12 @@
         wait_whole(out, sems.at[i])
 
 
-def join(groups, after=()):
+def join(groups, after=(), limit=12):
     counts = [len(group) for group in groups]
     outs = [((group[0].shape[0] * len(group), group[0].shape[1]), group[0].dtype) for group in groups]
     return run(
         functools.partial(join_kernel, counts), [], outs, [pltpu.SemaphoreType.DMA((len(groups),))],
-        raw=[part for group in groups for part in group], after=after)
+        raw=[part for group in groups for part in group], after=after, limit=limit)
 
 
 def spread_out(value, stage):
@@ -679,7 +687,14 @@
     out[:, to] = total.astype(out.dtype)
 
 
-def cut_three_kernel(u_own, u_got, a_own, a_got, b_own, b_got, u_0, u_1, u_2, u_3, keep, give):
+def add_tail(out, own, tail):
+    rows = own.shape[0] - HALO
+    out[:rows, :] = own[:rows, :].astype(BF16)
+    out[rows:, :] = (own[rows:, :] + tail[...]).astype(BF16)
+
+
+def cut_three_kernel(u_own, u_got, a_own, a_got, b_own, b_got, own, tail, own_out, u_0, u_1, u_2, u_3, keep, give):
+    add_tail(own_out, own, tail)
     rows = u_0.shape[0]
     for i, out in enumerate((u_0, u_1, u_2, u_3)):
         add_rows(out, slice(i * rows, (i + 1) * rows), (u_own, u_got))
@@ -717,15 +732,15 @@
         raw = [in_proj, x_proj, dt_proj, a_log.T, conv_weight.T, conv_bias[None], dt_bias[None], d_skip[None],
                mixer_gain[None], attn_gain[None], out_proj, w_query, w_key, w_value, w_output]
         pack_one, pack_two = run(
-            pack_kernel, [], [((16, 2 * E + 256), BF16), ((32, 3 * D), BF16)],
+            pack_kernel, [], [((16, E + 256), BF16), ((32, 4 * D), BF16)],
             [pltpu.VMEM((SMALL_ROWS, 32), F32)] + [pltpu.VMEM(value.shape, F32) for value in raw]
             + [pltpu.SemaphoreType.DMA((len(raw),))], far=raw, limit=60)
-        one, two, cot = join([[pack_one, send(pack_one, 4)], [pack_two], [cot0]], [tok, halo])
-        two_far = send(two, 4)
-        cot = lax.ppermute(cot, ALL, home)
-        one, two = join([[one, send(one, 2)], [two, two_far]], [cot])
+        two_far = send(pack_two, 4)
+        (one,) = join([[pack_one, send(pack_one, 4)]])
+        cot = lax.ppermute(cot0, ALL, home)
+        one, two = join([[one, send(one, 2)], [pack_two, two_far]], [tok, halo])
         two_far = send(two, 2)
-        one, two = join([spread_out(one, XY_MASKS), [two, two_far]])
+        one, two = join([spread_out(one, XY_MASKS), [two, two_far]], [cot])
         one = [one, send(one, CORE)]
         near_two = spread_out(two, XY_MASKS)
     else:
@@ -743,105 +758,120 @@
             [small_all[:ROW_G1], apart(ROW_G1), apart(ROW_G2), small_all[ROW_G2 + 1 :]], axis=0)
         small_all = small_all.reshape(8, 16, BLOCKS, 32).transpose(2, 1, 0, 3).reshape(BLOCKS * 16, 256)
         whole = lambda value: lax.all_gather(value.astype(BF16), ALL, axis=0, tiled=True)
-        one = [jnp.concatenate([whole(in_proj), small_all], axis=1)]
+        in_all = whole(in_proj)
+        one = [jnp.concatenate([in_all[:, :E], small_all], axis=1)]
         out_all, q_all, k_all, v_all, o_all = (whole(w) for w in (out_proj, w_query, w_key, w_value, w_output))
         cut = lambda value: value.reshape(BLOCKS, 16, D)
         side = jnp.concatenate(
             [jnp.concatenate([cut(q_all), cut(k_all)], axis=2), jnp.concatenate([cut(v_all), cut(o_all)], axis=2)], axis=1)
-        two = [jnp.concatenate([out_all.reshape(BLOCKS, 32, D), side], axis=2).reshape(BLOCKS * 32, 3 * D)]
+        gate = jnp.concatenate([cut(in_all[:, E : E + D]), cut(in_all[:, E + D :])], axis=1)
+        two = [jnp.concatenate([out_all.reshape(BLOCKS, 32, D), side, gate], axis=2).reshape(BLOCKS * 32, 4 * D)]
 
     no = len(plan.grad_masks)
     rows3 = count * LG
-    (normed, u_pre, z, conv, act, proj, sig, dt3, au3, a3, state, w_in, pm, gains) = run(
+    (normed, u_pre, conv, act, proj, sig, dt3, au3, a3, state, w_in, pm, gains, bx, cx) = run(
         functools.partial(front_kernel, plan, len(one), masks),
         [tok, halo],
-        [((HALO + count, D), BF16), ((HALO + count, E), F32), ((count, E), F32), ((count, E), F32),
+        [((HALO + count, D), BF16), ((HALO + count, E), F32), ((count, E), F32),
          ((count, E), BF16), ((count, 128), F32), ((count, E), F32), ((rows3, 128), F32), ((rows3, 128), F32),
-         ((128, 128), F32), ((144, 128), BF16), ((D, 2 * E), BF16), ((SMALL_ROWS, E), F32), ((8, D), F32)],
-        [pltpu.VMEM((NS, count, 128), F32), pltpu.VMEM((BLOCKS * 16, 256), BF16), pltpu.SemaphoreType.DMA((2,))],
+         ((128, 128), F32), ((144, 128), BF16), ((D, E), BF16), ((SMALL_ROWS, E), F32), ((8, D), F32),
+         ((NS, count, 128), F32), ((NS, count, 128), F32)],
+        [pltpu.VMEM((BLOCKS * 16, 256), BF16), pltpu.SemaphoreType.DMA((2,))],
         raw=one, us=6,
     )
-    entry = exchange(plan, state, a3, True)
+    entry, firsts = exchange(plan, state, a3, True)
     if plan.fast:
-        (held,) = join([near_two], [entry])
+        (held,) = join([near_two], firsts[:1], 12)
         two = [held, send(held, CORE)]
-    rows_scratch = pltpu.VMEM((NS, count, 128), F32)
-    pay, mamba, gated, middle, all_states, w_out, w_qk, w_vo = run(
+    pay, mamba, gated, middle, all_states, w_out, w_qk, w_vo, w_z, z = run(
         functools.partial(mid_kernel, plan, len(two), masks),
-        [tok, dt3, au3, proj, a3, z, pm, gains, cot, entry],
+        [tok, dt3, au3, a3, normed, pm, gains, cot, entry, bx, cx],
         [((HEADS * count, 4 * HDIM), BF16), ((count, E), F32), ((count, E), BF16), ((count, D), F32),
-         (((count + 1) * 128, 128), F32), ((E, D), BF16), ((D, 2 * D), BF16), ((D, 2 * D), BF16)],
-        [pltpu.VMEM((rows3, 128), F32), rows_scratch, rows_scratch, pltpu.SemaphoreType.DMA((3,))],
+         (((count + 1) * 128, 128), F32), ((E, D), BF16), ((D, 2 * D), BF16), ((D, 2 * D), BF16), ((D, E), BF16), ((count, E), F32)],
+        [pltpu.VMEM((rows3, 128), F32), pltpu.SemaphoreType.DMA((4,))],
         raw=two, us=6,
     )
     got = attend(plan, pay, count)
     (att, gq, gk, gv, grad_middle, mix, gz, gy3, later, gain_grad_two) = run(
         functools.partial(turn_kernel, plan),
-        [got, middle, cot, gains, z, mamba, dt3, proj, a3, w_out, w_qk, w_vo, state],
+        [got, middle, cot, gains, z, mamba, dt3, cx, a3, w_out, w_qk, w_vo, state],
         [((count, D), BF16)] * 4 + [((count, D), F32), ((count, D), BF16), ((count, E), BF16), ((rows3, 128), F32),
                                     ((144, 128), BF16), ((1, D), F32)],
-        [rows_scratch],
     )
     blocks = [len(masks_of) for masks_of in plan.grad_masks]
-    result, *one_grads = run(
-        functools.partial(weights_kernel, plan, no),
-        [att, gq, gk, gv, mix, gated, middle, gains, cot, w_vo, normed, gz],
-        [((count, D), BF16)] + [((n * 32, 4 * D), BF16) for n in blocks],
-        [pltpu.VMEM((D, D), F32), pltpu.VMEM((E, D), F32), pltpu.VMEM((D, E), F32)],
-    )
-    leaving = exchange(plan, later, a3, False)
+    (grad_c,) = run(grad_c_kernel, [gy3, all_states], [((count, 128), F32)])
+    blocks = [len(masks_of) for masks_of in plan.grad_masks]
+
+    def weight_grads(after):
+        return run(
+            functools.partial(weights_kernel, plan, no),
+            [att, gq, gk, gv, mix, gated, middle, gains, cot, w_vo, normed, gz],
+            [((count, D), BF16)] + [((n * 32, 4 * D), BF16) for n in blocks],
+            [pltpu.VMEM((D, D), F32), pltpu.VMEM((E, D), F32), pltpu.VMEM((D, E), F32)], after=after)
+
+    done = []
+
+    def beside(step, entry):
+        if step == 0:
+            return [grad_c]
+        if step == 1:
+            done.extend(weight_grads([entry]))
+            return done[:1]
+        return []
+
+    leaving, _ = exchange(plan, later, a3, False, beside)
+    result, *one_grads = done or weight_grads([])
     one_parts = []
     if plan.fast:
         result = lax.ppermute(result, ALL, [(b, a) for a, b in home])
         rows = blocks[0] * 32
         one_parts = run(
-            cut_one_kernel, [one_grads[0], send(one_grads[1], CORE)], [((rows // 2, 2 * D), BF16)] * 4, after=[leaving, result])
+            cut_one_kernel, [one_grads[0], send(one_grads[1], CORE)], [((rows // 2, 2 * D), BF16)] * 4, after=[leaving])
     small_grads, gu = run(
         functools.partial(back_kernel, plan),
-        [dt3, au3, gy3, a3, proj, pm, all_states, sig, act, conv, u_pre, leaving],
+        [dt3, au3, gy3, a3, proj, pm, all_states, sig, act, conv, u_pre, leaving, bx, cx, grad_c],
         [((SMALL_ROWS, E), F32), ((HALO + count, E), BF16)],
-        [rows_scratch, rows_scratch,
-         pltpu.VMEM((count * 128, 128), F32), pltpu.VMEM((rows3, 128), F32), pltpu.VMEM((rows3, 128), F32),
+        [pltpu.VMEM((count * 128, 128), F32), pltpu.VMEM((rows3, 128), F32), pltpu.VMEM((rows3, 128), F32),
          pltpu.VMEM((128, 128), F32), pltpu.VMEM((8, 128), F32), pltpu.VMEM((count, 128), F32),
          pltpu.VMEM((count + 2 * HALO, E), F32)],
         limit=32, after=one_parts[:1], us=11,
+    )
+    *two_grads, own, before = run(
+        functools.partial(last_kernel, plan, no),
+        [tok, halo, gains, gu, gz, grad_middle, w_in, w_z, normed, small_grads, gain_grad_two],
+        [((n * 16, E + 256), BF16) for n in blocks] + [((count, D), F32), ((HALO, D), F32)],
+        [pltpu.VMEM((D, E), F32), pltpu.VMEM((SMALL_ROWS, E), F32)], after=[result],
     )
     if plan.fast:
         a_keep, a_give, b_keep, b_give = one_parts
         one_parts = run(
             cut_two_kernel, [a_keep, send(a_give, 16), b_keep, send(b_give, 1)], [((rows // 4, 2 * D), BF16)] * 4,
-            after=[gu])
-    *two_grads, own, before = run(
-        functools.partial(last_kernel, plan, no),
-        [tok, halo, gains, gu, gz, grad_middle, w_in, normed, small_grads, gain_grad_two],
-        [((n * 16, E + 256), BF16) for n in blocks] + [((count, D), BF16), ((HALO, D), BF16)],
-        [pltpu.VMEM((D, E), F32), pltpu.VMEM((SMALL_ROWS, E), F32)], after=one_parts[:1],
-    )
+            after=[two_grads[0]])
     if plan.fast:
-        away = [(b, a) for a, b in home]
-        grad_tok = lax.ppermute(own, ALL, away)
         tail = lax.ppermute(
-            before, ALL, [(plan.place(s, c + 1), s * 8 + c) for s in range(4) for c in range(7)])
+            before, ALL, [(plan.place(s, c + 1), plan.place(s, c)) for s in range(4) for c in range(7)])
         a_keep, a_give, b_keep, b_give = one_parts
         sends = lambda parts, stage: [parts[0]] + [send(part, mask) for part, mask in zip(parts[1:], stage[1:])]
         n = blocks[0]
-        *u_parts, keep, give = run(
-            cut_three_kernel, [two_grads[0], send(two_grads[1], CORE), a_keep, send(a_give, 1), b_keep, send(b_give, 16)],
-            [((n * 4, E + 256), BF16)] * 4 + [((n * 4, 4 * D), BF16)] * 2, after=[grad_tok])
+        whole, *u_parts, keep, give = run(
+            cut_three_kernel,
+            [two_grads[0], send(two_grads[1], CORE), a_keep, send(a_give, 1), b_keep, send(b_give, 16), own, tail],
+            [((count, D), BF16)] + [((n * 4, E + 256), BF16)] * 4 + [((n * 4, 4 * D), BF16)] * 2)
+        grad_tok = lax.ppermute(whole, ALL, [(b, a) for a, b in home])
         *u_parts, keep, give = run(
             cut_four_kernel, [*sends(u_parts, XY_MASKS), keep, send(give, 2)],
-            [((n, E + 256), BF16)] * 4 + [((n * 2, 4 * D), BF16)] * 2, after=[tail])
-        out_g, q_g, k_g, v_g, o_g, in_g, x_g, dt_g, a_g, cw_g, cb_g, db_g, sk_g, g1_g, g2_g = run(
-            finish_kernel, [*sends(u_parts, Z_MASKS), keep, send(give, 4)],
-            [((32, D), F32)] + [((16, D), F32)] * 4
+            [((n, E + 256), BF16)] * 4 + [((n * 2, 4 * D), BF16)] * 2, after=[grad_tok])
+        grad_tok, result, out_g, q_g, k_g, v_g, o_g, in_g, x_g, dt_g, a_g, cw_g, cb_g, db_g, sk_g, g1_g, g2_g = run(
+            finish_kernel, [grad_tok, result, *sends(u_parts, Z_MASKS), keep, send(give, 4)],
+            [((count, D), BF16)] * 2 + [((32, D), F32)] + [((16, D), F32)] * 4
             + [((16, 2 * E), F32), ((32, 64), F32), ((32, 32), F32), ((NS, 32), F32), ((KW, 32), F32)]
             + [((1, 32), F32)] * 3 + [((1, 16), F32)] * 2,
             [pltpu.VMEM((SMALL_ROWS, 32), F32)], final=True)
         a_g, cw_g = a_g.T, cw_g.T
         vectors = [value[0] for value in (cb_g, db_g, sk_g, g1_g, g2_g)]
     else:
-        grad_tok = own
         tail = lax.ppermute(before, "ctx", [(c + 1, c) for c in range(chunks - 1)])
+        grad_tok = jnp.concatenate([own[: count - HALO], own[count - HALO :] + tail], axis=0).astype(BF16)
         scatter = lambda value, dim=0: lax.psum_scatter(value.astype(F32), ALL, scatter_dimension=dim, tiled=True)
         blocks_one = one_grads[0].reshape(BLOCKS, 32, 4 * D)
         part = lambda row, rows, col: scatter(blocks_one[:, row : row + rows, col * D : (col + 1) * D].reshape(-1, D))
@@ -854,8 +884,6 @@
         x_g, dt_g, a_g, cw_g = (
             mine[ROW_X : ROW_X + 64].T, mine[ROW_DT : ROW_DT + RANK], mine[ROW_A : ROW_A + NS].T, mine[ROW_CW : ROW_CW + KW].T)
         vectors = [mine[ROW_CB], mine[ROW_DB], mine[ROW_SK], g1, g2]
-    last = (grad_tok[count - HALO :].astype(F32) + tail.astype(F32)).astype(BF16)
-    grad_tok = jnp.concatenate([grad_tok[: count - HALO], last], axis=0)
     cb_v, db_v, sk_v, g1_v, g2_v = vectors
     return (
         result[None], grad_tok[None], g1_v, in_g, cw_g, cb_v, x_g, dt_g, db_v, a_g, sk_v, out_g, g2_v, q_g, k_g, v_g, o_g,

time: 191 us -> 178 us (0.932)
  waiting for transfers between devices: 64.1 us -> 56.7 us
  starting transfers between devices: 53.6 us -> 49.5 us
    ppermute x32, waiting for transfers between devices: 50.7 us -> 34.7 us  [send(): return lax.ppermute(value, ALL, [(i, i ^ mask) for i in range(32)])]
    ppermute x3, waiting for transfers between devices: 10 us -> 17.5 us  [the longest x1 7.53 us: body(): cot = lax.ppermute(cot0, ALL, home)]
    ppermute x32, starting transfers between devices: 33.6 us -> 28.6 us  [send(): return lax.ppermute(value, ALL, [(i, i ^ mask) for i in range(32)])]
    pallas_call x23 -> x24, Pallas kernels: 41.7 us -> 41.8 us  [run(): pl.pallas_call(inner, out_shape=[jax.ShapeDtypeStruct(shape, dtype) for s...]
  transfers between devices with their start and end apart: 38 -> 38, of which waited for: 18 -> 14; matrix products, arithmetic and copies ran while one was open for 1% -> 0% of each run, Pallas kernels for 11% -> 12%
where the time goes in v1:
time: 178 us; the launch traced here: 175 us
  waiting for transfers between devices  56.7 us (32%)
  starting transfers between devices  49.5 us (28%)
  Pallas kernels  41.8 us (23%)
  blocking collectives  23.2 us (13%)
  local copies, waits for them, and re-layouts  2.4 us (1%)
    pallas_call x24, Pallas kernels, run(): pl.pallas_call(inner, out_shape=[jax.ShapeDtypeStruct(shape, dtype) for s...  41.8 us
    ppermute x32, waiting for transfers between devices, send(): return lax.ppermute(value, ALL, [(i, i ^ mask) for i in range(32)])  34.7 us
    ppermute x32, starting transfers between devices, send(): return lax.ppermute(value, ALL, [(i, i ^ mask) for i in range(32)])  28.6 us
    all_to_all x2, blocking collectives, swap(): lax.all_to_all(value, ALL, 0, 0, tiled=True, axis_index_groups=groups)  23.2 us
    ppermute x1, waiting for transfers between devices, body(): cot = lax.ppermute(cot0, ALL, home)  7.53 us
    ppermute x1, waiting for transfers between devices, body(): grad_tok = lax.ppermute(whole, ALL, [(b, a) for a, b in home])  6.82 us
    ppermute x1, waiting for transfers between devices, body(): lax.ppermute(tok0[count - HALO:], ALL, [(s * 8 + c, plan.place(s, c + 1))...  4.45 us
    ppermute x1, starting transfers between devices, body(): result = lax.ppermute(result, ALL, [(b, a) for a, b in home])  4.21 us
  transfers between devices with their start and end apart: 38, of which 14 were waited for; matrix products, arithmetic and copies ran while one was open for 0% of the time, Pallas kernels for 12%

profile of v1, /device:TPU:6, one launch (start us, length us, event | category | flops | bytes accessed | tf_op | source)
XLA Modules:
  0.0 174.7 jit_solution(13776803759162393530)
XLA Ops:
  0.7 2.0 %shard_map.296 = (bf16[16,1280]{1,0:T(8,128)(2,1)}, bf16[32,2048]{1,0:T(8,128)(2,1)}) custom-call(f32[16,2048]{1,0:T(8,128)} %refs_0_.1, f32[32,64]{1,0:T(8,128)} %refs_1_.1, f32[32,32]{1,0:T(8,128)} %refs_2_.1, f32[16,32]{1,0:T(8,128)} %bitcast.28, f32[4,32]{1,0:T(4,128)} %bitcast.29, f32[1,32]{1,0:T(1,128)} %bitcast.31, f32[1,32]{1,0:T(1,128)} %bitcast.32, ...), custom_call_target="tpu_custom_call" | custom-call | flops 2000 | bytes 6000 | tf_op jit(solution)/shard_map/pallas_call | solution.py:58
  2.6 2.7 %collective-permute-start.2 = (bf16[16,1280]{1,0:T(8,128)(2,1)}, bf16[16,1280]{1,0:T(8,128)(2,1)S(1)}, u32[]{:S(2)}, u32[]{:S(2)}) collective-permute-start(bf16[16,1280]{1,0:T(8,128)(2,1)} %get-tuple-element.115.refs_0_), channel_id=1, source_target_pairs={{0,4},{1,5},{2,6},{3,7},{4,0},{5,1},{6,2},{7,3},{8,12},{9,13},{10,... | collective-permute-start | bytes 122888 | tf_op jit(solution)/shard_map/ppermute | solution.py:117
  5.3 3.4 %collective-permute-start = (bf16[128,512]{1,0:T(8,128)(2,1)}, bf16[128,512]{1,0:T(8,128)(2,1)S(1)}, u32[]{:S(2)}, u32[]{:S(2)}) collective-permute-start(bf16[128,512]{1,0:T(8,128)(2,1)} %bitcast.30), channel_id=1, source_target_pairs={{0,0},{1,16},{2,1},{3,17},{4,8},{5,24},{6,9},{7,25},{8,4},{9,20},{... | collective-permute-start | bytes 393224 | tf_op jit(solution)/shard_map/ppermute | solution.py:728
  10.3 1.6 collective-permute-start.3
  12.6 3.2 %collective-permute-start.1 = (bf16[16,512]{1,0:T(8,128)(2,1)S(1)}, bf16[16,512]{1,0:T(8,128)(2,1)S(1)}, u32[]{:S(2)}, u32[]{:S(2)}) collective-permute-start(bf16[16,512]{1,0:T(8,128)(2,1)S(1)} %slice_bitcast_fusion), channel_id=1, source_target_pairs={{0,16},{1,1},{2,17},{3,8},{4,24},{5,9},{6,25},{8,20},{9,5},{10,21}... | collective-permute-start | bytes 49160 | tf_op jit(solution)/shard_map/ppermute | solution.py:729
  15.8 4.4 %collective-permute-done.1.refs_5_.refs_1_ = bf16[16,512]{1,0:T(8,128)(2,1)S(1)} collective-permute-done((bf16[16,512]{1,0:T(8,128)(2,1)S(1)}, bf16[16,512]{1,0:T(8,128)(2,1)S(1)}, u32[]{:S(2)}, u32[]{:S(2)}) %collective-permute-start.1) | collective-permute-done | bytes 16416 | tf_op jit(solution)/shard_map/ppermute | solution.py:729
  20.2 0.9 copy-done
  22.2 1.0 collective-permute-start.6
  23.2 2.1 %collective-permute-start.5 = (bf16[64,1280]{1,0:T(8,128)(2,1)S(1)}, bf16[64,1280]{1,0:T(8,128)(2,1)S(1)}, u32[]{:S(2)}, u32[]{:S(2)}) collective-permute-start(bf16[64,1280]{1,0:T(8,128)(2,1)S(1)} %get-tuple-element.117.refs_0_), channel_id=1, source_target_pairs={{0,1},{1,0},{2,3},{3,2},{4,5},{5,4},{6,7},{7,6},{8,9},{9,8},{10,11... | collective-permute-start | bytes 491528 | tf_op jit(solution)/shard_map/ppermute | solution.py:117
  25.3 3.3 %collective-permute-start.9 = (bf16[128,512]{1,0:T(8,128)(2,1)}, bf16[128,512]{1,0:T(8,128)(2,1)S(1)}, u32[]{:S(2)}, u32[]{:S(2)}) collective-permute-start(bf16[128,512]{1,0:T(8,128)(2,1)} %bitcast.36), channel_id=1, source_target_pairs={{0,0},{1,16},{2,1},{3,17},{4,8},{5,24},{6,9},{7,25},{8,4},{9,20},{... | collective-permute-start | bytes 393224 | tf_op jit(solution)/shard_map/ppermute | solution.py:740
  28.6 7.5 %collective-permute-done.9.refs_6_.refs_7_.refs_2_.refs_8_ = bf16[128,512]{1,0:T(8,128)(2,1)S(1)} collective-permute-done((bf16[128,512]{1,0:T(8,128)(2,1)}, bf16[128,512]{1,0:T(8,128)(2,1)S(1)}, u32[]{:S(2)}, u32[]{:S(2)}) %collective-permute-start.9) | collective-permute-done | bytes 131104 | tf_op jit(solution)/shard_map/ppermute | solution.py:740
  36.2 0.9 shard_map.299
  37.2 3.4 %collective-permute-start.15 = (bf16[128,2048]{1,0:T(8,128)(2,1)S(1)}, bf16[128,2048]{1,0:T(8,128)(2,1)S(1)}, u32[]{:S(2)}, u32[]{:S(2)}) collective-permute-start(bf16[128,2048]{1,0:T(8,128)(2,1)S(1)} %get-tuple-element.134.refs_0_), channel_id=1, source_target_pairs={{0,16},{1,17},{2,18},{3,19},{4,20},{5,21},{6,22},{7,23},{8,24},{9,... | collective-permute-start | bytes 1572872 | tf_op jit(solution)/shard_map/ppermute | solution.py:117
  40.7 5.8 %shard_map.300 = (bf16[144,512]{1,0:T(8,128)(2,1)S(1)}, f32[144,1024]{1,0:T(8,128)S(1)}, f32[128,1024]{1,0:T(8,128)S(1)}, bf16[128,1024]{1,0:T(8,128)(2,1)S(1)},...) custom-call(bf16[128,512]{1,0:T(8,128)(2,1)S(1)} %collective-permute, ...), custom_call_target="tpu_custom_call" | custom-call | flops 6000 | bytes 18000 | tf_op jit(solution)/shard_map/pallas_call | solution.py:58
  46.5 0.8 collective-permute-start.11
  47.3 17.7 %collective-permute-done.11.refs_1_ = bf16[144,128]{1,0:T(8,128)(2,1)S(1)} collective-permute-done((bf16[144,128]{1,0:T(8,128)(2,1)S(1)}, bf16[144,128]{1,0:T(8,128)(2,1)S(1)}, u32[]{:S(2)}, u32[]{:S(2)}) %collective-permute-start.11) | collective-permute-done | bytes 36896 | tf_op jit(solution)/shard_map/ppermute | solution.py:117
  65.9 3.4 %collective-permute-done.12.refs_1_ = bf16[144,128]{1,0:T(8,128)(2,1)S(1)} collective-permute-done((bf16[144,128]{1,0:T(8,128)(2,1)S(1)}, bf16[144,128]{1,0:T(8,128)(2,1)S(1)}, u32[]{:S(2)}, u32[]{:S(2)}) %collective-permute-start.12) | collective-permute-done | bytes 36896 | tf_op jit(solution)/shard_map/ppermute | solution.py:117
  69.5 1.2 collective-permute-done.13.refs_1_
  71.3 6.8 %shard_map.305 = (bf16[1024,256]{1,0:T(8,128)(2,1)S(1)}, f32[128,1024]{1,0:T(8,128)S(1)}, bf16[128,1024]{1,0:T(8,128)(2,1)S(1)}, f32[128,512]{1,0:T(8,128)S(1)},...) custom-call(bf16[128,512]{1,0:T(8,128)(2,1)S(1)} %collective-permute, ...), custom_call_target="tpu_custom_call" | custom-call | flops 6000 | bytes 18000 | tf_op jit(solution)/shard_map/pallas_call | solution.py:58
  78.2 11.4 %all_to_all.22 = bf16[8,128,256]{2,1,0:T(8,128)(2,1)S(1)} all-to-all(bf16[8,128,256]{2,1,0:T(8,128)(2,1)S(1)} %bitcast.27), channel_id=1, replica_groups={{0,16,1,17,8,24,9,25},{4,20,5,21,12,28,13,29},{2,18,3,19,10,26,11,27},{..., dimensions={0} | all-to-all | bytes 1048576 | tf_op jit(solution)/shard_map/all_to_all | solution.py:112
  89.5 3.9 %shard_map.306 = bf16[1024,256]{1,0:T(8,128)(2,1)S(1)} custom-call(bf16[1024,256]{1,0:T(8,128)(2,1)S(1)} %bitcast.25), custom_call_target="tpu_custom_call" | custom-call | flops 4000 | bytes 12000 | tf_op jit(solution)/shard_map/pallas_call | solution.py:58
  93.5 11.8 %all_to_all.23 = bf16[8,128,256]{2,1,0:T(8,128)(2,1)S(1)} all-to-all(bf16[8,128,256]{2,1,0:T(8,128)(2,1)S(1)} %bitcast.26), channel_id=1, replica_groups={{0,16,1,17,8,24,9,25},{4,20,5,21,12,28,13,29},{2,18,3,19,10,26,11,27},{..., dimensions={0} | all-to-all | bytes 1048576 | tf_op jit(solution)/shard_map/all_to_all | solution.py:112
  105.3 3.0 %shard_map.307 = (bf16[128,512]{1,0:T(8,128)(2,1)S(1)}, bf16[128,512]{1,0:T(8,128)(2,1)S(1)}, bf16[128,512]{1,0:T(8,128)(2,1)S(1)}, bf16[128,512]{1,0:T(8,128)(2...) custom-call(bf16[1024,256]{1,0:T(8,128)(2,1)S(1)} %bitcast.24, ...), custom_call_target="tpu_custom_call" | custom-call | flops 2000 | bytes 6000 | tf_op jit(solution)/shard_map/pallas_call | solution.py:58
  108.3 1.5 collective-permute-start.18
  109.8 3.2 %shard_map.308.refs_4_.refs_14_ = f32[128,128]{1,0:T(8,128)S(1)} custom-call(f32[1024,128]{1,0:T(8,128)S(1)} %get-tuple-element.142.refs_0_.refs_2_, f32[16512,128]{1,0:T(8,128)S(1)} %get-tuple-element.144.refs_1_.refs_6_), custom_call_target="tpu_custom_call" | custom-call | flops 2000 | bytes 6000 | tf_op jit(solution)/shard_map/pallas_call | solution.py:58
  113.1 1.7 shard_map.310
  114.8 1.2 collective-permute-start.19
  116.0 2.8 %collective-permute-done.19.refs_1_ = bf16[144,128]{1,0:T(8,128)(2,1)S(1)} collective-permute-done((bf16[144,128]{1,0:T(8,128)(2,1)S(1)}, bf16[144,128]{1,0:T(8,128)(2,1)S(1)}, u32[]{:S(2)}, u32[]{:S(2)}) %collective-permute-start.19) | collective-permute-done | bytes 36896 | tf_op jit(solution)/shard_map/ppermute | solution.py:117
  119.0 4.2 %collective-permute-start.22 = (bf16[128,512]{1,0:T(8,128)(2,1)S(1)}, bf16[128,512]{1,0:T(8,128)(2,1)S(1)}, u32[]{:S(2)}, u32[]{:S(2)}) collective-permute-start(bf16[128,512]{1,0:T(8,128)(2,1)S(1)} %get-tuple-element.159.refs_4_), channel_id=1, source_target_pairs={{0,0},{16,1},{1,2},{17,3},{8,4},{24,5},{9,6},{25,7},{4,8},{20,9},{... | collective-permute-start | bytes 393224 | tf_op jit(solution)/shard_map/ppermute | solution.py:826
  124.4 1.3 collective-permute-start.24
  125.7 8.4 %shard_map.314 = (f32[128,1024]{1,0:T(8,128)S(1)}, bf16[144,1024]{1,0:T(8,128)(2,1)S(1)}) custom-call(f32[1024,128]{1,0:T(8,128)S(1)} %get-tuple-element.121.refs_1_.refs_6_.refs_0_, f32[1024,128]{1,0:T(8,128)S(1)} %get-tuple-element.122.refs_2_.refs_1_, f32[1024,128]{1,0:T(8,128)S(1)} %get-tuple-element.142.refs_0_.refs_2_, ...), custom_call_target="tpu_custom_call" | custom-call | flops 11000 | bytes 33000 | tf_op jit(solution)/shard_map/pallas_call | solution.py:58
  134.1 1.8 %shard_map.315 = (bf16[256,1280]{1,0:T(8,128)(2,1)S(1)}, bf16[256,1280]{1,0:T(8,128)(2,1)S(1)}, f32[128,512]{1,0:T(8,128)S(1)}, f32[16,512]{1,0:T(8,128)S(1)}) custom-call(bf16[128,512]{1,0:T(8,128)(2,1)S(1)} %collective-permute-done.refs_4_.refs_0_, bf16[16,512]{1,0:T(8,128)(2,1)S(1)} %collective-permute-done.1.refs_5_.refs_1_, ...), custom_call_target="tpu_custom_call" | custom-call | flops 2000 | bytes 6000 | tf_op jit(solution)/shard_map/pallas_call | solution.py:58
  136.0 1.3 collective-permute-done.24.refs_1_
  137.3 2.5 %collective-permute-done.25.refs_3_ = bf16[256,1024]{1,0:T(8,128)(2,1)S(1)} collective-permute-done((bf16[256,1024]{1,0:T(8,128)(2,1)S(1)}, bf16[256,1024]{1,0:T(8,128)(2,1)S(1)}, u32[]{:S(2)}, u32[]{:S(2)}) %collective-permute-start.25) | collective-permute-done | bytes 524320 | tf_op jit(solution)/shard_map/ppermute | solution.py:117
  140.1 1.4 collective-permute-start.26
  141.5 3.9 %collective-permute-start.28 = (f32[16,512]{1,0:T(8,128)S(1)}, f32[16,512]{1,0:T(8,128)S(1)}, u32[]{:S(2)}, u32[]{:S(2)}) collective-permute-start(f32[16,512]{1,0:T(8,128)S(1)} %get-tuple-element.182), channel_id=1, source_target_pairs={{16,0},{1,16},{17,1},{8,17},{24,8},{9,24},{25,9},{20,4},{5,20},{21... | collective-permute-start | bytes 98312 | tf_op jit(solution)/shard_map/ppermute | solution.py:851
  145.4 3.1 %collective-permute-done.28.refs_7_ = f32[16,512]{1,0:T(8,128)S(1)} collective-permute-done((f32[16,512]{1,0:T(8,128)S(1)}, f32[16,512]{1,0:T(8,128)S(1)}, u32[]{:S(2)}, u32[]{:S(2)}) %collective-permute-start.28) | collective-permute-done | bytes 32800 | tf_op jit(solution)/shard_map/ppermute | solution.py:851
  148.5 1.4 collective-permute-done.27.refs_5_
  150.2 1.2 collective-permute-start.33
  151.4 1.8 %collective-permute-start.30 = (bf16[64,1280]{1,0:T(8,128)(2,1)S(1)}, bf16[64,1280]{1,0:T(8,128)(2,1)S(1)}, u32[]{:S(2)}, u32[]{:S(2)}) collective-permute-start(bf16[64,1280]{1,0:T(8,128)(2,1)S(1)} %get-tuple-element.185), channel_id=1, source_target_pairs={{0,1},{1,0},{2,3},{3,2},{4,5},{5,4},{6,7},{7,6},{8,9},{9,8},{10,11... | collective-permute-start | bytes 491528 | tf_op jit(solution)/shard_map/ppermute | solution.py:117
  153.6 1.3 collective-permute-start.32
  154.9 2.9 %collective-permute-start.29 = (bf16[128,512]{1,0:T(8,128)(2,1)S(1)}, bf16[128,512]{1,0:T(8,128)(2,1)S(1)}, u32[]{:S(2)}, u32[]{:S(2)}) collective-permute-start(bf16[128,512]{1,0:T(8,128)(2,1)S(1)} %get-tuple-element.183), channel_id=1, source_target_pairs={{0,0},{16,1},{1,2},{17,3},{8,4},{24,5},{9,6},{25,7},{4,8},{20,9},{... | collective-permute-start | bytes 393224 | tf_op jit(solution)/shard_map/ppermute | solution.py:860
  157.8 6.8 %collective-permute-done.29.refs_6_.refs_0_ = bf16[128,512]{1,0:T(8,128)(2,1)S(1)} collective-permute-done((bf16[128,512]{1,0:T(8,128)(2,1)S(1)}, bf16[128,512]{1,0:T(8,128)(2,1)S(1)}, u32[]{:S(2)}, u32[]{:S(2)}) %collective-permute-start.29) | collective-permute-done | bytes 131104 | tf_op jit(solution)/shard_map/ppermute | solution.py:860
  164.8 2.9 %collective-permute-start.34 = (bf16[16,1280]{1,0:T(8,128)(2,1)S(1)}, bf16[16,1280]{1,0:T(8,128)(2,1)S(1)}, u32[]{:S(2)}, u32[]{:S(2)}) collective-permute-start(bf16[16,1280]{1,0:T(8,128)(2,1)S(1)} %get-tuple-element.191), channel_id=1, source_target_pairs={{0,4},{1,5},{2,6},{3,7},{4,0},{5,1},{6,2},{7,3},{8,12},{9,13},{10,... | collective-permute-start | bytes 122888 | tf_op jit(solution)/shard_map/ppermute | solution.py:117
  167.8 1.5 collective-permute-start.36
  169.3 3.3 %collective-permute-done.34.refs_3_ = bf16[16,1280]{1,0:T(8,128)(2,1)S(1)} collective-permute-done((bf16[16,1280]{1,0:T(8,128)(2,1)S(1)}, bf16[16,1280]{1,0:T(8,128)(2,1)S(1)}, u32[]{:S(2)}, u32[]{:S(2)}) %collective-permute-start.34) | collective-permute-done | bytes 40992 | tf_op jit(solution)/shard_map/ppermute | solution.py:117
  172.8 0.9 collective-permute-done.36.refs_5_
  173.7 0.9 shard_map.319
  (60 shorter events, 8.0 us)
Async XLA Ops:
  2.6 6.8 %collective-permute-start.2 = (bf16[16,1280]{1,0:T(8,128)(2,1)}, bf16[16,1280]{1,0:T(8,128)(2,1)S(1)}, u32[]{:S(2)}, u32[]{:S(2)}) collective-permute-start(bf16[16,1280]{1,0:T(8,128)(2,1)} %get-tuple-element.115.refs_0_), channel_id=1, source_target_pairs={{0,4},{1,5},{2,6},{3,7},{4,0},{5,1},{6,2},{7,3},{8,12},{9,13},{10,... | collective-permute-start | bytes 122888 | tf_op jit(solution)/shard_map/ppermute | solution.py:117
  5.3 14.9 %collective-permute-start = (bf16[128,512]{1,0:T(8,128)(2,1)}, bf16[128,512]{1,0:T(8,128)(2,1)S(1)}, u32[]{:S(2)}, u32[]{:S(2)}) collective-permute-start(bf16[128,512]{1,0:T(8,128)(2,1)} %bitcast.30), channel_id=1, source_target_pairs={{0,0},{1,16},{2,1},{3,17},{4,8},{5,24},{6,9},{7,25},{8,4},{9,20},{... | collective-permute-start | bytes 393224 | tf_op jit(solution)/shard_map/ppermute | solution.py:728
  8.7 11.5 %collective-permute-start.4 = (bf16[32,2048]{1,0:T(8,128)(2,1)}, bf16[32,2048]{1,0:T(8,128)(2,1)S(1)}, u32[]{:S(2)}, u32[]{:S(2)}) collective-permute-start(bf16[32,2048]{1,0:T(8,128)(2,1)} %get-tuple-element.116.refs_2_), channel_id=1, source_target_pairs={{0,4},{1,5},{2,6},{3,7},{4,0},{5,1},{6,2},{7,3},{8,12},{9,13},{10,... | collective-permute-start | bytes 393224 | tf_op jit(solution)/shard_map/ppermute | solution.py:117
  9.4 0.8 copy-start.1
  10.3 10.0 %collective-permute-start.3 = (bf16[32,1280]{1,0:T(8,128)(2,1)S(1)}, bf16[32,1280]{1,0:T(8,128)(2,1)S(1)}, u32[]{:S(2)}, u32[]{:S(2)}) collective-permute-start(bf16[32,1280]{1,0:T(8,128)(2,1)S(1)} %shard_map.297.refs_0_), channel_id=1, source_target_pairs={{0,2},{1,3},{2,0},{3,1},{4,6},{5,7},{6,4},{7,5},{8,10},{9,11},{10,... | collective-permute-start | bytes 245768 | tf_op jit(solution)/shard_map/ppermute | solution.py:117
  12.6 7.6 %collective-permute-start.1 = (bf16[16,512]{1,0:T(8,128)(2,1)S(1)}, bf16[16,512]{1,0:T(8,128)(2,1)S(1)}, u32[]{:S(2)}, u32[]{:S(2)}) collective-permute-start(bf16[16,512]{1,0:T(8,128)(2,1)S(1)} %slice_bitcast_fusion), channel_id=1, source_target_pairs={{0,16},{1,1},{2,17},{3,8},{4,24},{5,9},{6,25},{8,20},{9,5},{10,21}... | collective-permute-start | bytes 49160 | tf_op jit(solution)/shard_map/ppermute | solution.py:729
  20.2 0.9 copy-start
  21.7 14.5 %collective-permute-start.8 = (bf16[64,2048]{1,0:T(8,128)(2,1)S(1)}, bf16[64,2048]{1,0:T(8,128)(2,1)S(1)}, u32[]{:S(2)}, u32[]{:S(2)}) collective-permute-start(bf16[64,2048]{1,0:T(8,128)(2,1)S(1)} %get-tuple-element.118.refs_4_), channel_id=1, source_target_pairs={{0,2},{1,3},{2,0},{3,1},{4,6},{5,7},{6,4},{7,5},{8,10},{9,11},{10,... | collective-permute-start | bytes 786440 | tf_op jit(solution)/shard_map/ppermute | solution.py:117
  21.8 14.4 %collective-permute-start.7 = (bf16[64,1280]{1,0:T(8,128)(2,1)S(1)}, bf16[64,1280]{1,0:T(8,128)(2,1)S(1)}, u32[]{:S(2)}, u32[]{:S(2)}) collective-permute-start(bf16[64,1280]{1,0:T(8,128)(2,1)S(1)} %get-tuple-element.117.refs_0_), channel_id=1, source_target_pairs={{0,17},{1,16},{2,19},{3,18},{4,21},{5,20},{6,23},{7,22},{8,25},{9,... | collective-permute-start | bytes 491528 | tf_op jit(solution)/shard_map/ppermute | solution.py:117
  22.2 13.9 %collective-permute-start.6 = (bf16[64,1280]{1,0:T(8,128)(2,1)S(1)}, bf16[64,1280]{1,0:T(8,128)(2,1)S(1)}, u32[]{:S(2)}, u32[]{:S(2)}) collective-permute-start(bf16[64,1280]{1,0:T(8,128)(2,1)S(1)} %get-tuple-element.117.refs_0_), channel_id=1, source_target_pairs={{0,16},{1,17},{2,18},{3,19},{4,20},{5,21},{6,22},{7,23},{8,24},{9,... | collective-permute-start | bytes 491528 | tf_op jit(solution)/shard_map/ppermute | solution.py:117
  23.2 12.9 %collective-permute-start.5 = (bf16[64,1280]{1,0:T(8,128)(2,1)S(1)}, bf16[64,1280]{1,0:T(8,128)(2,1)S(1)}, u32[]{:S(2)}, u32[]{:S(2)}) collective-permute-start(bf16[64,1280]{1,0:T(8,128)(2,1)S(1)} %get-tuple-element.117.refs_0_), channel_id=1, source_target_pairs={{0,1},{1,0},{2,3},{3,2},{4,5},{5,4},{6,7},{7,6},{8,9},{9,8},{10,11... | collective-permute-start | bytes 491528 | tf_op jit(solution)/shard_map/ppermute | solution.py:117
  25.3 10.8 %collective-permute-start.9 = (bf16[128,512]{1,0:T(8,128)(2,1)}, bf16[128,512]{1,0:T(8,128)(2,1)S(1)}, u32[]{:S(2)}, u32[]{:S(2)}) collective-permute-start(bf16[128,512]{1,0:T(8,128)(2,1)} %bitcast.36), channel_id=1, source_target_pairs={{0,0},{1,16},{2,1},{3,17},{4,8},{5,24},{6,9},{7,25},{8,4},{9,20},{... | collective-permute-start | bytes 393224 | tf_op jit(solution)/shard_map/ppermute | solution.py:740
  37.1 3.6 %collective-permute-start.10 = (bf16[256,1280]{1,0:T(8,128)(2,1)S(1)}, bf16[256,1280]{1,0:T(8,128)(2,1)S(1)}, u32[]{:S(2)}, u32[]{:S(2)}) collective-permute-start(bf16[256,1280]{1,0:T(8,128)(2,1)S(1)} %get-tuple-element.119.refs_2_), channel_id=1, source_target_pairs={{0,8},{1,9},{2,10},{3,11},{4,12},{5,13},{6,14},{7,15},{8,0},{9,1},... | collective-permute-start | bytes 1966088 | tf_op jit(solution)/shard_map/ppermute | solution.py:117
  37.1 27.9 %collective-permute-start.16 = (bf16[128,2048]{1,0:T(8,128)(2,1)S(1)}, bf16[128,2048]{1,0:T(8,128)(2,1)S(1)}, u32[]{:S(2)}, u32[]{:S(2)}) collective-permute-start(bf16[128,2048]{1,0:T(8,128)(2,1)S(1)} %get-tuple-element.134.refs_0_), channel_id=1, source_target_pairs={{0,17},{1,16},{2,19},{3,18},{4,21},{5,20},{6,23},{7,22},{8,25},{9,... | collective-permute-start | bytes 1572872 | tf_op jit(solution)/shard_map/ppermute | solution.py:117
  37.2 27.8 %collective-permute-start.15 = (bf16[128,2048]{1,0:T(8,128)(2,1)S(1)}, bf16[128,2048]{1,0:T(8,128)(2,1)S(1)}, u32[]{:S(2)}, u32[]{:S(2)}) collective-permute-start(bf16[128,2048]{1,0:T(8,128)(2,1)S(1)} %get-tuple-element.134.refs_0_), channel_id=1, source_target_pairs={{0,16},{1,17},{2,18},{3,19},{4,20},{5,21},{6,22},{7,23},{8,24},{9,... | collective-permute-start | bytes 1572872 | tf_op jit(solution)/shard_map/ppermute | solution.py:117
  40.7 24.4 %collective-permute-start.14 = (bf16[128,2048]{1,0:T(8,128)(2,1)S(1)}, bf16[128,2048]{1,0:T(8,128)(2,1)S(1)}, u32[]{:S(2)}, u32[]{:S(2)}) collective-permute-start(bf16[128,2048]{1,0:T(8,128)(2,1)S(1)} %get-tuple-element.134.refs_0_), channel_id=1, source_target_pairs={{0,1},{1,0},{2,3},{3,2},{4,5},{5,4},{6,7},{7,6},{8,9},{9,8},{10,11... | collective-permute-start | bytes 1572872 | tf_op jit(solution)/shard_map/ppermute | solution.py:117
  46.5 18.5 %collective-permute-start.11 = (bf16[144,128]{1,0:T(8,128)(2,1)S(1)}, bf16[144,128]{1,0:T(8,128)(2,1)S(1)}, u32[]{:S(2)}, u32[]{:S(2)}) collective-permute-start(bf16[144,128]{1,0:T(8,128)(2,1)S(1)} %get-tuple-element.126.refs_0_.refs_12_), channel_id=1, source_target_pairs={{0,16},{1,17},{2,18},{3,19},{4,20},{5,21},{6,22},{7,23},{8,24},{9,... | collective-permute-start | bytes 110600 | tf_op jit(solution)/shard_map/ppermute | solution.py:117
  65.2 6.1 %collective-permute-start.17 = (bf16[512,2048]{1,0:T(8,128)(2,1)S(1)}, bf16[512,2048]{1,0:T(8,128)(2,1)S(1)}, u32[]{:S(2)}, u32[]{:S(2)}) collective-permute-start(bf16[512,2048]{1,0:T(8,128)(2,1)S(1)} %shard_map.304.refs_11_), channel_id=1, source_target_pairs={{0,8},{1,9},{2,10},{3,11},{4,12},{5,13},{6,14},{7,15},{8,0},{9,1},... | collective-permute-start | bytes 6291464 | tf_op jit(solution)/shard_map/ppermute | solution.py:117
  65.3 4.0 %collective-permute-start.12 = (bf16[144,128]{1,0:T(8,128)(2,1)S(1)}, bf16[144,128]{1,0:T(8,128)(2,1)S(1)}, u32[]{:S(2)}, u32[]{:S(2)}) collective-permute-start(bf16[144,128]{1,0:T(8,128)(2,1)S(1)} %get-tuple-element.127.refs_0_), channel_id=1, source_target_pairs={{0,1},{1,0},{2,3},{3,2},{4,5},{5,4},{6,7},{7,6},{8,9},{9,8},{10,11... | collective-permute-start | bytes 110600 | tf_op jit(solution)/shard_map/ppermute | solution.py:117
  69.4 1.3 collective-permute-start.13
  108.3 4.7 %collective-permute-start.18 = (bf16[144,128]{1,0:T(8,128)(2,1)S(1)}, bf16[144,128]{1,0:T(8,128)(2,1)S(1)}, u32[]{:S(2)}, u32[]{:S(2)}) collective-permute-start(bf16[144,128]{1,0:T(8,128)(2,1)S(1)} %get-tuple-element.149.refs_0_), channel_id=1, source_target_pairs={{0,16},{1,17},{2,18},{3,19},{4,20},{5,21},{6,22},{7,23},{8,24},{9,... | collective-permute-start | bytes 110600 | tf_op jit(solution)/shard_map/ppermute | solution.py:117
  114.7 9.1 %collective-permute-start.21 = (bf16[512,2048]{1,0:T(8,128)(2,1)S(1)}, bf16[512,2048]{1,0:T(8,128)(2,1)S(1)}, u32[]{:S(2)}, u32[]{:S(2)}) collective-permute-start(bf16[512,2048]{1,0:T(8,128)(2,1)S(1)} %get-tuple-element.164), channel_id=1, source_target_pairs={{0,8},{1,9},{2,10},{3,11},{4,12},{5,13},{6,14},{7,15},{8,0},{9,1},... | collective-permute-start | bytes 6291464 | tf_op jit(solution)/shard_map/ppermute | solution.py:117
  114.8 4.0 %collective-permute-start.19 = (bf16[144,128]{1,0:T(8,128)(2,1)S(1)}, bf16[144,128]{1,0:T(8,128)(2,1)S(1)}, u32[]{:S(2)}, u32[]{:S(2)}) collective-permute-start(bf16[144,128]{1,0:T(8,128)(2,1)S(1)} %get-tuple-element.150.refs_0_), channel_id=1, source_target_pairs={{0,1},{1,0},{2,3},{3,2},{4,5},{5,4},{6,7},{7,6},{8,9},{9,8},{10,11... | collective-permute-start | bytes 110600 | tf_op jit(solution)/shard_map/ppermute | solution.py:117
  118.9 4.3 %collective-permute-start.20 = (bf16[144,128]{1,0:T(8,128)(2,1)S(1)}, bf16[144,128]{1,0:T(8,128)(2,1)S(1)}, u32[]{:S(2)}, u32[]{:S(2)}) collective-permute-start(bf16[144,128]{1,0:T(8,128)(2,1)S(1)} %get-tuple-element.160.refs_0_), channel_id=1, source_target_pairs={{0,8},{1,9},{2,10},{3,11},{4,12},{5,13},{6,14},{7,15},{8,0},{9,1},... | collective-permute-start | bytes 110600 | tf_op jit(solution)/shard_map/ppermute | solution.py:117
  119.0 15.2 %collective-permute-start.22 = (bf16[128,512]{1,0:T(8,128)(2,1)S(1)}, bf16[128,512]{1,0:T(8,128)(2,1)S(1)}, u32[]{:S(2)}, u32[]{:S(2)}) collective-permute-start(bf16[128,512]{1,0:T(8,128)(2,1)S(1)} %get-tuple-element.159.refs_4_), channel_id=1, source_target_pairs={{0,0},{16,1},{1,2},{17,3},{8,4},{24,5},{9,6},{25,7},{4,8},{20,9},{... | collective-permute-start | bytes 393224 | tf_op jit(solution)/shard_map/ppermute | solution.py:826
  124.4 13.0 %collective-permute-start.24 = (bf16[256,1024]{1,0:T(8,128)(2,1)S(1)}, bf16[256,1024]{1,0:T(8,128)(2,1)S(1)}, u32[]{:S(2)}, u32[]{:S(2)}) collective-permute-start(bf16[256,1024]{1,0:T(8,128)(2,1)S(1)} %get-tuple-element.174), channel_id=1, source_target_pairs={{0,16},{1,17},{2,18},{3,19},{4,20},{5,21},{6,22},{7,23},{8,24},{9,... | collective-permute-start | bytes 1572872 | tf_op jit(solution)/shard_map/ppermute | solution.py:117
  125.7 14.2 %collective-permute-start.25 = (bf16[256,1024]{1,0:T(8,128)(2,1)S(1)}, bf16[256,1024]{1,0:T(8,128)(2,1)S(1)}, u32[]{:S(2)}, u32[]{:S(2)}) collective-permute-start(bf16[256,1024]{1,0:T(8,128)(2,1)S(1)} %get-tuple-element.176), channel_id=1, source_target_pairs={{0,1},{1,0},{2,3},{3,2},{4,5},{5,4},{6,7},{7,6},{8,9},{9,8},{10,11... | collective-permute-start | bytes 1572872 | tf_op jit(solution)/shard_map/ppermute | solution.py:117
  136.0 12.6 %collective-permute-start.23 = (bf16[256,1280]{1,0:T(8,128)(2,1)S(1)}, bf16[256,1280]{1,0:T(8,128)(2,1)S(1)}, u32[]{:S(2)}, u32[]{:S(2)}) collective-permute-start(bf16[256,1280]{1,0:T(8,128)(2,1)S(1)} %get-tuple-element.173), channel_id=1, source_target_pairs={{0,8},{1,9},{2,10},{3,11},{4,12},{5,13},{6,14},{7,15},{8,0},{9,1},... | collective-permute-start | bytes 1966088 | tf_op jit(solution)/shard_map/ppermute | solution.py:117
  140.1 8.5 %collective-permute-start.26 = (bf16[128,1024]{1,0:T(8,128)(2,1)S(1)}, bf16[128,1024]{1,0:T(8,128)(2,1)S(1)}, u32[]{:S(2)}, u32[]{:S(2)}) collective-permute-start(bf16[128,1024]{1,0:T(8,128)(2,1)S(1)} %get-tuple-element.178), channel_id=1, source_target_pairs={{0,1},{1,0},{2,3},{3,2},{4,5},{5,4},{6,7},{7,6},{8,9},{9,8},{10,11... | collective-permute-start | bytes 786440 | tf_op jit(solution)/shard_map/ppermute | solution.py:117
  141.5 8.4 %collective-permute-start.27 = (bf16[128,1024]{1,0:T(8,128)(2,1)S(1)}, bf16[128,1024]{1,0:T(8,128)(2,1)S(1)}, u32[]{:S(2)}, u32[]{:S(2)}) collective-permute-start(bf16[128,1024]{1,0:T(8,128)(2,1)S(1)} %get-tuple-element.180), channel_id=1, source_target_pairs={{0,16},{1,17},{2,18},{3,19},{4,20},{5,21},{6,22},{7,23},{8,24},{9,... | collective-permute-start | bytes 786440 | tf_op jit(solution)/shard_map/ppermute | solution.py:117
  141.5 7.0 %collective-permute-start.28 = (f32[16,512]{1,0:T(8,128)S(1)}, f32[16,512]{1,0:T(8,128)S(1)}, u32[]{:S(2)}, u32[]{:S(2)}) collective-permute-start(f32[16,512]{1,0:T(8,128)S(1)} %get-tuple-element.182), channel_id=1, source_target_pairs={{16,0},{1,16},{17,1},{8,17},{24,8},{9,24},{25,9},{20,4},{5,20},{21... | collective-permute-start | bytes 98312 | tf_op jit(solution)/shard_map/ppermute | solution.py:851
  150.2 14.4 %collective-permute-start.33 = (bf16[64,2048]{1,0:T(8,128)(2,1)S(1)}, bf16[64,2048]{1,0:T(8,128)(2,1)S(1)}, u32[]{:S(2)}, u32[]{:S(2)}) collective-permute-start(bf16[64,2048]{1,0:T(8,128)(2,1)S(1)} %get-tuple-element.189), channel_id=1, source_target_pairs={{0,2},{1,3},{2,0},{3,1},{4,6},{5,7},{6,4},{7,5},{8,10},{9,11},{10,... | collective-permute-start | bytes 786440 | tf_op jit(solution)/shard_map/ppermute | solution.py:117
  151.4 13.2 %collective-permute-start.30 = (bf16[64,1280]{1,0:T(8,128)(2,1)S(1)}, bf16[64,1280]{1,0:T(8,128)(2,1)S(1)}, u32[]{:S(2)}, u32[]{:S(2)}) collective-permute-start(bf16[64,1280]{1,0:T(8,128)(2,1)S(1)} %get-tuple-element.185), channel_id=1, source_target_pairs={{0,1},{1,0},{2,3},{3,2},{4,5},{5,4},{6,7},{7,6},{8,9},{9,8},{10,11... | collective-permute-start | bytes 491528 | tf_op jit(solution)/shard_map/ppermute | solution.py:117
  153.2 11.4 %collective-permute-start.31 = (bf16[64,1280]{1,0:T(8,128)(2,1)S(1)}, bf16[64,1280]{1,0:T(8,128)(2,1)S(1)}, u32[]{:S(2)}, u32[]{:S(2)}) collective-permute-start(bf16[64,1280]{1,0:T(8,128)(2,1)S(1)} %get-tuple-element.186), channel_id=1, source_target_pairs={{0,16},{1,17},{2,18},{3,19},{4,20},{5,21},{6,22},{7,23},{8,24},{9,... | collective-permute-start | bytes 491528 | tf_op jit(solution)/shard_map/ppermute | solution.py:117
  153.6 11.0 %collective-permute-start.32 = (bf16[64,1280]{1,0:T(8,128)(2,1)S(1)}, bf16[64,1280]{1,0:T(8,128)(2,1)S(1)}, u32[]{:S(2)}, u32[]{:S(2)}) collective-permute-start(bf16[64,1280]{1,0:T(8,128)(2,1)S(1)} %get-tuple-element.187), channel_id=1, source_target_pairs={{0,17},{1,16},{2,19},{3,18},{4,21},{5,20},{6,23},{7,22},{8,25},{9,... | collective-permute-start | bytes 491528 | tf_op jit(solution)/shard_map/ppermute | solution.py:117
  154.9 9.7 %collective-permute-start.29 = (bf16[128,512]{1,0:T(8,128)(2,1)S(1)}, bf16[128,512]{1,0:T(8,128)(2,1)S(1)}, u32[]{:S(2)}, u32[]{:S(2)}) collective-permute-start(bf16[128,512]{1,0:T(8,128)(2,1)S(1)} %get-tuple-element.183), channel_id=1, source_target_pairs={{0,0},{16,1},{1,2},{17,3},{8,4},{24,5},{9,6},{25,7},{4,8},{20,9},{... | collective-permute-start | bytes 393224 | tf_op jit(solution)/shard_map/ppermute | solution.py:860
  164.8 8.9 %collective-permute-start.37 = (bf16[32,2048]{1,0:T(8,128)(2,1)S(1)}, bf16[32,2048]{1,0:T(8,128)(2,1)S(1)}, u32[]{:S(2)}, u32[]{:S(2)}) collective-permute-start(bf16[32,2048]{1,0:T(8,128)(2,1)S(1)} %get-tuple-element.195), channel_id=1, source_target_pairs={{0,4},{1,5},{2,6},{3,7},{4,0},{5,1},{6,2},{7,3},{8,12},{9,13},{10,... | collective-permute-start | bytes 393224 | tf_op jit(solution)/shard_map/ppermute | solution.py:117
  164.8 7.8 %collective-permute-start.34 = (bf16[16,1280]{1,0:T(8,128)(2,1)S(1)}, bf16[16,1280]{1,0:T(8,128)(2,1)S(1)}, u32[]{:S(2)}, u32[]{:S(2)}) collective-permute-start(bf16[16,1280]{1,0:T(8,128)(2,1)S(1)} %get-tuple-element.191), channel_id=1, source_target_pairs={{0,4},{1,5},{2,6},{3,7},{4,0},{5,1},{6,2},{7,3},{8,12},{9,13},{10,... | collective-permute-start | bytes 122888 | tf_op jit(solution)/shard_map/ppermute | solution.py:117
  167.7 5.0 %collective-permute-start.35 = (bf16[16,1280]{1,0:T(8,128)(2,1)S(1)}, bf16[16,1280]{1,0:T(8,128)(2,1)S(1)}, u32[]{:S(2)}, u32[]{:S(2)}) collective-permute-start(bf16[16,1280]{1,0:T(8,128)(2,1)S(1)} %get-tuple-element.192), channel_id=1, source_target_pairs={{0,2},{1,3},{2,0},{3,1},{4,6},{5,7},{6,4},{7,5},{8,10},{9,11},{10,... | collective-permute-start | bytes 122888 | tf_op jit(solution)/shard_map/ppermute | solution.py:117
  167.8 5.9 %collective-permute-start.36 = (bf16[16,1280]{1,0:T(8,128)(2,1)S(1)}, bf16[16,1280]{1,0:T(8,128)(2,1)S(1)}, u32[]{:S(2)}, u32[]{:S(2)}) collective-permute-start(bf16[16,1280]{1,0:T(8,128)(2,1)S(1)} %get-tuple-element.193), channel_id=1, source_target_pairs={{0,6},{1,7},{2,4},{3,5},{4,2},{5,3},{6,0},{7,1},{8,14},{9,15},{10,... | collective-permute-start | bytes 122888 | tf_op jit(solution)/shard_map/ppermute | solution.py:117

commit v2 on v1

--- a/solution.py
+++ b/solution.py
@@ -30,7 +30,7 @@
 CORE = 8
 HALF_MASKS = tuple(xy | zz for xy in XY_MASKS for zz in Z_MASKS)
 FULL_MASKS = HALF_MASKS + tuple(mask | CORE for mask in HALF_MASKS)
-CHUNK_MASKS = tuple((16 if c & 1 else 0) | (1 if c & 2 else 0) | (8 if c & 4 else 0) for c in range(8))
+CHUNK_MASKS = tuple((8 if c & 1 else 0) | (16 if c & 2 else 0) | (1 if c & 4 else 0) for c in range(8))
 
 ROW_X = 0
 ROW_DT = 64
@@ -103,8 +103,11 @@
     def chunk(self):
         if self.fast:
             lin = lax.axis_index("dp") * 8 + lax.axis_index("ctx")
-            return ((lin >> 4) & 1) + (lin & 1) * 2 + ((lin >> 3) & 1) * 4
+            return ((lin >> 3) & 1) + ((lin >> 4) & 1) * 2 + (lin & 1) * 4
         return lax.axis_index("ctx")
+
+    def side(self):
+        return ((lax.axis_index("ctx") + lax.axis_index("dp") * 8) & CORE) != 0 if self.fast else False
 
     def swap(self, value):
         if self.fast:
@@ -117,17 +120,22 @@
     return lax.ppermute(value, ALL, [(i, i ^ mask) for i in range(32)])
 
 
-def start_blocks(target, pieces, masks, me, sem, row_in, rows, first, cols, to=0):
-    per_piece = len(masks) // len(pieces)
-    height = pieces[0].shape[0] // per_piece
-    for i, piece in enumerate(pieces):
-        for k in range(per_piece):
-            block = me ^ masks[i * per_piece + k]
-            pltpu.make_async_copy(
-                piece.at[pl.ds(k * height + row_in, rows), pl.ds(first, cols)],
-                target.at[pl.ds(pl.multiple_of(block * rows, 16), rows), pl.ds(to, cols)],
-                sem,
-            ).start()
+def own_first(value, side, width):
+    groups = [value[:, i * width : (i + 1) * width] for i in range(4)]
+    pick = lambda x, own: jnp.where(side, groups[2 * x + own], groups[2 * x + 1 - own])
+    return jnp.concatenate([pick(0, 1), pick(1, 1), pick(0, 0), pick(1, 0)], axis=1)
+
+
+def in_order(value, side, width):
+    own_a, own_b, far_a, far_b = (value[:, i * width : (i + 1) * width] for i in range(4))
+    return jnp.concatenate(
+        [jnp.where(side, far_a, own_a), jnp.where(side, own_a, far_a),
+         jnp.where(side, far_b, own_b), jnp.where(side, own_b, far_b)], axis=1)
+
+
+def rows_of(ref, half, first, cols):
+    return jnp.concatenate(
+        [ref[k * 32 + half * 16 : k * 32 + half * 16 + 16, first : first + cols] for k in range(ref.shape[0] // 32)], axis=0)
 
 
 def wait_whole(target, sem):
@@ -187,15 +195,11 @@
     one[:, E:] = jnp.concatenate([rows[16 * q : 16 * q + 16, :] for q in range(8)], axis=1).astype(BF16)
 
 
-def join_smalls(target, smalls, masks, me):
-    place = {mask: p for p, mask in enumerate(masks)}
+def join_smalls(target, own, far, side):
     for q in range(8):
-        for g in range(LG):
-            target[16 * q : 16 * q + 16, 128 * g : 128 * g + 128] = jnp.concatenate(
-                [smalls[16 * place[m] : 16 * place[m] + 16, 32 * q : 32 * q + 32].astype(F32) for m in range(4 * g, 4 * g + 4)],
-                axis=1,
-            )
-    target[...] = swap_blocks(target[...], me)
+        rows = jnp.concatenate(
+            [ref[16 * k : 16 * k + 16, E + 32 * q : E + 32 * q + 32].astype(F32) for ref in (own, far) for k in range(16)], axis=1)
+        target[16 * q : 16 * q + 16, :] = in_order(rows, side, 256)
 
 
 def gain_row(pm, row):
@@ -221,27 +225,21 @@
     return ref[pl.ds(pl.multiple_of(index * 8, 8), 8), :]
 
 
-def front_kernel(plan, np_, masks, tok, halo, *refs):
-    pieces = refs[:np_]
-    (normed, u_out, conv_out, act_out, proj_out, sig_out, dt3, au3, a3, state, weight, pm, gains, bx, cx, smalls, sems) = refs[np_:]
-    me = plan.me()
-    start_blocks(weight, pieces, masks, me, sems.at[0], 0, 16, 0, E)
-    height = smalls.shape[0] // np_
-    for i, piece in enumerate(pieces):
-        pltpu.make_async_copy(
-            piece.at[:, pl.ds(E, 256)], smalls.at[pl.ds(i * height, height), :], sems.at[1]).start()
-    wait_whole(smalls, sems.at[1])
-    join_smalls(pm, smalls, masks, me)
+def front_kernel(plan, tok, halo, own, far, normed, turned, u_out, conv_out, act_out, proj_out, sig_out, dt3, au3, a3,
+                 state, pm, gains, bx, cx):
+    side = plan.side()
+    join_smalls(pm, own, far, side)
     gain = gain_row(pm, ROW_G1)
     gains[0:1, :] = gain
     gains[1:2, :] = gain_row(pm, ROW_G2)
     tokens = tok.shape[0]
     x = jnp.concatenate([halo[...].astype(F32), tok[...].astype(F32)], axis=0)
     r = lax.rsqrt(jnp.mean(x * x, axis=-1, keepdims=True) + EPS)
-    low = (x * r * gain).astype(BF16)
-    normed[...] = low
-    wait_whole(weight, sems.at[0])
-    u_out[...] = nn(low, weight[...])
+    low = x * r * gain
+    normed[...] = low.astype(BF16)
+    low = own_first(low, side, 128).astype(BF16)
+    turned[...] = low
+    u_out[...] = nn(low[:, : D // 2], own[:, :E]) + nn(low[:, D // 2 :], far[:, :E])
     conv = pm[ROW_CB : ROW_CB + 1, :]
     for k in range(KW):
         conv = conv + pm[ROW_CW + k : ROW_CW + k + 1, :] * u_out[HALO - 3 + k : HALO - 3 + k + tokens, :]
@@ -324,17 +322,12 @@
         [pltpu.VMEM((144 * plan.chunks, 128), F32)])[0], []
 
 
-def mid_kernel(plan, nb, masks, *refs):
-    tok, dt3, au3, a3, normed, pm, gains, cot, entry, bx, cx = refs[:11]
-    pieces = refs[11 : 11 + nb]
-    pay, mamba, gated_out, middle_out, all_states, w_out, w_qk, w_vo, w_z, z_out, y3, sems = refs[11 + nb :]
+def mid_kernel(plan, tok, dt3, au3, a3, turned, pm, gains, cot, entry, bx, cx, own, far,
+               pay, mamba, gated_out, middle_out, all_states, z_out, y3):
     tokens = tok.shape[0]
-    me = plan.me()
-    start_blocks(w_z, pieces, masks, me, sems.at[3], 0, 16, 3 * D, D)
-    start_blocks(w_z, pieces, masks, me, sems.at[3], 16, 16, 3 * D, D, D)
-    start_blocks(w_out, pieces, masks, me, sems.at[0], 0, 32, 0, D)
-    start_blocks(w_qk, pieces, masks, me, sems.at[1], 0, 16, D, 2 * D)
-    start_blocks(w_vo, pieces, masks, me, sems.at[2], 16, 16, D, 2 * D)
+    side = plan.side()
+    both = lambda left, half, first, cols: nn(left[:, : D // 2], rows_of(own, half, first, cols)) + nn(
+        left[:, D // 2 :], rows_of(far, half, first, cols))
     decay = [a3[8 * n : 8 * n + 8, :] for n in range(NS)]
     held = tuple(entry[8 * n : 8 * n + 8, :] for n in range(NS))
     all_states[:128, :] = entry[:128, :]
@@ -358,24 +351,19 @@
     act = gathered(au3, tokens)
     y = gathered(y3, tokens) + pm[ROW_SK : ROW_SK + 1, :] * act
     mamba[...] = y
-    wait_whole(w_z, sems.at[3])
-    z = nn(normed[HALO:, :], w_z[...])
+    low = turned[HALO:, :]
+    z = jnp.concatenate([both(low, 0, 3 * D, D), both(low, 1, 3 * D, D)], axis=1)
     z_out[...] = z
-    gated = (y * (z * sigmoid(z))).astype(BF16)
-    gated_out[...] = gated
-    wait_whole(w_out, sems.at[0])
-    wait_whole(w_qk, sems.at[1])
-    wait_whole(w_vo, sems.at[2])
-    middle = tok[...].astype(F32) + nn(gated, w_out[...])
+    gated = y * (z * sigmoid(z))
+    gated_out[...] = gated.astype(BF16)
+    gated = own_first(gated, side, 256).astype(BF16)
+    middle = tok[...].astype(F32) + nn(gated[:, : E // 2], own[:, :D]) + nn(gated[:, E // 2 :], far[:, :D])
     middle_out[...] = middle
     r = lax.rsqrt(jnp.mean(middle * middle, axis=-1, keepdims=True) + EPS)
-    low = (middle * r * gains[1:2, :]).astype(BF16)
-    quads = (
-        nn(low, w_qk[:, :D]).astype(BF16),
-        nn(low, w_qk[:, D:]).astype(BF16),
-        nn(low, w_vo[:, :D]).astype(BF16),
-        nt(cot[...], w_vo[:, D:]).astype(BF16),
-    )
+    low = own_first(middle * r * gains[1:2, :], side, 128).astype(BF16)
+    query_key, value = both(low, 0, D, 2 * D), both(low, 1, D, D)
+    grad = jnp.concatenate([nt(cot[...], rows_of(ref, 1, 2 * D, D)) for ref in (own, far)], axis=1)
+    quads = tuple(part.astype(BF16) for part in (query_key[:, :D], query_key[:, D:], value, in_order(grad, side, 128)))
     for h in range(HEADS):
         for i, part in enumerate(quads):
             pay[h * tokens : (h + 1) * tokens, i * HDIM : (i + 1) * HDIM] = part[:, h * HDIM : (h + 1) * HDIM]
@@ -418,13 +406,16 @@
     back[:, 3 * HDIM :] = dv[...].astype(BF16)
 
 
-def turn_kernel(plan, got, middle, cot, gains, z_in, mamba, dt3, cx, a3, w_out, w_qk, w_vo, first,
+def turn_kernel(plan, got, middle, cot, gains, z_in, mamba, dt3, cx, a3, own, far, first,
                 att, gq, gk, gv, grad_middle, mix, gz, gy3, state, gain_grad):
     tokens = middle.shape[0]
     for h in range(HEADS):
         for i, part in enumerate((att, gq, gk, gv)):
             part[:, h * HDIM : (h + 1) * HDIM] = got[h * tokens : (h + 1) * tokens, i * HDIM : (i + 1) * HDIM]
-    grad_n = nt(gq[...], w_qk[:, :D]) + nt(gk[...], w_qk[:, D:]) + nt(gv[...], w_vo[:, :D])
+    side = plan.side()
+    grad_n = in_order(jnp.concatenate(
+        [nt(gq[...], rows_of(ref, 0, D, D)) + nt(gk[...], rows_of(ref, 0, 2 * D, D)) + nt(gv[...], rows_of(ref, 1, D, D))
+         for ref in (own, far)], axis=1), side, 128)
     mid = middle[...]
     r = lax.rsqrt(jnp.mean(mid * mid, axis=-1, keepdims=True) + EPS)
     gain_grad[...] = jnp.sum(grad_n * mid * r, axis=0, keepdims=True)
@@ -433,7 +424,7 @@
     grad_middle[...] = gm
     low = gm.astype(BF16)
     mix[...] = low
-    grad_gated = nt(low, w_out[...])
+    grad_gated = in_order(jnp.concatenate([nt(low, ref[:, :D]) for ref in (own, far)], axis=1), side, 256)
     z = z_in[...]
     s = sigmoid(z)
     spread(gy3, grad_gated * (z * s))
@@ -469,11 +460,14 @@
     diagonal_sums(grad_c, 0, lambda rows: gy3[rows, :], all_states, 1)
 
 
-def weights_kernel(plan, no, att, gq, gk, gv, mix, gated, middle, gains, cot, w_vo, normed, gz, *refs):
+def weights_kernel(plan, no, att, gq, gk, gv, mix, gated, middle, gains, cot, own, far, normed, gz, *refs):
     result, outs = refs[0], refs[1 : 1 + no]
     small, large, wide = refs[1 + no :]
     mid = middle[...]
-    result[...] = (mid + nn(att[...], w_vo[:, D:])).astype(BF16)
+    held = own_first(att[...], plan.side(), 128)
+    result[...] = (
+        mid + nn(held[:, : D // 2], rows_of(own, 1, 2 * D, D)) + nn(held[:, D // 2 :], rows_of(far, 1, 2 * D, D))
+    ).astype(BF16)
     r = lax.rsqrt(jnp.mean(mid * mid, axis=-1, keepdims=True) + EPS)
     low = (mid * r * gains[1:2, :]).astype(BF16)
     large[...] = tn(gated[...], mix[...])
@@ -575,7 +569,7 @@
     gu_out[...] = gu.astype(BF16)
 
 
-def last_kernel(plan, no, tok, halo, gains, gu, gz, grad_middle, w_u, w_z, normed, small_grads, gain_two, *refs):
+def last_kernel(plan, no, tok, halo, gains, gu, gz, grad_middle, own_u, far_u, own_z, far_z, normed, small_grads, gain_two, *refs):
     outs = refs[:no]
     own, before, large, spaced = refs[no:]
     me = plan.me()
@@ -583,13 +577,15 @@
     pack_blocks(plan, outs, large, 16, 16, 0, 0)
     x = jnp.concatenate([halo[...].astype(F32), tok[...].astype(F32)], axis=0)
     r = lax.rsqrt(jnp.mean(x * x, axis=-1, keepdims=True) + EPS)
-    from_z = nt(gz[...], w_z[...])
-    grad_n = nt(gu[...], w_u[...]) + jnp.concatenate([jnp.zeros((HALO, D), F32), from_z], axis=0)
+    from_z = jnp.concatenate(
+        [nt(gz[:, :D], rows_of(ref, 0, 3 * D, D)) + nt(gz[:, D:], rows_of(ref, 1, 3 * D, D)) for ref in (own_z, far_z)], axis=1)
+    from_u = jnp.concatenate([nt(gu[...], ref[:, :E]) for ref in (own_u, far_u)], axis=1)
+    grad_n = in_order(from_u + jnp.concatenate([jnp.zeros((HALO, D), F32), from_z], axis=0), plan.side(), 128)
     gain_one = jnp.sum(grad_n * x * r, axis=0, keepdims=True)
     q = grad_n * gains[0:1, :]
     base = r * q - x * (r * r * r) * jnp.mean(q * x, axis=-1, keepdims=True)
-    own[...] = grad_middle[...] + base[HALO:, :]
-    before[...] = base[:HALO, :]
+    own[...] = (grad_middle[...] + base[HALO:, :]).astype(BF16)
+    before[...] = base[:HALO, :].astype(BF16)
     spaced[...] = small_grads[...]
     blank = jnp.zeros((1, 16), F32)
     for row, grad in ((ROW_G1, gain_one), (ROW_G2, gain_two[...])):
@@ -610,9 +606,11 @@
 
 
 def finish_kernel(*refs):
-    (own, result), refs = refs[:2], refs[2:]
+    (own, tail, result), refs = refs[:3], refs[3:]
     u_ins, ins, (own_out, result_out), refs = refs[:4], refs[4:6], refs[6:8], refs[2:]
-    own_out[...] = own[...]
+    rows = own.shape[0] - HALO
+    own_out[:rows, :] = own[:rows, :]
+    own_out[rows:, :] = (own[rows:, :].astype(F32) + tail[...].astype(F32)).astype(BF16)
     result_out[...] = result[...]
     out_g, q_g, k_g, v_g, o_g, in_g, x_g, dt_g, a_g, cw_g, cb_g, db_g, sk_g, g1_g, g2_g, rows = refs[6:]
     total = total_of(ins)
@@ -638,24 +636,30 @@
     g2_g[...] = rows[ROW_G2 : ROW_G2 + 1, :16]
 
 
-def join_kernel(counts, *refs):
-    ins, outs, sems = refs[: sum(counts)], refs[sum(counts) : -1], refs[-1]
+def join_kernel(plan, counts, placed, *refs):
+    ins, outs = refs[: sum(counts)], refs[sum(counts) :]
     at = 0
     for i, count in enumerate(counts):
         rows = outs[i].shape[0] // count
         for k in range(count):
-            pltpu.make_async_copy(ins[at + k], outs[i].at[pl.ds(k * rows, rows), :], sems.at[i]).start()
+            part = ins[at + k]
+            if not placed[i]:
+                outs[i][k * rows : (k + 1) * rows, :] = part[...]
+                continue
+            height = rows // len(Z_MASKS)
+            for j, zz in enumerate(Z_MASKS):
+                owner = plan.me() ^ (XY_MASKS[k] | zz)
+                to = (((owner >> 4) & 1) * 8 + (owner & 7)) * height
+                outs[i][pl.ds(pl.multiple_of(to, 16), height), :] = part[j * height : (j + 1) * height, :]
         at += count
-    for i, out in enumerate(outs):
-        wait_whole(out, sems.at[i])
-
-
-def join(groups, after=(), limit=12):
+
+
+def join(plan, groups, after=(), placed=()):
     counts = [len(group) for group in groups]
     outs = [((group[0].shape[0] * len(group), group[0].shape[1]), group[0].dtype) for group in groups]
     return run(
-        functools.partial(join_kernel, counts), [], outs, [pltpu.SemaphoreType.DMA((len(groups),))],
-        raw=[part for group in groups for part in group], after=after, limit=limit)
+        functools.partial(join_kernel, plan, counts, [i in placed for i in range(len(groups))]),
+        [part for group in groups for part in group], outs, after=after, us=1)
 
 
 def spread_out(value, stage):
@@ -687,14 +691,7 @@
     out[:, to] = total.astype(out.dtype)
 
 
-def add_tail(out, own, tail):
-    rows = own.shape[0] - HALO
-    out[:rows, :] = own[:rows, :].astype(BF16)
-    out[rows:, :] = (own[rows:, :] + tail[...]).astype(BF16)
-
-
-def cut_three_kernel(u_own, u_got, a_own, a_got, b_own, b_got, own, tail, own_out, u_0, u_1, u_2, u_3, keep, give):
-    add_tail(own_out, own, tail)
+def cut_three_kernel(u_own, u_got, a_own, a_got, b_own, b_got, u_0, u_1, u_2, u_3, keep, give):
     rows = u_0.shape[0]
     for i, out in enumerate((u_0, u_1, u_2, u_3)):
         add_rows(out, slice(i * rows, (i + 1) * rows), (u_own, u_got))
@@ -723,7 +720,6 @@
     devices = plan.dp * plan.ctx
     share, width = E // devices, D // devices
     if plan.fast:
-        masks = FULL_MASKS
         home = [(s * 8 + c, plan.place(s, c)) for s in range(4) for c in range(8)]
         tok = lax.ppermute(tok0, ALL, home)
         halo = lax.ppermute(
@@ -736,15 +732,14 @@
             [pltpu.VMEM((SMALL_ROWS, 32), F32)] + [pltpu.VMEM(value.shape, F32) for value in raw]
             + [pltpu.SemaphoreType.DMA((len(raw),))], far=raw, limit=60)
         two_far = send(pack_two, 4)
-        (one,) = join([[pack_one, send(pack_one, 4)]])
+        (one,) = join(plan, [[pack_one, send(pack_one, 4)]])
         cot = lax.ppermute(cot0, ALL, home)
-        one, two = join([[one, send(one, 2)], [pack_two, two_far]], [tok, halo])
+        one, two = join(plan, [[one, send(one, 2)], [pack_two, two_far]], [tok, halo])
         two_far = send(two, 2)
-        one, two = join([spread_out(one, XY_MASKS), [two, two_far]], [cot])
+        one, two = join(plan, [spread_out(one, XY_MASKS), [two, two_far]], [cot], (0,))
         one = [one, send(one, CORE)]
         near_two = spread_out(two, XY_MASKS)
     else:
-        masks = tuple(range(BLOCKS))
         tok, cot = tok0, cot0
         halo = lax.ppermute(tok0[count - HALO :], "ctx", [(c, c + 1) for c in range(chunks - 1)])
         smalls = jnp.concatenate(
@@ -759,68 +754,68 @@
         small_all = small_all.reshape(8, 16, BLOCKS, 32).transpose(2, 1, 0, 3).reshape(BLOCKS * 16, 256)
         whole = lambda value: lax.all_gather(value.astype(BF16), ALL, axis=0, tiled=True)
         in_all = whole(in_proj)
-        one = [jnp.concatenate([in_all[:, :E], small_all], axis=1)]
+        halves = lambda value: [value.reshape(2, 2, -1, value.shape[1])[:, i].reshape(-1, value.shape[1]) for i in range(2)]
+        one = halves(jnp.concatenate([in_all[:, :E], small_all], axis=1))
         out_all, q_all, k_all, v_all, o_all = (whole(w) for w in (out_proj, w_query, w_key, w_value, w_output))
         cut = lambda value: value.reshape(BLOCKS, 16, D)
         side = jnp.concatenate(
             [jnp.concatenate([cut(q_all), cut(k_all)], axis=2), jnp.concatenate([cut(v_all), cut(o_all)], axis=2)], axis=1)
         gate = jnp.concatenate([cut(in_all[:, E : E + D]), cut(in_all[:, E + D :])], axis=1)
-        two = [jnp.concatenate([out_all.reshape(BLOCKS, 32, D), side, gate], axis=2).reshape(BLOCKS * 32, 4 * D)]
+        two = halves(jnp.concatenate([out_all.reshape(BLOCKS, 32, D), side, gate], axis=2).reshape(BLOCKS * 32, 4 * D))
 
     no = len(plan.grad_masks)
     rows3 = count * LG
-    (normed, u_pre, conv, act, proj, sig, dt3, au3, a3, state, w_in, pm, gains, bx, cx) = run(
-        functools.partial(front_kernel, plan, len(one), masks),
-        [tok, halo],
-        [((HALO + count, D), BF16), ((HALO + count, E), F32), ((count, E), F32),
+    (normed, turned, u_pre, conv, act, proj, sig, dt3, au3, a3, state, pm, gains, bx, cx) = run(
+        functools.partial(front_kernel, plan),
+        [tok, halo, *one],
+        [((HALO + count, D), BF16), ((HALO + count, D), BF16), ((HALO + count, E), F32), ((count, E), F32),
          ((count, E), BF16), ((count, 128), F32), ((count, E), F32), ((rows3, 128), F32), ((rows3, 128), F32),
-         ((128, 128), F32), ((144, 128), BF16), ((D, E), BF16), ((SMALL_ROWS, E), F32), ((8, D), F32),
-         ((NS, count, 128), F32), ((NS, count, 128), F32)],
-        [pltpu.VMEM((BLOCKS * 16, 256), BF16), pltpu.SemaphoreType.DMA((2,))],
-        raw=one, us=6,
+         ((128, 128), F32), ((144, 128), BF16), ((SMALL_ROWS, E), F32), ((8, D), F32),
+         ((NS, count, 128), F32), ((NS, count, 128), F32)], us=6,
     )
     entry, firsts = exchange(plan, state, a3, True)
     if plan.fast:
-        (held,) = join([near_two], firsts[:1], 12)
+        (held,) = join(plan, [near_two], firsts[1:2], (0,))
         two = [held, send(held, CORE)]
-    pay, mamba, gated, middle, all_states, w_out, w_qk, w_vo, w_z, z = run(
-        functools.partial(mid_kernel, plan, len(two), masks),
-        [tok, dt3, au3, a3, normed, pm, gains, cot, entry, bx, cx],
+    pay, mamba, gated, middle, all_states, z = run(
+        functools.partial(mid_kernel, plan),
+        [tok, dt3, au3, a3, turned, pm, gains, cot, entry, bx, cx, *two],
         [((HEADS * count, 4 * HDIM), BF16), ((count, E), F32), ((count, E), BF16), ((count, D), F32),
-         (((count + 1) * 128, 128), F32), ((E, D), BF16), ((D, 2 * D), BF16), ((D, 2 * D), BF16), ((D, E), BF16), ((count, E), F32)],
-        [pltpu.VMEM((rows3, 128), F32), pltpu.SemaphoreType.DMA((4,))],
-        raw=two, us=6,
+         (((count + 1) * 128, 128), F32), ((count, E), F32)],
+        [pltpu.VMEM((rows3, 128), F32)], us=6,
     )
     got = attend(plan, pay, count)
     (att, gq, gk, gv, grad_middle, mix, gz, gy3, later, gain_grad_two) = run(
         functools.partial(turn_kernel, plan),
-        [got, middle, cot, gains, z, mamba, dt3, cx, a3, w_out, w_qk, w_vo, state],
+        [got, middle, cot, gains, z, mamba, dt3, cx, a3, *two, state],
         [((count, D), BF16)] * 4 + [((count, D), F32), ((count, D), BF16), ((count, E), BF16), ((rows3, 128), F32),
                                     ((144, 128), BF16), ((1, D), F32)],
     )
     blocks = [len(masks_of) for masks_of in plan.grad_masks]
-    (grad_c,) = run(grad_c_kernel, [gy3, all_states], [((count, 128), F32)])
-    blocks = [len(masks_of) for masks_of in plan.grad_masks]
 
     def weight_grads(after):
         return run(
             functools.partial(weights_kernel, plan, no),
-            [att, gq, gk, gv, mix, gated, middle, gains, cot, w_vo, normed, gz],
+            [att, gq, gk, gv, mix, gated, middle, gains, cot, *two, normed, gz],
             [((count, D), BF16)] + [((n * 32, 4 * D), BF16) for n in blocks],
             [pltpu.VMEM((D, D), F32), pltpu.VMEM((E, D), F32), pltpu.VMEM((D, E), F32)], after=after)
 
-    done = []
+    def c_grads(after):
+        return run(grad_c_kernel, [gy3, all_states], [((count, 128), F32)], after=after)
+
+    done, extra = [], []
 
     def beside(step, entry):
-        if step == 0:
-            return [grad_c]
         if step == 1:
             done.extend(weight_grads([entry]))
             return done[:1]
-        return []
+        if step == 2:
+            extra.extend(c_grads([entry]))
+        return list(extra)
 
     leaving, _ = exchange(plan, later, a3, False, beside)
     result, *one_grads = done or weight_grads([])
+    (grad_c,) = extra or c_grads([])
     one_parts = []
     if plan.fast:
         result = lax.ppermute(result, ALL, [(b, a) for a, b in home])
@@ -838,8 +833,8 @@
     )
     *two_grads, own, before = run(
         functools.partial(last_kernel, plan, no),
-        [tok, halo, gains, gu, gz, grad_middle, w_in, w_z, normed, small_grads, gain_grad_two],
-        [((n * 16, E + 256), BF16) for n in blocks] + [((count, D), F32), ((HALO, D), F32)],
+        [tok, halo, gains, gu, gz, grad_middle, *one, *two, normed, small_grads, gain_grad_two],
+        [((n * 16, E + 256), BF16) for n in blocks] + [((count, D), BF16), ((HALO, D), BF16)],
         [pltpu.VMEM((D, E), F32), pltpu.VMEM((SMALL_ROWS, E), F32)], after=[result],
     )
     if plan.fast:
@@ -848,21 +843,22 @@
             cut_two_kernel, [a_keep, send(a_give, 16), b_keep, send(b_give, 1)], [((rows // 4, 2 * D), BF16)] * 4,
             after=[two_grads[0]])
     if plan.fast:
+        back = [(b, a) for a, b in home]
+        grad_tok = lax.ppermute(own, ALL, back)
         tail = lax.ppermute(
-            before, ALL, [(plan.place(s, c + 1), plan.place(s, c)) for s in range(4) for c in range(7)])
+            before, ALL, [(plan.place(s, c + 1), s * 8 + c) for s in range(4) for c in range(7)])
         a_keep, a_give, b_keep, b_give = one_parts
         sends = lambda parts, stage: [parts[0]] + [send(part, mask) for part, mask in zip(parts[1:], stage[1:])]
         n = blocks[0]
-        whole, *u_parts, keep, give = run(
+        *u_parts, keep, give = run(
             cut_three_kernel,
-            [two_grads[0], send(two_grads[1], CORE), a_keep, send(a_give, 1), b_keep, send(b_give, 16), own, tail],
-            [((count, D), BF16)] + [((n * 4, E + 256), BF16)] * 4 + [((n * 4, 4 * D), BF16)] * 2)
-        grad_tok = lax.ppermute(whole, ALL, [(b, a) for a, b in home])
+            [two_grads[0], send(two_grads[1], CORE), a_keep, send(a_give, 1), b_keep, send(b_give, 16)],
+            [((n * 4, E + 256), BF16)] * 4 + [((n * 4, 4 * D), BF16)] * 2)
         *u_parts, keep, give = run(
             cut_four_kernel, [*sends(u_parts, XY_MASKS), keep, send(give, 2)],
             [((n, E + 256), BF16)] * 4 + [((n * 2, 4 * D), BF16)] * 2, after=[grad_tok])
         grad_tok, result, out_g, q_g, k_g, v_g, o_g, in_g, x_g, dt_g, a_g, cw_g, cb_g, db_g, sk_g, g1_g, g2_g = run(
-            finish_kernel, [grad_tok, result, *sends(u_parts, Z_MASKS), keep, send(give, 4)],
+            finish_kernel, [grad_tok, tail, result, *sends(u_parts, Z_MASKS), keep, send(give, 4)],
             [((count, D), BF16)] * 2 + [((32, D), F32)] + [((16, D), F32)] * 4
             + [((16, 2 * E), F32), ((32, 64), F32), ((32, 32), F32), ((NS, 32), F32), ((KW, 32), F32)]
             + [((1, 32), F32)] * 3 + [((1, 16), F32)] * 2,
@@ -871,7 +867,8 @@
         vectors = [value[0] for value in (cb_g, db_g, sk_g, g1_g, g2_g)]
     else:
         tail = lax.ppermute(before, "ctx", [(c + 1, c) for c in range(chunks - 1)])
-        grad_tok = jnp.concatenate([own[: count - HALO], own[count - HALO :] + tail], axis=0).astype(BF16)
+        end = (own[count - HALO :].astype(F32) + tail.astype(F32)).astype(BF16)
+        grad_tok = jnp.concatenate([own[: count - HALO], end], axis=0)
         scatter = lambda value, dim=0: lax.psum_scatter(value.astype(F32), ALL, scatter_dimension=dim, tiled=True)
         blocks_one = one_grads[0].reshape(BLOCKS, 32, 4 * D)
         part = lambda row, rows, col: scatter(blocks_one[:, row : row + rows, col * D : (col + 1) * D].reshape(-1, D))

time: 178 us -> 179 us (level); the launches traced: 175 us -> 178 us
  waiting for transfers between devices: 56.7 us -> 67.9 us
  Pallas kernels: 41.8 us -> 36 us
  starting transfers between devices: 49.5 us -> 47.1 us
    ppermute x2, waiting for transfers between devices: 9.92 us -> 17 us  [the longest x1 12.4 us: body(): grad_tok = lax.ppermute(own, ALL, back)]
    pallas_call x24, Pallas kernels: 41.8 us -> 36 us  [run(): pl.pallas_call(inner, out_shape=[jax.ShapeDtypeStruct(shape, dtype) for s...]
    ppermute x32, waiting for transfers between devices: 34.7 us -> 38.6 us  [send(): return lax.ppermute(value, ALL, [(i, i ^ mask) for i in range(32)])]
  transfers between devices with their start and end apart: 38 -> 38, of which waited for: 14 -> 13; matrix products, arithmetic and copies ran while one was open for 0% -> 0% of each run, Pallas kernels for 12% -> 11%
where the time goes in v2:
time: 179 us; the launch traced here: 178 us
  waiting for transfers between devices  67.9 us (38%)
  starting transfers between devices  47.1 us (26%)
  Pallas kernels  36 us (20%)
  blocking collectives  23.5 us (13%)
  local copies, waits for them, and re-layouts  2.4 us (1%)
    ppermute x32, waiting for transfers between devices, send(): return lax.ppermute(value, ALL, [(i, i ^ mask) for i in range(32)])  38.6 us
    pallas_call x24, Pallas kernels, run(): pl.pallas_call(inner, out_shape=[jax.ShapeDtypeStruct(shape, dtype) for s...  36 us
    ppermute x32, starting transfers between devices, send(): return lax.ppermute(value, ALL, [(i, i ^ mask) for i in range(32)])  27.3 us
    all_to_all x2, blocking collectives, swap(): lax.all_to_all(value, ALL, 0, 0, tiled=True, axis_index_groups=groups)  23.5 us
    ppermute x1, waiting for transfers between devices, body(): grad_tok = lax.ppermute(own, ALL, back)  12.4 us
    ppermute x1, waiting for transfers between devices, body(): cot = lax.ppermute(cot0, ALL, home)  8.54 us
    ppermute x1, starting transfers between devices, body(): result = lax.ppermute(result, ALL, [(b, a) for a, b in home])  4.99 us
    ppermute x1, waiting for transfers between devices, body(): lax.ppermute(before, ALL, [(plan.place(s, c + 1), s * 8 + c) for s in ran...  4.6 us
  transfers between devices with their start and end apart: 38, of which 13 were waited for; matrix products, arithmetic and copies ran while one was open for 0% of the time, Pallas kernels for 11%

profile of v2, /device:TPU:6, one launch (start us, length us, event | category | flops | bytes accessed | tf_op | source)
XLA Modules:
  0.0 178.0 jit_solution(13838818796432608652)
XLA Ops:
  0.7 2.0 %shard_map.296 = (bf16[16,1280]{1,0:T(8,128)(2,1)}, bf16[32,2048]{1,0:T(8,128)(2,1)}) custom-call(f32[16,2048]{1,0:T(8,128)} %refs_0_.1, f32[32,64]{1,0:T(8,128)} %refs_1_.1, f32[32,32]{1,0:T(8,128)} %refs_2_.1, f32[16,32]{1,0:T(8,128)} %bitcast.28, f32[4,32]{1,0:T(4,128)} %bitcast.29, f32[1,32]{1,0:T(1,128)} %bitcast.31, f32[1,32]{1,0:T(1,128)} %bitcast.32, ...), custom_call_target="tpu_custom_call" | custom-call | flops 2000 | bytes 6000 | tf_op jit(solution)/shard_map/pallas_call | solution.py:58
  2.6 2.7 %collective-permute-start.2 = (bf16[16,1280]{1,0:T(8,128)(2,1)}, bf16[16,1280]{1,0:T(8,128)(2,1)S(1)}, u32[]{:S(2)}, u32[]{:S(2)}) collective-permute-start(bf16[16,1280]{1,0:T(8,128)(2,1)} %get-tuple-element.110.refs_0_), channel_id=1, source_target_pairs={{0,4},{1,5},{2,6},{3,7},{4,0},{5,1},{6,2},{7,3},{8,12},{9,13},{10,... | collective-permute-start | bytes 122888 | tf_op jit(solution)/shard_map/ppermute | solution.py:120
  5.3 2.5 %collective-permute-start = (bf16[128,512]{1,0:T(8,128)(2,1)}, bf16[128,512]{1,0:T(8,128)(2,1)S(1)}, u32[]{:S(2)}, u32[]{:S(2)}) collective-permute-start(bf16[128,512]{1,0:T(8,128)(2,1)} %bitcast.30), channel_id=1, source_target_pairs={{0,0},{1,8},{2,16},{3,24},{4,1},{5,9},{6,17},{7,25},{8,4},{9,12},{... | collective-permute-start | bytes 393224 | tf_op jit(solution)/shard_map/ppermute | solution.py:724
  7.8 1.6 collective-permute-start.4
  9.4 0.8 copy-done.1
  10.2 1.5 collective-permute-start.3
  11.7 0.7 slice_bitcast_fusion
  12.4 4.2 %collective-permute-start.1 = (bf16[16,512]{1,0:T(8,128)(2,1)S(1)}, bf16[16,512]{1,0:T(8,128)(2,1)S(1)}, u32[]{:S(2)}, u32[]{:S(2)}) collective-permute-start(bf16[16,512]{1,0:T(8,128)(2,1)S(1)} %slice_bitcast_fusion), channel_id=1, source_target_pairs={{0,8},{1,16},{2,24},{3,1},{4,9},{5,17},{6,25},{8,12},{9,20},{10,28... | collective-permute-start | bytes 49160 | tf_op jit(solution)/shard_map/ppermute | solution.py:725
  16.6 3.7 %collective-permute-done.1.refs_5_.refs_1_ = bf16[16,512]{1,0:T(8,128)(2,1)S(1)} collective-permute-done((bf16[16,512]{1,0:T(8,128)(2,1)S(1)}, bf16[16,512]{1,0:T(8,128)(2,1)S(1)}, u32[]{:S(2)}, u32[]{:S(2)}) %collective-permute-start.1) | collective-permute-done | bytes 16416 | tf_op jit(solution)/shard_map/ppermute | solution.py:725
  20.3 0.9 copy-done
  21.3 1.5 collective-permute-start.5
  22.8 2.1 %collective-permute-start.7 = (bf16[64,1280]{1,0:T(8,128)(2,1)S(1)}, bf16[64,1280]{1,0:T(8,128)(2,1)S(1)}, u32[]{:S(2)}, u32[]{:S(2)}) collective-permute-start(bf16[64,1280]{1,0:T(8,128)(2,1)S(1)} %get-tuple-element.112.refs_0_), channel_id=1, source_target_pairs={{0,17},{1,16},{2,19},{3,18},{4,21},{5,20},{6,23},{7,22},{8,25},{9,... | collective-permute-start | bytes 491528 | tf_op jit(solution)/shard_map/ppermute | solution.py:120
  24.9 2.5 %collective-permute-start.9 = (bf16[128,512]{1,0:T(8,128)(2,1)}, bf16[128,512]{1,0:T(8,128)(2,1)S(1)}, u32[]{:S(2)}, u32[]{:S(2)}) collective-permute-start(bf16[128,512]{1,0:T(8,128)(2,1)} %bitcast.36), channel_id=1, source_target_pairs={{0,0},{1,8},{2,16},{3,24},{4,1},{5,9},{6,17},{7,25},{8,4},{9,12},{... | collective-permute-start | bytes 393224 | tf_op jit(solution)/shard_map/ppermute | solution.py:736
  27.4 8.5 %collective-permute-done.9.refs_6_.refs_7_.refs_2_.refs_8_ = bf16[128,512]{1,0:T(8,128)(2,1)S(1)} collective-permute-done((bf16[128,512]{1,0:T(8,128)(2,1)}, bf16[128,512]{1,0:T(8,128)(2,1)S(1)}, u32[]{:S(2)}, u32[]{:S(2)}) %collective-permute-start.9) | collective-permute-done | bytes 131104 | tf_op jit(solution)/shard_map/ppermute | solution.py:736
  36.2 1.1 collective-permute-start.14
  37.3 2.4 %collective-permute-start.16 = (bf16[128,2048]{1,0:T(8,128)(2,1)S(1)}, bf16[128,2048]{1,0:T(8,128)(2,1)S(1)}, u32[]{:S(2)}, u32[]{:S(2)}) collective-permute-start(bf16[128,2048]{1,0:T(8,128)(2,1)S(1)} %get-tuple-element.129.refs_0_), channel_id=1, source_target_pairs={{0,17},{1,16},{2,19},{3,18},{4,21},{5,20},{6,23},{7,22},{8,25},{9,... | collective-permute-start | bytes 1572872 | tf_op jit(solution)/shard_map/ppermute | solution.py:120
  39.7 4.0 %shard_map.300 = (bf16[144,512]{1,0:T(8,128)(2,1)S(1)}, bf16[144,512]{1,0:T(8,128)(2,1)S(1)}, f32[144,1024]{1,0:T(8,128)S(1)}, f32[128,1024]{1,0:T(8,128)S(1)}, ...) custom-call(bf16[128,512]{1,0:T(8,128)(2,1)S(1)} %collective-permute, ...), custom_call_target="tpu_custom_call" | custom-call | flops 6000 | bytes 18000 | tf_op jit(solution)/shard_map/pallas_call | solution.py:58
  43.8 1.2 collective-permute-done.11.refs_1_
  45.2 18.2 %collective-permute-done.12.refs_1_ = bf16[144,128]{1,0:T(8,128)(2,1)S(1)} collective-permute-done((bf16[144,128]{1,0:T(8,128)(2,1)S(1)}, bf16[144,128]{1,0:T(8,128)(2,1)S(1)}, u32[]{:S(2)}, u32[]{:S(2)}) %collective-permute-start.12) | collective-permute-done | bytes 36896 | tf_op jit(solution)/shard_map/ppermute | solution.py:120
  63.7 1.0 collective-permute-start.13
  64.8 3.0 %collective-permute-done.13.refs_1_ = bf16[144,128]{1,0:T(8,128)(2,1)S(1)} collective-permute-done((bf16[144,128]{1,0:T(8,128)(2,1)S(1)}, bf16[144,128]{1,0:T(8,128)(2,1)S(1)}, u32[]{:S(2)}, u32[]{:S(2)}) %collective-permute-start.13) | collective-permute-done | bytes 36896 | tf_op jit(solution)/shard_map/ppermute | solution.py:120
  68.4 3.8 %shard_map.305 = (bf16[1024,256]{1,0:T(8,128)(2,1)S(1)}, f32[128,1024]{1,0:T(8,128)S(1)}, bf16[128,1024]{1,0:T(8,128)(2,1)S(1)}, f32[128,512]{1,0:T(8,128)S(1)},...) custom-call(bf16[128,512]{1,0:T(8,128)(2,1)S(1)} %collective-permute-done.refs_4_.refs_0_, ...), custom_call_target="tpu_custom_call" | custom-call | flops 6000 | bytes 18000 | tf_op jit(solution)/shard_map/pallas_call | solution.py:58
  72.2 11.4 %all_to_all.22 = bf16[8,128,256]{2,1,0:T(8,128)(2,1)S(1)} all-to-all(bf16[8,128,256]{2,1,0:T(8,128)(2,1)S(1)} %bitcast.27), channel_id=1, replica_groups={{0,8,16,24,1,9,17,25},{4,12,20,28,5,13,21,29},{2,10,18,26,3,11,19,27},{..., dimensions={0} | all-to-all | bytes 1048576 | tf_op jit(solution)/shard_map/all_to_all | solution.py:115
  83.6 3.9 %shard_map.306 = bf16[1024,256]{1,0:T(8,128)(2,1)S(1)} custom-call(bf16[1024,256]{1,0:T(8,128)(2,1)S(1)} %bitcast.25), custom_call_target="tpu_custom_call" | custom-call | flops 4000 | bytes 12000 | tf_op jit(solution)/shard_map/pallas_call | solution.py:58
  87.5 12.1 %all_to_all.23 = bf16[8,128,256]{2,1,0:T(8,128)(2,1)S(1)} all-to-all(bf16[8,128,256]{2,1,0:T(8,128)(2,1)S(1)} %bitcast.26), channel_id=1, replica_groups={{0,8,16,24,1,9,17,25},{4,12,20,28,5,13,21,29},{2,10,18,26,3,11,19,27},{..., dimensions={0} | all-to-all | bytes 1048576 | tf_op jit(solution)/shard_map/all_to_all | solution.py:115
  99.7 3.1 %shard_map.307 = (bf16[128,512]{1,0:T(8,128)(2,1)S(1)}, bf16[128,512]{1,0:T(8,128)(2,1)S(1)}, bf16[128,512]{1,0:T(8,128)(2,1)S(1)}, bf16[128,512]{1,0:T(8,128)(2...) custom-call(bf16[1024,256]{1,0:T(8,128)(2,1)S(1)} %bitcast.24, ...), custom_call_target="tpu_custom_call" | custom-call | flops 2000 | bytes 6000 | tf_op jit(solution)/shard_map/pallas_call | solution.py:58
  102.9 1.2 collective-permute-done.18.refs_1_
  104.2 1.7 shard_map.309
  106.1 1.5 collective-permute-start.19
  107.6 2.5 %collective-permute-done.19.refs_1_ = bf16[144,128]{1,0:T(8,128)(2,1)S(1)} collective-permute-done((bf16[144,128]{1,0:T(8,128)(2,1)S(1)}, bf16[144,128]{1,0:T(8,128)(2,1)S(1)}, u32[]{:S(2)}, u32[]{:S(2)}) %collective-permute-start.19) | collective-permute-done | bytes 36896 | tf_op jit(solution)/shard_map/ppermute | solution.py:120
  110.1 1.5 collective-permute-start.20
  111.6 5.0 %collective-permute-start.22 = (bf16[128,512]{1,0:T(8,128)(2,1)S(1)}, bf16[128,512]{1,0:T(8,128)(2,1)S(1)}, u32[]{:S(2)}, u32[]{:S(2)}) collective-permute-start(bf16[128,512]{1,0:T(8,128)(2,1)S(1)} %get-tuple-element.152.refs_4_), channel_id=1, source_target_pairs={{0,0},{8,1},{16,2},{24,3},{1,4},{9,5},{17,6},{25,7},{4,8},{12,9},{... | collective-permute-start | bytes 393224 | tf_op jit(solution)/shard_map/ppermute | solution.py:821
  116.6 3.2 %shard_map.311.refs_4_.refs_14_ = f32[128,128]{1,0:T(8,128)S(1)} custom-call(f32[1024,128]{1,0:T(8,128)S(1)} %get-tuple-element.134.refs_0_.refs_2_, f32[16512,128]{1,0:T(8,128)S(1)} %get-tuple-element.136.refs_1_.refs_6_, f32[144,128]{1,0:T(8,128)S(1)} %get-tuple-element.154.refs_2_), custom_call_target="tpu_custom_call" | custom-call | flops 2000 | bytes 6000 | tf_op jit(solution)/shard_map/pallas_call | solution.py:58
  121.2 8.4 %shard_map.314 = (f32[128,1024]{1,0:T(8,128)S(1)}, bf16[144,1024]{1,0:T(8,128)(2,1)S(1)}) custom-call(f32[1024,128]{1,0:T(8,128)S(1)} %get-tuple-element.116.refs_1_.refs_6_.refs_0_, f32[1024,128]{1,0:T(8,128)S(1)} %get-tuple-element.117.refs_2_.refs_1_, f32[1024,128]{1,0:T(8,128)S(1)} %get-tuple-element.134.refs_0_.refs_2_, ...), custom_call_target="tpu_custom_call" | custom-call | flops 11000 | bytes 33000 | tf_op jit(solution)/shard_map/pallas_call | solution.py:58
  129.6 1.8 %shard_map.315 = (bf16[256,1280]{1,0:T(8,128)(2,1)S(1)}, bf16[256,1280]{1,0:T(8,128)(2,1)S(1)}, bf16[128,512]{1,0:T(8,128)(2,1)S(1)}, bf16[16,512]{1,0:T(8,128)(2,1)S(1)}) custom-call(bf16[128,512]{1,0:T(8,128)(2,1)S(1)} %collective-permute-done.refs_4_.refs_0_, bf16[16,512]{1,0:T(8,128)(2,1)S(1)} %collective-permute-done.1.refs_5_.refs_1_, ...), custom_call_target="tpu_custom_call" | custom-call | flops 2000 | bytes 6000 | tf_op jit(solution)/shard_map/pallas_call | solution.py:58
  131.7 3.4 %collective-permute-done.26.refs_1_ = bf16[256,1024]{1,0:T(8,128)(2,1)S(1)} collective-permute-done((bf16[256,1024]{1,0:T(8,128)(2,1)S(1)}, bf16[256,1024]{1,0:T(8,128)(2,1)S(1)}, u32[]{:S(2)}, u32[]{:S(2)}) %collective-permute-start.26) | collective-permute-done | bytes 524320 | tf_op jit(solution)/shard_map/ppermute | solution.py:120
  135.0 1.1 collective-permute-done.27.refs_3_
  136.4 1.3 collective-permute-start.28
  137.7 6.7 %collective-permute-done.28.refs_3_ = bf16[128,1024]{1,0:T(8,128)(2,1)S(1)} collective-permute-done((bf16[128,1024]{1,0:T(8,128)(2,1)S(1)}, bf16[128,1024]{1,0:T(8,128)(2,1)S(1)}, u32[]{:S(2)}, u32[]{:S(2)}) %collective-permute-start.28) | collective-permute-done | bytes 262176 | tf_op jit(solution)/shard_map/ppermute | solution.py:120
  144.4 1.3 collective-permute-done.29.refs_5_
  146.8 2.8 %collective-permute-start.32 = (bf16[64,1280]{1,0:T(8,128)(2,1)S(1)}, bf16[64,1280]{1,0:T(8,128)(2,1)S(1)}, u32[]{:S(2)}, u32[]{:S(2)}) collective-permute-start(bf16[64,1280]{1,0:T(8,128)(2,1)S(1)} %get-tuple-element.177), channel_id=1, source_target_pairs={{0,17},{1,16},{2,19},{3,18},{4,21},{5,20},{6,23},{7,22},{8,25},{9,... | collective-permute-start | bytes 491528 | tf_op jit(solution)/shard_map/ppermute | solution.py:120
  149.6 3.6 %collective-permute-start.23 = (bf16[128,512]{1,0:T(8,128)(2,1)S(1)}, bf16[128,512]{1,0:T(8,128)(2,1)S(1)}, u32[]{:S(2)}, u32[]{:S(2)}) collective-permute-start(bf16[128,512]{1,0:T(8,128)(2,1)S(1)} %get-tuple-element.163), channel_id=1, source_target_pairs={{0,0},{8,1},{16,2},{24,3},{1,4},{9,5},{17,6},{25,7},{4,8},{12,9},{... | collective-permute-start | bytes 393224 | tf_op jit(solution)/shard_map/ppermute | solution.py:847
  153.3 12.4 %collective-permute-done.23.refs_6_.refs_0_ = bf16[128,512]{1,0:T(8,128)(2,1)S(1)} collective-permute-done((bf16[128,512]{1,0:T(8,128)(2,1)S(1)}, bf16[128,512]{1,0:T(8,128)(2,1)S(1)}, u32[]{:S(2)}, u32[]{:S(2)}) %collective-permute-start.23) | collective-permute-done | bytes 131104 | tf_op jit(solution)/shard_map/ppermute | solution.py:847
  166.0 2.9 %collective-permute-start.34 = (bf16[16,1280]{1,0:T(8,128)(2,1)S(1)}, bf16[16,1280]{1,0:T(8,128)(2,1)S(1)}, u32[]{:S(2)}, u32[]{:S(2)}) collective-permute-start(bf16[16,1280]{1,0:T(8,128)(2,1)S(1)} %get-tuple-element.181), channel_id=1, source_target_pairs={{0,4},{1,5},{2,6},{3,7},{4,0},{5,1},{6,2},{7,3},{8,12},{9,13},{10,... | collective-permute-start | bytes 122888 | tf_op jit(solution)/shard_map/ppermute | solution.py:120
  168.9 1.5 collective-permute-start.36
  170.4 1.9 %collective-permute-start.24 = (bf16[16,512]{1,0:T(8,128)(2,1)S(1)}, bf16[16,512]{1,0:T(8,128)(2,1)S(1)}, u32[]{:S(2)}, u32[]{:S(2)}) collective-permute-start(bf16[16,512]{1,0:T(8,128)(2,1)S(1)} %get-tuple-element.164), channel_id=1, source_target_pairs={{8,0},{16,1},{24,2},{1,3},{9,4},{17,5},{25,6},{12,8},{20,9},{28,10... | collective-permute-start | bytes 49160 | tf_op jit(solution)/shard_map/ppermute | solution.py:848
  172.3 4.6 %collective-permute-done.24.refs_1_ = bf16[16,512]{1,0:T(8,128)(2,1)S(1)} collective-permute-done((bf16[16,512]{1,0:T(8,128)(2,1)S(1)}, bf16[16,512]{1,0:T(8,128)(2,1)S(1)}, u32[]{:S(2)}, u32[]{:S(2)}) %collective-permute-start.24) | collective-permute-done | bytes 16416 | tf_op jit(solution)/shard_map/ppermute | solution.py:848
  177.0 0.9 shard_map.319
  (60 shorter events, 5.0 us)
Async XLA Ops:
  2.6 6.8 %collective-permute-start.2 = (bf16[16,1280]{1,0:T(8,128)(2,1)}, bf16[16,1280]{1,0:T(8,128)(2,1)S(1)}, u32[]{:S(2)}, u32[]{:S(2)}) collective-permute-start(bf16[16,1280]{1,0:T(8,128)(2,1)} %get-tuple-element.110.refs_0_), channel_id=1, source_target_pairs={{0,4},{1,5},{2,6},{3,7},{4,0},{5,1},{6,2},{7,3},{8,12},{9,13},{10,... | collective-permute-start | bytes 122888 | tf_op jit(solution)/shard_map/ppermute | solution.py:120
  5.3 15.0 %collective-permute-start = (bf16[128,512]{1,0:T(8,128)(2,1)}, bf16[128,512]{1,0:T(8,128)(2,1)S(1)}, u32[]{:S(2)}, u32[]{:S(2)}) collective-permute-start(bf16[128,512]{1,0:T(8,128)(2,1)} %bitcast.30), channel_id=1, source_target_pairs={{0,0},{1,8},{2,16},{3,24},{4,1},{5,9},{6,17},{7,25},{8,4},{9,12},{... | collective-permute-start | bytes 393224 | tf_op jit(solution)/shard_map/ppermute | solution.py:724
  7.8 12.5 %collective-permute-start.4 = (bf16[32,2048]{1,0:T(8,128)(2,1)}, bf16[32,2048]{1,0:T(8,128)(2,1)S(1)}, u32[]{:S(2)}, u32[]{:S(2)}) collective-permute-start(bf16[32,2048]{1,0:T(8,128)(2,1)} %get-tuple-element.111.refs_2_), channel_id=1, source_target_pairs={{0,4},{1,5},{2,6},{3,7},{4,0},{5,1},{6,2},{7,3},{8,12},{9,13},{10,... | collective-permute-start | bytes 393224 | tf_op jit(solution)/shard_map/ppermute | solution.py:120
  9.4 0.8 copy-start.1
  10.2 10.1 %collective-permute-start.3 = (bf16[32,1280]{1,0:T(8,128)(2,1)S(1)}, bf16[32,1280]{1,0:T(8,128)(2,1)S(1)}, u32[]{:S(2)}, u32[]{:S(2)}) collective-permute-start(bf16[32,1280]{1,0:T(8,128)(2,1)S(1)} %shard_map.297.refs_0_), channel_id=1, source_target_pairs={{0,2},{1,3},{2,0},{3,1},{4,6},{5,7},{6,4},{7,5},{8,10},{9,11},{10,... | collective-permute-start | bytes 245768 | tf_op jit(solution)/shard_map/ppermute | solution.py:120
  12.4 7.9 %collective-permute-start.1 = (bf16[16,512]{1,0:T(8,128)(2,1)S(1)}, bf16[16,512]{1,0:T(8,128)(2,1)S(1)}, u32[]{:S(2)}, u32[]{:S(2)}) collective-permute-start(bf16[16,512]{1,0:T(8,128)(2,1)S(1)} %slice_bitcast_fusion), channel_id=1, source_target_pairs={{0,8},{1,16},{2,24},{3,1},{4,9},{5,17},{6,25},{8,12},{9,20},{10,28... | collective-permute-start | bytes 49160 | tf_op jit(solution)/shard_map/ppermute | solution.py:725
  20.3 0.9 copy-start
  21.3 14.7 %collective-permute-start.8 = (bf16[64,2048]{1,0:T(8,128)(2,1)S(1)}, bf16[64,2048]{1,0:T(8,128)(2,1)S(1)}, u32[]{:S(2)}, u32[]{:S(2)}) collective-permute-start(bf16[64,2048]{1,0:T(8,128)(2,1)S(1)} %get-tuple-element.113.refs_4_), channel_id=1, source_target_pairs={{0,2},{1,3},{2,0},{3,1},{4,6},{5,7},{6,4},{7,5},{8,10},{9,11},{10,... | collective-permute-start | bytes 786440 | tf_op jit(solution)/shard_map/ppermute | solution.py:120
  21.3 14.7 %collective-permute-start.5 = (bf16[64,1280]{1,0:T(8,128)(2,1)S(1)}, bf16[64,1280]{1,0:T(8,128)(2,1)S(1)}, u32[]{:S(2)}, u32[]{:S(2)}) collective-permute-start(bf16[64,1280]{1,0:T(8,128)(2,1)S(1)} %get-tuple-element.112.refs_0_), channel_id=1, source_target_pairs={{0,1},{1,0},{2,3},{3,2},{4,5},{5,4},{6,7},{7,6},{8,9},{9,8},{10,11... | collective-permute-start | bytes 491528 | tf_op jit(solution)/shard_map/ppermute | solution.py:120
  22.8 13.2 %collective-permute-start.6 = (bf16[64,1280]{1,0:T(8,128)(2,1)S(1)}, bf16[64,1280]{1,0:T(8,128)(2,1)S(1)}, u32[]{:S(2)}, u32[]{:S(2)}) collective-permute-start(bf16[64,1280]{1,0:T(8,128)(2,1)S(1)} %get-tuple-element.112.refs_0_), channel_id=1, source_target_pairs={{0,16},{1,17},{2,18},{3,19},{4,20},{5,21},{6,22},{7,23},{8,24},{9,... | collective-permute-start | bytes 491528 | tf_op jit(solution)/shard_map/ppermute | solution.py:120
  22.8 13.2 %collective-permute-start.7 = (bf16[64,1280]{1,0:T(8,128)(2,1)S(1)}, bf16[64,1280]{1,0:T(8,128)(2,1)S(1)}, u32[]{:S(2)}, u32[]{:S(2)}) collective-permute-start(bf16[64,1280]{1,0:T(8,128)(2,1)S(1)} %get-tuple-element.112.refs_0_), channel_id=1, source_target_pairs={{0,17},{1,16},{2,19},{3,18},{4,21},{5,20},{6,23},{7,22},{8,25},{9,... | collective-permute-start | bytes 491528 | tf_op jit(solution)/shard_map/ppermute | solution.py:120
  24.9 11.1 %collective-permute-start.9 = (bf16[128,512]{1,0:T(8,128)(2,1)}, bf16[128,512]{1,0:T(8,128)(2,1)S(1)}, u32[]{:S(2)}, u32[]{:S(2)}) collective-permute-start(bf16[128,512]{1,0:T(8,128)(2,1)} %bitcast.36), channel_id=1, source_target_pairs={{0,0},{1,8},{2,16},{3,24},{4,1},{5,9},{6,17},{7,25},{8,4},{9,12},{... | collective-permute-start | bytes 393224 | tf_op jit(solution)/shard_map/ppermute | solution.py:736
  36.1 3.6 %collective-permute-start.10 = (bf16[256,1280]{1,0:T(8,128)(2,1)S(1)}, bf16[256,1280]{1,0:T(8,128)(2,1)S(1)}, u32[]{:S(2)}, u32[]{:S(2)}) collective-permute-start(bf16[256,1280]{1,0:T(8,128)(2,1)S(1)} %get-tuple-element.114.refs_2_.refs_6_), channel_id=1, source_target_pairs={{0,8},{1,9},{2,10},{3,11},{4,12},{5,13},{6,14},{7,15},{8,0},{9,1},... | collective-permute-start | bytes 1966088 | tf_op jit(solution)/shard_map/ppermute | solution.py:120
  36.2 27.2 %collective-permute-start.14 = (bf16[128,2048]{1,0:T(8,128)(2,1)S(1)}, bf16[128,2048]{1,0:T(8,128)(2,1)S(1)}, u32[]{:S(2)}, u32[]{:S(2)}) collective-permute-start(bf16[128,2048]{1,0:T(8,128)(2,1)S(1)} %get-tuple-element.129.refs_0_), channel_id=1, source_target_pairs={{0,1},{1,0},{2,3},{3,2},{4,5},{5,4},{6,7},{7,6},{8,9},{9,8},{10,11... | collective-permute-start | bytes 1572872 | tf_op jit(solution)/shard_map/ppermute | solution.py:120
  37.3 26.1 %collective-permute-start.15 = (bf16[128,2048]{1,0:T(8,128)(2,1)S(1)}, bf16[128,2048]{1,0:T(8,128)(2,1)S(1)}, u32[]{:S(2)}, u32[]{:S(2)}) collective-permute-start(bf16[128,2048]{1,0:T(8,128)(2,1)S(1)} %get-tuple-element.129.refs_0_), channel_id=1, source_target_pairs={{0,16},{1,17},{2,18},{3,19},{4,20},{5,21},{6,22},{7,23},{8,24},{9,... | collective-permute-start | bytes 1572872 | tf_op jit(solution)/shard_map/ppermute | solution.py:120
  37.3 26.1 %collective-permute-start.16 = (bf16[128,2048]{1,0:T(8,128)(2,1)S(1)}, bf16[128,2048]{1,0:T(8,128)(2,1)S(1)}, u32[]{:S(2)}, u32[]{:S(2)}) collective-permute-start(bf16[128,2048]{1,0:T(8,128)(2,1)S(1)} %get-tuple-element.129.refs_0_), channel_id=1, source_target_pairs={{0,17},{1,16},{2,19},{3,18},{4,21},{5,20},{6,23},{7,22},{8,25},{9,... | collective-permute-start | bytes 1572872 | tf_op jit(solution)/shard_map/ppermute | solution.py:120
  43.8 1.3 collective-permute-start.11
  45.1 18.2 %collective-permute-start.12 = (bf16[144,128]{1,0:T(8,128)(2,1)S(1)}, bf16[144,128]{1,0:T(8,128)(2,1)S(1)}, u32[]{:S(2)}, u32[]{:S(2)}) collective-permute-start(bf16[144,128]{1,0:T(8,128)(2,1)S(1)} %get-tuple-element.122.refs_0_), channel_id=1, source_target_pairs={{0,16},{1,17},{2,18},{3,19},{4,20},{5,21},{6,22},{7,23},{8,24},{9,... | collective-permute-start | bytes 110600 | tf_op jit(solution)/shard_map/ppermute | solution.py:120
  63.6 4.8 %collective-permute-start.17 = (bf16[512,2048]{1,0:T(8,128)(2,1)S(1)}, bf16[512,2048]{1,0:T(8,128)(2,1)S(1)}, u32[]{:S(2)}, u32[]{:S(2)}) collective-permute-start(bf16[512,2048]{1,0:T(8,128)(2,1)S(1)} %shard_map.304.refs_11_.refs_9_.refs_8_), channel_id=1, source_target_pairs={{0,8},{1,9},{2,10},{3,11},{4,12},{5,13},{6,14},{7,15},{8,0},{9,1},... | collective-permute-start | bytes 6291464 | tf_op jit(solution)/shard_map/ppermute | solution.py:120
  63.7 4.0 %collective-permute-start.13 = (bf16[144,128]{1,0:T(8,128)(2,1)S(1)}, bf16[144,128]{1,0:T(8,128)(2,1)S(1)}, u32[]{:S(2)}, u32[]{:S(2)}) collective-permute-start(bf16[144,128]{1,0:T(8,128)(2,1)S(1)} %get-tuple-element.124.refs_0_), channel_id=1, source_target_pairs={{0,1},{1,0},{2,3},{3,2},{4,5},{5,4},{6,7},{7,6},{8,9},{9,8},{10,11... | collective-permute-start | bytes 110600 | tf_op jit(solution)/shard_map/ppermute | solution.py:120
  102.8 1.3 collective-permute-start.18
  105.9 14.7 %collective-permute-start.21 = (bf16[512,2048]{1,0:T(8,128)(2,1)S(1)}, bf16[512,2048]{1,0:T(8,128)(2,1)S(1)}, u32[]{:S(2)}, u32[]{:S(2)}) collective-permute-start(bf16[512,2048]{1,0:T(8,128)(2,1)S(1)} %get-tuple-element.157), channel_id=1, source_target_pairs={{0,8},{1,9},{2,10},{3,11},{4,12},{5,13},{6,14},{7,15},{8,0},{9,1},... | collective-permute-start | bytes 6291464 | tf_op jit(solution)/shard_map/ppermute | solution.py:120
  106.1 4.0 %collective-permute-start.19 = (bf16[144,128]{1,0:T(8,128)(2,1)S(1)}, bf16[144,128]{1,0:T(8,128)(2,1)S(1)}, u32[]{:S(2)}, u32[]{:S(2)}) collective-permute-start(bf16[144,128]{1,0:T(8,128)(2,1)S(1)} %get-tuple-element.142.refs_0_), channel_id=1, source_target_pairs={{0,16},{1,17},{2,18},{3,19},{4,20},{5,21},{6,22},{7,23},{8,24},{9,... | collective-permute-start | bytes 110600 | tf_op jit(solution)/shard_map/ppermute | solution.py:120
  110.1 9.7 %collective-permute-start.20 = (bf16[144,128]{1,0:T(8,128)(2,1)S(1)}, bf16[144,128]{1,0:T(8,128)(2,1)S(1)}, u32[]{:S(2)}, u32[]{:S(2)}) collective-permute-start(bf16[144,128]{1,0:T(8,128)(2,1)S(1)} %get-tuple-element.153.refs_0_), channel_id=1, source_target_pairs={{0,1},{1,0},{2,3},{3,2},{4,5},{5,4},{6,7},{7,6},{8,9},{9,8},{10,11... | collective-permute-start | bytes 110600 | tf_op jit(solution)/shard_map/ppermute | solution.py:120
  111.6 18.0 %collective-permute-start.22 = (bf16[128,512]{1,0:T(8,128)(2,1)S(1)}, bf16[128,512]{1,0:T(8,128)(2,1)S(1)}, u32[]{:S(2)}, u32[]{:S(2)}) collective-permute-start(bf16[128,512]{1,0:T(8,128)(2,1)S(1)} %get-tuple-element.152.refs_4_), channel_id=1, source_target_pairs={{0,0},{8,1},{16,2},{24,3},{1,4},{9,5},{17,6},{25,7},{4,8},{12,9},{... | collective-permute-start | bytes 393224 | tf_op jit(solution)/shard_map/ppermute | solution.py:821
  121.0 14.0 %collective-permute-start.26 = (bf16[256,1024]{1,0:T(8,128)(2,1)S(1)}, bf16[256,1024]{1,0:T(8,128)(2,1)S(1)}, u32[]{:S(2)}, u32[]{:S(2)}) collective-permute-start(bf16[256,1024]{1,0:T(8,128)(2,1)S(1)} %get-tuple-element.167), channel_id=1, source_target_pairs={{0,16},{1,17},{2,18},{3,19},{4,20},{5,21},{6,22},{7,23},{8,24},{9,... | collective-permute-start | bytes 1572872 | tf_op jit(solution)/shard_map/ppermute | solution.py:120
  121.1 15.1 %collective-permute-start.27 = (bf16[256,1024]{1,0:T(8,128)(2,1)S(1)}, bf16[256,1024]{1,0:T(8,128)(2,1)S(1)}, u32[]{:S(2)}, u32[]{:S(2)}) collective-permute-start(bf16[256,1024]{1,0:T(8,128)(2,1)S(1)} %get-tuple-element.169), channel_id=1, source_target_pairs={{0,1},{1,0},{2,3},{3,2},{4,5},{5,4},{6,7},{7,6},{8,9},{9,8},{10,11... | collective-permute-start | bytes 1572872 | tf_op jit(solution)/shard_map/ppermute | solution.py:120
  131.5 6.2 %collective-permute-start.25 = (bf16[256,1280]{1,0:T(8,128)(2,1)S(1)}, bf16[256,1280]{1,0:T(8,128)(2,1)S(1)}, u32[]{:S(2)}, u32[]{:S(2)}) collective-permute-start(bf16[256,1280]{1,0:T(8,128)(2,1)S(1)} %get-tuple-element.166), channel_id=1, source_target_pairs={{0,8},{1,9},{2,10},{3,11},{4,12},{5,13},{6,14},{7,15},{8,0},{9,1},... | collective-permute-start | bytes 1966088 | tf_op jit(solution)/shard_map/ppermute | solution.py:120
  136.4 8.0 %collective-permute-start.28 = (bf16[128,1024]{1,0:T(8,128)(2,1)S(1)}, bf16[128,1024]{1,0:T(8,128)(2,1)S(1)}, u32[]{:S(2)}, u32[]{:S(2)}) collective-permute-start(bf16[128,1024]{1,0:T(8,128)(2,1)S(1)} %get-tuple-element.171), channel_id=1, source_target_pairs={{0,1},{1,0},{2,3},{3,2},{4,5},{5,4},{6,7},{7,6},{8,9},{9,8},{10,11... | collective-permute-start | bytes 786440 | tf_op jit(solution)/shard_map/ppermute | solution.py:120
  137.7 8.0 %collective-permute-start.29 = (bf16[128,1024]{1,0:T(8,128)(2,1)S(1)}, bf16[128,1024]{1,0:T(8,128)(2,1)S(1)}, u32[]{:S(2)}, u32[]{:S(2)}) collective-permute-start(bf16[128,1024]{1,0:T(8,128)(2,1)S(1)} %get-tuple-element.173), channel_id=1, source_target_pairs={{0,16},{1,17},{2,18},{3,19},{4,20},{5,21},{6,22},{7,23},{8,24},{9,... | collective-permute-start | bytes 786440 | tf_op jit(solution)/shard_map/ppermute | solution.py:120
  146.0 19.7 %collective-permute-start.33 = (bf16[64,2048]{1,0:T(8,128)(2,1)S(1)}, bf16[64,2048]{1,0:T(8,128)(2,1)S(1)}, u32[]{:S(2)}, u32[]{:S(2)}) collective-permute-start(bf16[64,2048]{1,0:T(8,128)(2,1)S(1)} %get-tuple-element.179), channel_id=1, source_target_pairs={{0,2},{1,3},{2,0},{3,1},{4,6},{5,7},{6,4},{7,5},{8,10},{9,11},{10,... | collective-permute-start | bytes 786440 | tf_op jit(solution)/shard_map/ppermute | solution.py:120
  146.1 19.6 %collective-permute-start.30 = (bf16[64,1280]{1,0:T(8,128)(2,1)S(1)}, bf16[64,1280]{1,0:T(8,128)(2,1)S(1)}, u32[]{:S(2)}, u32[]{:S(2)}) collective-permute-start(bf16[64,1280]{1,0:T(8,128)(2,1)S(1)} %get-tuple-element.175), channel_id=1, source_target_pairs={{0,1},{1,0},{2,3},{3,2},{4,5},{5,4},{6,7},{7,6},{8,9},{9,8},{10,11... | collective-permute-start | bytes 491528 | tf_op jit(solution)/shard_map/ppermute | solution.py:120
  146.5 19.2 %collective-permute-start.31 = (bf16[64,1280]{1,0:T(8,128)(2,1)S(1)}, bf16[64,1280]{1,0:T(8,128)(2,1)S(1)}, u32[]{:S(2)}, u32[]{:S(2)}) collective-permute-start(bf16[64,1280]{1,0:T(8,128)(2,1)S(1)} %get-tuple-element.176), channel_id=1, source_target_pairs={{0,16},{1,17},{2,18},{3,19},{4,20},{5,21},{6,22},{7,23},{8,24},{9,... | collective-permute-start | bytes 491528 | tf_op jit(solution)/shard_map/ppermute | solution.py:120
  146.8 18.9 %collective-permute-start.32 = (bf16[64,1280]{1,0:T(8,128)(2,1)S(1)}, bf16[64,1280]{1,0:T(8,128)(2,1)S(1)}, u32[]{:S(2)}, u32[]{:S(2)}) collective-permute-start(bf16[64,1280]{1,0:T(8,128)(2,1)S(1)} %get-tuple-element.177), channel_id=1, source_target_pairs={{0,17},{1,16},{2,19},{3,18},{4,21},{5,20},{6,23},{7,22},{8,25},{9,... | collective-permute-start | bytes 491528 | tf_op jit(solution)/shard_map/ppermute | solution.py:120
  149.6 16.1 %collective-permute-start.23 = (bf16[128,512]{1,0:T(8,128)(2,1)S(1)}, bf16[128,512]{1,0:T(8,128)(2,1)S(1)}, u32[]{:S(2)}, u32[]{:S(2)}) collective-permute-start(bf16[128,512]{1,0:T(8,128)(2,1)S(1)} %get-tuple-element.163), channel_id=1, source_target_pairs={{0,0},{8,1},{16,2},{24,3},{1,4},{9,5},{17,6},{25,7},{4,8},{12,9},{... | collective-permute-start | bytes 393224 | tf_op jit(solution)/shard_map/ppermute | solution.py:847
  165.9 11.1 %collective-permute-start.37 = (bf16[32,2048]{1,0:T(8,128)(2,1)S(1)}, bf16[32,2048]{1,0:T(8,128)(2,1)S(1)}, u32[]{:S(2)}, u32[]{:S(2)}) collective-permute-start(bf16[32,2048]{1,0:T(8,128)(2,1)S(1)} %get-tuple-element.185), channel_id=1, source_target_pairs={{0,4},{1,5},{2,6},{3,7},{4,0},{5,1},{6,2},{7,3},{8,12},{9,13},{10,... | collective-permute-start | bytes 393224 | tf_op jit(solution)/shard_map/ppermute | solution.py:120
  166.0 11.0 %collective-permute-start.34 = (bf16[16,1280]{1,0:T(8,128)(2,1)S(1)}, bf16[16,1280]{1,0:T(8,128)(2,1)S(1)}, u32[]{:S(2)}, u32[]{:S(2)}) collective-permute-start(bf16[16,1280]{1,0:T(8,128)(2,1)S(1)} %get-tuple-element.181), channel_id=1, source_target_pairs={{0,4},{1,5},{2,6},{3,7},{4,0},{5,1},{6,2},{7,3},{8,12},{9,13},{10,... | collective-permute-start | bytes 122888 | tf_op jit(solution)/shard_map/ppermute | solution.py:120
  168.9 8.1 %collective-permute-start.35 = (bf16[16,1280]{1,0:T(8,128)(2,1)S(1)}, bf16[16,1280]{1,0:T(8,128)(2,1)S(1)}, u32[]{:S(2)}, u32[]{:S(2)}) collective-permute-start(bf16[16,1280]{1,0:T(8,128)(2,1)S(1)} %get-tuple-element.182), channel_id=1, source_target_pairs={{0,2},{1,3},{2,0},{3,1},{4,6},{5,7},{6,4},{7,5},{8,10},{9,11},{10,... | collective-permute-start | bytes 122888 | tf_op jit(solution)/shard_map/ppermute | solution.py:120
  168.9 8.1 %collective-permute-start.36 = (bf16[16,1280]{1,0:T(8,128)(2,1)S(1)}, bf16[16,1280]{1,0:T(8,128)(2,1)S(1)}, u32[]{:S(2)}, u32[]{:S(2)}) collective-permute-start(bf16[16,1280]{1,0:T(8,128)(2,1)S(1)} %get-tuple-element.183), channel_id=1, source_target_pairs={{0,6},{1,7},{2,4},{3,5},{4,2},{5,3},{6,0},{7,1},{8,14},{9,15},{10,... | collective-permute-start | bytes 122888 | tf_op jit(solution)/shard_map/ppermute | solution.py:120
  170.4 6.5 %collective-permute-start.24 = (bf16[16,512]{1,0:T(8,128)(2,1)S(1)}, bf16[16,512]{1,0:T(8,128)(2,1)S(1)}, u32[]{:S(2)}, u32[]{:S(2)}) collective-permute-start(bf16[16,512]{1,0:T(8,128)(2,1)S(1)} %get-tuple-element.164), channel_id=1, source_target_pairs={{8,0},{16,1},{24,2},{1,3},{9,4},{17,5},{25,6},{12,8},{20,9},{28,10... | collective-permute-start | bytes 49160 | tf_op jit(solution)/shard_map/ppermute | solution.py:848

commit v3 on v2

--- a/solution.py
+++ b/solution.py
@@ -1,4 +1,5 @@
 import functools
+import math
 
 import jax
 import jax.numpy as jnp
@@ -30,7 +31,7 @@
 CORE = 8
 HALF_MASKS = tuple(xy | zz for xy in XY_MASKS for zz in Z_MASKS)
 FULL_MASKS = HALF_MASKS + tuple(mask | CORE for mask in HALF_MASKS)
-CHUNK_MASKS = tuple((8 if c & 1 else 0) | (16 if c & 2 else 0) | (1 if c & 4 else 0) for c in range(8))
+CHUNK_MASKS = tuple((8 if c & 1 else 0) | (2 if c & 2 else 0) | (1 if c & 4 else 0) for c in range(8))
 
 ROW_X = 0
 ROW_DT = 64
@@ -93,7 +94,7 @@
             self.grad_masks = (tuple(range(BLOCKS)),)
 
     def place(self, seq, chunk):
-        return CHUNK_MASKS[chunk] | ((0, 2, 1, 3)[seq] << 1)
+        return CHUNK_MASKS[chunk] | ((seq >> 1) << 4) | ((seq & 1) << 2)
 
     def me(self):
         if self.fast:
@@ -103,7 +104,7 @@
     def chunk(self):
         if self.fast:
             lin = lax.axis_index("dp") * 8 + lax.axis_index("ctx")
-            return ((lin >> 3) & 1) + ((lin >> 4) & 1) * 2 + (lin & 1) * 4
+            return ((lin >> 3) & 1) + ((lin >> 1) & 1) * 2 + (lin & 1) * 4
         return lax.axis_index("ctx")
 
     def side(self):
@@ -371,7 +372,7 @@
 
 def attention_kernel(pay, back, q_s, k_s, v_s, g_s, kt, vt, dk, dv):
     length = pay.shape[0]
-    rows = 256
+    rows = math.gcd(length, 512)
     q_s[...] = pay[:, :HDIM]
     k_s[...] = pay[:, HDIM : 2 * HDIM]
     v_s[...] = pay[:, 2 * HDIM : 3 * HDIM]
@@ -853,7 +854,7 @@
         *u_parts, keep, give = run(
             cut_three_kernel,
             [two_grads[0], send(two_grads[1], CORE), a_keep, send(a_give, 1), b_keep, send(b_give, 16)],
-            [((n * 4, E + 256), BF16)] * 4 + [((n * 4, 4 * D), BF16)] * 2)
+            [((n * 4, E + 256), BF16)] * 4 + [((n * 4, 4 * D), BF16)] * 2, after=[tail])
         *u_parts, keep, give = run(
             cut_four_kernel, [*sends(u_parts, XY_MASKS), keep, send(give, 2)],
             [((n, E + 256), BF16)] * 4 + [((n * 2, 4 * D), BF16)] * 2, after=[grad_tok])

time: 179 us -> 170 us (0.950)
  waiting for transfers between devices: 67.9 us -> 55.5 us
  starting transfers between devices: 47.1 us -> 49.5 us
    ppermute x1, waiting for transfers between devices: 12.4 us -> 5.1 us  [body(): grad_tok = lax.ppermute(own, ALL, back)]
    ppermute x32, starting transfers between devices: 27.3 us -> 32.8 us  [send(): return lax.ppermute(value, ALL, [(i, i ^ mask) for i in range(32)])]
    ppermute x1, starting transfers between devices: 4.99 us -> 1.91 us  [body(): result = lax.ppermute(result, ALL, [(b, a) for a, b in home])]
    ppermute x32, waiting for transfers between devices: 38.6 us -> 35.6 us  [send(): return lax.ppermute(value, ALL, [(i, i ^ mask) for i in range(32)])]
  transfers between devices with their start and end apart: 38 -> 38, of which waited for: 13 -> 17; matrix products, arithmetic and copies ran while one was open for 0% -> 0% of each run, Pallas kernels for 11% -> 12%
where the time goes in v3:
time: 170 us; the launch traced here: 168 us
  waiting for transfers between devices  55.5 us (33%)
  starting transfers between devices  49.5 us (29%)
  Pallas kernels  35.6 us (21%)
  blocking collectives  23.5 us (14%)
  local copies, waits for them, and re-layouts  2.4 us (1%)
    ppermute x32, waiting for transfers between devices, send(): return lax.ppermute(value, ALL, [(i, i ^ mask) for i in range(32)])  35.6 us
    pallas_call x24, Pallas kernels, run(): pl.pallas_call(inner, out_shape=[jax.ShapeDtypeStruct(shape, dtype) for s...  35.6 us
    ppermute x32, starting transfers between devices, send(): return lax.ppermute(value, ALL, [(i, i ^ mask) for i in range(32)])  32.8 us
    all_to_all x2, blocking collectives, swap(): lax.all_to_all(value, ALL, 0, 0, tiled=True, axis_index_groups=groups)  23.5 us
    ppermute x1, waiting for transfers between devices, body(): cot = lax.ppermute(cot0, ALL, home)  7.98 us
    ppermute x1, waiting for transfers between devices, body(): grad_tok = lax.ppermute(own, ALL, back)  5.1 us
    ppermute x1, starting transfers between devices, body(): grad_tok = lax.ppermute(own, ALL, back)  4.4 us
    ppermute x1, waiting for transfers between devices, body(): lax.ppermute(before, ALL, [(plan.place(s, c + 1), s * 8 + c) for s in ran...  4.16 us
  transfers between devices with their start and end apart: 38, of which 17 were waited for; matrix products, arithmetic and copies ran while one was open for 0% of the time, Pallas kernels for 12%

profile of v3, /device:TPU:6, one launch (start us, length us, event | category | flops | bytes accessed | tf_op | source)
XLA Modules:
  0.0 167.7 jit_solution(12642291827929278615)
XLA Ops:
  0.7 2.0 %shard_map.296 = (bf16[16,1280]{1,0:T(8,128)(2,1)}, bf16[32,2048]{1,0:T(8,128)(2,1)}) custom-call(f32[16,2048]{1,0:T(8,128)} %refs_0_.1, f32[32,64]{1,0:T(8,128)} %refs_1_.1, f32[32,32]{1,0:T(8,128)} %refs_2_.1, f32[16,32]{1,0:T(8,128)} %bitcast.28, f32[4,32]{1,0:T(4,128)} %bitcast.29, f32[1,32]{1,0:T(1,128)} %bitcast.31, f32[1,32]{1,0:T(1,128)} %bitcast.32, ...), custom_call_target="tpu_custom_call" | custom-call | flops 2000 | bytes 6000 | tf_op jit(solution)/shard_map/pallas_call | solution.py:59
  2.6 2.7 %collective-permute-start.2 = (bf16[16,1280]{1,0:T(8,128)(2,1)}, bf16[16,1280]{1,0:T(8,128)(2,1)S(1)}, u32[]{:S(2)}, u32[]{:S(2)}) collective-permute-start(bf16[16,1280]{1,0:T(8,128)(2,1)} %get-tuple-element.110.refs_0_), channel_id=1, source_target_pairs={{0,4},{1,5},{2,6},{3,7},{4,0},{5,1},{6,2},{7,3},{8,12},{9,13},{10,... | collective-permute-start | bytes 122888 | tf_op jit(solution)/shard_map/ppermute | solution.py:121
  5.3 1.9 %collective-permute-start = (bf16[128,512]{1,0:T(8,128)(2,1)}, bf16[128,512]{1,0:T(8,128)(2,1)S(1)}, u32[]{:S(2)}, u32[]{:S(2)}) collective-permute-start(bf16[128,512]{1,0:T(8,128)(2,1)} %bitcast.30), channel_id=1, source_target_pairs={{0,0},{1,8},{2,2},{3,10},{4,1},{5,9},{6,3},{7,11},{8,4},{9,12},{10... | collective-permute-start | bytes 393224 | tf_op jit(solution)/shard_map/ppermute | solution.py:725
  7.2 2.1 %collective-permute-start.4 = (bf16[32,2048]{1,0:T(8,128)(2,1)}, bf16[32,2048]{1,0:T(8,128)(2,1)S(1)}, u32[]{:S(2)}, u32[]{:S(2)}) collective-permute-start(bf16[32,2048]{1,0:T(8,128)(2,1)} %get-tuple-element.111.refs_2_), channel_id=1, source_target_pairs={{0,4},{1,5},{2,6},{3,7},{4,0},{5,1},{6,2},{7,3},{8,12},{9,13},{10,... | collective-permute-start | bytes 393224 | tf_op jit(solution)/shard_map/ppermute | solution.py:121
  10.1 1.6 collective-permute-start.3
  12.4 4.1 %collective-permute-start.1 = (bf16[16,512]{1,0:T(8,128)(2,1)S(1)}, bf16[16,512]{1,0:T(8,128)(2,1)S(1)}, u32[]{:S(2)}, u32[]{:S(2)}) collective-permute-start(bf16[16,512]{1,0:T(8,128)(2,1)S(1)} %slice_bitcast_fusion), channel_id=1, source_target_pairs={{0,8},{1,2},{2,10},{3,1},{4,9},{5,3},{6,11},{8,12},{9,6},{10,14},{... | collective-permute-start | bytes 49160 | tf_op jit(solution)/shard_map/ppermute | solution.py:726
  16.5 2.7 %collective-permute-done.1.refs_5_.refs_1_ = bf16[16,512]{1,0:T(8,128)(2,1)S(1)} collective-permute-done((bf16[16,512]{1,0:T(8,128)(2,1)S(1)}, bf16[16,512]{1,0:T(8,128)(2,1)S(1)}, u32[]{:S(2)}, u32[]{:S(2)}) %collective-permute-start.1) | collective-permute-done | bytes 16416 | tf_op jit(solution)/shard_map/ppermute | solution.py:726
  20.1 1.9 %collective-permute-start.8 = (bf16[64,2048]{1,0:T(8,128)(2,1)S(1)}, bf16[64,2048]{1,0:T(8,128)(2,1)S(1)}, u32[]{:S(2)}, u32[]{:S(2)}) collective-permute-start(bf16[64,2048]{1,0:T(8,128)(2,1)S(1)} %get-tuple-element.113.refs_4_), channel_id=1, source_target_pairs={{0,2},{1,3},{2,0},{3,1},{4,6},{5,7},{6,4},{7,5},{8,10},{9,11},{10,... | collective-permute-start | bytes 786440 | tf_op jit(solution)/shard_map/ppermute | solution.py:121
  23.2 2.3 %collective-permute-start.7 = (bf16[64,1280]{1,0:T(8,128)(2,1)S(1)}, bf16[64,1280]{1,0:T(8,128)(2,1)S(1)}, u32[]{:S(2)}, u32[]{:S(2)}) collective-permute-start(bf16[64,1280]{1,0:T(8,128)(2,1)S(1)} %get-tuple-element.112.refs_0_), channel_id=1, source_target_pairs={{0,17},{1,16},{2,19},{3,18},{4,21},{5,20},{6,23},{7,22},{8,25},{9,... | collective-permute-start | bytes 491528 | tf_op jit(solution)/shard_map/ppermute | solution.py:121
  25.5 1.9 %collective-permute-start.9 = (bf16[128,512]{1,0:T(8,128)(2,1)}, bf16[128,512]{1,0:T(8,128)(2,1)S(1)}, u32[]{:S(2)}, u32[]{:S(2)}) collective-permute-start(bf16[128,512]{1,0:T(8,128)(2,1)} %bitcast.36), channel_id=1, source_target_pairs={{0,0},{1,8},{2,2},{3,10},{4,1},{5,9},{6,3},{7,11},{8,4},{9,12},{10... | collective-permute-start | bytes 393224 | tf_op jit(solution)/shard_map/ppermute | solution.py:737
  27.4 8.0 %collective-permute-done.9.refs_6_.refs_7_.refs_2_.refs_8_ = bf16[128,512]{1,0:T(8,128)(2,1)S(1)} collective-permute-done((bf16[128,512]{1,0:T(8,128)(2,1)}, bf16[128,512]{1,0:T(8,128)(2,1)S(1)}, u32[]{:S(2)}, u32[]{:S(2)}) %collective-permute-start.9) | collective-permute-done | bytes 131104 | tf_op jit(solution)/shard_map/ppermute | solution.py:737
  36.3 2.9 %collective-permute-start.16 = (bf16[128,2048]{1,0:T(8,128)(2,1)S(1)}, bf16[128,2048]{1,0:T(8,128)(2,1)S(1)}, u32[]{:S(2)}, u32[]{:S(2)}) collective-permute-start(bf16[128,2048]{1,0:T(8,128)(2,1)S(1)} %get-tuple-element.129.refs_0_), channel_id=1, source_target_pairs={{0,17},{1,16},{2,19},{3,18},{4,21},{5,20},{6,23},{7,22},{8,25},{9,... | collective-permute-start | bytes 1572872 | tf_op jit(solution)/shard_map/ppermute | solution.py:121
  39.2 4.0 %shard_map.300 = (bf16[144,512]{1,0:T(8,128)(2,1)S(1)}, bf16[144,512]{1,0:T(8,128)(2,1)S(1)}, f32[144,1024]{1,0:T(8,128)S(1)}, f32[128,1024]{1,0:T(8,128)S(1)}, ...) custom-call(bf16[128,512]{1,0:T(8,128)(2,1)S(1)} %collective-permute, ...), custom_call_target="tpu_custom_call" | custom-call | flops 6000 | bytes 18000 | tf_op jit(solution)/shard_map/pallas_call | solution.py:59
  43.3 1.2 collective-permute-done.11.refs_1_
  44.6 3.9 %collective-permute-done.12.refs_1_ = bf16[144,128]{1,0:T(8,128)(2,1)S(1)} collective-permute-done((bf16[144,128]{1,0:T(8,128)(2,1)S(1)}, bf16[144,128]{1,0:T(8,128)(2,1)S(1)}, u32[]{:S(2)}, u32[]{:S(2)}) %collective-permute-start.12) | collective-permute-done | bytes 36896 | tf_op jit(solution)/shard_map/ppermute | solution.py:121
  48.6 1.3 collective-permute-done.14.refs_1_
  50.5 11.9 %collective-permute-done.16.refs_3_ = bf16[128,2048]{1,0:T(8,128)(2,1)S(1)} collective-permute-done((bf16[128,2048]{1,0:T(8,128)(2,1)S(1)}, bf16[128,2048]{1,0:T(8,128)(2,1)S(1)}, u32[]{:S(2)}, u32[]{:S(2)}) %collective-permute-start.16) | collective-permute-done | bytes 524320 | tf_op jit(solution)/shard_map/ppermute | solution.py:121
  63.0 3.7 %collective-permute-done.13.refs_1_ = bf16[144,128]{1,0:T(8,128)(2,1)S(1)} collective-permute-done((bf16[144,128]{1,0:T(8,128)(2,1)S(1)}, bf16[144,128]{1,0:T(8,128)(2,1)S(1)}, u32[]{:S(2)}, u32[]{:S(2)}) %collective-permute-start.13) | collective-permute-done | bytes 36896 | tf_op jit(solution)/shard_map/ppermute | solution.py:121
  67.3 3.8 %shard_map.305 = (bf16[1024,256]{1,0:T(8,128)(2,1)S(1)}, f32[128,1024]{1,0:T(8,128)S(1)}, bf16[128,1024]{1,0:T(8,128)(2,1)S(1)}, f32[128,512]{1,0:T(8,128)S(1)},...) custom-call(bf16[128,512]{1,0:T(8,128)(2,1)S(1)} %collective-permute-done.refs_4_.refs_0_, ...), custom_call_target="tpu_custom_call" | custom-call | flops 6000 | bytes 18000 | tf_op jit(solution)/shard_map/pallas_call | solution.py:59
  71.2 11.4 %all_to_all.22 = bf16[8,128,256]{2,1,0:T(8,128)(2,1)S(1)} all-to-all(bf16[8,128,256]{2,1,0:T(8,128)(2,1)S(1)} %bitcast.27), channel_id=1, replica_groups={{0,8,2,10,1,9,3,11},{4,12,6,14,5,13,7,15},{16,24,18,26,17,25,19,27},{20..., dimensions={0} | all-to-all | bytes 1048576 | tf_op jit(solution)/shard_map/all_to_all | solution.py:116
  82.5 3.6 %shard_map.306 = bf16[1024,256]{1,0:T(8,128)(2,1)S(1)} custom-call(bf16[1024,256]{1,0:T(8,128)(2,1)S(1)} %bitcast.25), custom_call_target="tpu_custom_call" | custom-call | flops 4000 | bytes 12000 | tf_op jit(solution)/shard_map/pallas_call | solution.py:59
  86.2 12.1 %all_to_all.23 = bf16[8,128,256]{2,1,0:T(8,128)(2,1)S(1)} all-to-all(bf16[8,128,256]{2,1,0:T(8,128)(2,1)S(1)} %bitcast.26), channel_id=1, replica_groups={{0,8,2,10,1,9,3,11},{4,12,6,14,5,13,7,15},{16,24,18,26,17,25,19,27},{20..., dimensions={0} | all-to-all | bytes 1048576 | tf_op jit(solution)/shard_map/all_to_all | solution.py:116
  98.3 3.1 %shard_map.307 = (bf16[128,512]{1,0:T(8,128)(2,1)S(1)}, bf16[128,512]{1,0:T(8,128)(2,1)S(1)}, bf16[128,512]{1,0:T(8,128)(2,1)S(1)}, bf16[128,512]{1,0:T(8,128)(2...) custom-call(bf16[1024,256]{1,0:T(8,128)(2,1)S(1)} %bitcast.24, ...), custom_call_target="tpu_custom_call" | custom-call | flops 2000 | bytes 6000 | tf_op jit(solution)/shard_map/pallas_call | solution.py:59
  101.5 1.2 collective-permute-done.18.refs_1_
  102.8 1.7 %shard_map.309 = (bf16[128,512]{1,0:T(8,128)(2,1)S(1)}, bf16[512,2048]{1,0:T(8,128)(2,1)S(1)}, bf16[512,2048]{1,0:T(8,128)(2,1)S(1)}) custom-call(bf16[128,512]{1,0:T(8,128)(2,1)S(1)} %get-tuple-element.144.refs_0_, bf16[128,512]{1,0:T(8,128)(2,1)S(1)} %get-tuple-element.145.refs_1_, bf16[128,512]{1,0:T(8,128)(2,1)S(1)} %get-tuple-element.146.refs_2_, ...), custom_call_target="tpu_custom_call" | custom-call | flops 2000 | bytes 6000 | tf_op jit(solution)/shard_map/pallas_call | solution.py:59
  105.3 3.4 %collective-permute-done.19.refs_1_ = bf16[144,128]{1,0:T(8,128)(2,1)S(1)} collective-permute-done((bf16[144,128]{1,0:T(8,128)(2,1)S(1)}, bf16[144,128]{1,0:T(8,128)(2,1)S(1)}, u32[]{:S(2)}, u32[]{:S(2)}) %collective-permute-start.19) | collective-permute-done | bytes 36896 | tf_op jit(solution)/shard_map/ppermute | solution.py:121
  108.7 1.5 collective-permute-start.20
  110.3 1.9 %collective-permute-start.22 = (bf16[128,512]{1,0:T(8,128)(2,1)S(1)}, bf16[128,512]{1,0:T(8,128)(2,1)S(1)}, u32[]{:S(2)}, u32[]{:S(2)}) collective-permute-start(bf16[128,512]{1,0:T(8,128)(2,1)S(1)} %get-tuple-element.152.refs_4_), channel_id=1, source_target_pairs={{0,0},{8,1},{2,2},{10,3},{1,4},{9,5},{3,6},{11,7},{4,8},{12,9},{6,... | collective-permute-start | bytes 393224 | tf_op jit(solution)/shard_map/ppermute | solution.py:822
  112.2 3.2 %shard_map.311.refs_4_.refs_14_ = f32[128,128]{1,0:T(8,128)S(1)} custom-call(f32[1024,128]{1,0:T(8,128)S(1)} %get-tuple-element.134.refs_0_.refs_2_, f32[16512,128]{1,0:T(8,128)S(1)} %get-tuple-element.136.refs_1_.refs_6_, f32[144,128]{1,0:T(8,128)S(1)} %get-tuple-element.154.refs_2_), custom_call_target="tpu_custom_call" | custom-call | flops 2000 | bytes 6000 | tf_op jit(solution)/shard_map/pallas_call | solution.py:59
  117.2 8.4 %shard_map.314 = (f32[128,1024]{1,0:T(8,128)S(1)}, bf16[144,1024]{1,0:T(8,128)(2,1)S(1)}) custom-call(f32[1024,128]{1,0:T(8,128)S(1)} %get-tuple-element.116.refs_1_.refs_6_.refs_0_, f32[1024,128]{1,0:T(8,128)S(1)} %get-tuple-element.117.refs_2_.refs_1_, f32[1024,128]{1,0:T(8,128)S(1)} %get-tuple-element.134.refs_0_.refs_2_, ...), custom_call_target="tpu_custom_call" | custom-call | flops 11000 | bytes 33000 | tf_op jit(solution)/shard_map/pallas_call | solution.py:59
  125.6 1.8 %shard_map.315 = (bf16[256,1280]{1,0:T(8,128)(2,1)S(1)}, bf16[256,1280]{1,0:T(8,128)(2,1)S(1)}, bf16[128,512]{1,0:T(8,128)(2,1)S(1)}, bf16[16,512]{1,0:T(8,128)(2,1)S(1)}) custom-call(bf16[128,512]{1,0:T(8,128)(2,1)S(1)} %collective-permute-done.refs_4_.refs_0_, bf16[16,512]{1,0:T(8,128)(2,1)S(1)} %collective-permute-done.1.refs_5_.refs_1_, ...), custom_call_target="tpu_custom_call" | custom-call | flops 2000 | bytes 6000 | tf_op jit(solution)/shard_map/pallas_call | solution.py:59
  127.5 1.6 collective-permute-start.25
  129.1 1.2 collective-permute-done.26.refs_1_
  130.3 1.3 collective-permute-done.27.refs_3_
  131.9 1.1 collective-permute-start.29
  133.0 2.5 %collective-permute-start.24 = (bf16[16,512]{1,0:T(8,128)(2,1)S(1)}, bf16[16,512]{1,0:T(8,128)(2,1)S(1)}, u32[]{:S(2)}, u32[]{:S(2)}) collective-permute-start(bf16[16,512]{1,0:T(8,128)(2,1)S(1)} %get-tuple-element.164), channel_id=1, source_target_pairs={{8,0},{2,1},{10,2},{1,3},{9,4},{3,5},{11,6},{12,8},{6,9},{14,10},{... | collective-permute-start | bytes 49160 | tf_op jit(solution)/shard_map/ppermute | solution.py:849
  135.4 4.2 %collective-permute-done.24.refs_6_.refs_1_ = bf16[16,512]{1,0:T(8,128)(2,1)S(1)} collective-permute-done((bf16[16,512]{1,0:T(8,128)(2,1)S(1)}, bf16[16,512]{1,0:T(8,128)(2,1)S(1)}, u32[]{:S(2)}, u32[]{:S(2)}) %collective-permute-start.24) | collective-permute-done | bytes 16416 | tf_op jit(solution)/shard_map/ppermute | solution.py:849
  140.9 1.0 collective-permute-start.30
  141.9 1.1 collective-permute-start.31
  143.0 1.4 collective-permute-start.32
  144.4 4.4 %collective-permute-start.23 = (bf16[128,512]{1,0:T(8,128)(2,1)S(1)}, bf16[128,512]{1,0:T(8,128)(2,1)S(1)}, u32[]{:S(2)}, u32[]{:S(2)}) collective-permute-start(bf16[128,512]{1,0:T(8,128)(2,1)S(1)} %get-tuple-element.163), channel_id=1, source_target_pairs={{0,0},{8,1},{2,2},{10,3},{1,4},{9,5},{3,6},{11,7},{4,8},{12,9},{6,... | collective-permute-start | bytes 393224 | tf_op jit(solution)/shard_map/ppermute | solution.py:848
  148.8 5.1 %collective-permute-done.23.refs_6_.refs_0_ = bf16[128,512]{1,0:T(8,128)(2,1)S(1)} collective-permute-done((bf16[128,512]{1,0:T(8,128)(2,1)S(1)}, bf16[128,512]{1,0:T(8,128)(2,1)S(1)}, u32[]{:S(2)}, u32[]{:S(2)}) %collective-permute-start.23) | collective-permute-done | bytes 131104 | tf_op jit(solution)/shard_map/ppermute | solution.py:848
  154.1 1.1 collective-permute-start.37
  155.2 1.9 %collective-permute-start.34 = (bf16[16,1280]{1,0:T(8,128)(2,1)S(1)}, bf16[16,1280]{1,0:T(8,128)(2,1)S(1)}, u32[]{:S(2)}, u32[]{:S(2)}) collective-permute-start(bf16[16,1280]{1,0:T(8,128)(2,1)S(1)} %get-tuple-element.181), channel_id=1, source_target_pairs={{0,4},{1,5},{2,6},{3,7},{4,0},{5,1},{6,2},{7,3},{8,12},{9,13},{10,... | collective-permute-start | bytes 122888 | tf_op jit(solution)/shard_map/ppermute | solution.py:121
  157.1 2.5 %collective-permute-start.35 = (bf16[16,1280]{1,0:T(8,128)(2,1)S(1)}, bf16[16,1280]{1,0:T(8,128)(2,1)S(1)}, u32[]{:S(2)}, u32[]{:S(2)}) collective-permute-start(bf16[16,1280]{1,0:T(8,128)(2,1)S(1)} %get-tuple-element.182), channel_id=1, source_target_pairs={{0,2},{1,3},{2,0},{3,1},{4,6},{5,7},{6,4},{7,5},{8,10},{9,11},{10,... | collective-permute-start | bytes 122888 | tf_op jit(solution)/shard_map/ppermute | solution.py:121
  159.6 1.5 collective-permute-start.36
  161.1 5.5 %collective-permute-done.34.refs_4_ = bf16[16,1280]{1,0:T(8,128)(2,1)S(1)} collective-permute-done((bf16[16,1280]{1,0:T(8,128)(2,1)S(1)}, bf16[16,1280]{1,0:T(8,128)(2,1)S(1)}, u32[]{:S(2)}, u32[]{:S(2)}) %collective-permute-start.34) | collective-permute-done | bytes 40992 | tf_op jit(solution)/shard_map/ppermute | solution.py:121
  166.6 0.9 shard_map.319
  (60 shorter events, 11.1 us)
Async XLA Ops:
  2.6 6.7 %collective-permute-start.2 = (bf16[16,1280]{1,0:T(8,128)(2,1)}, bf16[16,1280]{1,0:T(8,128)(2,1)S(1)}, u32[]{:S(2)}, u32[]{:S(2)}) collective-permute-start(bf16[16,1280]{1,0:T(8,128)(2,1)} %get-tuple-element.110.refs_0_), channel_id=1, source_target_pairs={{0,4},{1,5},{2,6},{3,7},{4,0},{5,1},{6,2},{7,3},{8,12},{9,13},{10,... | collective-permute-start | bytes 122888 | tf_op jit(solution)/shard_map/ppermute | solution.py:121
  5.3 13.9 %collective-permute-start = (bf16[128,512]{1,0:T(8,128)(2,1)}, bf16[128,512]{1,0:T(8,128)(2,1)S(1)}, u32[]{:S(2)}, u32[]{:S(2)}) collective-permute-start(bf16[128,512]{1,0:T(8,128)(2,1)} %bitcast.30), channel_id=1, source_target_pairs={{0,0},{1,8},{2,2},{3,10},{4,1},{5,9},{6,3},{7,11},{8,4},{9,12},{10... | collective-permute-start | bytes 393224 | tf_op jit(solution)/shard_map/ppermute | solution.py:725
  7.2 12.0 %collective-permute-start.4 = (bf16[32,2048]{1,0:T(8,128)(2,1)}, bf16[32,2048]{1,0:T(8,128)(2,1)S(1)}, u32[]{:S(2)}, u32[]{:S(2)}) collective-permute-start(bf16[32,2048]{1,0:T(8,128)(2,1)} %get-tuple-element.111.refs_2_), channel_id=1, source_target_pairs={{0,4},{1,5},{2,6},{3,7},{4,0},{5,1},{6,2},{7,3},{8,12},{9,13},{10,... | collective-permute-start | bytes 393224 | tf_op jit(solution)/shard_map/ppermute | solution.py:121
  9.3 0.8 copy-start.1
  10.1 9.0 %collective-permute-start.3 = (bf16[32,1280]{1,0:T(8,128)(2,1)S(1)}, bf16[32,1280]{1,0:T(8,128)(2,1)S(1)}, u32[]{:S(2)}, u32[]{:S(2)}) collective-permute-start(bf16[32,1280]{1,0:T(8,128)(2,1)S(1)} %shard_map.297.refs_0_), channel_id=1, source_target_pairs={{0,2},{1,3},{2,0},{3,1},{4,6},{5,7},{6,4},{7,5},{8,10},{9,11},{10,... | collective-permute-start | bytes 245768 | tf_op jit(solution)/shard_map/ppermute | solution.py:121
  12.4 6.7 %collective-permute-start.1 = (bf16[16,512]{1,0:T(8,128)(2,1)S(1)}, bf16[16,512]{1,0:T(8,128)(2,1)S(1)}, u32[]{:S(2)}, u32[]{:S(2)}) collective-permute-start(bf16[16,512]{1,0:T(8,128)(2,1)S(1)} %slice_bitcast_fusion), channel_id=1, source_target_pairs={{0,8},{1,2},{2,10},{3,1},{4,9},{5,3},{6,11},{8,12},{9,6},{10,14},{... | collective-permute-start | bytes 49160 | tf_op jit(solution)/shard_map/ppermute | solution.py:726
  19.2 0.9 copy-start
  20.1 15.3 %collective-permute-start.8 = (bf16[64,2048]{1,0:T(8,128)(2,1)S(1)}, bf16[64,2048]{1,0:T(8,128)(2,1)S(1)}, u32[]{:S(2)}, u32[]{:S(2)}) collective-permute-start(bf16[64,2048]{1,0:T(8,128)(2,1)S(1)} %get-tuple-element.113.refs_4_), channel_id=1, source_target_pairs={{0,2},{1,3},{2,0},{3,1},{4,6},{5,7},{6,4},{7,5},{8,10},{9,11},{10,... | collective-permute-start | bytes 786440 | tf_op jit(solution)/shard_map/ppermute | solution.py:121
  22.0 13.4 %collective-permute-start.5 = (bf16[64,1280]{1,0:T(8,128)(2,1)S(1)}, bf16[64,1280]{1,0:T(8,128)(2,1)S(1)}, u32[]{:S(2)}, u32[]{:S(2)}) collective-permute-start(bf16[64,1280]{1,0:T(8,128)(2,1)S(1)} %get-tuple-element.112.refs_0_), channel_id=1, source_target_pairs={{0,1},{1,0},{2,3},{3,2},{4,5},{5,4},{6,7},{7,6},{8,9},{9,8},{10,11... | collective-permute-start | bytes 491528 | tf_op jit(solution)/shard_map/ppermute | solution.py:121
  22.7 12.7 %collective-permute-start.6 = (bf16[64,1280]{1,0:T(8,128)(2,1)S(1)}, bf16[64,1280]{1,0:T(8,128)(2,1)S(1)}, u32[]{:S(2)}, u32[]{:S(2)}) collective-permute-start(bf16[64,1280]{1,0:T(8,128)(2,1)S(1)} %get-tuple-element.112.refs_0_), channel_id=1, source_target_pairs={{0,16},{1,17},{2,18},{3,19},{4,20},{5,21},{6,22},{7,23},{8,24},{9,... | collective-permute-start | bytes 491528 | tf_op jit(solution)/shard_map/ppermute | solution.py:121
  23.2 12.2 %collective-permute-start.7 = (bf16[64,1280]{1,0:T(8,128)(2,1)S(1)}, bf16[64,1280]{1,0:T(8,128)(2,1)S(1)}, u32[]{:S(2)}, u32[]{:S(2)}) collective-permute-start(bf16[64,1280]{1,0:T(8,128)(2,1)S(1)} %get-tuple-element.112.refs_0_), channel_id=1, source_target_pairs={{0,17},{1,16},{2,19},{3,18},{4,21},{5,20},{6,23},{7,22},{8,25},{9,... | collective-permute-start | bytes 491528 | tf_op jit(solution)/shard_map/ppermute | solution.py:121
  25.5 9.9 %collective-permute-start.9 = (bf16[128,512]{1,0:T(8,128)(2,1)}, bf16[128,512]{1,0:T(8,128)(2,1)S(1)}, u32[]{:S(2)}, u32[]{:S(2)}) collective-permute-start(bf16[128,512]{1,0:T(8,128)(2,1)} %bitcast.36), channel_id=1, source_target_pairs={{0,0},{1,8},{2,2},{3,10},{4,1},{5,9},{6,3},{7,11},{8,4},{9,12},{10... | collective-permute-start | bytes 393224 | tf_op jit(solution)/shard_map/ppermute | solution.py:737
  35.5 3.6 %collective-permute-start.10 = (bf16[256,1280]{1,0:T(8,128)(2,1)S(1)}, bf16[256,1280]{1,0:T(8,128)(2,1)S(1)}, u32[]{:S(2)}, u32[]{:S(2)}) collective-permute-start(bf16[256,1280]{1,0:T(8,128)(2,1)S(1)} %get-tuple-element.114.refs_2_.refs_6_), channel_id=1, source_target_pairs={{0,8},{1,9},{2,10},{3,11},{4,12},{5,13},{6,14},{7,15},{8,0},{9,1},... | collective-permute-start | bytes 1966088 | tf_op jit(solution)/shard_map/ppermute | solution.py:121
  35.6 14.3 %collective-permute-start.14 = (bf16[128,2048]{1,0:T(8,128)(2,1)S(1)}, bf16[128,2048]{1,0:T(8,128)(2,1)S(1)}, u32[]{:S(2)}, u32[]{:S(2)}) collective-permute-start(bf16[128,2048]{1,0:T(8,128)(2,1)S(1)} %get-tuple-element.129.refs_0_), channel_id=1, source_target_pairs={{0,1},{1,0},{2,3},{3,2},{4,5},{5,4},{6,7},{7,6},{8,9},{9,8},{10,11... | collective-permute-start | bytes 1572872 | tf_op jit(solution)/shard_map/ppermute | solution.py:121
  35.7 14.8 %collective-permute-start.15 = (bf16[128,2048]{1,0:T(8,128)(2,1)S(1)}, bf16[128,2048]{1,0:T(8,128)(2,1)S(1)}, u32[]{:S(2)}, u32[]{:S(2)}) collective-permute-start(bf16[128,2048]{1,0:T(8,128)(2,1)S(1)} %get-tuple-element.129.refs_0_), channel_id=1, source_target_pairs={{0,16},{1,17},{2,18},{3,19},{4,20},{5,21},{6,22},{7,23},{8,24},{9,... | collective-permute-start | bytes 1572872 | tf_op jit(solution)/shard_map/ppermute | solution.py:121
  36.3 26.1 %collective-permute-start.16 = (bf16[128,2048]{1,0:T(8,128)(2,1)S(1)}, bf16[128,2048]{1,0:T(8,128)(2,1)S(1)}, u32[]{:S(2)}, u32[]{:S(2)}) collective-permute-start(bf16[128,2048]{1,0:T(8,128)(2,1)S(1)} %get-tuple-element.129.refs_0_), channel_id=1, source_target_pairs={{0,17},{1,16},{2,19},{3,18},{4,21},{5,20},{6,23},{7,22},{8,25},{9,... | collective-permute-start | bytes 1572872 | tf_op jit(solution)/shard_map/ppermute | solution.py:121
  43.2 1.3 collective-permute-start.11
  44.5 4.0 %collective-permute-start.12 = (bf16[144,128]{1,0:T(8,128)(2,1)S(1)}, bf16[144,128]{1,0:T(8,128)(2,1)S(1)}, u32[]{:S(2)}, u32[]{:S(2)}) collective-permute-start(bf16[144,128]{1,0:T(8,128)(2,1)S(1)} %get-tuple-element.122.refs_0_), channel_id=1, source_target_pairs={{0,2},{1,3},{2,0},{3,1},{4,6},{5,7},{6,4},{7,5},{8,10},{9,11},{10,... | collective-permute-start | bytes 110600 | tf_op jit(solution)/shard_map/ppermute | solution.py:121
  62.6 4.8 %collective-permute-start.17 = (bf16[512,2048]{1,0:T(8,128)(2,1)S(1)}, bf16[512,2048]{1,0:T(8,128)(2,1)S(1)}, u32[]{:S(2)}, u32[]{:S(2)}) collective-permute-start(bf16[512,2048]{1,0:T(8,128)(2,1)S(1)} %shard_map.304.refs_11_.refs_9_.refs_8_), channel_id=1, source_target_pairs={{0,8},{1,9},{2,10},{3,11},{4,12},{5,13},{6,14},{7,15},{8,0},{9,1},... | collective-permute-start | bytes 6291464 | tf_op jit(solution)/shard_map/ppermute | solution.py:121
  62.6 4.0 %collective-permute-start.13 = (bf16[144,128]{1,0:T(8,128)(2,1)S(1)}, bf16[144,128]{1,0:T(8,128)(2,1)S(1)}, u32[]{:S(2)}, u32[]{:S(2)}) collective-permute-start(bf16[144,128]{1,0:T(8,128)(2,1)S(1)} %get-tuple-element.124.refs_0_), channel_id=1, source_target_pairs={{0,1},{1,0},{2,3},{3,2},{4,5},{5,4},{6,7},{7,6},{8,9},{9,8},{10,11... | collective-permute-start | bytes 110600 | tf_op jit(solution)/shard_map/ppermute | solution.py:121
  101.4 1.3 collective-permute-start.18
  104.5 11.6 %collective-permute-start.21 = (bf16[512,2048]{1,0:T(8,128)(2,1)S(1)}, bf16[512,2048]{1,0:T(8,128)(2,1)S(1)}, u32[]{:S(2)}, u32[]{:S(2)}) collective-permute-start(bf16[512,2048]{1,0:T(8,128)(2,1)S(1)} %get-tuple-element.157), channel_id=1, source_target_pairs={{0,8},{1,9},{2,10},{3,11},{4,12},{5,13},{6,14},{7,15},{8,0},{9,1},... | collective-permute-start | bytes 6291464 | tf_op jit(solution)/shard_map/ppermute | solution.py:121
  104.7 4.0 %collective-permute-start.19 = (bf16[144,128]{1,0:T(8,128)(2,1)S(1)}, bf16[144,128]{1,0:T(8,128)(2,1)S(1)}, u32[]{:S(2)}, u32[]{:S(2)}) collective-permute-start(bf16[144,128]{1,0:T(8,128)(2,1)S(1)} %get-tuple-element.142.refs_0_), channel_id=1, source_target_pairs={{0,2},{1,3},{2,0},{3,1},{4,6},{5,7},{6,4},{7,5},{8,10},{9,11},{10,... | collective-permute-start | bytes 110600 | tf_op jit(solution)/shard_map/ppermute | solution.py:121
  108.7 6.7 %collective-permute-start.20 = (bf16[144,128]{1,0:T(8,128)(2,1)S(1)}, bf16[144,128]{1,0:T(8,128)(2,1)S(1)}, u32[]{:S(2)}, u32[]{:S(2)}) collective-permute-start(bf16[144,128]{1,0:T(8,128)(2,1)S(1)} %get-tuple-element.153.refs_0_), channel_id=1, source_target_pairs={{0,1},{1,0},{2,3},{3,2},{4,5},{5,4},{6,7},{7,6},{8,9},{9,8},{10,11... | collective-permute-start | bytes 110600 | tf_op jit(solution)/shard_map/ppermute | solution.py:121
  110.3 15.4 %collective-permute-start.22 = (bf16[128,512]{1,0:T(8,128)(2,1)S(1)}, bf16[128,512]{1,0:T(8,128)(2,1)S(1)}, u32[]{:S(2)}, u32[]{:S(2)}) collective-permute-start(bf16[128,512]{1,0:T(8,128)(2,1)S(1)} %get-tuple-element.152.refs_4_), channel_id=1, source_target_pairs={{0,0},{8,1},{2,2},{10,3},{1,4},{9,5},{3,6},{11,7},{4,8},{12,9},{6,... | collective-permute-start | bytes 393224 | tf_op jit(solution)/shard_map/ppermute | solution.py:822
  116.5 13.8 %collective-permute-start.26 = (bf16[256,1024]{1,0:T(8,128)(2,1)S(1)}, bf16[256,1024]{1,0:T(8,128)(2,1)S(1)}, u32[]{:S(2)}, u32[]{:S(2)}) collective-permute-start(bf16[256,1024]{1,0:T(8,128)(2,1)S(1)} %get-tuple-element.167), channel_id=1, source_target_pairs={{0,16},{1,17},{2,18},{3,19},{4,20},{5,21},{6,22},{7,23},{8,24},{9,... | collective-permute-start | bytes 1572872 | tf_op jit(solution)/shard_map/ppermute | solution.py:121
  117.2 14.4 %collective-permute-start.27 = (bf16[256,1024]{1,0:T(8,128)(2,1)S(1)}, bf16[256,1024]{1,0:T(8,128)(2,1)S(1)}, u32[]{:S(2)}, u32[]{:S(2)}) collective-permute-start(bf16[256,1024]{1,0:T(8,128)(2,1)S(1)} %get-tuple-element.169), channel_id=1, source_target_pairs={{0,1},{1,0},{2,3},{3,2},{4,5},{5,4},{6,7},{7,6},{8,9},{9,8},{10,11... | collective-permute-start | bytes 1572872 | tf_op jit(solution)/shard_map/ppermute | solution.py:121
  127.5 12.1 %collective-permute-start.25 = (bf16[256,1280]{1,0:T(8,128)(2,1)S(1)}, bf16[256,1280]{1,0:T(8,128)(2,1)S(1)}, u32[]{:S(2)}, u32[]{:S(2)}) collective-permute-start(bf16[256,1280]{1,0:T(8,128)(2,1)S(1)} %get-tuple-element.166), channel_id=1, source_target_pairs={{0,8},{1,9},{2,10},{3,11},{4,12},{5,13},{6,14},{7,15},{8,0},{9,1},... | collective-permute-start | bytes 1966088 | tf_op jit(solution)/shard_map/ppermute | solution.py:121
  131.8 8.1 %collective-permute-start.28 = (bf16[128,1024]{1,0:T(8,128)(2,1)S(1)}, bf16[128,1024]{1,0:T(8,128)(2,1)S(1)}, u32[]{:S(2)}, u32[]{:S(2)}) collective-permute-start(bf16[128,1024]{1,0:T(8,128)(2,1)S(1)} %get-tuple-element.171), channel_id=1, source_target_pairs={{0,1},{1,0},{2,3},{3,2},{4,5},{5,4},{6,7},{7,6},{8,9},{9,8},{10,11... | collective-permute-start | bytes 786440 | tf_op jit(solution)/shard_map/ppermute | solution.py:121
  131.9 8.1 %collective-permute-start.29 = (bf16[128,1024]{1,0:T(8,128)(2,1)S(1)}, bf16[128,1024]{1,0:T(8,128)(2,1)S(1)}, u32[]{:S(2)}, u32[]{:S(2)}) collective-permute-start(bf16[128,1024]{1,0:T(8,128)(2,1)S(1)} %get-tuple-element.173), channel_id=1, source_target_pairs={{0,16},{1,17},{2,18},{3,19},{4,20},{5,21},{6,22},{7,23},{8,24},{9,... | collective-permute-start | bytes 786440 | tf_op jit(solution)/shard_map/ppermute | solution.py:121
  133.0 6.6 %collective-permute-start.24 = (bf16[16,512]{1,0:T(8,128)(2,1)S(1)}, bf16[16,512]{1,0:T(8,128)(2,1)S(1)}, u32[]{:S(2)}, u32[]{:S(2)}) collective-permute-start(bf16[16,512]{1,0:T(8,128)(2,1)S(1)} %get-tuple-element.164), channel_id=1, source_target_pairs={{8,0},{2,1},{10,2},{1,3},{9,4},{3,5},{11,6},{12,8},{6,9},{14,10},{... | collective-permute-start | bytes 49160 | tf_op jit(solution)/shard_map/ppermute | solution.py:849
  140.3 13.6 %collective-permute-start.33 = (bf16[64,2048]{1,0:T(8,128)(2,1)S(1)}, bf16[64,2048]{1,0:T(8,128)(2,1)S(1)}, u32[]{:S(2)}, u32[]{:S(2)}) collective-permute-start(bf16[64,2048]{1,0:T(8,128)(2,1)S(1)} %get-tuple-element.179), channel_id=1, source_target_pairs={{0,2},{1,3},{2,0},{3,1},{4,6},{5,7},{6,4},{7,5},{8,10},{9,11},{10,... | collective-permute-start | bytes 786440 | tf_op jit(solution)/shard_map/ppermute | solution.py:121
  140.9 13.0 %collective-permute-start.30 = (bf16[64,1280]{1,0:T(8,128)(2,1)S(1)}, bf16[64,1280]{1,0:T(8,128)(2,1)S(1)}, u32[]{:S(2)}, u32[]{:S(2)}) collective-permute-start(bf16[64,1280]{1,0:T(8,128)(2,1)S(1)} %get-tuple-element.175), channel_id=1, source_target_pairs={{0,1},{1,0},{2,3},{3,2},{4,5},{5,4},{6,7},{7,6},{8,9},{9,8},{10,11... | collective-permute-start | bytes 491528 | tf_op jit(solution)/shard_map/ppermute | solution.py:121
  141.9 12.0 %collective-permute-start.31 = (bf16[64,1280]{1,0:T(8,128)(2,1)S(1)}, bf16[64,1280]{1,0:T(8,128)(2,1)S(1)}, u32[]{:S(2)}, u32[]{:S(2)}) collective-permute-start(bf16[64,1280]{1,0:T(8,128)(2,1)S(1)} %get-tuple-element.176), channel_id=1, source_target_pairs={{0,16},{1,17},{2,18},{3,19},{4,20},{5,21},{6,22},{7,23},{8,24},{9,... | collective-permute-start | bytes 491528 | tf_op jit(solution)/shard_map/ppermute | solution.py:121
  143.0 10.9 %collective-permute-start.32 = (bf16[64,1280]{1,0:T(8,128)(2,1)S(1)}, bf16[64,1280]{1,0:T(8,128)(2,1)S(1)}, u32[]{:S(2)}, u32[]{:S(2)}) collective-permute-start(bf16[64,1280]{1,0:T(8,128)(2,1)S(1)} %get-tuple-element.177), channel_id=1, source_target_pairs={{0,17},{1,16},{2,19},{3,18},{4,21},{5,20},{6,23},{7,22},{8,25},{9,... | collective-permute-start | bytes 491528 | tf_op jit(solution)/shard_map/ppermute | solution.py:121
  144.4 9.5 %collective-permute-start.23 = (bf16[128,512]{1,0:T(8,128)(2,1)S(1)}, bf16[128,512]{1,0:T(8,128)(2,1)S(1)}, u32[]{:S(2)}, u32[]{:S(2)}) collective-permute-start(bf16[128,512]{1,0:T(8,128)(2,1)S(1)} %get-tuple-element.163), channel_id=1, source_target_pairs={{0,0},{8,1},{2,2},{10,3},{1,4},{9,5},{3,6},{11,7},{4,8},{12,9},{6,... | collective-permute-start | bytes 393224 | tf_op jit(solution)/shard_map/ppermute | solution.py:848
  154.1 12.5 %collective-permute-start.37 = (bf16[32,2048]{1,0:T(8,128)(2,1)S(1)}, bf16[32,2048]{1,0:T(8,128)(2,1)S(1)}, u32[]{:S(2)}, u32[]{:S(2)}) collective-permute-start(bf16[32,2048]{1,0:T(8,128)(2,1)S(1)} %get-tuple-element.185), channel_id=1, source_target_pairs={{0,4},{1,5},{2,6},{3,7},{4,0},{5,1},{6,2},{7,3},{8,12},{9,13},{10,... | collective-permute-start | bytes 393224 | tf_op jit(solution)/shard_map/ppermute | solution.py:121
  155.2 11.5 %collective-permute-start.34 = (bf16[16,1280]{1,0:T(8,128)(2,1)S(1)}, bf16[16,1280]{1,0:T(8,128)(2,1)S(1)}, u32[]{:S(2)}, u32[]{:S(2)}) collective-permute-start(bf16[16,1280]{1,0:T(8,128)(2,1)S(1)} %get-tuple-element.181), channel_id=1, source_target_pairs={{0,4},{1,5},{2,6},{3,7},{4,0},{5,1},{6,2},{7,3},{8,12},{9,13},{10,... | collective-permute-start | bytes 122888 | tf_op jit(solution)/shard_map/ppermute | solution.py:121
  157.1 9.5 %collective-permute-start.35 = (bf16[16,1280]{1,0:T(8,128)(2,1)S(1)}, bf16[16,1280]{1,0:T(8,128)(2,1)S(1)}, u32[]{:S(2)}, u32[]{:S(2)}) collective-permute-start(bf16[16,1280]{1,0:T(8,128)(2,1)S(1)} %get-tuple-element.182), channel_id=1, source_target_pairs={{0,2},{1,3},{2,0},{3,1},{4,6},{5,7},{6,4},{7,5},{8,10},{9,11},{10,... | collective-permute-start | bytes 122888 | tf_op jit(solution)/shard_map/ppermute | solution.py:121
  159.6 7.1 %collective-permute-start.36 = (bf16[16,1280]{1,0:T(8,128)(2,1)S(1)}, bf16[16,1280]{1,0:T(8,128)(2,1)S(1)}, u32[]{:S(2)}, u32[]{:S(2)}) collective-permute-start(bf16[16,1280]{1,0:T(8,128)(2,1)S(1)} %get-tuple-element.183), channel_id=1, source_target_pairs={{0,6},{1,7},{2,4},{3,5},{4,2},{5,3},{6,0},{7,1},{8,14},{9,15},{10,... | collective-permute-start | bytes 122888 | tf_op jit(solution)/shard_map/ppermute | solution.py:121

commit v4 on v3

--- a/solution.py
+++ b/solution.py
@@ -570,9 +570,11 @@
     gu_out[...] = gu.astype(BF16)
 
 
-def last_kernel(plan, no, tok, halo, gains, gu, gz, grad_middle, own_u, far_u, own_z, far_z, normed, small_grads, gain_two, *refs):
+def last_kernel(plan, no, tok, halo, gains, gu, gz, grad_middle, own_u, far_u, own_z, far_z, normed, small_grads, gain_two, result, *refs):
     outs = refs[:no]
-    own, before, large, spaced = refs[no:]
+    both, before, large, spaced = refs[no:]
+    tokens = tok.shape[0]
+    both[tokens:, :] = result[...]
     me = plan.me()
     large[...] = tn(normed[...], gu[...])
     pack_blocks(plan, outs, large, 16, 16, 0, 0)
@@ -585,7 +587,7 @@
     gain_one = jnp.sum(grad_n * x * r, axis=0, keepdims=True)
     q = grad_n * gains[0:1, :]
     base = r * q - x * (r * r * r) * jnp.mean(q * x, axis=-1, keepdims=True)
-    own[...] = (grad_middle[...] + base[HALO:, :]).astype(BF16)
+    both[:tokens, :] = (grad_middle[...] + base[HALO:, :]).astype(BF16)
     before[...] = base[:HALO, :].astype(BF16)
     spaced[...] = small_grads[...]
     blank = jnp.zeros((1, 16), F32)
@@ -607,12 +609,13 @@
 
 
 def finish_kernel(*refs):
-    (own, tail, result), refs = refs[:3], refs[3:]
+    (both, tail), refs = refs[:2], refs[2:]
     u_ins, ins, (own_out, result_out), refs = refs[:4], refs[4:6], refs[6:8], refs[2:]
-    rows = own.shape[0] - HALO
-    own_out[:rows, :] = own[:rows, :]
-    own_out[rows:, :] = (own[rows:, :].astype(F32) + tail[...].astype(F32)).astype(BF16)
-    result_out[...] = result[...]
+    count = own_out.shape[0]
+    rows = count - HALO
+    own_out[:rows, :] = both[:rows, :]
+    own_out[rows:, :] = (both[rows:count, :].astype(F32) + tail[...].astype(F32)).astype(BF16)
+    result_out[...] = both[count:, :]
     out_g, q_g, k_g, v_g, o_g, in_g, x_g, dt_g, a_g, cw_g, cb_g, db_g, sk_g, g1_g, g2_g, rows = refs[6:]
     total = total_of(ins)
     out_g[...] = total[:, :D]
@@ -732,12 +735,11 @@
             pack_kernel, [], [((16, E + 256), BF16), ((32, 4 * D), BF16)],
             [pltpu.VMEM((SMALL_ROWS, 32), F32)] + [pltpu.VMEM(value.shape, F32) for value in raw]
             + [pltpu.SemaphoreType.DMA((len(raw),))], far=raw, limit=60)
-        two_far = send(pack_two, 4)
-        (one,) = join(plan, [[pack_one, send(pack_one, 4)]])
+        (one,) = join(plan, [spread_out(pack_one, Z_MASKS)])
+        near_one = spread_out(one, XY_MASKS)
+        (two,) = join(plan, [[pack_two, send(pack_two, 4)]], [one, tok])
         cot = lax.ppermute(cot0, ALL, home)
-        one, two = join(plan, [[one, send(one, 2)], [pack_two, two_far]], [tok, halo])
-        two_far = send(two, 2)
-        one, two = join(plan, [spread_out(one, XY_MASKS), [two, two_far]], [cot], (0,))
+        one, two = join(plan, [near_one, [two, send(two, 2)]], [halo], (0,))
         one = [one, send(one, CORE)]
         near_two = spread_out(two, XY_MASKS)
     else:
@@ -776,7 +778,7 @@
     )
     entry, firsts = exchange(plan, state, a3, True)
     if plan.fast:
-        (held,) = join(plan, [near_two], firsts[1:2], (0,))
+        (held,) = join(plan, [near_two], [*firsts[1:2], cot], (0,))
         two = [held, send(held, CORE)]
     pay, mamba, gated, middle, all_states, z = run(
         functools.partial(mid_kernel, plan),
@@ -819,7 +821,6 @@
     (grad_c,) = extra or c_grads([])
     one_parts = []
     if plan.fast:
-        result = lax.ppermute(result, ALL, [(b, a) for a, b in home])
         rows = blocks[0] * 32
         one_parts = run(
             cut_one_kernel, [one_grads[0], send(one_grads[1], CORE)], [((rows // 2, 2 * D), BF16)] * 4, after=[leaving])
@@ -832,12 +833,11 @@
          pltpu.VMEM((count + 2 * HALO, E), F32)],
         limit=32, after=one_parts[:1], us=11,
     )
-    *two_grads, own, before = run(
+    *two_grads, both, before = run(
         functools.partial(last_kernel, plan, no),
-        [tok, halo, gains, gu, gz, grad_middle, *one, *two, normed, small_grads, gain_grad_two],
-        [((n * 16, E + 256), BF16) for n in blocks] + [((count, D), BF16), ((HALO, D), BF16)],
-        [pltpu.VMEM((D, E), F32), pltpu.VMEM((SMALL_ROWS, E), F32)], after=[result],
-    )
+        [tok, halo, gains, gu, gz, grad_middle, *one, *two, normed, small_grads, gain_grad_two, result],
+        [((n * 16, E + 256), BF16) for n in blocks] + [((2 * count, D), BF16), ((HALO, D), BF16)],
+        [pltpu.VMEM((D, E), F32), pltpu.VMEM((SMALL_ROWS, E), F32)],     )
     if plan.fast:
         a_keep, a_give, b_keep, b_give = one_parts
         one_parts = run(
@@ -845,7 +845,7 @@
             after=[two_grads[0]])
     if plan.fast:
         back = [(b, a) for a, b in home]
-        grad_tok = lax.ppermute(own, ALL, back)
+        both = lax.ppermute(both, ALL, back)
         tail = lax.ppermute(
             before, ALL, [(plan.place(s, c + 1), s * 8 + c) for s in range(4) for c in range(7)])
         a_keep, a_give, b_keep, b_give = one_parts
@@ -857,9 +857,9 @@
             [((n * 4, E + 256), BF16)] * 4 + [((n * 4, 4 * D), BF16)] * 2, after=[tail])
         *u_parts, keep, give = run(
             cut_four_kernel, [*sends(u_parts, XY_MASKS), keep, send(give, 2)],
-            [((n, E + 256), BF16)] * 4 + [((n * 2, 4 * D), BF16)] * 2, after=[grad_tok])
+            [((n, E + 256), BF16)] * 4 + [((n * 2, 4 * D), BF16)] * 2, after=[both])
         grad_tok, result, out_g, q_g, k_g, v_g, o_g, in_g, x_g, dt_g, a_g, cw_g, cb_g, db_g, sk_g, g1_g, g2_g = run(
-            finish_kernel, [grad_tok, tail, result, *sends(u_parts, Z_MASKS), keep, send(give, 4)],
+            finish_kernel, [both, tail, *sends(u_parts, Z_MASKS), keep, send(give, 4)],
             [((count, D), BF16)] * 2 + [((32, D), F32)] + [((16, D), F32)] * 4
             + [((16, 2 * E), F32), ((32, 64), F32), ((32, 32), F32), ((NS, 32), F32), ((KW, 32), F32)]
             + [((1, 32), F32)] * 3 + [((1, 16), F32)] * 2,
@@ -868,6 +868,7 @@
         vectors = [value[0] for value in (cb_g, db_g, sk_g, g1_g, g2_g)]
     else:
         tail = lax.ppermute(before, "ctx", [(c + 1, c) for c in range(chunks - 1)])
+        own, result = both[:count], both[count:]
         end = (own[count - HALO :].astype(F32) + tail.astype(F32)).astype(BF16)
         grad_tok = jnp.concatenate([own[: count - HALO], end], axis=0)
         scatter = lambda value, dim=0: lax.psum_scatter(value.astype(F32), ALL, scatter_dimension=dim, tiled=True)

time: 170 us -> 164 us (0.965)
  waiting for transfers between devices: 55.5 us -> 45 us
  starting transfers between devices: 49.5 us -> 53.9 us
    ppermute x1, waiting for transfers between devices: 7.98 us -> 0.01 us  [body(): cot = lax.ppermute(cot0, ALL, home)]
    ppermute x32 -> x33, waiting for transfers between devices: 35.6 us -> 41.7 us  [send(): return lax.ppermute(value, ALL, [(i, i ^ mask) for i in range(32)])]
    ppermute x32 -> x33, starting transfers between devices: 32.8 us -> 37.9 us  [send(): return lax.ppermute(value, ALL, [(i, i ^ mask) for i in range(32)])]
    ppermute x1, waiting for transfers between devices: 4.16 us -> 0.01 us  [body(): lax.ppermute(before, ALL, [(plan.place(s, c + 1), s * 8 + c) for s in ran...]
    ppermute x2 -> x1, waiting for transfers between devices: 5.1 us -> 1.61 us  [body(): both = lax.ppermute(both, ALL, back)]
    ppermute x2 -> x1, starting transfers between devices: 6.31 us -> 4.86 us  [body(): both = lax.ppermute(both, ALL, back)]
  transfers between devices with their start and end apart: 38 -> 38, of which waited for: 17 -> 16; matrix products, arithmetic and copies ran while one was open for 0% -> 0% of each run, Pallas kernels for 12% -> 13%
where the time goes in v4:
time: 164 us; the launch traced here: 162 us
  starting transfers between devices  53.9 us (33%)
  waiting for transfers between devices  45 us (27%)
  Pallas kernels  35.7 us (22%)
  blocking collectives  24.3 us (15%)
  local copies, waits for them, and re-layouts  2.41 us (1%)
    ppermute x33, waiting for transfers between devices, send(): return lax.ppermute(value, ALL, [(i, i ^ mask) for i in range(32)])  41.7 us
    ppermute x33, starting transfers between devices, send(): return lax.ppermute(value, ALL, [(i, i ^ mask) for i in range(32)])  37.9 us
    pallas_call x24, Pallas kernels, run(): pl.pallas_call(inner, out_shape=[jax.ShapeDtypeStruct(shape, dtype) for s...  35.7 us
    all_to_all x2, blocking collectives, swap(): lax.all_to_all(value, ALL, 0, 0, tiled=True, axis_index_groups=groups)  24.3 us
    ppermute x1, starting transfers between devices, body(): both = lax.ppermute(both, ALL, back)  4.86 us
    ppermute x1, starting transfers between devices, body(): lax.ppermute(tok0[count - HALO:], ALL, [(s * 8 + c, plan.place(s, c + 1))...  3.95 us
  transfers between devices with their start and end apart: 38, of which 16 were waited for; matrix products, arithmetic and copies ran while one was open for 0% of the time, Pallas kernels for 13%

profile of v4, /device:TPU:6, one launch (start us, length us, event | category | flops | bytes accessed | tf_op | source)
XLA Modules:
  0.0 162.3 jit_solution(7090328605333329663)
XLA Ops:
  0.7 2.1 %collective-permute-start = (bf16[128,512]{1,0:T(8,128)(2,1)}, bf16[128,512]{1,0:T(8,128)(2,1)S(1)}, u32[]{:S(2)}, u32[]{:S(2)}) collective-permute-start(bf16[128,512]{1,0:T(8,128)(2,1)} %bitcast.30), channel_id=1, source_target_pairs={{0,0},{1,8},{2,2},{3,10},{4,1},{5,9},{6,3},{7,11},{8,4},{9,12},{10... | collective-permute-start | bytes 393224 | tf_op jit(solution)/shard_map/ppermute | solution.py:728
  2.7 2.0 %shard_map.296 = (bf16[16,1280]{1,0:T(8,128)(2,1)}, bf16[32,2048]{1,0:T(8,128)(2,1)}) custom-call(f32[16,2048]{1,0:T(8,128)} %refs_0_.1, f32[32,64]{1,0:T(8,128)} %refs_1_.1, f32[32,32]{1,0:T(8,128)} %refs_2_.1, f32[16,32]{1,0:T(8,128)} %bitcast.28, f32[4,32]{1,0:T(4,128)} %bitcast.29, f32[1,32]{1,0:T(1,128)} %bitcast.31, f32[1,32]{1,0:T(1,128)} %bitcast.32, ...), custom_call_target="tpu_custom_call" | custom-call | flops 2000 | bytes 6000 | tf_op jit(solution)/shard_map/pallas_call | solution.py:59
  4.7 2.7 %collective-permute-start.8 = (bf16[32,2048]{1,0:T(8,128)(2,1)}, bf16[32,2048]{1,0:T(8,128)(2,1)S(1)}, u32[]{:S(2)}, u32[]{:S(2)}) collective-permute-start(bf16[32,2048]{1,0:T(8,128)(2,1)} %get-tuple-element.109.refs_0_), channel_id=1, source_target_pairs={{0,4},{1,5},{2,6},{3,7},{4,0},{5,1},{6,2},{7,3},{8,12},{9,13},{10,... | collective-permute-start | bytes 393224 | tf_op jit(solution)/shard_map/ppermute | solution.py:121
  7.7 1.6 collective-permute-start.3
  9.3 2.5 %collective-permute-start.4 = (bf16[16,1280]{1,0:T(8,128)(2,1)}, bf16[16,1280]{1,0:T(8,128)(2,1)S(1)}, u32[]{:S(2)}, u32[]{:S(2)}) collective-permute-start(bf16[16,1280]{1,0:T(8,128)(2,1)} %get-tuple-element.108.refs_0_), channel_id=1, source_target_pairs={{0,6},{1,7},{2,4},{3,5},{4,2},{5,3},{6,0},{7,1},{8,14},{9,15},{10,... | collective-permute-start | bytes 122888 | tf_op jit(solution)/shard_map/ppermute | solution.py:121
  11.7 5.6 %collective-permute-done.2.refs_1_ = bf16[16,1280]{1,0:T(8,128)(2,1)S(1)} collective-permute-done((bf16[16,1280]{1,0:T(8,128)(2,1)}, bf16[16,1280]{1,0:T(8,128)(2,1)S(1)}, u32[]{:S(2)}, u32[]{:S(2)}) %collective-permute-start.2) | collective-permute-done | bytes 40992 | tf_op jit(solution)/shard_map/ppermute | solution.py:121
  19.1 1.5 collective-permute-start.9
  20.6 2.4 %collective-permute-start.5 = (bf16[64,1280]{1,0:T(8,128)(2,1)S(1)}, bf16[64,1280]{1,0:T(8,128)(2,1)S(1)}, u32[]{:S(2)}, u32[]{:S(2)}) collective-permute-start(bf16[64,1280]{1,0:T(8,128)(2,1)S(1)} %shard_map.297.refs_2_.refs_0_), channel_id=1, source_target_pairs={{0,1},{1,0},{2,3},{3,2},{4,5},{5,4},{6,7},{7,6},{8,9},{9,8},{10,11... | collective-permute-start | bytes 491528 | tf_op jit(solution)/shard_map/ppermute | solution.py:121
  23.6 0.9 collective-permute-start.7
  25.2 3.9 %collective-permute-start.1 = (bf16[16,512]{1,0:T(8,128)(2,1)S(1)}, bf16[16,512]{1,0:T(8,128)(2,1)S(1)}, u32[]{:S(2)}, u32[]{:S(2)}) collective-permute-start(bf16[16,512]{1,0:T(8,128)(2,1)S(1)} %slice_bitcast_fusion), channel_id=1, source_target_pairs={{0,8},{1,2},{2,10},{3,1},{4,9},{5,3},{6,11},{8,12},{9,6},{10,14},{... | collective-permute-start | bytes 49160 | tf_op jit(solution)/shard_map/ppermute | solution.py:729
  29.2 1.7 %collective-permute-done.1.refs_6_.refs_1_ = bf16[16,512]{1,0:T(8,128)(2,1)S(1)} collective-permute-done((bf16[16,512]{1,0:T(8,128)(2,1)S(1)}, bf16[16,512]{1,0:T(8,128)(2,1)S(1)}, u32[]{:S(2)}, u32[]{:S(2)}) %collective-permute-start.1) | collective-permute-done | bytes 16416 | tf_op jit(solution)/shard_map/ppermute | solution.py:729
  30.9 1.3 collective-permute-done.7.refs_3_
  32.3 1.6 %collective-permute-start.15 = (bf16[128,2048]{1,0:T(8,128)(2,1)S(1)}, bf16[128,2048]{1,0:T(8,128)(2,1)S(1)}, u32[]{:S(2)}, u32[]{:S(2)}) collective-permute-start(bf16[128,2048]{1,0:T(8,128)(2,1)S(1)} %get-tuple-element.125.refs_0_), channel_id=1, source_target_pairs={{0,1},{1,0},{2,3},{3,2},{4,5},{5,4},{6,7},{7,6},{8,9},{9,8},{10,11... | collective-permute-start | bytes 1572872 | tf_op jit(solution)/shard_map/ppermute | solution.py:121
  34.5 1.4 collective-permute-start.17
  35.8 2.7 %collective-permute-start.11 = (bf16[128,512]{1,0:T(8,128)(2,1)S(1)}, bf16[128,512]{1,0:T(8,128)(2,1)S(1)}, u32[]{:S(2)}, u32[]{:S(2)}) collective-permute-start(bf16[128,512]{1,0:T(8,128)(2,1)S(1)} %bitcast.36), channel_id=1, source_target_pairs={{0,0},{1,8},{2,2},{3,10},{4,1},{5,9},{6,3},{7,11},{8,4},{9,12},{10... | collective-permute-start | bytes 393224 | tf_op jit(solution)/shard_map/ppermute | solution.py:741
  38.5 4.0 %shard_map.300 = (bf16[144,512]{1,0:T(8,128)(2,1)S(1)}, bf16[144,512]{1,0:T(8,128)(2,1)S(1)}, f32[144,1024]{1,0:T(8,128)S(1)}, f32[128,1024]{1,0:T(8,128)S(1)}, ...) custom-call(bf16[128,512]{1,0:T(8,128)(2,1)S(1)} %collective-permute, ...), custom_call_target="tpu_custom_call" | custom-call | flops 6000 | bytes 18000 | tf_op jit(solution)/shard_map/pallas_call | solution.py:59
  42.6 1.2 collective-permute-start.12
  44.7 2.9 %collective-permute-start.13 = (bf16[144,128]{1,0:T(8,128)(2,1)S(1)}, bf16[144,128]{1,0:T(8,128)(2,1)S(1)}, u32[]{:S(2)}, u32[]{:S(2)}) collective-permute-start(bf16[144,128]{1,0:T(8,128)(2,1)S(1)} %get-tuple-element.118.refs_0_), channel_id=1, source_target_pairs={{0,2},{1,3},{2,0},{3,1},{4,6},{5,7},{6,4},{7,5},{8,10},{9,11},{10,... | collective-permute-start | bytes 110600 | tf_op jit(solution)/shard_map/ppermute | solution.py:121
  47.6 2.0 %collective-permute-done.13.refs_1_ = bf16[144,128]{1,0:T(8,128)(2,1)S(1)} collective-permute-done((bf16[144,128]{1,0:T(8,128)(2,1)S(1)}, bf16[144,128]{1,0:T(8,128)(2,1)S(1)}, u32[]{:S(2)}, u32[]{:S(2)}) %collective-permute-start.13) | collective-permute-done | bytes 36896 | tf_op jit(solution)/shard_map/ppermute | solution.py:121
  49.7 9.6 %collective-permute-done.15.refs_1_ = bf16[128,2048]{1,0:T(8,128)(2,1)S(1)} collective-permute-done((bf16[128,2048]{1,0:T(8,128)(2,1)S(1)}, bf16[128,2048]{1,0:T(8,128)(2,1)S(1)}, u32[]{:S(2)}, u32[]{:S(2)}) %collective-permute-start.15) | collective-permute-done | bytes 524320 | tf_op jit(solution)/shard_map/ppermute | solution.py:121
  59.6 1.5 collective-permute-start.14
  61.1 2.5 %collective-permute-done.14.refs_1_ = bf16[144,128]{1,0:T(8,128)(2,1)S(1)} collective-permute-done((bf16[144,128]{1,0:T(8,128)(2,1)S(1)}, bf16[144,128]{1,0:T(8,128)(2,1)S(1)}, u32[]{:S(2)}, u32[]{:S(2)}) %collective-permute-start.14) | collective-permute-done | bytes 36896 | tf_op jit(solution)/shard_map/ppermute | solution.py:121
  64.2 3.9 %shard_map.305 = (bf16[1024,256]{1,0:T(8,128)(2,1)S(1)}, f32[128,1024]{1,0:T(8,128)S(1)}, bf16[128,1024]{1,0:T(8,128)(2,1)S(1)}, f32[128,512]{1,0:T(8,128)S(1)},...) custom-call(bf16[128,512]{1,0:T(8,128)(2,1)S(1)} %collective-permute-done.refs_3_.refs_0_, ...), custom_call_target="tpu_custom_call" | custom-call | flops 6000 | bytes 18000 | tf_op jit(solution)/shard_map/pallas_call | solution.py:59
  68.1 12.1 %all_to_all.22 = bf16[8,128,256]{2,1,0:T(8,128)(2,1)S(1)} all-to-all(bf16[8,128,256]{2,1,0:T(8,128)(2,1)S(1)} %bitcast.27), channel_id=1, replica_groups={{0,8,2,10,1,9,3,11},{4,12,6,14,5,13,7,15},{16,24,18,26,17,25,19,27},{20..., dimensions={0} | all-to-all | bytes 1048576 | tf_op jit(solution)/shard_map/all_to_all | solution.py:116
  80.2 3.6 %shard_map.306 = bf16[1024,256]{1,0:T(8,128)(2,1)S(1)} custom-call(bf16[1024,256]{1,0:T(8,128)(2,1)S(1)} %bitcast.25), custom_call_target="tpu_custom_call" | custom-call | flops 4000 | bytes 12000 | tf_op jit(solution)/shard_map/pallas_call | solution.py:59
  83.8 12.1 %all_to_all.23 = bf16[8,128,256]{2,1,0:T(8,128)(2,1)S(1)} all-to-all(bf16[8,128,256]{2,1,0:T(8,128)(2,1)S(1)} %bitcast.26), channel_id=1, replica_groups={{0,8,2,10,1,9,3,11},{4,12,6,14,5,13,7,15},{16,24,18,26,17,25,19,27},{20..., dimensions={0} | all-to-all | bytes 1048576 | tf_op jit(solution)/shard_map/all_to_all | solution.py:116
  96.0 3.1 %shard_map.307 = (bf16[128,512]{1,0:T(8,128)(2,1)S(1)}, bf16[128,512]{1,0:T(8,128)(2,1)S(1)}, bf16[128,512]{1,0:T(8,128)(2,1)S(1)}, bf16[128,512]{1,0:T(8,128)(2...) custom-call(bf16[1024,256]{1,0:T(8,128)(2,1)S(1)} %bitcast.24, ...), custom_call_target="tpu_custom_call" | custom-call | flops 2000 | bytes 6000 | tf_op jit(solution)/shard_map/pallas_call | solution.py:59
  99.2 1.2 collective-permute-done.19.refs_1_
  100.5 1.7 %shard_map.309 = (bf16[128,512]{1,0:T(8,128)(2,1)S(1)}, bf16[512,2048]{1,0:T(8,128)(2,1)S(1)}, bf16[512,2048]{1,0:T(8,128)(2,1)S(1)}) custom-call(bf16[128,512]{1,0:T(8,128)(2,1)S(1)} %get-tuple-element.140.refs_0_, bf16[128,512]{1,0:T(8,128)(2,1)S(1)} %get-tuple-element.141.refs_1_, bf16[128,512]{1,0:T(8,128)(2,1)S(1)} %get-tuple-element.142.refs_2_, ...), custom_call_target="tpu_custom_call" | custom-call | flops 2000 | bytes 6000 | tf_op jit(solution)/shard_map/pallas_call | solution.py:59
  102.9 3.4 %collective-permute-done.20.refs_1_ = bf16[144,128]{1,0:T(8,128)(2,1)S(1)} collective-permute-done((bf16[144,128]{1,0:T(8,128)(2,1)S(1)}, bf16[144,128]{1,0:T(8,128)(2,1)S(1)}, u32[]{:S(2)}, u32[]{:S(2)}) %collective-permute-start.20) | collective-permute-done | bytes 36896 | tf_op jit(solution)/shard_map/ppermute | solution.py:121
  106.4 1.5 collective-permute-start.21
  107.9 3.2 %shard_map.311.refs_4_.refs_14_ = f32[128,128]{1,0:T(8,128)S(1)} custom-call(f32[1024,128]{1,0:T(8,128)S(1)} %get-tuple-element.130.refs_0_.refs_2_, f32[16512,128]{1,0:T(8,128)S(1)} %get-tuple-element.132.refs_1_.refs_6_, f32[144,128]{1,0:T(8,128)S(1)} %get-tuple-element.150.refs_2_), custom_call_target="tpu_custom_call" | custom-call | flops 2000 | bytes 6000 | tf_op jit(solution)/shard_map/pallas_call | solution.py:59
  113.6 8.4 %shard_map.314 = (f32[128,1024]{1,0:T(8,128)S(1)}, bf16[144,1024]{1,0:T(8,128)(2,1)S(1)}) custom-call(f32[1024,128]{1,0:T(8,128)S(1)} %get-tuple-element.112.refs_1_.refs_6_.refs_0_, f32[1024,128]{1,0:T(8,128)S(1)} %get-tuple-element.113.refs_2_.refs_1_, f32[1024,128]{1,0:T(8,128)S(1)} %get-tuple-element.130.refs_0_.refs_2_, ...), custom_call_target="tpu_custom_call" | custom-call | flops 11000 | bytes 33000 | tf_op jit(solution)/shard_map/pallas_call | solution.py:59
  122.1 1.8 %shard_map.315 = (bf16[256,1280]{1,0:T(8,128)(2,1)S(1)}, bf16[256,1280]{1,0:T(8,128)(2,1)S(1)}, bf16[256,512]{1,0:T(8,128)(2,1)S(1)}, bf16[16,512]{1,0:T(8,128)(2,1)S(1)}) custom-call(bf16[128,512]{1,0:T(8,128)(2,1)S(1)} %collective-permute-done.refs_3_.refs_0_, bf16[16,512]{1,0:T(8,128)(2,1)S(1)} %collective-permute-done.1.refs_6_.refs_1_, ...), custom_call_target="tpu_custom_call" | custom-call | flops 2000 | bytes 6000 | tf_op jit(solution)/shard_map/pallas_call | solution.py:59
  124.0 1.1 collective-permute-done.26.refs_1_
  126.2 1.5 collective-permute-start.29
  127.7 2.5 %collective-permute-start.24 = (bf16[16,512]{1,0:T(8,128)(2,1)S(1)}, bf16[16,512]{1,0:T(8,128)(2,1)S(1)}, u32[]{:S(2)}, u32[]{:S(2)}) collective-permute-start(bf16[16,512]{1,0:T(8,128)(2,1)S(1)} %get-tuple-element.160), channel_id=1, source_target_pairs={{8,0},{2,1},{10,2},{1,3},{9,4},{3,5},{11,6},{12,8},{6,9},{14,10},{... | collective-permute-start | bytes 49160 | tf_op jit(solution)/shard_map/ppermute | solution.py:849
  130.2 4.9 %collective-permute-start.23 = (bf16[256,512]{1,0:T(8,128)(2,1)S(1)}, bf16[256,512]{1,0:T(8,128)(2,1)S(1)}, u32[]{:S(2)}, u32[]{:S(2)}) collective-permute-start(bf16[256,512]{1,0:T(8,128)(2,1)S(1)} %get-tuple-element.159), channel_id=1, source_target_pairs={{0,0},{8,1},{2,2},{10,3},{1,4},{9,5},{3,6},{11,7},{4,8},{12,9},{6,... | collective-permute-start | bytes 786440 | tf_op jit(solution)/shard_map/ppermute | solution.py:848
  135.4 1.3 collective-permute-start.33
  137.2 2.9 %collective-permute-start.32 = (bf16[64,1280]{1,0:T(8,128)(2,1)S(1)}, bf16[64,1280]{1,0:T(8,128)(2,1)S(1)}, u32[]{:S(2)}, u32[]{:S(2)}) collective-permute-start(bf16[64,1280]{1,0:T(8,128)(2,1)S(1)} %get-tuple-element.173), channel_id=1, source_target_pairs={{0,17},{1,16},{2,19},{3,18},{4,21},{5,20},{6,23},{7,22},{8,25},{9,... | collective-permute-start | bytes 491528 | tf_op jit(solution)/shard_map/ppermute | solution.py:121
  140.1 1.6 collective-permute-done.23.refs_6_.refs_0_
  141.7 1.7 %collective-permute-done.30.refs_1_ = bf16[64,1280]{1,0:T(8,128)(2,1)S(1)} collective-permute-done((bf16[64,1280]{1,0:T(8,128)(2,1)S(1)}, bf16[64,1280]{1,0:T(8,128)(2,1)S(1)}, u32[]{:S(2)}, u32[]{:S(2)}) %collective-permute-start.30) | collective-permute-done | bytes 163872 | tf_op jit(solution)/shard_map/ppermute | solution.py:121
  143.7 4.9 %collective-permute-done.32.refs_3_ = bf16[64,1280]{1,0:T(8,128)(2,1)S(1)} collective-permute-done((bf16[64,1280]{1,0:T(8,128)(2,1)S(1)}, bf16[64,1280]{1,0:T(8,128)(2,1)S(1)}, u32[]{:S(2)}, u32[]{:S(2)}) %collective-permute-start.32) | collective-permute-done | bytes 163872 | tf_op jit(solution)/shard_map/ppermute | solution.py:121
  148.7 1.1 collective-permute-start.37
  149.8 1.9 %collective-permute-start.34 = (bf16[16,1280]{1,0:T(8,128)(2,1)S(1)}, bf16[16,1280]{1,0:T(8,128)(2,1)S(1)}, u32[]{:S(2)}, u32[]{:S(2)}) collective-permute-start(bf16[16,1280]{1,0:T(8,128)(2,1)S(1)} %get-tuple-element.177), channel_id=1, source_target_pairs={{0,4},{1,5},{2,6},{3,7},{4,0},{5,1},{6,2},{7,3},{8,12},{9,13},{10,... | collective-permute-start | bytes 122888 | tf_op jit(solution)/shard_map/ppermute | solution.py:121
  151.7 2.2 %collective-permute-start.35 = (bf16[16,1280]{1,0:T(8,128)(2,1)S(1)}, bf16[16,1280]{1,0:T(8,128)(2,1)S(1)}, u32[]{:S(2)}, u32[]{:S(2)}) collective-permute-start(bf16[16,1280]{1,0:T(8,128)(2,1)S(1)} %get-tuple-element.178), channel_id=1, source_target_pairs={{0,2},{1,3},{2,0},{3,1},{4,6},{5,7},{6,4},{7,5},{8,10},{9,11},{10,... | collective-permute-start | bytes 122888 | tf_op jit(solution)/shard_map/ppermute | solution.py:121
  154.2 7.0 %collective-permute-done.34.refs_3_ = bf16[16,1280]{1,0:T(8,128)(2,1)S(1)} collective-permute-done((bf16[16,1280]{1,0:T(8,128)(2,1)S(1)}, bf16[16,1280]{1,0:T(8,128)(2,1)S(1)}, u32[]{:S(2)}, u32[]{:S(2)}) %collective-permute-start.34) | collective-permute-done | bytes 40992 | tf_op jit(solution)/shard_map/ppermute | solution.py:121
  161.3 0.9 shard_map.319
  (62 shorter events, 12.1 us)
Async XLA Ops:
  0.7 35.2 %copy-start.2 = (bf16[1,128,512]{2,1,0:T(8,128)(2,1)S(1)}, bf16[1,128,512]{2,1,0:T(8,128)(2,1)}, u32[]{:S(2)}) copy-start(bf16[1,128,512]{2,1,0:T(8,128)(2,1)} %param.33) | copy-start | bytes 393220
  0.7 17.5 %collective-permute-start = (bf16[128,512]{1,0:T(8,128)(2,1)}, bf16[128,512]{1,0:T(8,128)(2,1)S(1)}, u32[]{:S(2)}, u32[]{:S(2)}) collective-permute-start(bf16[128,512]{1,0:T(8,128)(2,1)} %bitcast.30), channel_id=1, source_target_pairs={{0,0},{1,8},{2,2},{3,10},{4,1},{5,9},{6,3},{7,11},{8,4},{9,12},{10... | collective-permute-start | bytes 393224 | tf_op jit(solution)/shard_map/ppermute | solution.py:728
  4.7 13.5 %collective-permute-start.8 = (bf16[32,2048]{1,0:T(8,128)(2,1)}, bf16[32,2048]{1,0:T(8,128)(2,1)S(1)}, u32[]{:S(2)}, u32[]{:S(2)}) collective-permute-start(bf16[32,2048]{1,0:T(8,128)(2,1)} %get-tuple-element.109.refs_0_), channel_id=1, source_target_pairs={{0,4},{1,5},{2,6},{3,7},{4,0},{5,1},{6,2},{7,3},{8,12},{9,13},{10,... | collective-permute-start | bytes 393224 | tf_op jit(solution)/shard_map/ppermute | solution.py:121
  7.3 10.0 %collective-permute-start.2 = (bf16[16,1280]{1,0:T(8,128)(2,1)}, bf16[16,1280]{1,0:T(8,128)(2,1)S(1)}, u32[]{:S(2)}, u32[]{:S(2)}) collective-permute-start(bf16[16,1280]{1,0:T(8,128)(2,1)} %get-tuple-element.108.refs_0_), channel_id=1, source_target_pairs={{0,4},{1,5},{2,6},{3,7},{4,0},{5,1},{6,2},{7,3},{8,12},{9,13},{10,... | collective-permute-start | bytes 122888 | tf_op jit(solution)/shard_map/ppermute | solution.py:121
  7.7 9.7 %collective-permute-start.3 = (bf16[16,1280]{1,0:T(8,128)(2,1)}, bf16[16,1280]{1,0:T(8,128)(2,1)S(1)}, u32[]{:S(2)}, u32[]{:S(2)}) collective-permute-start(bf16[16,1280]{1,0:T(8,128)(2,1)} %get-tuple-element.108.refs_0_), channel_id=1, source_target_pairs={{0,2},{1,3},{2,0},{3,1},{4,6},{5,7},{6,4},{7,5},{8,10},{9,11},{10,... | collective-permute-start | bytes 122888 | tf_op jit(solution)/shard_map/ppermute | solution.py:121
  9.3 8.1 %collective-permute-start.4 = (bf16[16,1280]{1,0:T(8,128)(2,1)}, bf16[16,1280]{1,0:T(8,128)(2,1)S(1)}, u32[]{:S(2)}, u32[]{:S(2)}) collective-permute-start(bf16[16,1280]{1,0:T(8,128)(2,1)} %get-tuple-element.108.refs_0_), channel_id=1, source_target_pairs={{0,6},{1,7},{2,4},{3,5},{4,2},{5,3},{6,0},{7,1},{8,14},{9,15},{10,... | collective-permute-start | bytes 122888 | tf_op jit(solution)/shard_map/ppermute | solution.py:121
  17.4 0.8 copy-start.1
  18.2 0.9 copy-start
  19.1 13.0 %collective-permute-start.9 = (bf16[64,2048]{1,0:T(8,128)(2,1)S(1)}, bf16[64,2048]{1,0:T(8,128)(2,1)S(1)}, u32[]{:S(2)}, u32[]{:S(2)}) collective-permute-start(bf16[64,2048]{1,0:T(8,128)(2,1)S(1)} %shard_map.298.refs_4_), channel_id=1, source_target_pairs={{0,2},{1,3},{2,0},{3,1},{4,6},{5,7},{6,4},{7,5},{8,10},{9,11},{10,... | collective-permute-start | bytes 786440 | tf_op jit(solution)/shard_map/ppermute | solution.py:121
  20.6 10.2 %collective-permute-start.5 = (bf16[64,1280]{1,0:T(8,128)(2,1)S(1)}, bf16[64,1280]{1,0:T(8,128)(2,1)S(1)}, u32[]{:S(2)}, u32[]{:S(2)}) collective-permute-start(bf16[64,1280]{1,0:T(8,128)(2,1)S(1)} %shard_map.297.refs_2_.refs_0_), channel_id=1, source_target_pairs={{0,1},{1,0},{2,3},{3,2},{4,5},{5,4},{6,7},{7,6},{8,9},{9,8},{10,11... | collective-permute-start | bytes 491528 | tf_op jit(solution)/shard_map/ppermute | solution.py:121
  23.0 7.8 %collective-permute-start.6 = (bf16[64,1280]{1,0:T(8,128)(2,1)S(1)}, bf16[64,1280]{1,0:T(8,128)(2,1)S(1)}, u32[]{:S(2)}, u32[]{:S(2)}) collective-permute-start(bf16[64,1280]{1,0:T(8,128)(2,1)S(1)} %shard_map.297.refs_2_.refs_0_), channel_id=1, source_target_pairs={{0,16},{1,17},{2,18},{3,19},{4,20},{5,21},{6,22},{7,23},{8,24},{9,... | collective-permute-start | bytes 491528 | tf_op jit(solution)/shard_map/ppermute | solution.py:121
  23.6 8.5 %collective-permute-start.7 = (bf16[64,1280]{1,0:T(8,128)(2,1)S(1)}, bf16[64,1280]{1,0:T(8,128)(2,1)S(1)}, u32[]{:S(2)}, u32[]{:S(2)}) collective-permute-start(bf16[64,1280]{1,0:T(8,128)(2,1)S(1)} %shard_map.297.refs_2_.refs_0_), channel_id=1, source_target_pairs={{0,17},{1,16},{2,19},{3,18},{4,21},{5,20},{6,23},{7,22},{8,25},{9,... | collective-permute-start | bytes 491528 | tf_op jit(solution)/shard_map/ppermute | solution.py:121
  25.2 5.6 %collective-permute-start.1 = (bf16[16,512]{1,0:T(8,128)(2,1)S(1)}, bf16[16,512]{1,0:T(8,128)(2,1)S(1)}, u32[]{:S(2)}, u32[]{:S(2)}) collective-permute-start(bf16[16,512]{1,0:T(8,128)(2,1)S(1)} %slice_bitcast_fusion), channel_id=1, source_target_pairs={{0,8},{1,2},{2,10},{3,1},{4,9},{5,3},{6,11},{8,12},{9,6},{10,14},{... | collective-permute-start | bytes 49160 | tf_op jit(solution)/shard_map/ppermute | solution.py:729
  32.2 6.3 %collective-permute-start.10 = (bf16[256,1280]{1,0:T(8,128)(2,1)S(1)}, bf16[256,1280]{1,0:T(8,128)(2,1)S(1)}, u32[]{:S(2)}, u32[]{:S(2)}) collective-permute-start(bf16[256,1280]{1,0:T(8,128)(2,1)S(1)} %get-tuple-element.110.refs_2_.refs_6_), channel_id=1, source_target_pairs={{0,8},{1,9},{2,10},{3,11},{4,12},{5,13},{6,14},{7,15},{8,0},{9,1},... | collective-permute-start | bytes 1966088 | tf_op jit(solution)/shard_map/ppermute | solution.py:121
  32.3 27.0 %collective-permute-start.15 = (bf16[128,2048]{1,0:T(8,128)(2,1)S(1)}, bf16[128,2048]{1,0:T(8,128)(2,1)S(1)}, u32[]{:S(2)}, u32[]{:S(2)}) collective-permute-start(bf16[128,2048]{1,0:T(8,128)(2,1)S(1)} %get-tuple-element.125.refs_0_), channel_id=1, source_target_pairs={{0,1},{1,0},{2,3},{3,2},{4,5},{5,4},{6,7},{7,6},{8,9},{9,8},{10,11... | collective-permute-start | bytes 1572872 | tf_op jit(solution)/shard_map/ppermute | solution.py:121
  33.9 25.3 %collective-permute-start.16 = (bf16[128,2048]{1,0:T(8,128)(2,1)S(1)}, bf16[128,2048]{1,0:T(8,128)(2,1)S(1)}, u32[]{:S(2)}, u32[]{:S(2)}) collective-permute-start(bf16[128,2048]{1,0:T(8,128)(2,1)S(1)} %get-tuple-element.125.refs_0_), channel_id=1, source_target_pairs={{0,16},{1,17},{2,18},{3,19},{4,20},{5,21},{6,22},{7,23},{8,24},{9,... | collective-permute-start | bytes 1572872 | tf_op jit(solution)/shard_map/ppermute | solution.py:121
  34.5 24.8 %collective-permute-start.17 = (bf16[128,2048]{1,0:T(8,128)(2,1)S(1)}, bf16[128,2048]{1,0:T(8,128)(2,1)S(1)}, u32[]{:S(2)}, u32[]{:S(2)}) collective-permute-start(bf16[128,2048]{1,0:T(8,128)(2,1)S(1)} %get-tuple-element.125.refs_0_), channel_id=1, source_target_pairs={{0,17},{1,16},{2,19},{3,18},{4,21},{5,20},{6,23},{7,22},{8,25},{9,... | collective-permute-start | bytes 1572872 | tf_op jit(solution)/shard_map/ppermute | solution.py:121
  35.8 13.8 %collective-permute-start.11 = (bf16[128,512]{1,0:T(8,128)(2,1)S(1)}, bf16[128,512]{1,0:T(8,128)(2,1)S(1)}, u32[]{:S(2)}, u32[]{:S(2)}) collective-permute-start(bf16[128,512]{1,0:T(8,128)(2,1)S(1)} %bitcast.36), channel_id=1, source_target_pairs={{0,0},{1,8},{2,2},{3,10},{4,1},{5,9},{6,3},{7,11},{8,4},{9,12},{10... | collective-permute-start | bytes 393224 | tf_op jit(solution)/shard_map/ppermute | solution.py:741
  42.6 2.1 %collective-permute-start.12 = (bf16[144,128]{1,0:T(8,128)(2,1)S(1)}, bf16[144,128]{1,0:T(8,128)(2,1)S(1)}, u32[]{:S(2)}, u32[]{:S(2)}) collective-permute-start(bf16[144,128]{1,0:T(8,128)(2,1)S(1)} %get-tuple-element.117.refs_0_.refs_11_), channel_id=1, source_target_pairs={{0,8},{1,9},{2,10},{3,11},{4,12},{5,13},{6,14},{7,15},{8,0},{9,1},... | collective-permute-start | bytes 110600 | tf_op jit(solution)/shard_map/ppermute | solution.py:121
  44.7 4.9 %collective-permute-start.13 = (bf16[144,128]{1,0:T(8,128)(2,1)S(1)}, bf16[144,128]{1,0:T(8,128)(2,1)S(1)}, u32[]{:S(2)}, u32[]{:S(2)}) collective-permute-start(bf16[144,128]{1,0:T(8,128)(2,1)S(1)} %get-tuple-element.118.refs_0_), channel_id=1, source_target_pairs={{0,2},{1,3},{2,0},{3,1},{4,6},{5,7},{6,4},{7,5},{8,10},{9,11},{10,... | collective-permute-start | bytes 110600 | tf_op jit(solution)/shard_map/ppermute | solution.py:121
  59.5 4.8 %collective-permute-start.18 = (bf16[512,2048]{1,0:T(8,128)(2,1)S(1)}, bf16[512,2048]{1,0:T(8,128)(2,1)S(1)}, u32[]{:S(2)}, u32[]{:S(2)}) collective-permute-start(bf16[512,2048]{1,0:T(8,128)(2,1)S(1)} %shard_map.304.refs_11_.refs_9_.refs_8_), channel_id=1, source_target_pairs={{0,8},{1,9},{2,10},{3,11},{4,12},{5,13},{6,14},{7,15},{8,0},{9,1},... | collective-permute-start | bytes 6291464 | tf_op jit(solution)/shard_map/ppermute | solution.py:121
  59.6 4.0 %collective-permute-start.14 = (bf16[144,128]{1,0:T(8,128)(2,1)S(1)}, bf16[144,128]{1,0:T(8,128)(2,1)S(1)}, u32[]{:S(2)}, u32[]{:S(2)}) collective-permute-start(bf16[144,128]{1,0:T(8,128)(2,1)S(1)} %get-tuple-element.120.refs_0_), channel_id=1, source_target_pairs={{0,1},{1,0},{2,3},{3,2},{4,5},{5,4},{6,7},{7,6},{8,9},{9,8},{10,11... | collective-permute-start | bytes 110600 | tf_op jit(solution)/shard_map/ppermute | solution.py:121
  99.1 1.3 collective-permute-start.19
  102.2 9.7 %collective-permute-start.22 = (bf16[512,2048]{1,0:T(8,128)(2,1)S(1)}, bf16[512,2048]{1,0:T(8,128)(2,1)S(1)}, u32[]{:S(2)}, u32[]{:S(2)}) collective-permute-start(bf16[512,2048]{1,0:T(8,128)(2,1)S(1)} %get-tuple-element.153), channel_id=1, source_target_pairs={{0,8},{1,9},{2,10},{3,11},{4,12},{5,13},{6,14},{7,15},{8,0},{9,1},... | collective-permute-start | bytes 6291464 | tf_op jit(solution)/shard_map/ppermute | solution.py:121
  102.4 4.0 %collective-permute-start.20 = (bf16[144,128]{1,0:T(8,128)(2,1)S(1)}, bf16[144,128]{1,0:T(8,128)(2,1)S(1)}, u32[]{:S(2)}, u32[]{:S(2)}) collective-permute-start(bf16[144,128]{1,0:T(8,128)(2,1)S(1)} %get-tuple-element.138.refs_0_), channel_id=1, source_target_pairs={{0,2},{1,3},{2,0},{3,1},{4,6},{5,7},{6,4},{7,5},{8,10},{9,11},{10,... | collective-permute-start | bytes 110600 | tf_op jit(solution)/shard_map/ppermute | solution.py:121
  106.4 4.7 %collective-permute-start.21 = (bf16[144,128]{1,0:T(8,128)(2,1)S(1)}, bf16[144,128]{1,0:T(8,128)(2,1)S(1)}, u32[]{:S(2)}, u32[]{:S(2)}) collective-permute-start(bf16[144,128]{1,0:T(8,128)(2,1)S(1)} %get-tuple-element.149.refs_0_), channel_id=1, source_target_pairs={{0,1},{1,0},{2,3},{3,2},{4,5},{5,4},{6,7},{7,6},{8,9},{9,8},{10,11... | collective-permute-start | bytes 110600 | tf_op jit(solution)/shard_map/ppermute | solution.py:121
  112.3 12.8 %collective-permute-start.26 = (bf16[256,1024]{1,0:T(8,128)(2,1)S(1)}, bf16[256,1024]{1,0:T(8,128)(2,1)S(1)}, u32[]{:S(2)}, u32[]{:S(2)}) collective-permute-start(bf16[256,1024]{1,0:T(8,128)(2,1)S(1)} %get-tuple-element.163), channel_id=1, source_target_pairs={{0,16},{1,17},{2,18},{3,19},{4,20},{5,21},{6,22},{7,23},{8,24},{9,... | collective-permute-start | bytes 1572872 | tf_op jit(solution)/shard_map/ppermute | solution.py:121
  112.9 12.5 %collective-permute-start.27 = (bf16[256,1024]{1,0:T(8,128)(2,1)S(1)}, bf16[256,1024]{1,0:T(8,128)(2,1)S(1)}, u32[]{:S(2)}, u32[]{:S(2)}) collective-permute-start(bf16[256,1024]{1,0:T(8,128)(2,1)S(1)} %get-tuple-element.165), channel_id=1, source_target_pairs={{0,1},{1,0},{2,3},{3,2},{4,5},{5,4},{6,7},{7,6},{8,9},{9,8},{10,11... | collective-permute-start | bytes 1572872 | tf_op jit(solution)/shard_map/ppermute | solution.py:121
  123.9 11.1 %collective-permute-start.25 = (bf16[256,1280]{1,0:T(8,128)(2,1)S(1)}, bf16[256,1280]{1,0:T(8,128)(2,1)S(1)}, u32[]{:S(2)}, u32[]{:S(2)}) collective-permute-start(bf16[256,1280]{1,0:T(8,128)(2,1)S(1)} %get-tuple-element.162), channel_id=1, source_target_pairs={{0,8},{1,9},{2,10},{3,11},{4,12},{5,13},{6,14},{7,15},{8,0},{9,1},... | collective-permute-start | bytes 1966088 | tf_op jit(solution)/shard_map/ppermute | solution.py:121
  125.6 9.5 %collective-permute-start.28 = (bf16[128,1024]{1,0:T(8,128)(2,1)S(1)}, bf16[128,1024]{1,0:T(8,128)(2,1)S(1)}, u32[]{:S(2)}, u32[]{:S(2)}) collective-permute-start(bf16[128,1024]{1,0:T(8,128)(2,1)S(1)} %get-tuple-element.167), channel_id=1, source_target_pairs={{0,1},{1,0},{2,3},{3,2},{4,5},{5,4},{6,7},{7,6},{8,9},{9,8},{10,11... | collective-permute-start | bytes 786440 | tf_op jit(solution)/shard_map/ppermute | solution.py:121
  126.2 8.9 %collective-permute-start.29 = (bf16[128,1024]{1,0:T(8,128)(2,1)S(1)}, bf16[128,1024]{1,0:T(8,128)(2,1)S(1)}, u32[]{:S(2)}, u32[]{:S(2)}) collective-permute-start(bf16[128,1024]{1,0:T(8,128)(2,1)S(1)} %get-tuple-element.169), channel_id=1, source_target_pairs={{0,16},{1,17},{2,18},{3,19},{4,20},{5,21},{6,22},{7,23},{8,24},{9,... | collective-permute-start | bytes 786440 | tf_op jit(solution)/shard_map/ppermute | solution.py:121
  127.7 7.3 %collective-permute-start.24 = (bf16[16,512]{1,0:T(8,128)(2,1)S(1)}, bf16[16,512]{1,0:T(8,128)(2,1)S(1)}, u32[]{:S(2)}, u32[]{:S(2)}) collective-permute-start(bf16[16,512]{1,0:T(8,128)(2,1)S(1)} %get-tuple-element.160), channel_id=1, source_target_pairs={{8,0},{2,1},{10,2},{1,3},{9,4},{3,5},{11,6},{12,8},{6,9},{14,10},{... | collective-permute-start | bytes 49160 | tf_op jit(solution)/shard_map/ppermute | solution.py:849
  130.2 11.5 %collective-permute-start.23 = (bf16[256,512]{1,0:T(8,128)(2,1)S(1)}, bf16[256,512]{1,0:T(8,128)(2,1)S(1)}, u32[]{:S(2)}, u32[]{:S(2)}) collective-permute-start(bf16[256,512]{1,0:T(8,128)(2,1)S(1)} %get-tuple-element.159), channel_id=1, source_target_pairs={{0,0},{8,1},{2,2},{10,3},{1,4},{9,5},{3,6},{11,7},{4,8},{12,9},{6,... | collective-permute-start | bytes 786440 | tf_op jit(solution)/shard_map/ppermute | solution.py:848
  135.4 13.2 %collective-permute-start.33 = (bf16[64,2048]{1,0:T(8,128)(2,1)S(1)}, bf16[64,2048]{1,0:T(8,128)(2,1)S(1)}, u32[]{:S(2)}, u32[]{:S(2)}) collective-permute-start(bf16[64,2048]{1,0:T(8,128)(2,1)S(1)} %get-tuple-element.175), channel_id=1, source_target_pairs={{0,2},{1,3},{2,0},{3,1},{4,6},{5,7},{6,4},{7,5},{8,10},{9,11},{10,... | collective-permute-start | bytes 786440 | tf_op jit(solution)/shard_map/ppermute | solution.py:121
  136.6 6.8 %collective-permute-start.30 = (bf16[64,1280]{1,0:T(8,128)(2,1)S(1)}, bf16[64,1280]{1,0:T(8,128)(2,1)S(1)}, u32[]{:S(2)}, u32[]{:S(2)}) collective-permute-start(bf16[64,1280]{1,0:T(8,128)(2,1)S(1)} %get-tuple-element.171), channel_id=1, source_target_pairs={{0,1},{1,0},{2,3},{3,2},{4,5},{5,4},{6,7},{7,6},{8,9},{9,8},{10,11... | collective-permute-start | bytes 491528 | tf_op jit(solution)/shard_map/ppermute | solution.py:121
  136.6 7.1 %collective-permute-start.31 = (bf16[64,1280]{1,0:T(8,128)(2,1)S(1)}, bf16[64,1280]{1,0:T(8,128)(2,1)S(1)}, u32[]{:S(2)}, u32[]{:S(2)}) collective-permute-start(bf16[64,1280]{1,0:T(8,128)(2,1)S(1)} %get-tuple-element.172), channel_id=1, source_target_pairs={{0,16},{1,17},{2,18},{3,19},{4,20},{5,21},{6,22},{7,23},{8,24},{9,... | collective-permute-start | bytes 491528 | tf_op jit(solution)/shard_map/ppermute | solution.py:121
  137.2 11.4 %collective-permute-start.32 = (bf16[64,1280]{1,0:T(8,128)(2,1)S(1)}, bf16[64,1280]{1,0:T(8,128)(2,1)S(1)}, u32[]{:S(2)}, u32[]{:S(2)}) collective-permute-start(bf16[64,1280]{1,0:T(8,128)(2,1)S(1)} %get-tuple-element.173), channel_id=1, source_target_pairs={{0,17},{1,16},{2,19},{3,18},{4,21},{5,20},{6,23},{7,22},{8,25},{9,... | collective-permute-start | bytes 491528 | tf_op jit(solution)/shard_map/ppermute | solution.py:121
  148.7 12.5 %collective-permute-start.37 = (bf16[32,2048]{1,0:T(8,128)(2,1)S(1)}, bf16[32,2048]{1,0:T(8,128)(2,1)S(1)}, u32[]{:S(2)}, u32[]{:S(2)}) collective-permute-start(bf16[32,2048]{1,0:T(8,128)(2,1)S(1)} %get-tuple-element.181), channel_id=1, source_target_pairs={{0,4},{1,5},{2,6},{3,7},{4,0},{5,1},{6,2},{7,3},{8,12},{9,13},{10,... | collective-permute-start | bytes 393224 | tf_op jit(solution)/shard_map/ppermute | solution.py:121
  149.8 11.4 %collective-permute-start.34 = (bf16[16,1280]{1,0:T(8,128)(2,1)S(1)}, bf16[16,1280]{1,0:T(8,128)(2,1)S(1)}, u32[]{:S(2)}, u32[]{:S(2)}) collective-permute-start(bf16[16,1280]{1,0:T(8,128)(2,1)S(1)} %get-tuple-element.177), channel_id=1, source_target_pairs={{0,4},{1,5},{2,6},{3,7},{4,0},{5,1},{6,2},{7,3},{8,12},{9,13},{10,... | collective-permute-start | bytes 122888 | tf_op jit(solution)/shard_map/ppermute | solution.py:121
  151.7 9.5 %collective-permute-start.35 = (bf16[16,1280]{1,0:T(8,128)(2,1)S(1)}, bf16[16,1280]{1,0:T(8,128)(2,1)S(1)}, u32[]{:S(2)}, u32[]{:S(2)}) collective-permute-start(bf16[16,1280]{1,0:T(8,128)(2,1)S(1)} %get-tuple-element.178), channel_id=1, source_target_pairs={{0,2},{1,3},{2,0},{3,1},{4,6},{5,7},{6,4},{7,5},{8,10},{9,11},{10,... | collective-permute-start | bytes 122888 | tf_op jit(solution)/shard_map/ppermute | solution.py:121
  153.9 7.4 %collective-permute-start.36 = (bf16[16,1280]{1,0:T(8,128)(2,1)S(1)}, bf16[16,1280]{1,0:T(8,128)(2,1)S(1)}, u32[]{:S(2)}, u32[]{:S(2)}) collective-permute-start(bf16[16,1280]{1,0:T(8,128)(2,1)S(1)} %get-tuple-element.179), channel_id=1, source_target_pairs={{0,6},{1,7},{2,4},{3,5},{4,2},{5,3},{6,0},{7,1},{8,14},{9,15},{10,... | collective-permute-start | bytes 122888 | tf_op jit(solution)/shard_map/ppermute | solution.py:121

commit v5 on v4

--- a/solution.py
+++ b/solution.py
@@ -725,7 +725,6 @@
     share, width = E // devices, D // devices
     if plan.fast:
         home = [(s * 8 + c, plan.place(s, c)) for s in range(4) for c in range(8)]
-        tok = lax.ppermute(tok0, ALL, home)
         halo = lax.ppermute(
             tok0[count - HALO :], ALL, [(s * 8 + c, plan.place(s, c + 1)) for s in range(4) for c in range(7)]
         )
@@ -735,11 +734,12 @@
             pack_kernel, [], [((16, E + 256), BF16), ((32, 4 * D), BF16)],
             [pltpu.VMEM((SMALL_ROWS, 32), F32)] + [pltpu.VMEM(value.shape, F32) for value in raw]
             + [pltpu.SemaphoreType.DMA((len(raw),))], far=raw, limit=60)
-        (one,) = join(plan, [spread_out(pack_one, Z_MASKS)])
+        one, tok = join(plan, [spread_out(pack_one, Z_MASKS), [tok0]])
+        tok = lax.ppermute(tok, ALL, home)
         near_one = spread_out(one, XY_MASKS)
-        (two,) = join(plan, [[pack_two, send(pack_two, 4)]], [one, tok])
+        (two,) = join(plan, [[pack_two, send(pack_two, 4)]], [one, halo])
         cot = lax.ppermute(cot0, ALL, home)
-        one, two = join(plan, [near_one, [two, send(two, 2)]], [halo], (0,))
+        one, two = join(plan, [near_one, [two, send(two, 2)]], [tok], (0,))
         one = [one, send(one, CORE)]
         near_two = spread_out(two, XY_MASKS)
     else:

time: 164 us -> 161 us (0.982)
  starting transfers between devices: 53.9 us -> 43.1 us
  waiting for transfers between devices: 45 us -> 53.4 us
    ppermute x1, waiting for transfers between devices: 0.01 us -> 8.14 us  [body(): tok = lax.ppermute(tok, ALL, home)]
    ppermute x33, starting transfers between devices: 37.9 us -> 30.5 us  [send(): return lax.ppermute(value, ALL, [(i, i ^ mask) for i in range(32)])]
    ppermute x1, starting transfers between devices: 4.86 us -> 2.06 us  [body(): both = lax.ppermute(both, ALL, back)]
    ppermute x1, waiting for transfers between devices: 0.01 us -> 1.96 us  [body(): lax.ppermute(before, ALL, [(plan.place(s, c + 1), s * 8 + c) for s in ran...]
  transfers between devices with their start and end apart: 38 -> 38, of which waited for: 16 -> 15; matrix products, arithmetic and copies ran while one was open for 0% -> 0% of each run, Pallas kernels for 13% -> 12%
where the time goes in v5:
time: 161 us; the launch traced here: 160 us
  waiting for transfers between devices  53.4 us (33%)
  starting transfers between devices  43.1 us (27%)
  Pallas kernels  35.7 us (22%)
  blocking collectives  23.5 us (15%)
  local copies, waits for them, and re-layouts  3.31 us (2%)
    ppermute x33, waiting for transfers between devices, send(): return lax.ppermute(value, ALL, [(i, i ^ mask) for i in range(32)])  41.9 us
    pallas_call x24, Pallas kernels, run(): pl.pallas_call(inner, out_shape=[jax.ShapeDtypeStruct(shape, dtype) for s...  35.7 us
    ppermute x33, starting transfers between devices, send(): return lax.ppermute(value, ALL, [(i, i ^ mask) for i in range(32)])  30.5 us
    all_to_all x2, blocking collectives, swap(): lax.all_to_all(value, ALL, 0, 0, tiled=True, axis_index_groups=groups)  23.5 us
    ppermute x1, waiting for transfers between devices, body(): tok = lax.ppermute(tok, ALL, home)  8.14 us
    ppermute x1, starting transfers between devices, body(): lax.ppermute(tok0[count - HALO:], ALL, [(s * 8 + c, plan.place(s, c + 1))...  4.32 us
  transfers between devices with their start and end apart: 38, of which 15 were waited for; matrix products, arithmetic and copies ran while one was open for 0% of the time, Pallas kernels for 12%

profile of v5, /device:TPU:6, one launch (start us, length us, event | category | flops | bytes accessed | tf_op | source)
XLA Modules:
  0.0 160.1 jit_solution(16899098321854768566)
XLA Ops:
  0.7 2.0 %shard_map.296 = (bf16[16,1280]{1,0:T(8,128)(2,1)}, bf16[32,2048]{1,0:T(8,128)(2,1)}) custom-call(f32[16,2048]{1,0:T(8,128)} %refs_0_.1, f32[32,64]{1,0:T(8,128)} %refs_1_.1, f32[32,32]{1,0:T(8,128)} %refs_2_.1, f32[16,32]{1,0:T(8,128)} %bitcast.29, f32[4,32]{1,0:T(4,128)} %bitcast.30, f32[1,32]{1,0:T(1,128)} %bitcast.31, f32[1,32]{1,0:T(1,128)} %bitcast.32, ...), custom_call_target="tpu_custom_call" | custom-call | flops 2000 | bytes 6000 | tf_op jit(solution)/shard_map/pallas_call | solution.py:59
  2.7 2.7 %collective-permute-start = (bf16[16,1280]{1,0:T(8,128)(2,1)}, bf16[16,1280]{1,0:T(8,128)(2,1)S(1)}, u32[]{:S(2)}, u32[]{:S(2)}) collective-permute-start(bf16[16,1280]{1,0:T(8,128)(2,1)} %get-tuple-element.110.refs_0_), channel_id=1, source_target_pairs={{0,4},{1,5},{2,6},{3,7},{4,0},{5,1},{6,2},{7,3},{8,12},{9,13},{10,... | collective-permute-start | bytes 122888 | tf_op jit(solution)/shard_map/ppermute | solution.py:121
  5.3 1.6 collective-permute-start.1
  7.1 1.7 %collective-permute-start.8 = (bf16[32,2048]{1,0:T(8,128)(2,1)}, bf16[32,2048]{1,0:T(8,128)(2,1)S(1)}, u32[]{:S(2)}, u32[]{:S(2)}) collective-permute-start(bf16[32,2048]{1,0:T(8,128)(2,1)} %get-tuple-element.113.refs_0_), channel_id=1, source_target_pairs={{0,4},{1,5},{2,6},{3,7},{4,0},{5,1},{6,2},{7,3},{8,12},{9,13},{10,... | collective-permute-start | bytes 393224 | tf_op jit(solution)/shard_map/ppermute | solution.py:121
  8.8 0.7 slice_bitcast_fusion
  9.5 4.3 %collective-permute-start.4 = (bf16[16,512]{1,0:T(8,128)(2,1)S(1)}, bf16[16,512]{1,0:T(8,128)(2,1)S(1)}, u32[]{:S(2)}, u32[]{:S(2)}) collective-permute-start(bf16[16,512]{1,0:T(8,128)(2,1)S(1)} %slice_bitcast_fusion), channel_id=1, source_target_pairs={{0,8},{1,2},{2,10},{3,1},{4,9},{5,3},{6,11},{8,12},{9,6},{10,14},{... | collective-permute-start | bytes 49160 | tf_op jit(solution)/shard_map/ppermute | solution.py:728
  13.9 0.9 copy-done
  14.8 0.8 copy-done.2
  15.6 1.4 collective-permute-done.4.refs_3_.refs_1_
  17.0 0.9 copy-done.1
  18.6 1.4 collective-permute-start.5
  20.5 1.5 collective-permute-start.7
  22.1 1.9 %collective-permute-start.3 = (bf16[128,512]{1,0:T(8,128)(2,1)S(1)}, bf16[128,512]{1,0:T(8,128)(2,1)S(1)}, u32[]{:S(2)}, u32[]{:S(2)}) collective-permute-start(bf16[128,512]{1,0:T(8,128)(2,1)S(1)} %get-tuple-element.111), channel_id=1, source_target_pairs={{0,0},{1,8},{2,2},{3,10},{4,1},{5,9},{6,3},{7,11},{8,4},{9,12},{10... | collective-permute-start | bytes 393224 | tf_op jit(solution)/shard_map/ppermute | solution.py:738
  24.0 8.1 %collective-permute-done.3.refs_6_.refs_0_ = bf16[128,512]{1,0:T(8,128)(2,1)S(1)} collective-permute-done((bf16[128,512]{1,0:T(8,128)(2,1)S(1)}, bf16[128,512]{1,0:T(8,128)(2,1)S(1)}, u32[]{:S(2)}, u32[]{:S(2)}) %collective-permute-start.3) | collective-permute-done | bytes 131104 | tf_op jit(solution)/shard_map/ppermute | solution.py:738
  33.0 2.9 %collective-permute-start.17 = (bf16[128,2048]{1,0:T(8,128)(2,1)S(1)}, bf16[128,2048]{1,0:T(8,128)(2,1)S(1)}, u32[]{:S(2)}, u32[]{:S(2)}) collective-permute-start(bf16[128,2048]{1,0:T(8,128)(2,1)S(1)} %get-tuple-element.129.refs_0_), channel_id=1, source_target_pairs={{0,17},{1,16},{2,19},{3,18},{4,21},{5,20},{6,23},{7,22},{8,25},{9,... | collective-permute-start | bytes 1572872 | tf_op jit(solution)/shard_map/ppermute | solution.py:121
  35.9 1.9 %collective-permute-start.11 = (bf16[128,512]{1,0:T(8,128)(2,1)S(1)}, bf16[128,512]{1,0:T(8,128)(2,1)S(1)}, u32[]{:S(2)}, u32[]{:S(2)}) collective-permute-start(bf16[128,512]{1,0:T(8,128)(2,1)S(1)} %bitcast.36), channel_id=1, source_target_pairs={{0,0},{1,8},{2,2},{3,10},{4,1},{5,9},{6,3},{7,11},{8,4},{9,12},{10... | collective-permute-start | bytes 393224 | tf_op jit(solution)/shard_map/ppermute | solution.py:741
  37.8 4.0 %shard_map.300 = (bf16[144,512]{1,0:T(8,128)(2,1)S(1)}, bf16[144,512]{1,0:T(8,128)(2,1)S(1)}, f32[144,1024]{1,0:T(8,128)S(1)}, f32[128,1024]{1,0:T(8,128)S(1)}, ...) custom-call(bf16[128,512]{1,0:T(8,128)(2,1)S(1)} %collective-permute, ...), custom_call_target="tpu_custom_call" | custom-call | flops 6000 | bytes 18000 | tf_op jit(solution)/shard_map/pallas_call | solution.py:59
  41.9 1.2 collective-permute-done.12.refs_1_
  43.4 3.9 %collective-permute-done.13.refs_1_ = bf16[144,128]{1,0:T(8,128)(2,1)S(1)} collective-permute-done((bf16[144,128]{1,0:T(8,128)(2,1)S(1)}, bf16[144,128]{1,0:T(8,128)(2,1)S(1)}, u32[]{:S(2)}, u32[]{:S(2)}) %collective-permute-start.13) | collective-permute-done | bytes 36896 | tf_op jit(solution)/shard_map/ppermute | solution.py:121
  47.3 12.0 %collective-permute-done.15.refs_1_ = bf16[128,2048]{1,0:T(8,128)(2,1)S(1)} collective-permute-done((bf16[128,2048]{1,0:T(8,128)(2,1)S(1)}, bf16[128,2048]{1,0:T(8,128)(2,1)S(1)}, u32[]{:S(2)}, u32[]{:S(2)}) %collective-permute-start.15) | collective-permute-done | bytes 524320 | tf_op jit(solution)/shard_map/ppermute | solution.py:121
  59.8 3.8 %collective-permute-done.14.refs_1_ = bf16[144,128]{1,0:T(8,128)(2,1)S(1)} collective-permute-done((bf16[144,128]{1,0:T(8,128)(2,1)S(1)}, bf16[144,128]{1,0:T(8,128)(2,1)S(1)}, u32[]{:S(2)}, u32[]{:S(2)}) %collective-permute-start.14) | collective-permute-done | bytes 36896 | tf_op jit(solution)/shard_map/ppermute | solution.py:121
  64.3 3.8 %shard_map.305 = (bf16[1024,256]{1,0:T(8,128)(2,1)S(1)}, f32[128,1024]{1,0:T(8,128)S(1)}, bf16[128,1024]{1,0:T(8,128)(2,1)S(1)}, f32[128,512]{1,0:T(8,128)S(1)},...) custom-call(bf16[128,512]{1,0:T(8,128)(2,1)S(1)} %collective-permute-done.3.refs_6_.refs_0_, ...), custom_call_target="tpu_custom_call" | custom-call | flops 6000 | bytes 18000 | tf_op jit(solution)/shard_map/pallas_call | solution.py:59
  68.2 11.4 %all_to_all.22 = bf16[8,128,256]{2,1,0:T(8,128)(2,1)S(1)} all-to-all(bf16[8,128,256]{2,1,0:T(8,128)(2,1)S(1)} %bitcast.27), channel_id=1, replica_groups={{0,8,2,10,1,9,3,11},{4,12,6,14,5,13,7,15},{16,24,18,26,17,25,19,27},{20..., dimensions={0} | all-to-all | bytes 1048576 | tf_op jit(solution)/shard_map/all_to_all | solution.py:116
  79.5 3.6 %shard_map.306 = bf16[1024,256]{1,0:T(8,128)(2,1)S(1)} custom-call(bf16[1024,256]{1,0:T(8,128)(2,1)S(1)} %bitcast.25), custom_call_target="tpu_custom_call" | custom-call | flops 4000 | bytes 12000 | tf_op jit(solution)/shard_map/pallas_call | solution.py:59
  83.2 12.1 %all_to_all.23 = bf16[8,128,256]{2,1,0:T(8,128)(2,1)S(1)} all-to-all(bf16[8,128,256]{2,1,0:T(8,128)(2,1)S(1)} %bitcast.26), channel_id=1, replica_groups={{0,8,2,10,1,9,3,11},{4,12,6,14,5,13,7,15},{16,24,18,26,17,25,19,27},{20..., dimensions={0} | all-to-all | bytes 1048576 | tf_op jit(solution)/shard_map/all_to_all | solution.py:116
  95.3 3.1 %shard_map.307 = (bf16[128,512]{1,0:T(8,128)(2,1)S(1)}, bf16[128,512]{1,0:T(8,128)(2,1)S(1)}, bf16[128,512]{1,0:T(8,128)(2,1)S(1)}, bf16[128,512]{1,0:T(8,128)(2...) custom-call(bf16[1024,256]{1,0:T(8,128)(2,1)S(1)} %bitcast.24, ...), custom_call_target="tpu_custom_call" | custom-call | flops 2000 | bytes 6000 | tf_op jit(solution)/shard_map/pallas_call | solution.py:59
  98.5 1.2 collective-permute-done.19.refs_1_
  99.8 1.7 %shard_map.309 = (bf16[128,512]{1,0:T(8,128)(2,1)S(1)}, bf16[512,2048]{1,0:T(8,128)(2,1)S(1)}, bf16[512,2048]{1,0:T(8,128)(2,1)S(1)}) custom-call(bf16[128,512]{1,0:T(8,128)(2,1)S(1)} %get-tuple-element.144.refs_0_, bf16[128,512]{1,0:T(8,128)(2,1)S(1)} %get-tuple-element.145.refs_1_, bf16[128,512]{1,0:T(8,128)(2,1)S(1)} %get-tuple-element.146.refs_2_, ...), custom_call_target="tpu_custom_call" | custom-call | flops 2000 | bytes 6000 | tf_op jit(solution)/shard_map/pallas_call | solution.py:59
  102.3 3.4 %collective-permute-done.20.refs_1_ = bf16[144,128]{1,0:T(8,128)(2,1)S(1)} collective-permute-done((bf16[144,128]{1,0:T(8,128)(2,1)S(1)}, bf16[144,128]{1,0:T(8,128)(2,1)S(1)}, u32[]{:S(2)}, u32[]{:S(2)}) %collective-permute-start.20) | collective-permute-done | bytes 36896 | tf_op jit(solution)/shard_map/ppermute | solution.py:121
  105.7 1.5 collective-permute-start.21
  107.2 3.2 %shard_map.311.refs_4_.refs_14_ = f32[128,128]{1,0:T(8,128)S(1)} custom-call(f32[1024,128]{1,0:T(8,128)S(1)} %get-tuple-element.134.refs_0_.refs_2_, f32[16512,128]{1,0:T(8,128)S(1)} %get-tuple-element.136.refs_1_.refs_6_, f32[144,128]{1,0:T(8,128)S(1)} %get-tuple-element.154.refs_2_), custom_call_target="tpu_custom_call" | custom-call | flops 2000 | bytes 6000 | tf_op jit(solution)/shard_map/pallas_call | solution.py:59
  112.2 0.7 collective-permute-start.27
  113.0 8.4 %shard_map.314 = (f32[128,1024]{1,0:T(8,128)S(1)}, bf16[144,1024]{1,0:T(8,128)(2,1)S(1)}) custom-call(f32[1024,128]{1,0:T(8,128)S(1)} %get-tuple-element.116.refs_1_.refs_6_.refs_0_, f32[1024,128]{1,0:T(8,128)S(1)} %get-tuple-element.117.refs_2_.refs_1_, f32[1024,128]{1,0:T(8,128)S(1)} %get-tuple-element.134.refs_0_.refs_2_, ...), custom_call_target="tpu_custom_call" | custom-call | flops 11000 | bytes 33000 | tf_op jit(solution)/shard_map/pallas_call | solution.py:59
  121.4 1.8 %shard_map.315 = (bf16[256,1280]{1,0:T(8,128)(2,1)S(1)}, bf16[256,1280]{1,0:T(8,128)(2,1)S(1)}, bf16[256,512]{1,0:T(8,128)(2,1)S(1)}, bf16[16,512]{1,0:T(8,128)(2,1)S(1)}) custom-call(bf16[128,512]{1,0:T(8,128)(2,1)S(1)} %collective-permute-done.3.refs_6_.refs_0_, bf16[16,512]{1,0:T(8,128)(2,1)S(1)} %collective-permute-done.4.refs_3_.refs_1_, ...), custom_call_target="tpu_custom_call" | custom-call | flops 2000 | bytes 6000 | tf_op jit(solution)/shard_map/pallas_call | solution.py:59
  123.3 1.1 collective-permute-done.26.refs_1_
  125.6 1.5 collective-permute-start.29
  127.0 2.5 %collective-permute-start.24 = (bf16[16,512]{1,0:T(8,128)(2,1)S(1)}, bf16[16,512]{1,0:T(8,128)(2,1)S(1)}, u32[]{:S(2)}, u32[]{:S(2)}) collective-permute-start(bf16[16,512]{1,0:T(8,128)(2,1)S(1)} %get-tuple-element.164), channel_id=1, source_target_pairs={{8,0},{2,1},{10,2},{1,3},{9,4},{3,5},{11,6},{12,8},{6,9},{14,10},{... | collective-permute-start | bytes 49160 | tf_op jit(solution)/shard_map/ppermute | solution.py:849
  129.5 2.1 %collective-permute-start.23 = (bf16[256,512]{1,0:T(8,128)(2,1)S(1)}, bf16[256,512]{1,0:T(8,128)(2,1)S(1)}, u32[]{:S(2)}, u32[]{:S(2)}) collective-permute-start(bf16[256,512]{1,0:T(8,128)(2,1)S(1)} %get-tuple-element.163), channel_id=1, source_target_pairs={{0,0},{8,1},{2,2},{10,3},{1,4},{9,5},{3,6},{11,7},{4,8},{12,9},{6,... | collective-permute-start | bytes 786440 | tf_op jit(solution)/shard_map/ppermute | solution.py:848
  131.6 2.0 %collective-permute-done.24.refs_6_.refs_1_ = bf16[16,512]{1,0:T(8,128)(2,1)S(1)} collective-permute-done((bf16[16,512]{1,0:T(8,128)(2,1)S(1)}, bf16[16,512]{1,0:T(8,128)(2,1)S(1)}, u32[]{:S(2)}, u32[]{:S(2)}) %collective-permute-start.24) | collective-permute-done | bytes 16416 | tf_op jit(solution)/shard_map/ppermute | solution.py:849
  133.8 1.6 %collective-permute-start.33 = (bf16[64,2048]{1,0:T(8,128)(2,1)S(1)}, bf16[64,2048]{1,0:T(8,128)(2,1)S(1)}, u32[]{:S(2)}, u32[]{:S(2)}) collective-permute-start(bf16[64,2048]{1,0:T(8,128)(2,1)S(1)} %get-tuple-element.179), channel_id=1, source_target_pairs={{0,2},{1,3},{2,0},{3,1},{4,6},{5,7},{6,4},{7,5},{8,10},{9,11},{10,... | collective-permute-start | bytes 786440 | tf_op jit(solution)/shard_map/ppermute | solution.py:121
  135.5 1.0 collective-permute-start.31
  136.5 2.5 %collective-permute-start.32 = (bf16[64,1280]{1,0:T(8,128)(2,1)S(1)}, bf16[64,1280]{1,0:T(8,128)(2,1)S(1)}, u32[]{:S(2)}, u32[]{:S(2)}) collective-permute-start(bf16[64,1280]{1,0:T(8,128)(2,1)S(1)} %get-tuple-element.177), channel_id=1, source_target_pairs={{0,17},{1,16},{2,19},{3,18},{4,21},{5,20},{6,23},{7,22},{8,25},{9,... | collective-permute-start | bytes 491528 | tf_op jit(solution)/shard_map/ppermute | solution.py:121
  139.0 3.2 %collective-permute-done.30.refs_1_ = bf16[64,1280]{1,0:T(8,128)(2,1)S(1)} collective-permute-done((bf16[64,1280]{1,0:T(8,128)(2,1)S(1)}, bf16[64,1280]{1,0:T(8,128)(2,1)S(1)}, u32[]{:S(2)}, u32[]{:S(2)}) %collective-permute-start.30) | collective-permute-done | bytes 163872 | tf_op jit(solution)/shard_map/ppermute | solution.py:121
  142.5 3.9 %collective-permute-done.32.refs_3_ = bf16[64,1280]{1,0:T(8,128)(2,1)S(1)} collective-permute-done((bf16[64,1280]{1,0:T(8,128)(2,1)S(1)}, bf16[64,1280]{1,0:T(8,128)(2,1)S(1)}, u32[]{:S(2)}, u32[]{:S(2)}) %collective-permute-start.32) | collective-permute-done | bytes 163872 | tf_op jit(solution)/shard_map/ppermute | solution.py:121
  147.1 2.4 %collective-permute-start.34 = (bf16[16,1280]{1,0:T(8,128)(2,1)S(1)}, bf16[16,1280]{1,0:T(8,128)(2,1)S(1)}, u32[]{:S(2)}, u32[]{:S(2)}) collective-permute-start(bf16[16,1280]{1,0:T(8,128)(2,1)S(1)} %get-tuple-element.181), channel_id=1, source_target_pairs={{0,4},{1,5},{2,6},{3,7},{4,0},{5,1},{6,2},{7,3},{8,12},{9,13},{10,... | collective-permute-start | bytes 122888 | tf_op jit(solution)/shard_map/ppermute | solution.py:121
  149.5 1.5 collective-permute-start.35
  151.5 7.5 %collective-permute-done.34.refs_3_ = bf16[16,1280]{1,0:T(8,128)(2,1)S(1)} collective-permute-done((bf16[16,1280]{1,0:T(8,128)(2,1)S(1)}, bf16[16,1280]{1,0:T(8,128)(2,1)S(1)}, u32[]{:S(2)}, u32[]{:S(2)}) %collective-permute-start.34) | collective-permute-done | bytes 40992 | tf_op jit(solution)/shard_map/ppermute | solution.py:121
  159.0 0.9 shard_map.319
  (64 shorter events, 9.6 us)
Async XLA Ops:
  0.7 35.2 %copy-start.3 = (bf16[1,128,512]{2,1,0:T(8,128)(2,1)S(1)}, bf16[1,128,512]{2,1,0:T(8,128)(2,1)}, u32[]{:S(2)}) copy-start(bf16[1,128,512]{2,1,0:T(8,128)(2,1)} %param.33) | copy-start | bytes 393220
  2.7 11.2 %collective-permute-start = (bf16[16,1280]{1,0:T(8,128)(2,1)}, bf16[16,1280]{1,0:T(8,128)(2,1)S(1)}, u32[]{:S(2)}, u32[]{:S(2)}) collective-permute-start(bf16[16,1280]{1,0:T(8,128)(2,1)} %get-tuple-element.110.refs_0_), channel_id=1, source_target_pairs={{0,4},{1,5},{2,6},{3,7},{4,0},{5,1},{6,2},{7,3},{8,12},{9,13},{10,... | collective-permute-start | bytes 122888 | tf_op jit(solution)/shard_map/ppermute | solution.py:121
  5.3 8.5 %collective-permute-start.1 = (bf16[16,1280]{1,0:T(8,128)(2,1)}, bf16[16,1280]{1,0:T(8,128)(2,1)S(1)}, u32[]{:S(2)}, u32[]{:S(2)}) collective-permute-start(bf16[16,1280]{1,0:T(8,128)(2,1)} %get-tuple-element.110.refs_0_), channel_id=1, source_target_pairs={{0,2},{1,3},{2,0},{3,1},{4,6},{5,7},{6,4},{7,5},{8,10},{9,11},{10,... | collective-permute-start | bytes 122888 | tf_op jit(solution)/shard_map/ppermute | solution.py:121
  6.9 7.0 %collective-permute-start.2 = (bf16[16,1280]{1,0:T(8,128)(2,1)}, bf16[16,1280]{1,0:T(8,128)(2,1)S(1)}, u32[]{:S(2)}, u32[]{:S(2)}) collective-permute-start(bf16[16,1280]{1,0:T(8,128)(2,1)} %get-tuple-element.110.refs_0_), channel_id=1, source_target_pairs={{0,6},{1,7},{2,4},{3,5},{4,2},{5,3},{6,0},{7,1},{8,14},{9,15},{10,... | collective-permute-start | bytes 122888 | tf_op jit(solution)/shard_map/ppermute | solution.py:121
  7.1 9.9 %collective-permute-start.8 = (bf16[32,2048]{1,0:T(8,128)(2,1)}, bf16[32,2048]{1,0:T(8,128)(2,1)S(1)}, u32[]{:S(2)}, u32[]{:S(2)}) collective-permute-start(bf16[32,2048]{1,0:T(8,128)(2,1)} %get-tuple-element.113.refs_0_), channel_id=1, source_target_pairs={{0,4},{1,5},{2,6},{3,7},{4,0},{5,1},{6,2},{7,3},{8,12},{9,13},{10,... | collective-permute-start | bytes 393224 | tf_op jit(solution)/shard_map/ppermute | solution.py:121
  9.5 7.5 %collective-permute-start.4 = (bf16[16,512]{1,0:T(8,128)(2,1)S(1)}, bf16[16,512]{1,0:T(8,128)(2,1)S(1)}, u32[]{:S(2)}, u32[]{:S(2)}) collective-permute-start(bf16[16,512]{1,0:T(8,128)(2,1)S(1)} %slice_bitcast_fusion), channel_id=1, source_target_pairs={{0,8},{1,2},{2,10},{3,1},{4,9},{5,3},{6,11},{8,12},{9,6},{10,14},{... | collective-permute-start | bytes 49160 | tf_op jit(solution)/shard_map/ppermute | solution.py:728
  13.9 0.9 copy-start
  14.8 0.8 copy-start.2
  17.0 0.9 copy-start.1
  17.9 14.3 %collective-permute-start.9 = (bf16[64,2048]{1,0:T(8,128)(2,1)S(1)}, bf16[64,2048]{1,0:T(8,128)(2,1)S(1)}, u32[]{:S(2)}, u32[]{:S(2)}) collective-permute-start(bf16[64,2048]{1,0:T(8,128)(2,1)S(1)} %shard_map.298.refs_4_), channel_id=1, source_target_pairs={{0,2},{1,3},{2,0},{3,1},{4,6},{5,7},{6,4},{7,5},{8,10},{9,11},{10,... | collective-permute-start | bytes 786440 | tf_op jit(solution)/shard_map/ppermute | solution.py:121
  18.6 13.5 %collective-permute-start.5 = (bf16[64,1280]{1,0:T(8,128)(2,1)S(1)}, bf16[64,1280]{1,0:T(8,128)(2,1)S(1)}, u32[]{:S(2)}, u32[]{:S(2)}) collective-permute-start(bf16[64,1280]{1,0:T(8,128)(2,1)S(1)} %get-tuple-element.112.refs_2_.refs_0_), channel_id=1, source_target_pairs={{0,1},{1,0},{2,3},{3,2},{4,5},{5,4},{6,7},{7,6},{8,9},{9,8},{10,11... | collective-permute-start | bytes 491528 | tf_op jit(solution)/shard_map/ppermute | solution.py:121
  20.0 12.1 %collective-permute-start.6 = (bf16[64,1280]{1,0:T(8,128)(2,1)S(1)}, bf16[64,1280]{1,0:T(8,128)(2,1)S(1)}, u32[]{:S(2)}, u32[]{:S(2)}) collective-permute-start(bf16[64,1280]{1,0:T(8,128)(2,1)S(1)} %get-tuple-element.112.refs_2_.refs_0_), channel_id=1, source_target_pairs={{0,16},{1,17},{2,18},{3,19},{4,20},{5,21},{6,22},{7,23},{8,24},{9,... | collective-permute-start | bytes 491528 | tf_op jit(solution)/shard_map/ppermute | solution.py:121
  20.5 11.6 %collective-permute-start.7 = (bf16[64,1280]{1,0:T(8,128)(2,1)S(1)}, bf16[64,1280]{1,0:T(8,128)(2,1)S(1)}, u32[]{:S(2)}, u32[]{:S(2)}) collective-permute-start(bf16[64,1280]{1,0:T(8,128)(2,1)S(1)} %get-tuple-element.112.refs_2_.refs_0_), channel_id=1, source_target_pairs={{0,17},{1,16},{2,19},{3,18},{4,21},{5,20},{6,23},{7,22},{8,25},{9,... | collective-permute-start | bytes 491528 | tf_op jit(solution)/shard_map/ppermute | solution.py:121
  22.1 10.1 %collective-permute-start.3 = (bf16[128,512]{1,0:T(8,128)(2,1)S(1)}, bf16[128,512]{1,0:T(8,128)(2,1)S(1)}, u32[]{:S(2)}, u32[]{:S(2)}) collective-permute-start(bf16[128,512]{1,0:T(8,128)(2,1)S(1)} %get-tuple-element.111), channel_id=1, source_target_pairs={{0,0},{1,8},{2,2},{3,10},{4,1},{5,9},{6,3},{7,11},{8,4},{9,12},{10... | collective-permute-start | bytes 393224 | tf_op jit(solution)/shard_map/ppermute | solution.py:738
  32.3 5.6 %collective-permute-start.10 = (bf16[256,1280]{1,0:T(8,128)(2,1)S(1)}, bf16[256,1280]{1,0:T(8,128)(2,1)S(1)}, u32[]{:S(2)}, u32[]{:S(2)}) collective-permute-start(bf16[256,1280]{1,0:T(8,128)(2,1)S(1)} %get-tuple-element.114.refs_2_.refs_6_), channel_id=1, source_target_pairs={{0,8},{1,9},{2,10},{3,11},{4,12},{5,13},{6,14},{7,15},{8,0},{9,1},... | collective-permute-start | bytes 1966088 | tf_op jit(solution)/shard_map/ppermute | solution.py:121
  32.4 27.0 %collective-permute-start.15 = (bf16[128,2048]{1,0:T(8,128)(2,1)S(1)}, bf16[128,2048]{1,0:T(8,128)(2,1)S(1)}, u32[]{:S(2)}, u32[]{:S(2)}) collective-permute-start(bf16[128,2048]{1,0:T(8,128)(2,1)S(1)} %get-tuple-element.129.refs_0_), channel_id=1, source_target_pairs={{0,1},{1,0},{2,3},{3,2},{4,5},{5,4},{6,7},{7,6},{8,9},{9,8},{10,11... | collective-permute-start | bytes 1572872 | tf_op jit(solution)/shard_map/ppermute | solution.py:121
  32.4 26.9 %collective-permute-start.16 = (bf16[128,2048]{1,0:T(8,128)(2,1)S(1)}, bf16[128,2048]{1,0:T(8,128)(2,1)S(1)}, u32[]{:S(2)}, u32[]{:S(2)}) collective-permute-start(bf16[128,2048]{1,0:T(8,128)(2,1)S(1)} %get-tuple-element.129.refs_0_), channel_id=1, source_target_pairs={{0,16},{1,17},{2,18},{3,19},{4,20},{5,21},{6,22},{7,23},{8,24},{9,... | collective-permute-start | bytes 1572872 | tf_op jit(solution)/shard_map/ppermute | solution.py:121
  33.0 26.3 %collective-permute-start.17 = (bf16[128,2048]{1,0:T(8,128)(2,1)S(1)}, bf16[128,2048]{1,0:T(8,128)(2,1)S(1)}, u32[]{:S(2)}, u32[]{:S(2)}) collective-permute-start(bf16[128,2048]{1,0:T(8,128)(2,1)S(1)} %get-tuple-element.129.refs_0_), channel_id=1, source_target_pairs={{0,17},{1,16},{2,19},{3,18},{4,21},{5,20},{6,23},{7,22},{8,25},{9,... | collective-permute-start | bytes 1572872 | tf_op jit(solution)/shard_map/ppermute | solution.py:121
  35.9 11.4 %collective-permute-start.11 = (bf16[128,512]{1,0:T(8,128)(2,1)S(1)}, bf16[128,512]{1,0:T(8,128)(2,1)S(1)}, u32[]{:S(2)}, u32[]{:S(2)}) collective-permute-start(bf16[128,512]{1,0:T(8,128)(2,1)S(1)} %bitcast.36), channel_id=1, source_target_pairs={{0,0},{1,8},{2,2},{3,10},{4,1},{5,9},{6,3},{7,11},{8,4},{9,12},{10... | collective-permute-start | bytes 393224 | tf_op jit(solution)/shard_map/ppermute | solution.py:741
  41.9 1.3 collective-permute-start.12
  43.2 4.0 %collective-permute-start.13 = (bf16[144,128]{1,0:T(8,128)(2,1)S(1)}, bf16[144,128]{1,0:T(8,128)(2,1)S(1)}, u32[]{:S(2)}, u32[]{:S(2)}) collective-permute-start(bf16[144,128]{1,0:T(8,128)(2,1)S(1)} %get-tuple-element.122.refs_0_), channel_id=1, source_target_pairs={{0,2},{1,3},{2,0},{3,1},{4,6},{5,7},{6,4},{7,5},{8,10},{9,11},{10,... | collective-permute-start | bytes 110600 | tf_op jit(solution)/shard_map/ppermute | solution.py:121
  59.5 4.8 %collective-permute-start.18 = (bf16[512,2048]{1,0:T(8,128)(2,1)S(1)}, bf16[512,2048]{1,0:T(8,128)(2,1)S(1)}, u32[]{:S(2)}, u32[]{:S(2)}) collective-permute-start(bf16[512,2048]{1,0:T(8,128)(2,1)S(1)} %shard_map.304.refs_11_.refs_9_.refs_8_), channel_id=1, source_target_pairs={{0,8},{1,9},{2,10},{3,11},{4,12},{5,13},{6,14},{7,15},{8,0},{9,1},... | collective-permute-start | bytes 6291464 | tf_op jit(solution)/shard_map/ppermute | solution.py:121
  59.6 4.0 %collective-permute-start.14 = (bf16[144,128]{1,0:T(8,128)(2,1)S(1)}, bf16[144,128]{1,0:T(8,128)(2,1)S(1)}, u32[]{:S(2)}, u32[]{:S(2)}) collective-permute-start(bf16[144,128]{1,0:T(8,128)(2,1)S(1)} %get-tuple-element.124.refs_0_), channel_id=1, source_target_pairs={{0,1},{1,0},{2,3},{3,2},{4,5},{5,4},{6,7},{7,6},{8,9},{9,8},{10,11... | collective-permute-start | bytes 110600 | tf_op jit(solution)/shard_map/ppermute | solution.py:121
  98.4 1.3 collective-permute-start.19
  101.5 9.7 %collective-permute-start.22 = (bf16[512,2048]{1,0:T(8,128)(2,1)S(1)}, bf16[512,2048]{1,0:T(8,128)(2,1)S(1)}, u32[]{:S(2)}, u32[]{:S(2)}) collective-permute-start(bf16[512,2048]{1,0:T(8,128)(2,1)S(1)} %get-tuple-element.157), channel_id=1, source_target_pairs={{0,8},{1,9},{2,10},{3,11},{4,12},{5,13},{6,14},{7,15},{8,0},{9,1},... | collective-permute-start | bytes 6291464 | tf_op jit(solution)/shard_map/ppermute | solution.py:121
  101.7 4.0 %collective-permute-start.20 = (bf16[144,128]{1,0:T(8,128)(2,1)S(1)}, bf16[144,128]{1,0:T(8,128)(2,1)S(1)}, u32[]{:S(2)}, u32[]{:S(2)}) collective-permute-start(bf16[144,128]{1,0:T(8,128)(2,1)S(1)} %get-tuple-element.142.refs_0_), channel_id=1, source_target_pairs={{0,2},{1,3},{2,0},{3,1},{4,6},{5,7},{6,4},{7,5},{8,10},{9,11},{10,... | collective-permute-start | bytes 110600 | tf_op jit(solution)/shard_map/ppermute | solution.py:121
  105.7 4.7 %collective-permute-start.21 = (bf16[144,128]{1,0:T(8,128)(2,1)S(1)}, bf16[144,128]{1,0:T(8,128)(2,1)S(1)}, u32[]{:S(2)}, u32[]{:S(2)}) collective-permute-start(bf16[144,128]{1,0:T(8,128)(2,1)S(1)} %get-tuple-element.153.refs_0_), channel_id=1, source_target_pairs={{0,1},{1,0},{2,3},{3,2},{4,5},{5,4},{6,7},{7,6},{8,9},{9,8},{10,11... | collective-permute-start | bytes 110600 | tf_op jit(solution)/shard_map/ppermute | solution.py:121
  111.6 12.8 %collective-permute-start.26 = (bf16[256,1024]{1,0:T(8,128)(2,1)S(1)}, bf16[256,1024]{1,0:T(8,128)(2,1)S(1)}, u32[]{:S(2)}, u32[]{:S(2)}) collective-permute-start(bf16[256,1024]{1,0:T(8,128)(2,1)S(1)} %get-tuple-element.167), channel_id=1, source_target_pairs={{0,16},{1,17},{2,18},{3,19},{4,20},{5,21},{6,22},{7,23},{8,24},{9,... | collective-permute-start | bytes 1572872 | tf_op jit(solution)/shard_map/ppermute | solution.py:121
  112.2 12.5 %collective-permute-start.27 = (bf16[256,1024]{1,0:T(8,128)(2,1)S(1)}, bf16[256,1024]{1,0:T(8,128)(2,1)S(1)}, u32[]{:S(2)}, u32[]{:S(2)}) collective-permute-start(bf16[256,1024]{1,0:T(8,128)(2,1)S(1)} %get-tuple-element.169), channel_id=1, source_target_pairs={{0,1},{1,0},{2,3},{3,2},{4,5},{5,4},{6,7},{7,6},{8,9},{9,8},{10,11... | collective-permute-start | bytes 1572872 | tf_op jit(solution)/shard_map/ppermute | solution.py:121
  123.3 10.3 %collective-permute-start.25 = (bf16[256,1280]{1,0:T(8,128)(2,1)S(1)}, bf16[256,1280]{1,0:T(8,128)(2,1)S(1)}, u32[]{:S(2)}, u32[]{:S(2)}) collective-permute-start(bf16[256,1280]{1,0:T(8,128)(2,1)S(1)} %get-tuple-element.166), channel_id=1, source_target_pairs={{0,8},{1,9},{2,10},{3,11},{4,12},{5,13},{6,14},{7,15},{8,0},{9,1},... | collective-permute-start | bytes 1966088 | tf_op jit(solution)/shard_map/ppermute | solution.py:121
  124.9 8.6 %collective-permute-start.28 = (bf16[128,1024]{1,0:T(8,128)(2,1)S(1)}, bf16[128,1024]{1,0:T(8,128)(2,1)S(1)}, u32[]{:S(2)}, u32[]{:S(2)}) collective-permute-start(bf16[128,1024]{1,0:T(8,128)(2,1)S(1)} %get-tuple-element.171), channel_id=1, source_target_pairs={{0,1},{1,0},{2,3},{3,2},{4,5},{5,4},{6,7},{7,6},{8,9},{9,8},{10,11... | collective-permute-start | bytes 786440 | tf_op jit(solution)/shard_map/ppermute | solution.py:121
  125.6 8.0 %collective-permute-start.29 = (bf16[128,1024]{1,0:T(8,128)(2,1)S(1)}, bf16[128,1024]{1,0:T(8,128)(2,1)S(1)}, u32[]{:S(2)}, u32[]{:S(2)}) collective-permute-start(bf16[128,1024]{1,0:T(8,128)(2,1)S(1)} %get-tuple-element.173), channel_id=1, source_target_pairs={{0,16},{1,17},{2,18},{3,19},{4,20},{5,21},{6,22},{7,23},{8,24},{9,... | collective-permute-start | bytes 786440 | tf_op jit(solution)/shard_map/ppermute | solution.py:121
  127.0 6.5 %collective-permute-start.24 = (bf16[16,512]{1,0:T(8,128)(2,1)S(1)}, bf16[16,512]{1,0:T(8,128)(2,1)S(1)}, u32[]{:S(2)}, u32[]{:S(2)}) collective-permute-start(bf16[16,512]{1,0:T(8,128)(2,1)S(1)} %get-tuple-element.164), channel_id=1, source_target_pairs={{8,0},{2,1},{10,2},{1,3},{9,4},{3,5},{11,6},{12,8},{6,9},{14,10},{... | collective-permute-start | bytes 49160 | tf_op jit(solution)/shard_map/ppermute | solution.py:849
  129.5 9.4 %collective-permute-start.23 = (bf16[256,512]{1,0:T(8,128)(2,1)S(1)}, bf16[256,512]{1,0:T(8,128)(2,1)S(1)}, u32[]{:S(2)}, u32[]{:S(2)}) collective-permute-start(bf16[256,512]{1,0:T(8,128)(2,1)S(1)} %get-tuple-element.163), channel_id=1, source_target_pairs={{0,0},{8,1},{2,2},{10,3},{1,4},{9,5},{3,6},{11,7},{4,8},{12,9},{6,... | collective-permute-start | bytes 786440 | tf_op jit(solution)/shard_map/ppermute | solution.py:848
  133.8 12.6 %collective-permute-start.33 = (bf16[64,2048]{1,0:T(8,128)(2,1)S(1)}, bf16[64,2048]{1,0:T(8,128)(2,1)S(1)}, u32[]{:S(2)}, u32[]{:S(2)}) collective-permute-start(bf16[64,2048]{1,0:T(8,128)(2,1)S(1)} %get-tuple-element.179), channel_id=1, source_target_pairs={{0,2},{1,3},{2,0},{3,1},{4,6},{5,7},{6,4},{7,5},{8,10},{9,11},{10,... | collective-permute-start | bytes 786440 | tf_op jit(solution)/shard_map/ppermute | solution.py:121
  135.5 6.7 %collective-permute-start.30 = (bf16[64,1280]{1,0:T(8,128)(2,1)S(1)}, bf16[64,1280]{1,0:T(8,128)(2,1)S(1)}, u32[]{:S(2)}, u32[]{:S(2)}) collective-permute-start(bf16[64,1280]{1,0:T(8,128)(2,1)S(1)} %get-tuple-element.175), channel_id=1, source_target_pairs={{0,1},{1,0},{2,3},{3,2},{4,5},{5,4},{6,7},{7,6},{8,9},{9,8},{10,11... | collective-permute-start | bytes 491528 | tf_op jit(solution)/shard_map/ppermute | solution.py:121
  135.5 7.0 %collective-permute-start.31 = (bf16[64,1280]{1,0:T(8,128)(2,1)S(1)}, bf16[64,1280]{1,0:T(8,128)(2,1)S(1)}, u32[]{:S(2)}, u32[]{:S(2)}) collective-permute-start(bf16[64,1280]{1,0:T(8,128)(2,1)S(1)} %get-tuple-element.176), channel_id=1, source_target_pairs={{0,16},{1,17},{2,18},{3,19},{4,20},{5,21},{6,22},{7,23},{8,24},{9,... | collective-permute-start | bytes 491528 | tf_op jit(solution)/shard_map/ppermute | solution.py:121
  136.5 9.9 %collective-permute-start.32 = (bf16[64,1280]{1,0:T(8,128)(2,1)S(1)}, bf16[64,1280]{1,0:T(8,128)(2,1)S(1)}, u32[]{:S(2)}, u32[]{:S(2)}) collective-permute-start(bf16[64,1280]{1,0:T(8,128)(2,1)S(1)} %get-tuple-element.177), channel_id=1, source_target_pairs={{0,17},{1,16},{2,19},{3,18},{4,21},{5,20},{6,23},{7,22},{8,25},{9,... | collective-permute-start | bytes 491528 | tf_op jit(solution)/shard_map/ppermute | solution.py:121
  146.5 12.5 %collective-permute-start.37 = (bf16[32,2048]{1,0:T(8,128)(2,1)S(1)}, bf16[32,2048]{1,0:T(8,128)(2,1)S(1)}, u32[]{:S(2)}, u32[]{:S(2)}) collective-permute-start(bf16[32,2048]{1,0:T(8,128)(2,1)S(1)} %get-tuple-element.185), channel_id=1, source_target_pairs={{0,4},{1,5},{2,6},{3,7},{4,0},{5,1},{6,2},{7,3},{8,12},{9,13},{10,... | collective-permute-start | bytes 393224 | tf_op jit(solution)/shard_map/ppermute | solution.py:121
  147.1 11.9 %collective-permute-start.34 = (bf16[16,1280]{1,0:T(8,128)(2,1)S(1)}, bf16[16,1280]{1,0:T(8,128)(2,1)S(1)}, u32[]{:S(2)}, u32[]{:S(2)}) collective-permute-start(bf16[16,1280]{1,0:T(8,128)(2,1)S(1)} %get-tuple-element.181), channel_id=1, source_target_pairs={{0,4},{1,5},{2,6},{3,7},{4,0},{5,1},{6,2},{7,3},{8,12},{9,13},{10,... | collective-permute-start | bytes 122888 | tf_op jit(solution)/shard_map/ppermute | solution.py:121
  149.5 9.5 %collective-permute-start.35 = (bf16[16,1280]{1,0:T(8,128)(2,1)S(1)}, bf16[16,1280]{1,0:T(8,128)(2,1)S(1)}, u32[]{:S(2)}, u32[]{:S(2)}) collective-permute-start(bf16[16,1280]{1,0:T(8,128)(2,1)S(1)} %get-tuple-element.182), channel_id=1, source_target_pairs={{0,2},{1,3},{2,0},{3,1},{4,6},{5,7},{6,4},{7,5},{8,10},{9,11},{10,... | collective-permute-start | bytes 122888 | tf_op jit(solution)/shard_map/ppermute | solution.py:121
  151.0 8.0 %collective-permute-start.36 = (bf16[16,1280]{1,0:T(8,128)(2,1)S(1)}, bf16[16,1280]{1,0:T(8,128)(2,1)S(1)}, u32[]{:S(2)}, u32[]{:S(2)}) collective-permute-start(bf16[16,1280]{1,0:T(8,128)(2,1)S(1)} %get-tuple-element.183), channel_id=1, source_target_pairs={{0,6},{1,7},{2,4},{3,5},{4,2},{5,3},{6,0},{7,1},{8,14},{9,15},{10,... | collective-permute-start | bytes 122888 | tf_op jit(solution)/shard_map/ppermute | solution.py:121

commit v6 on v5

--- a/solution.py
+++ b/solution.py
@@ -270,7 +270,7 @@
         return held, total + size
 
     zero = jnp.zeros((8, 128), F32)
-    held, total = lax.fori_loop(0, tokens, advance, ((zero,) * NS, zero), unroll=4)
+    held, total = lax.fori_loop(0, tokens, advance, ((zero,) * NS, zero), unroll=8)
     state[...] = jnp.concatenate([*held, total, zero], axis=0).astype(BF16)
 
 
@@ -292,15 +292,17 @@
     entry[...] = jnp.concatenate([*held, zero, zero], axis=0)
 
 
-def merge_kernel(plan, step, forward, own, other, before, a3, group, entry):
+def merge_kernel(plan, step, forward, own, other, before, a3, *outs):
     later = ((plan.chunk() >> step) & 1) == (1 if forward else 0)
     mine, theirs = own[...].astype(F32), other[...].astype(F32)
     first, second = jnp.where(later, theirs, mine), jnp.where(later, mine, theirs)
     decay = a3[...]
     spread_total = lambda value: jnp.concatenate([value[128:136, :]] * NS, axis=0)
-    joint = jnp.exp2(spread_total(second) * decay) * first[:128, :] + second[:128, :]
-    group[:128, :] = joint.astype(BF16)
-    group[128:, :] = (first[128:, :] + second[128:, :]).astype(BF16)
+    entry = outs[0]
+    for group in outs[1:]:
+        joint = jnp.exp2(spread_total(second) * decay) * first[:128, :] + second[:128, :]
+        group[:128, :] = joint.astype(BF16)
+        group[128:, :] = (first[128:, :] + second[128:, :]).astype(BF16)
     held = before[...]
     inner = held[:128, :] + jnp.exp2(spread_total(held) * decay) * theirs[:128, :]
     entry[:128, :] = jnp.where(later, inner, held[:128, :])
@@ -312,9 +314,10 @@
         group, entry, firsts = state, jnp.zeros((144, 128), F32), []
         for step in range(3):
             other = send(group, CHUNK_MASKS[1 << step])
-            group, entry = run(
+            entry, *more = run(
                 functools.partial(merge_kernel, plan, step, forward), [group, other, entry, a3],
-                [((144, 128), BF16), ((144, 128), F32)], after=beside(step, entry if step else group))
+                [((144, 128), F32)] + [((144, 128), BF16)] * (step < 2), after=beside(step, entry if step else group))
+            group = more[0] if more else None
             firsts.append(entry)
         return entry, firsts
     states = lax.all_gather(state, "ctx", axis=0, tiled=True)
@@ -348,7 +351,7 @@
         y3[pl.ds(pl.multiple_of(t * 8, 8), 8), :] = y
         return held
 
-    lax.fori_loop(0, tokens, advance, held, unroll=4)
+    lax.fori_loop(0, tokens, advance, held, unroll=8)
     act = gathered(au3, tokens)
     y = gathered(y3, tokens) + pm[ROW_SK : ROW_SK + 1, :] * act
     mamba[...] = y
@@ -441,7 +444,7 @@
         )
 
     zero = jnp.zeros((8, 128), F32)
-    carried = lax.fori_loop(0, tokens, retreat, (zero,) * NS, unroll=4)
+    carried = lax.fori_loop(0, tokens, retreat, (zero,) * NS, unroll=8)
     state[:128, :] = jnp.concatenate(carried, axis=0).astype(BF16)
     state[128:, :] = first[128:, :]
 
@@ -535,7 +538,7 @@
         ga3[at, :] = from_b * size + skip * grad
         return tuple(fresh), skipped + grad * value
 
-    _, skipped = lax.fori_loop(0, tokens, retreat, (carried, zero), unroll=4)
+    _, skipped = lax.fori_loop(0, tokens, retreat, (carried, zero), unroll=8)
 
     diagonal_sums(low_rank, RANK, lambda rows: dt3[rows, :] * au3[rows, :], grads, 0)
     low_rank[:, RANK + NS : RANK + 2 * NS] = grad_c[:, :NS]

time: 161 us -> 159 us (0.988)
  Pallas kernels: 35.7 us -> 33.6 us
    pallas_call x24, Pallas kernels: 35.7 us -> 33.6 us  [run(): pl.pallas_call(inner, out_shape=[jax.ShapeDtypeStruct(shape, dtype) for s...]
  transfers between devices with their start and end apart: 38 -> 38, of which waited for: 15 -> 15; matrix products, arithmetic and copies ran while one was open for 0% -> 0% of each run, Pallas kernels for 12% -> 11%
where the time goes in v6:
time: 159 us; the launch traced here: 158 us
  waiting for transfers between devices  53.9 us (34%)
  starting transfers between devices  42.9 us (27%)
  Pallas kernels  33.6 us (21%)
  blocking collectives  23.5 us (15%)
  local copies, waits for them, and re-layouts  3.31 us (2%)
    ppermute x33, waiting for transfers between devices, send(): return lax.ppermute(value, ALL, [(i, i ^ mask) for i in range(32)])  42.4 us
    pallas_call x24, Pallas kernels, run(): pl.pallas_call(inner, out_shape=[jax.ShapeDtypeStruct(shape, dtype) for s...  33.6 us
    ppermute x33, starting transfers between devices, send(): return lax.ppermute(value, ALL, [(i, i ^ mask) for i in range(32)])  30.2 us
    all_to_all x2, blocking collectives, swap(): lax.all_to_all(value, ALL, 0, 0, tiled=True, axis_index_groups=groups)  23.5 us
    ppermute x1, waiting for transfers between devices, body(): tok = lax.ppermute(tok, ALL, home)  8.14 us
    ppermute x1, starting transfers between devices, body(): lax.ppermute(tok0[count - HALO:], ALL, [(s * 8 + c, plan.place(s, c + 1))...  4.32 us
  transfers between devices with their start and end apart: 38, of which 15 were waited for; matrix products, arithmetic and copies ran while one was open for 0% of the time, Pallas kernels for 11%

profile of v6, /device:TPU:6, one launch (start us, length us, event | category | flops | bytes accessed | tf_op | source)
XLA Modules:
  0.0 158.4 jit_solution(7960708029916269729)
XLA Ops:
  0.7 2.0 %shard_map.296 = (bf16[16,1280]{1,0:T(8,128)(2,1)}, bf16[32,2048]{1,0:T(8,128)(2,1)}) custom-call(f32[16,2048]{1,0:T(8,128)} %refs_0_.1, f32[32,64]{1,0:T(8,128)} %refs_1_.1, f32[32,32]{1,0:T(8,128)} %refs_2_.1, f32[16,32]{1,0:T(8,128)} %bitcast.29, f32[4,32]{1,0:T(4,128)} %bitcast.30, f32[1,32]{1,0:T(1,128)} %bitcast.31, f32[1,32]{1,0:T(1,128)} %bitcast.32, ...), custom_call_target="tpu_custom_call" | custom-call | flops 2000 | bytes 6000 | tf_op jit(solution)/shard_map/pallas_call | solution.py:59
  2.7 2.7 %collective-permute-start = (bf16[16,1280]{1,0:T(8,128)(2,1)}, bf16[16,1280]{1,0:T(8,128)(2,1)S(1)}, u32[]{:S(2)}, u32[]{:S(2)}) collective-permute-start(bf16[16,1280]{1,0:T(8,128)(2,1)} %get-tuple-element.108.refs_0_), channel_id=1, source_target_pairs={{0,4},{1,5},{2,6},{3,7},{4,0},{5,1},{6,2},{7,3},{8,12},{9,13},{10,... | collective-permute-start | bytes 122888 | tf_op jit(solution)/shard_map/ppermute | solution.py:121
  5.3 1.6 collective-permute-start.1
  7.1 1.7 %collective-permute-start.8 = (bf16[32,2048]{1,0:T(8,128)(2,1)}, bf16[32,2048]{1,0:T(8,128)(2,1)S(1)}, u32[]{:S(2)}, u32[]{:S(2)}) collective-permute-start(bf16[32,2048]{1,0:T(8,128)(2,1)} %get-tuple-element.111.refs_0_), channel_id=1, source_target_pairs={{0,4},{1,5},{2,6},{3,7},{4,0},{5,1},{6,2},{7,3},{8,12},{9,13},{10,... | collective-permute-start | bytes 393224 | tf_op jit(solution)/shard_map/ppermute | solution.py:121
  8.8 0.7 slice_bitcast_fusion
  9.5 4.3 %collective-permute-start.4 = (bf16[16,512]{1,0:T(8,128)(2,1)S(1)}, bf16[16,512]{1,0:T(8,128)(2,1)S(1)}, u32[]{:S(2)}, u32[]{:S(2)}) collective-permute-start(bf16[16,512]{1,0:T(8,128)(2,1)S(1)} %slice_bitcast_fusion), channel_id=1, source_target_pairs={{0,8},{1,2},{2,10},{3,1},{4,9},{5,3},{6,11},{8,12},{9,6},{10,14},{... | collective-permute-start | bytes 49160 | tf_op jit(solution)/shard_map/ppermute | solution.py:731
  13.9 0.9 copy-done
  14.8 0.8 copy-done.2
  15.6 1.4 collective-permute-done.4.refs_3_.refs_1_
  17.0 0.9 copy-done.1
  18.6 1.4 collective-permute-start.5
  20.5 1.5 collective-permute-start.7
  22.1 1.9 %collective-permute-start.3 = (bf16[128,512]{1,0:T(8,128)(2,1)S(1)}, bf16[128,512]{1,0:T(8,128)(2,1)S(1)}, u32[]{:S(2)}, u32[]{:S(2)}) collective-permute-start(bf16[128,512]{1,0:T(8,128)(2,1)S(1)} %get-tuple-element.109), channel_id=1, source_target_pairs={{0,0},{1,8},{2,2},{3,10},{4,1},{5,9},{6,3},{7,11},{8,4},{9,12},{10... | collective-permute-start | bytes 393224 | tf_op jit(solution)/shard_map/ppermute | solution.py:741
  24.0 8.1 %collective-permute-done.3.refs_6_.refs_0_ = bf16[128,512]{1,0:T(8,128)(2,1)S(1)} collective-permute-done((bf16[128,512]{1,0:T(8,128)(2,1)S(1)}, bf16[128,512]{1,0:T(8,128)(2,1)S(1)}, u32[]{:S(2)}, u32[]{:S(2)}) %collective-permute-start.3) | collective-permute-done | bytes 131104 | tf_op jit(solution)/shard_map/ppermute | solution.py:741
  33.0 2.9 %collective-permute-start.17 = (bf16[128,2048]{1,0:T(8,128)(2,1)S(1)}, bf16[128,2048]{1,0:T(8,128)(2,1)S(1)}, u32[]{:S(2)}, u32[]{:S(2)}) collective-permute-start(bf16[128,2048]{1,0:T(8,128)(2,1)S(1)} %get-tuple-element.126.refs_0_), channel_id=1, source_target_pairs={{0,17},{1,16},{2,19},{3,18},{4,21},{5,20},{6,23},{7,22},{8,25},{9,... | collective-permute-start | bytes 1572872 | tf_op jit(solution)/shard_map/ppermute | solution.py:121
  35.9 1.9 %collective-permute-start.11 = (bf16[128,512]{1,0:T(8,128)(2,1)S(1)}, bf16[128,512]{1,0:T(8,128)(2,1)S(1)}, u32[]{:S(2)}, u32[]{:S(2)}) collective-permute-start(bf16[128,512]{1,0:T(8,128)(2,1)S(1)} %bitcast.36), channel_id=1, source_target_pairs={{0,0},{1,8},{2,2},{3,10},{4,1},{5,9},{6,3},{7,11},{8,4},{9,12},{10... | collective-permute-start | bytes 393224 | tf_op jit(solution)/shard_map/ppermute | solution.py:744
  37.8 3.8 %shard_map.300 = (bf16[144,512]{1,0:T(8,128)(2,1)S(1)}, bf16[144,512]{1,0:T(8,128)(2,1)S(1)}, f32[144,1024]{1,0:T(8,128)S(1)}, f32[128,1024]{1,0:T(8,128)S(1)}, ...) custom-call(bf16[128,512]{1,0:T(8,128)(2,1)S(1)} %collective-permute, ...), custom_call_target="tpu_custom_call" | custom-call | flops 6000 | bytes 18000 | tf_op jit(solution)/shard_map/pallas_call | solution.py:59
  41.7 1.2 collective-permute-done.12.refs_1_
  43.1 3.9 %collective-permute-done.13.refs_1_ = bf16[144,128]{1,0:T(8,128)(2,1)S(1)} collective-permute-done((bf16[144,128]{1,0:T(8,128)(2,1)S(1)}, bf16[144,128]{1,0:T(8,128)(2,1)S(1)}, u32[]{:S(2)}, u32[]{:S(2)}) %collective-permute-start.13) | collective-permute-done | bytes 36896 | tf_op jit(solution)/shard_map/ppermute | solution.py:121
  47.0 12.3 %collective-permute-done.15.refs_1_ = bf16[128,2048]{1,0:T(8,128)(2,1)S(1)} collective-permute-done((bf16[128,2048]{1,0:T(8,128)(2,1)S(1)}, bf16[128,2048]{1,0:T(8,128)(2,1)S(1)}, u32[]{:S(2)}, u32[]{:S(2)}) %collective-permute-start.15) | collective-permute-done | bytes 524320 | tf_op jit(solution)/shard_map/ppermute | solution.py:121
  59.8 3.8 %collective-permute-done.14.refs_1_ = bf16[144,128]{1,0:T(8,128)(2,1)S(1)} collective-permute-done((bf16[144,128]{1,0:T(8,128)(2,1)S(1)}, bf16[144,128]{1,0:T(8,128)(2,1)S(1)}, u32[]{:S(2)}, u32[]{:S(2)}) %collective-permute-start.14) | collective-permute-done | bytes 36896 | tf_op jit(solution)/shard_map/ppermute | solution.py:121
  63.8 3.6 %shard_map.305 = (bf16[1024,256]{1,0:T(8,128)(2,1)S(1)}, f32[128,1024]{1,0:T(8,128)S(1)}, bf16[128,1024]{1,0:T(8,128)(2,1)S(1)}, f32[128,512]{1,0:T(8,128)S(1)},...) custom-call(bf16[128,512]{1,0:T(8,128)(2,1)S(1)} %collective-permute-done.3.refs_6_.refs_0_, ...), custom_call_target="tpu_custom_call" | custom-call | flops 6000 | bytes 18000 | tf_op jit(solution)/shard_map/pallas_call | solution.py:59
  67.4 11.4 %all_to_all.22 = bf16[8,128,256]{2,1,0:T(8,128)(2,1)S(1)} all-to-all(bf16[8,128,256]{2,1,0:T(8,128)(2,1)S(1)} %bitcast.27), channel_id=1, replica_groups={{0,8,2,10,1,9,3,11},{4,12,6,14,5,13,7,15},{16,24,18,26,17,25,19,27},{20..., dimensions={0} | all-to-all | bytes 1048576 | tf_op jit(solution)/shard_map/all_to_all | solution.py:116
  78.8 3.6 %shard_map.306 = bf16[1024,256]{1,0:T(8,128)(2,1)S(1)} custom-call(bf16[1024,256]{1,0:T(8,128)(2,1)S(1)} %bitcast.25), custom_call_target="tpu_custom_call" | custom-call | flops 4000 | bytes 12000 | tf_op jit(solution)/shard_map/pallas_call | solution.py:59
  82.4 12.1 %all_to_all.23 = bf16[8,128,256]{2,1,0:T(8,128)(2,1)S(1)} all-to-all(bf16[8,128,256]{2,1,0:T(8,128)(2,1)S(1)} %bitcast.26), channel_id=1, replica_groups={{0,8,2,10,1,9,3,11},{4,12,6,14,5,13,7,15},{16,24,18,26,17,25,19,27},{20..., dimensions={0} | all-to-all | bytes 1048576 | tf_op jit(solution)/shard_map/all_to_all | solution.py:116
  94.5 3.0 %shard_map.307 = (bf16[128,512]{1,0:T(8,128)(2,1)S(1)}, bf16[128,512]{1,0:T(8,128)(2,1)S(1)}, bf16[128,512]{1,0:T(8,128)(2,1)S(1)}, bf16[128,512]{1,0:T(8,128)(2...) custom-call(bf16[1024,256]{1,0:T(8,128)(2,1)S(1)} %bitcast.24, ...), custom_call_target="tpu_custom_call" | custom-call | flops 2000 | bytes 6000 | tf_op jit(solution)/shard_map/pallas_call | solution.py:59
  97.6 1.2 collective-permute-done.19.refs_1_
  98.9 1.7 %shard_map.309 = (bf16[128,512]{1,0:T(8,128)(2,1)S(1)}, bf16[512,2048]{1,0:T(8,128)(2,1)S(1)}, bf16[512,2048]{1,0:T(8,128)(2,1)S(1)}) custom-call(bf16[128,512]{1,0:T(8,128)(2,1)S(1)} %get-tuple-element.141.refs_0_, bf16[128,512]{1,0:T(8,128)(2,1)S(1)} %get-tuple-element.142.refs_1_, bf16[128,512]{1,0:T(8,128)(2,1)S(1)} %get-tuple-element.143.refs_2_, ...), custom_call_target="tpu_custom_call" | custom-call | flops 2000 | bytes 6000 | tf_op jit(solution)/shard_map/pallas_call | solution.py:59
  101.3 3.4 %collective-permute-done.20.refs_1_ = bf16[144,128]{1,0:T(8,128)(2,1)S(1)} collective-permute-done((bf16[144,128]{1,0:T(8,128)(2,1)S(1)}, bf16[144,128]{1,0:T(8,128)(2,1)S(1)}, u32[]{:S(2)}, u32[]{:S(2)}) %collective-permute-start.20) | collective-permute-done | bytes 36896 | tf_op jit(solution)/shard_map/ppermute | solution.py:121
  104.8 1.5 collective-permute-start.21
  106.3 3.2 %shard_map.311.refs_4_.refs_14_ = f32[128,128]{1,0:T(8,128)S(1)} custom-call(f32[1024,128]{1,0:T(8,128)S(1)} %get-tuple-element.131.refs_0_.refs_2_, f32[16512,128]{1,0:T(8,128)S(1)} %get-tuple-element.133.refs_1_.refs_6_, f32[144,128]{1,0:T(8,128)S(1)} %get-tuple-element.151.refs_2_), custom_call_target="tpu_custom_call" | custom-call | flops 2000 | bytes 6000 | tf_op jit(solution)/shard_map/pallas_call | solution.py:59
  110.7 0.7 collective-permute-start.27
  111.4 8.2 %shard_map.314 = (f32[128,1024]{1,0:T(8,128)S(1)}, bf16[144,1024]{1,0:T(8,128)(2,1)S(1)}) custom-call(f32[1024,128]{1,0:T(8,128)S(1)} %get-tuple-element.114.refs_1_.refs_6_.refs_0_, f32[1024,128]{1,0:T(8,128)S(1)} %get-tuple-element.115.refs_2_.refs_1_, f32[1024,128]{1,0:T(8,128)S(1)} %get-tuple-element.131.refs_0_.refs_2_, ...), custom_call_target="tpu_custom_call" | custom-call | flops 11000 | bytes 33000 | tf_op jit(solution)/shard_map/pallas_call | solution.py:59
  119.6 1.8 %shard_map.315 = (bf16[256,1280]{1,0:T(8,128)(2,1)S(1)}, bf16[256,1280]{1,0:T(8,128)(2,1)S(1)}, bf16[256,512]{1,0:T(8,128)(2,1)S(1)}, bf16[16,512]{1,0:T(8,128)(2,1)S(1)}) custom-call(bf16[128,512]{1,0:T(8,128)(2,1)S(1)} %collective-permute-done.3.refs_6_.refs_0_, bf16[16,512]{1,0:T(8,128)(2,1)S(1)} %collective-permute-done.4.refs_3_.refs_1_, ...), custom_call_target="tpu_custom_call" | custom-call | flops 2000 | bytes 6000 | tf_op jit(solution)/shard_map/pallas_call | solution.py:59
  121.6 1.3 collective-permute-done.26.refs_1_
  124.0 1.5 collective-permute-start.29
  125.5 2.5 %collective-permute-start.24 = (bf16[16,512]{1,0:T(8,128)(2,1)S(1)}, bf16[16,512]{1,0:T(8,128)(2,1)S(1)}, u32[]{:S(2)}, u32[]{:S(2)}) collective-permute-start(bf16[16,512]{1,0:T(8,128)(2,1)S(1)} %get-tuple-element.160), channel_id=1, source_target_pairs={{8,0},{2,1},{10,2},{1,3},{9,4},{3,5},{11,6},{12,8},{6,9},{14,10},{... | collective-permute-start | bytes 49160 | tf_op jit(solution)/shard_map/ppermute | solution.py:852
  128.0 2.1 %collective-permute-start.23 = (bf16[256,512]{1,0:T(8,128)(2,1)S(1)}, bf16[256,512]{1,0:T(8,128)(2,1)S(1)}, u32[]{:S(2)}, u32[]{:S(2)}) collective-permute-start(bf16[256,512]{1,0:T(8,128)(2,1)S(1)} %get-tuple-element.159), channel_id=1, source_target_pairs={{0,0},{8,1},{2,2},{10,3},{1,4},{9,5},{3,6},{11,7},{4,8},{12,9},{6,... | collective-permute-start | bytes 786440 | tf_op jit(solution)/shard_map/ppermute | solution.py:851
  130.0 2.0 %collective-permute-done.24.refs_6_.refs_1_ = bf16[16,512]{1,0:T(8,128)(2,1)S(1)} collective-permute-done((bf16[16,512]{1,0:T(8,128)(2,1)S(1)}, bf16[16,512]{1,0:T(8,128)(2,1)S(1)}, u32[]{:S(2)}, u32[]{:S(2)}) %collective-permute-start.24) | collective-permute-done | bytes 16416 | tf_op jit(solution)/shard_map/ppermute | solution.py:852
  132.3 1.4 collective-permute-start.33
  133.7 1.0 collective-permute-start.31
  134.7 2.5 %collective-permute-start.32 = (bf16[64,1280]{1,0:T(8,128)(2,1)S(1)}, bf16[64,1280]{1,0:T(8,128)(2,1)S(1)}, u32[]{:S(2)}, u32[]{:S(2)}) collective-permute-start(bf16[64,1280]{1,0:T(8,128)(2,1)S(1)} %get-tuple-element.173), channel_id=1, source_target_pairs={{0,17},{1,16},{2,19},{3,18},{4,21},{5,20},{6,23},{7,22},{8,25},{9,... | collective-permute-start | bytes 491528 | tf_op jit(solution)/shard_map/ppermute | solution.py:121
  137.2 3.7 %collective-permute-done.30.refs_1_ = bf16[64,1280]{1,0:T(8,128)(2,1)S(1)} collective-permute-done((bf16[64,1280]{1,0:T(8,128)(2,1)S(1)}, bf16[64,1280]{1,0:T(8,128)(2,1)S(1)}, u32[]{:S(2)}, u32[]{:S(2)}) %collective-permute-start.30) | collective-permute-done | bytes 163872 | tf_op jit(solution)/shard_map/ppermute | solution.py:121
  140.9 3.7 %collective-permute-done.32.refs_3_ = bf16[64,1280]{1,0:T(8,128)(2,1)S(1)} collective-permute-done((bf16[64,1280]{1,0:T(8,128)(2,1)S(1)}, bf16[64,1280]{1,0:T(8,128)(2,1)S(1)}, u32[]{:S(2)}, u32[]{:S(2)}) %collective-permute-start.32) | collective-permute-done | bytes 163872 | tf_op jit(solution)/shard_map/ppermute | solution.py:121
  145.4 2.4 %collective-permute-start.34 = (bf16[16,1280]{1,0:T(8,128)(2,1)S(1)}, bf16[16,1280]{1,0:T(8,128)(2,1)S(1)}, u32[]{:S(2)}, u32[]{:S(2)}) collective-permute-start(bf16[16,1280]{1,0:T(8,128)(2,1)S(1)} %get-tuple-element.177), channel_id=1, source_target_pairs={{0,4},{1,5},{2,6},{3,7},{4,0},{5,1},{6,2},{7,3},{8,12},{9,13},{10,... | collective-permute-start | bytes 122888 | tf_op jit(solution)/shard_map/ppermute | solution.py:121
  147.8 1.6 collective-permute-start.35
  149.7 7.5 %collective-permute-done.34.refs_3_ = bf16[16,1280]{1,0:T(8,128)(2,1)S(1)} collective-permute-done((bf16[16,1280]{1,0:T(8,128)(2,1)S(1)}, bf16[16,1280]{1,0:T(8,128)(2,1)S(1)}, u32[]{:S(2)}, u32[]{:S(2)}) %collective-permute-start.34) | collective-permute-done | bytes 40992 | tf_op jit(solution)/shard_map/ppermute | solution.py:121
  157.3 0.9 shard_map.319
  (64 shorter events, 7.9 us)
Async XLA Ops:
  0.7 35.2 %copy-start.3 = (bf16[1,128,512]{2,1,0:T(8,128)(2,1)S(1)}, bf16[1,128,512]{2,1,0:T(8,128)(2,1)}, u32[]{:S(2)}) copy-start(bf16[1,128,512]{2,1,0:T(8,128)(2,1)} %param.33) | copy-start | bytes 393220
  2.7 11.2 %collective-permute-start = (bf16[16,1280]{1,0:T(8,128)(2,1)}, bf16[16,1280]{1,0:T(8,128)(2,1)S(1)}, u32[]{:S(2)}, u32[]{:S(2)}) collective-permute-start(bf16[16,1280]{1,0:T(8,128)(2,1)} %get-tuple-element.108.refs_0_), channel_id=1, source_target_pairs={{0,4},{1,5},{2,6},{3,7},{4,0},{5,1},{6,2},{7,3},{8,12},{9,13},{10,... | collective-permute-start | bytes 122888 | tf_op jit(solution)/shard_map/ppermute | solution.py:121
  5.3 8.5 %collective-permute-start.1 = (bf16[16,1280]{1,0:T(8,128)(2,1)}, bf16[16,1280]{1,0:T(8,128)(2,1)S(1)}, u32[]{:S(2)}, u32[]{:S(2)}) collective-permute-start(bf16[16,1280]{1,0:T(8,128)(2,1)} %get-tuple-element.108.refs_0_), channel_id=1, source_target_pairs={{0,2},{1,3},{2,0},{3,1},{4,6},{5,7},{6,4},{7,5},{8,10},{9,11},{10,... | collective-permute-start | bytes 122888 | tf_op jit(solution)/shard_map/ppermute | solution.py:121
  6.9 7.0 %collective-permute-start.2 = (bf16[16,1280]{1,0:T(8,128)(2,1)}, bf16[16,1280]{1,0:T(8,128)(2,1)S(1)}, u32[]{:S(2)}, u32[]{:S(2)}) collective-permute-start(bf16[16,1280]{1,0:T(8,128)(2,1)} %get-tuple-element.108.refs_0_), channel_id=1, source_target_pairs={{0,6},{1,7},{2,4},{3,5},{4,2},{5,3},{6,0},{7,1},{8,14},{9,15},{10,... | collective-permute-start | bytes 122888 | tf_op jit(solution)/shard_map/ppermute | solution.py:121
  7.1 9.9 %collective-permute-start.8 = (bf16[32,2048]{1,0:T(8,128)(2,1)}, bf16[32,2048]{1,0:T(8,128)(2,1)S(1)}, u32[]{:S(2)}, u32[]{:S(2)}) collective-permute-start(bf16[32,2048]{1,0:T(8,128)(2,1)} %get-tuple-element.111.refs_0_), channel_id=1, source_target_pairs={{0,4},{1,5},{2,6},{3,7},{4,0},{5,1},{6,2},{7,3},{8,12},{9,13},{10,... | collective-permute-start | bytes 393224 | tf_op jit(solution)/shard_map/ppermute | solution.py:121
  9.5 7.5 %collective-permute-start.4 = (bf16[16,512]{1,0:T(8,128)(2,1)S(1)}, bf16[16,512]{1,0:T(8,128)(2,1)S(1)}, u32[]{:S(2)}, u32[]{:S(2)}) collective-permute-start(bf16[16,512]{1,0:T(8,128)(2,1)S(1)} %slice_bitcast_fusion), channel_id=1, source_target_pairs={{0,8},{1,2},{2,10},{3,1},{4,9},{5,3},{6,11},{8,12},{9,6},{10,14},{... | collective-permute-start | bytes 49160 | tf_op jit(solution)/shard_map/ppermute | solution.py:731
  13.9 0.9 copy-start
  14.8 0.8 copy-start.2
  17.0 0.9 copy-start.1
  17.9 14.3 %collective-permute-start.9 = (bf16[64,2048]{1,0:T(8,128)(2,1)S(1)}, bf16[64,2048]{1,0:T(8,128)(2,1)S(1)}, u32[]{:S(2)}, u32[]{:S(2)}) collective-permute-start(bf16[64,2048]{1,0:T(8,128)(2,1)S(1)} %shard_map.298.refs_4_), channel_id=1, source_target_pairs={{0,2},{1,3},{2,0},{3,1},{4,6},{5,7},{6,4},{7,5},{8,10},{9,11},{10,... | collective-permute-start | bytes 786440 | tf_op jit(solution)/shard_map/ppermute | solution.py:121
  18.6 13.5 %collective-permute-start.5 = (bf16[64,1280]{1,0:T(8,128)(2,1)S(1)}, bf16[64,1280]{1,0:T(8,128)(2,1)S(1)}, u32[]{:S(2)}, u32[]{:S(2)}) collective-permute-start(bf16[64,1280]{1,0:T(8,128)(2,1)S(1)} %get-tuple-element.110.refs_2_.refs_0_), channel_id=1, source_target_pairs={{0,1},{1,0},{2,3},{3,2},{4,5},{5,4},{6,7},{7,6},{8,9},{9,8},{10,11... | collective-permute-start | bytes 491528 | tf_op jit(solution)/shard_map/ppermute | solution.py:121
  20.0 12.1 %collective-permute-start.6 = (bf16[64,1280]{1,0:T(8,128)(2,1)S(1)}, bf16[64,1280]{1,0:T(8,128)(2,1)S(1)}, u32[]{:S(2)}, u32[]{:S(2)}) collective-permute-start(bf16[64,1280]{1,0:T(8,128)(2,1)S(1)} %get-tuple-element.110.refs_2_.refs_0_), channel_id=1, source_target_pairs={{0,16},{1,17},{2,18},{3,19},{4,20},{5,21},{6,22},{7,23},{8,24},{9,... | collective-permute-start | bytes 491528 | tf_op jit(solution)/shard_map/ppermute | solution.py:121
  20.5 11.6 %collective-permute-start.7 = (bf16[64,1280]{1,0:T(8,128)(2,1)S(1)}, bf16[64,1280]{1,0:T(8,128)(2,1)S(1)}, u32[]{:S(2)}, u32[]{:S(2)}) collective-permute-start(bf16[64,1280]{1,0:T(8,128)(2,1)S(1)} %get-tuple-element.110.refs_2_.refs_0_), channel_id=1, source_target_pairs={{0,17},{1,16},{2,19},{3,18},{4,21},{5,20},{6,23},{7,22},{8,25},{9,... | collective-permute-start | bytes 491528 | tf_op jit(solution)/shard_map/ppermute | solution.py:121
  22.1 10.1 %collective-permute-start.3 = (bf16[128,512]{1,0:T(8,128)(2,1)S(1)}, bf16[128,512]{1,0:T(8,128)(2,1)S(1)}, u32[]{:S(2)}, u32[]{:S(2)}) collective-permute-start(bf16[128,512]{1,0:T(8,128)(2,1)S(1)} %get-tuple-element.109), channel_id=1, source_target_pairs={{0,0},{1,8},{2,2},{3,10},{4,1},{5,9},{6,3},{7,11},{8,4},{9,12},{10... | collective-permute-start | bytes 393224 | tf_op jit(solution)/shard_map/ppermute | solution.py:741
  32.3 5.6 %collective-permute-start.10 = (bf16[256,1280]{1,0:T(8,128)(2,1)S(1)}, bf16[256,1280]{1,0:T(8,128)(2,1)S(1)}, u32[]{:S(2)}, u32[]{:S(2)}) collective-permute-start(bf16[256,1280]{1,0:T(8,128)(2,1)S(1)} %get-tuple-element.112.refs_2_.refs_6_), channel_id=1, source_target_pairs={{0,8},{1,9},{2,10},{3,11},{4,12},{5,13},{6,14},{7,15},{8,0},{9,1},... | collective-permute-start | bytes 1966088 | tf_op jit(solution)/shard_map/ppermute | solution.py:121
  32.4 27.0 %collective-permute-start.15 = (bf16[128,2048]{1,0:T(8,128)(2,1)S(1)}, bf16[128,2048]{1,0:T(8,128)(2,1)S(1)}, u32[]{:S(2)}, u32[]{:S(2)}) collective-permute-start(bf16[128,2048]{1,0:T(8,128)(2,1)S(1)} %get-tuple-element.126.refs_0_), channel_id=1, source_target_pairs={{0,1},{1,0},{2,3},{3,2},{4,5},{5,4},{6,7},{7,6},{8,9},{9,8},{10,11... | collective-permute-start | bytes 1572872 | tf_op jit(solution)/shard_map/ppermute | solution.py:121
  32.4 26.9 %collective-permute-start.16 = (bf16[128,2048]{1,0:T(8,128)(2,1)S(1)}, bf16[128,2048]{1,0:T(8,128)(2,1)S(1)}, u32[]{:S(2)}, u32[]{:S(2)}) collective-permute-start(bf16[128,2048]{1,0:T(8,128)(2,1)S(1)} %get-tuple-element.126.refs_0_), channel_id=1, source_target_pairs={{0,16},{1,17},{2,18},{3,19},{4,20},{5,21},{6,22},{7,23},{8,24},{9,... | collective-permute-start | bytes 1572872 | tf_op jit(solution)/shard_map/ppermute | solution.py:121
  33.0 26.3 %collective-permute-start.17 = (bf16[128,2048]{1,0:T(8,128)(2,1)S(1)}, bf16[128,2048]{1,0:T(8,128)(2,1)S(1)}, u32[]{:S(2)}, u32[]{:S(2)}) collective-permute-start(bf16[128,2048]{1,0:T(8,128)(2,1)S(1)} %get-tuple-element.126.refs_0_), channel_id=1, source_target_pairs={{0,17},{1,16},{2,19},{3,18},{4,21},{5,20},{6,23},{7,22},{8,25},{9,... | collective-permute-start | bytes 1572872 | tf_op jit(solution)/shard_map/ppermute | solution.py:121
  35.9 11.1 %collective-permute-start.11 = (bf16[128,512]{1,0:T(8,128)(2,1)S(1)}, bf16[128,512]{1,0:T(8,128)(2,1)S(1)}, u32[]{:S(2)}, u32[]{:S(2)}) collective-permute-start(bf16[128,512]{1,0:T(8,128)(2,1)S(1)} %bitcast.36), channel_id=1, source_target_pairs={{0,0},{1,8},{2,2},{3,10},{4,1},{5,9},{6,3},{7,11},{8,4},{9,12},{10... | collective-permute-start | bytes 393224 | tf_op jit(solution)/shard_map/ppermute | solution.py:744
  41.6 1.3 collective-permute-start.12
  43.0 4.0 %collective-permute-start.13 = (bf16[144,128]{1,0:T(8,128)(2,1)S(1)}, bf16[144,128]{1,0:T(8,128)(2,1)S(1)}, u32[]{:S(2)}, u32[]{:S(2)}) collective-permute-start(bf16[144,128]{1,0:T(8,128)(2,1)S(1)} %get-tuple-element.120.refs_0_), channel_id=1, source_target_pairs={{0,2},{1,3},{2,0},{3,1},{4,6},{5,7},{6,4},{7,5},{8,10},{9,11},{10,... | collective-permute-start | bytes 110600 | tf_op jit(solution)/shard_map/ppermute | solution.py:121
  59.5 4.2 %collective-permute-start.18 = (bf16[512,2048]{1,0:T(8,128)(2,1)S(1)}, bf16[512,2048]{1,0:T(8,128)(2,1)S(1)}, u32[]{:S(2)}, u32[]{:S(2)}) collective-permute-start(bf16[512,2048]{1,0:T(8,128)(2,1)S(1)} %shard_map.304.refs_11_.refs_9_.refs_8_), channel_id=1, source_target_pairs={{0,8},{1,9},{2,10},{3,11},{4,12},{5,13},{6,14},{7,15},{8,0},{9,1},... | collective-permute-start | bytes 6291464 | tf_op jit(solution)/shard_map/ppermute | solution.py:121
  59.6 4.0 %collective-permute-start.14 = (bf16[144,128]{1,0:T(8,128)(2,1)S(1)}, bf16[144,128]{1,0:T(8,128)(2,1)S(1)}, u32[]{:S(2)}, u32[]{:S(2)}) collective-permute-start(bf16[144,128]{1,0:T(8,128)(2,1)S(1)} %get-tuple-element.122.refs_0_), channel_id=1, source_target_pairs={{0,1},{1,0},{2,3},{3,2},{4,5},{5,4},{6,7},{7,6},{8,9},{9,8},{10,11... | collective-permute-start | bytes 110600 | tf_op jit(solution)/shard_map/ppermute | solution.py:121
  97.5 1.3 collective-permute-start.19
  100.5 9.0 %collective-permute-start.22 = (bf16[512,2048]{1,0:T(8,128)(2,1)S(1)}, bf16[512,2048]{1,0:T(8,128)(2,1)S(1)}, u32[]{:S(2)}, u32[]{:S(2)}) collective-permute-start(bf16[512,2048]{1,0:T(8,128)(2,1)S(1)} %get-tuple-element.153), channel_id=1, source_target_pairs={{0,8},{1,9},{2,10},{3,11},{4,12},{5,13},{6,14},{7,15},{8,0},{9,1},... | collective-permute-start | bytes 6291464 | tf_op jit(solution)/shard_map/ppermute | solution.py:121
  100.8 4.0 %collective-permute-start.20 = (bf16[144,128]{1,0:T(8,128)(2,1)S(1)}, bf16[144,128]{1,0:T(8,128)(2,1)S(1)}, u32[]{:S(2)}, u32[]{:S(2)}) collective-permute-start(bf16[144,128]{1,0:T(8,128)(2,1)S(1)} %get-tuple-element.139.refs_0_), channel_id=1, source_target_pairs={{0,2},{1,3},{2,0},{3,1},{4,6},{5,7},{6,4},{7,5},{8,10},{9,11},{10,... | collective-permute-start | bytes 110600 | tf_op jit(solution)/shard_map/ppermute | solution.py:121
  104.8 4.7 %collective-permute-start.21 = (bf16[144,128]{1,0:T(8,128)(2,1)S(1)}, bf16[144,128]{1,0:T(8,128)(2,1)S(1)}, u32[]{:S(2)}, u32[]{:S(2)}) collective-permute-start(bf16[144,128]{1,0:T(8,128)(2,1)S(1)} %get-tuple-element.150.refs_0_), channel_id=1, source_target_pairs={{0,1},{1,0},{2,3},{3,2},{4,5},{5,4},{6,7},{7,6},{8,9},{9,8},{10,11... | collective-permute-start | bytes 110600 | tf_op jit(solution)/shard_map/ppermute | solution.py:121
  110.1 12.8 %collective-permute-start.26 = (bf16[256,1024]{1,0:T(8,128)(2,1)S(1)}, bf16[256,1024]{1,0:T(8,128)(2,1)S(1)}, u32[]{:S(2)}, u32[]{:S(2)}) collective-permute-start(bf16[256,1024]{1,0:T(8,128)(2,1)S(1)} %get-tuple-element.163), channel_id=1, source_target_pairs={{0,16},{1,17},{2,18},{3,19},{4,20},{5,21},{6,22},{7,23},{8,24},{9,... | collective-permute-start | bytes 1572872 | tf_op jit(solution)/shard_map/ppermute | solution.py:121
  110.7 12.5 %collective-permute-start.27 = (bf16[256,1024]{1,0:T(8,128)(2,1)S(1)}, bf16[256,1024]{1,0:T(8,128)(2,1)S(1)}, u32[]{:S(2)}, u32[]{:S(2)}) collective-permute-start(bf16[256,1024]{1,0:T(8,128)(2,1)S(1)} %get-tuple-element.165), channel_id=1, source_target_pairs={{0,1},{1,0},{2,3},{3,2},{4,5},{5,4},{6,7},{7,6},{8,9},{9,8},{10,11... | collective-permute-start | bytes 1572872 | tf_op jit(solution)/shard_map/ppermute | solution.py:121
  121.5 10.5 %collective-permute-start.25 = (bf16[256,1280]{1,0:T(8,128)(2,1)S(1)}, bf16[256,1280]{1,0:T(8,128)(2,1)S(1)}, u32[]{:S(2)}, u32[]{:S(2)}) collective-permute-start(bf16[256,1280]{1,0:T(8,128)(2,1)S(1)} %get-tuple-element.162), channel_id=1, source_target_pairs={{0,8},{1,9},{2,10},{3,11},{4,12},{5,13},{6,14},{7,15},{8,0},{9,1},... | collective-permute-start | bytes 1966088 | tf_op jit(solution)/shard_map/ppermute | solution.py:121
  123.4 8.6 %collective-permute-start.28 = (bf16[128,1024]{1,0:T(8,128)(2,1)S(1)}, bf16[128,1024]{1,0:T(8,128)(2,1)S(1)}, u32[]{:S(2)}, u32[]{:S(2)}) collective-permute-start(bf16[128,1024]{1,0:T(8,128)(2,1)S(1)} %get-tuple-element.167), channel_id=1, source_target_pairs={{0,1},{1,0},{2,3},{3,2},{4,5},{5,4},{6,7},{7,6},{8,9},{9,8},{10,11... | collective-permute-start | bytes 786440 | tf_op jit(solution)/shard_map/ppermute | solution.py:121
  124.0 8.0 %collective-permute-start.29 = (bf16[128,1024]{1,0:T(8,128)(2,1)S(1)}, bf16[128,1024]{1,0:T(8,128)(2,1)S(1)}, u32[]{:S(2)}, u32[]{:S(2)}) collective-permute-start(bf16[128,1024]{1,0:T(8,128)(2,1)S(1)} %get-tuple-element.169), channel_id=1, source_target_pairs={{0,16},{1,17},{2,18},{3,19},{4,20},{5,21},{6,22},{7,23},{8,24},{9,... | collective-permute-start | bytes 786440 | tf_op jit(solution)/shard_map/ppermute | solution.py:121
  125.5 6.5 %collective-permute-start.24 = (bf16[16,512]{1,0:T(8,128)(2,1)S(1)}, bf16[16,512]{1,0:T(8,128)(2,1)S(1)}, u32[]{:S(2)}, u32[]{:S(2)}) collective-permute-start(bf16[16,512]{1,0:T(8,128)(2,1)S(1)} %get-tuple-element.160), channel_id=1, source_target_pairs={{8,0},{2,1},{10,2},{1,3},{9,4},{3,5},{11,6},{12,8},{6,9},{14,10},{... | collective-permute-start | bytes 49160 | tf_op jit(solution)/shard_map/ppermute | solution.py:852
  128.0 9.3 %collective-permute-start.23 = (bf16[256,512]{1,0:T(8,128)(2,1)S(1)}, bf16[256,512]{1,0:T(8,128)(2,1)S(1)}, u32[]{:S(2)}, u32[]{:S(2)}) collective-permute-start(bf16[256,512]{1,0:T(8,128)(2,1)S(1)} %get-tuple-element.159), channel_id=1, source_target_pairs={{0,0},{8,1},{2,2},{10,3},{1,4},{9,5},{3,6},{11,7},{4,8},{12,9},{6,... | collective-permute-start | bytes 786440 | tf_op jit(solution)/shard_map/ppermute | solution.py:851
  132.3 12.4 %collective-permute-start.33 = (bf16[64,2048]{1,0:T(8,128)(2,1)S(1)}, bf16[64,2048]{1,0:T(8,128)(2,1)S(1)}, u32[]{:S(2)}, u32[]{:S(2)}) collective-permute-start(bf16[64,2048]{1,0:T(8,128)(2,1)S(1)} %get-tuple-element.175), channel_id=1, source_target_pairs={{0,2},{1,3},{2,0},{3,1},{4,6},{5,7},{6,4},{7,5},{8,10},{9,11},{10,... | collective-permute-start | bytes 786440 | tf_op jit(solution)/shard_map/ppermute | solution.py:121
  133.7 7.2 %collective-permute-start.30 = (bf16[64,1280]{1,0:T(8,128)(2,1)S(1)}, bf16[64,1280]{1,0:T(8,128)(2,1)S(1)}, u32[]{:S(2)}, u32[]{:S(2)}) collective-permute-start(bf16[64,1280]{1,0:T(8,128)(2,1)S(1)} %get-tuple-element.171), channel_id=1, source_target_pairs={{0,1},{1,0},{2,3},{3,2},{4,5},{5,4},{6,7},{7,6},{8,9},{9,8},{10,11... | collective-permute-start | bytes 491528 | tf_op jit(solution)/shard_map/ppermute | solution.py:121
  133.7 7.2 %collective-permute-start.31 = (bf16[64,1280]{1,0:T(8,128)(2,1)S(1)}, bf16[64,1280]{1,0:T(8,128)(2,1)S(1)}, u32[]{:S(2)}, u32[]{:S(2)}) collective-permute-start(bf16[64,1280]{1,0:T(8,128)(2,1)S(1)} %get-tuple-element.172), channel_id=1, source_target_pairs={{0,16},{1,17},{2,18},{3,19},{4,20},{5,21},{6,22},{7,23},{8,24},{9,... | collective-permute-start | bytes 491528 | tf_op jit(solution)/shard_map/ppermute | solution.py:121
  134.7 9.9 %collective-permute-start.32 = (bf16[64,1280]{1,0:T(8,128)(2,1)S(1)}, bf16[64,1280]{1,0:T(8,128)(2,1)S(1)}, u32[]{:S(2)}, u32[]{:S(2)}) collective-permute-start(bf16[64,1280]{1,0:T(8,128)(2,1)S(1)} %get-tuple-element.173), channel_id=1, source_target_pairs={{0,17},{1,16},{2,19},{3,18},{4,21},{5,20},{6,23},{7,22},{8,25},{9,... | collective-permute-start | bytes 491528 | tf_op jit(solution)/shard_map/ppermute | solution.py:121
  144.8 12.5 %collective-permute-start.37 = (bf16[32,2048]{1,0:T(8,128)(2,1)S(1)}, bf16[32,2048]{1,0:T(8,128)(2,1)S(1)}, u32[]{:S(2)}, u32[]{:S(2)}) collective-permute-start(bf16[32,2048]{1,0:T(8,128)(2,1)S(1)} %get-tuple-element.181), channel_id=1, source_target_pairs={{0,4},{1,5},{2,6},{3,7},{4,0},{5,1},{6,2},{7,3},{8,12},{9,13},{10,... | collective-permute-start | bytes 393224 | tf_op jit(solution)/shard_map/ppermute | solution.py:121
  145.4 11.9 %collective-permute-start.34 = (bf16[16,1280]{1,0:T(8,128)(2,1)S(1)}, bf16[16,1280]{1,0:T(8,128)(2,1)S(1)}, u32[]{:S(2)}, u32[]{:S(2)}) collective-permute-start(bf16[16,1280]{1,0:T(8,128)(2,1)S(1)} %get-tuple-element.177), channel_id=1, source_target_pairs={{0,4},{1,5},{2,6},{3,7},{4,0},{5,1},{6,2},{7,3},{8,12},{9,13},{10,... | collective-permute-start | bytes 122888 | tf_op jit(solution)/shard_map/ppermute | solution.py:121
  147.8 9.5 %collective-permute-start.35 = (bf16[16,1280]{1,0:T(8,128)(2,1)S(1)}, bf16[16,1280]{1,0:T(8,128)(2,1)S(1)}, u32[]{:S(2)}, u32[]{:S(2)}) collective-permute-start(bf16[16,1280]{1,0:T(8,128)(2,1)S(1)} %get-tuple-element.178), channel_id=1, source_target_pairs={{0,2},{1,3},{2,0},{3,1},{4,6},{5,7},{6,4},{7,5},{8,10},{9,11},{10,... | collective-permute-start | bytes 122888 | tf_op jit(solution)/shard_map/ppermute | solution.py:121
  149.4 7.9 %collective-permute-start.36 = (bf16[16,1280]{1,0:T(8,128)(2,1)S(1)}, bf16[16,1280]{1,0:T(8,128)(2,1)S(1)}, u32[]{:S(2)}, u32[]{:S(2)}) collective-permute-start(bf16[16,1280]{1,0:T(8,128)(2,1)S(1)} %get-tuple-element.179), channel_id=1, source_target_pairs={{0,6},{1,7},{2,4},{3,5},{4,2},{5,3},{6,0},{7,1},{8,14},{9,15},{10,... | collective-permute-start | bytes 122888 | tf_op jit(solution)/shard_map/ppermute | solution.py:121
